TPU v7x, 32 devices: a whole 2x2x4 slice. The times are simulated.
32 devices in a mesh: seq: 8 (over y, x, core), head: 4 (over z).
Axes of the slice: x: 2, y: 2, z: 4, core: 2. Of those that a mesh axis runs over, the one named last changes fastest.
Arguments:
- queries: bfloat16 [6144, 5120], P('seq', 'head'), may hold values from -8000 to 8000
- keys: bfloat16 [6144, 5120], P('seq', 'head'), may hold values from -8000 to 8000
- values: bfloat16 [6144, 5120], P('seq', 'head'), may hold values from -6 to 6
- query_gain: float32 [5120], P('head'), may hold values from 0.1 to 1.9
- key_gain: float32 [5120], P('head'), may hold values from 0.1 to 1.9
- head_kind: int32 [40], P('head'), may hold values from 0 to 1, as said below
Outputs:
- attended: bfloat16 [6144, 5120], P('seq', 'head')
Inputs may be any that keep to these rules, and one draw needn't show every extreme that they name: `head_kind`: among the heads h * 10 to (h + 1) * 10 - 1, for each h, exactly 2 are temporal.
All inputs are finite; a program needn't handle non-finite values.
Results may differ from a plain program's by a relative error of at most 0.011.
Values may be sent and summed in bfloat16 or wider, within the bound.
No kernel may reach another device: no remote copies, remote signals or barrier semaphores. Data moves between devices by JAX's collectives and lax.ppermute only.
A program may use at most 128 MiB of HBM per device.

v0:
```python
import jax
import jax.numpy as jnp
from jax import lax
from jax.sharding import PartitionSpec as P

HEAD_DIM = 128
D = 5120
FRAME = 1024
OFFSET = 512


def passed_along(block, axis, distance):
    devices = range(lax.axis_size(axis))
    route = [((i - distance) % len(devices), i) for i in devices]
    return lax.ppermute(block, axis, route)


def scaled_rows(rows, sums, gain):
    return (rows.astype(jnp.float32) * lax.rsqrt(sums / D + 1e-06)[:, None] * gain[None, :]).astype(
        jnp.bfloat16
    )


def spatial_part(query_heads, key_heads, value_heads, first):
    rows = query_heads.shape[0]
    count = query_heads.shape[1]
    block = rows // 3
    frame_len = 4 * block
    factor = HEAD_DIM ** (-0.5)
    paired = jnp.stack([key_heads, value_heads])
    below = passed_along(paired, "seq", 1)
    above = passed_along(paired, "seq", -1)
    widened = jnp.concatenate([below, paired, above], axis=1)

    def per_head(which):
        query_one = lax.dynamic_index_in_dim(query_heads, which, 1, keepdims=False)
        key_one = lax.dynamic_index_in_dim(widened[0], which, 1, keepdims=False)
        value_one = lax.dynamic_index_in_dim(widened[1], which, 1, keepdims=False)
        outputs = []
        for part_index in range(3):
            video_start = first + OFFSET + part_index * block
            anchor = part_index * block - video_start % frame_len + rows
            key_frame = lax.dynamic_slice_in_dim(key_one, anchor, frame_len, 0)
            value_frame = lax.dynamic_slice_in_dim(value_one, anchor, frame_len, 0)
            query_block = query_one[part_index * block : (part_index + 1) * block]
            scores = (
                lax.dot_general(
                    query_block,
                    key_frame,
                    (((1,), (1,)), ((), ())),
                    preferred_element_type=jnp.float32,
                )
                * factor
            )
            top = jnp.max(scores, axis=1, keepdims=True)
            expo = jnp.exp(scores - top)
            weights = (expo / jnp.sum(expo, axis=1, keepdims=True)).astype(jnp.bfloat16)
            outputs.append(
                jnp.dot(weights, value_frame, preferred_element_type=jnp.float32).astype(
                    jnp.bfloat16
                )
            )
        return jnp.concatenate(outputs, axis=0)

    results = lax.map(per_head, jnp.arange(count, dtype=jnp.int32))
    return jnp.transpose(results, (1, 0, 2))


def temporal_folded(query_heads, key_flat, value_flat, first):
    rows, count, size = query_heads.shape
    factor = HEAD_DIM ** (-0.5)
    query_wide = query_heads.astype(jnp.float32)
    token_ids = first + jnp.arange(rows, dtype=jnp.int32)
    running = jnp.full((rows, count), -1e30, jnp.float32)
    total = jnp.zeros((rows, count), jnp.float32)
    summed = jnp.zeros((rows, count, size), jnp.float32)
    key_piece = lax.all_gather(key_flat, "seq", axis=0, tiled=True)
    value_piece = lax.all_gather(value_flat, "seq", axis=0, tiled=True)
    length = key_piece.shape[0]
    offsets = token_ids % FRAME
    for step in range(-(-length // FRAME)):
        place = offsets + step * FRAME
        valid = (place < length)[:, None]
        clipped = jnp.minimum(place, length - 1)
        key_rows = (
            jnp.take(key_piece, clipped, axis=0).reshape(rows, count, size).astype(jnp.float32)
        )
        value_rows = (
            jnp.take(value_piece, clipped, axis=0).reshape(rows, count, size).astype(jnp.float32)
        )
        scores = jnp.sum(query_wide * key_rows, axis=2) * factor
        scores = jnp.where(valid, scores, -1e30)
        newest = jnp.maximum(running, scores)
        shrink = jnp.exp(running - newest)
        weight = jnp.where(valid, jnp.exp(scores - newest), 0.0)
        total = total * shrink + weight
        summed = summed * shrink[:, :, None] + weight[:, :, None] * value_rows
        running = newest
    running, total, summed = (running, total, summed)
    return (summed / total[:, :, None]).astype(jnp.bfloat16)


def per_device(queries, keys, values, query_gain, key_gain, head_kind):
    rows = queries.shape[0]
    heads = head_kind.shape[0]
    temporal_count = heads // 5
    spatial_count = heads - temporal_count
    sq_query = jnp.sum(jnp.square(queries.astype(jnp.float32)), axis=1)
    sq_key = jnp.sum(jnp.square(keys.astype(jnp.float32)), axis=1)
    sq_query, sq_key = lax.psum((sq_query, sq_key), "head")
    query_norm = scaled_rows(queries, sq_query, query_gain).reshape(rows, heads, HEAD_DIM)
    key_norm = scaled_rows(keys, sq_key, key_gain).reshape(rows, heads, HEAD_DIM)
    value_heads = values.reshape(rows, heads, HEAD_DIM)
    ordering = jnp.argsort(head_kind, stable=True)
    inverse = jnp.argsort(ordering)
    spatial_ids = ordering[:spatial_count]
    temporal_ids = ordering[spatial_count:]
    index = lax.axis_index("seq")
    first = index * rows
    spatial_out = spatial_part(
        jnp.take(query_norm, spatial_ids, axis=1),
        jnp.take(key_norm, spatial_ids, axis=1),
        jnp.take(value_heads, spatial_ids, axis=1),
        first,
    )
    temporal_query = jnp.take(query_norm, temporal_ids, axis=1)
    temporal_key = jnp.take(key_norm, temporal_ids, axis=1).reshape(rows, temporal_count * HEAD_DIM)
    temporal_value = jnp.take(value_heads, temporal_ids, axis=1).reshape(
        rows, temporal_count * HEAD_DIM
    )
    temporal_out = temporal_folded(temporal_query, temporal_key, temporal_value, first)
    merged = jnp.concatenate([spatial_out, temporal_out], axis=1)
    return jnp.take(merged, inverse, axis=1).reshape(rows, heads * HEAD_DIM)


def solution(mesh):
    placed = (P("seq", "head"), P("seq", "head"), P("seq", "head"), P("head"), P("head"), P("head"))
    return jax.shard_map(
        per_device, mesh=mesh, in_specs=placed, out_specs=P("seq", "head"), check_vma=False
    )
```

profile of v0, /device:TPU:0, one launch (start us, length us, event | category | flops | bytes accessed | tf_op | source)
XLA Modules:
  0.0 450.3 jit_solution(17873117246657261430)
XLA Ops:
  6.5 2.7 copy.32
  10.9 2.7 copy.30
  14.1 13.7 %all-reduce = (f32[768]{0:T(1024)S(1)}, f32[768]{0:T(1024)S(1)}) all-reduce(f32[768]{0:T(1024)S(1)} %fusion.25, f32[768]{0:T(1024)S(1)} %fusion.22), channel_id=1, replica_groups=mesh['seq'=8,'head'=4] {'head'}, use_global_device_ids=true, to_apply=%region_5.0 | all-reduce | flops 1536 | bytes 12288 | tf_op jit(solution)/shard_map/psum | solution.py:110
  27.8 3.3 fusion.27
  31.2 4.0 copy.33
  36.5 4.0 copy.34
  40.4 4.0 copy.35
  50.9 3.5 gather_fusion.2
  54.4 3.5 gather_fusion.3
  59.7 2.8 copy.31
  64.5 4.0 select_bitcast_fusion.1
  83.8 73.7 %collective-permute-done.1 = bf16[2,768,8,128]{3,1,2,0:T(8,128)(2,1)} collective-permute-done((bf16[2,768,8,128]{3,1,2,0:T(8,128)(2,1)}, bf16[2,768,8,128]{3,1,2,0:T(8,128)(2,1)}, u32[]{:S(2)}, u32[]{:S(2)}) %collective-permute-start.1) | collective-permute-done | bytes 3145760 | tf_op jit(solution)/shard_map/ppermute | solution.py:15
  157.5 3.3 collective-permute-done
  160.9 7.3 %pad_maximum_fusion = bf16[2,2304,8,128]{3,1,2,0:T(8,128)(2,1)} fusion(bf16[2,768,8,128]{3,1,2,0:T(8,128)(2,1)} %collective-permute-done.1, bf16[1,768,8,128]{3,1,2,0:T(8,128)(2,1)S(1)} %get-tuple-element.333, bf16[1,768,8,128]{3,1,2,0:T(8,128)(2,1)S(1)} %get-tuple-element.332, bf16[2,768,8,128]{3,1,2,0:T(8,128)(2,1)} %collective-permute-done), kind=kLoop, calls=%fused_computation.57 | loop fusion | flops 37748736 | bytes 18874368 | tf_op jit(solution)/shard_map/concatenate | solution.py:33
  168.2 166.7 %while.13 = (s32[]{:T(128)}, bf16[8,768,128]{2,1,0:T(8,128)(2,1)}, s32[8]{0:T(128)S(1)}, bf16[768,8,128]{2,0,1:T(8,128)(2,1)}, bf16[2,2304,8,128]{3,1,2,0:T(8,12...) while((s32[]{:T(128)}, bf16[8,768,128]{2,1,0:T(8,128)(2,1)}, ...), condition=%wide.region_13.15_spmd, body=%wide.region_6.14_spmd.sunk | while | flops 408844800 | bytes 30689552 | solution.py:65
  168.2 8.4 %fusion.77 = (bf16[1,2304,8,128]{3,1,2,0:T(8,128)(2,1)}, bf16[1,2304,8,128]{3,1,2,0:T(8,128)(2,1)}) fusion(bf16[2,2304,8,128]{3,1,2,0:T(8,128)(2,1)} %get-tuple-element.454), kind=kLoop, calls=%fused_computation.189.clone.1 | loop fusion | bytes 18874368 | tf_op jit(solution)/shard_map/while/body/eval_jaxpr/slice | solution.py:38
  189.1 8.4 %fusion.77 = (bf16[1,2304,8,128]{3,1,2,0:T(8,128)(2,1)}, bf16[1,2304,8,128]{3,1,2,0:T(8,128)(2,1)}) fusion(bf16[2,2304,8,128]{3,1,2,0:T(8,128)(2,1)} %get-tuple-element.454), kind=kLoop, calls=%fused_computation.189.clone.1 | loop fusion | bytes 18874368 | tf_op jit(solution)/shard_map/while/body/eval_jaxpr/slice | solution.py:38
  209.9 8.4 %fusion.77 = (bf16[1,2304,8,128]{3,1,2,0:T(8,128)(2,1)}, bf16[1,2304,8,128]{3,1,2,0:T(8,128)(2,1)}) fusion(bf16[2,2304,8,128]{3,1,2,0:T(8,128)(2,1)} %get-tuple-element.454), kind=kLoop, calls=%fused_computation.189.clone.1 | loop fusion | bytes 18874368 | tf_op jit(solution)/shard_map/while/body/eval_jaxpr/slice | solution.py:38
  230.7 8.4 %fusion.77 = (bf16[1,2304,8,128]{3,1,2,0:T(8,128)(2,1)}, bf16[1,2304,8,128]{3,1,2,0:T(8,128)(2,1)}) fusion(bf16[2,2304,8,128]{3,1,2,0:T(8,128)(2,1)} %get-tuple-element.454), kind=kLoop, calls=%fused_computation.189.clone.1 | loop fusion | bytes 18874368 | tf_op jit(solution)/shard_map/while/body/eval_jaxpr/slice | solution.py:38
  251.6 8.4 %fusion.77 = (bf16[1,2304,8,128]{3,1,2,0:T(8,128)(2,1)}, bf16[1,2304,8,128]{3,1,2,0:T(8,128)(2,1)}) fusion(bf16[2,2304,8,128]{3,1,2,0:T(8,128)(2,1)} %get-tuple-element.454), kind=kLoop, calls=%fused_computation.189.clone.1 | loop fusion | bytes 18874368 | tf_op jit(solution)/shard_map/while/body/eval_jaxpr/slice | solution.py:38
  272.4 8.4 %fusion.77 = (bf16[1,2304,8,128]{3,1,2,0:T(8,128)(2,1)}, bf16[1,2304,8,128]{3,1,2,0:T(8,128)(2,1)}) fusion(bf16[2,2304,8,128]{3,1,2,0:T(8,128)(2,1)} %get-tuple-element.454), kind=kLoop, calls=%fused_computation.189.clone.1 | loop fusion | bytes 18874368 | tf_op jit(solution)/shard_map/while/body/eval_jaxpr/slice | solution.py:38
  293.3 8.4 %fusion.77 = (bf16[1,2304,8,128]{3,1,2,0:T(8,128)(2,1)}, bf16[1,2304,8,128]{3,1,2,0:T(8,128)(2,1)}) fusion(bf16[2,2304,8,128]{3,1,2,0:T(8,128)(2,1)} %get-tuple-element.454), kind=kLoop, calls=%fused_computation.189.clone.1 | loop fusion | bytes 18874368 | tf_op jit(solution)/shard_map/while/body/eval_jaxpr/slice | solution.py:38
  314.1 8.4 %fusion.77 = (bf16[1,2304,8,128]{3,1,2,0:T(8,128)(2,1)}, bf16[1,2304,8,128]{3,1,2,0:T(8,128)(2,1)}) fusion(bf16[2,2304,8,128]{3,1,2,0:T(8,128)(2,1)} %get-tuple-element.454), kind=kLoop, calls=%fused_computation.189.clone.1 | loop fusion | bytes 18874368 | tf_op jit(solution)/shard_map/while/body/eval_jaxpr/slice | solution.py:38
  334.9 4.4 gather_fusion.15
  339.4 4.4 gather_fusion.16
  345.1 2.4 copy.55
  349.8 3.4 gather_fusion.9
  353.2 5.3 %gather_fusion.10 = bf16[768,256]{1,0:T(8,128)(2,1)} fusion(bf16[6144,256]{1,0:T(8,128)(2,1)} %all-gather.5.cloned.1.call-done, s32[1024]{0:T(1024)} %pad_clamp_fusion.5), kind=kCustom, calls=%fused_computation.9.clone | custom fusion | bytes 789504 | tf_op jit(solution)/shard_map/jit(_take)/gather | solution.py:89
  358.5 2.4 select_convert_fusion.4
  365.6 3.3 gather_fusion.11
  368.9 5.2 %gather_fusion.12 = bf16[768,256]{1,0:T(8,128)(2,1)} fusion(bf16[6144,256]{1,0:T(8,128)(2,1)} %all-gather.5.cloned.1.call-done, s32[1024]{0:T(1024)S(1)} %pad_clamp_fusion.4), kind=kCustom, calls=%fused_computation.11.clone | custom fusion | bytes 789504 | tf_op jit(solution)/shard_map/jit(_take)/gather | solution.py:89
  374.0 2.5 select_convert_fusion.3
  381.1 3.3 gather_fusion.13
  384.4 5.1 %gather_fusion.14 = bf16[768,256]{1,0:T(8,128)(2,1)} fusion(bf16[6144,256]{1,0:T(8,128)(2,1)} %all-gather.5.cloned.1.call-done, s32[1024]{0:T(1024)S(1)} %pad_clamp_fusion.3), kind=kCustom, calls=%fused_computation.13.clone | custom fusion | bytes 789504 | tf_op jit(solution)/shard_map/jit(_take)/gather | solution.py:89
  389.5 2.5 select_convert_fusion.2
  396.6 3.3 gather_fusion.17
  399.9 5.1 %gather_fusion.18 = bf16[768,256]{1,0:T(8,128)(2,1)} fusion(bf16[6144,256]{1,0:T(8,128)(2,1)} %all-gather.5.cloned.1.call-done, s32[1024]{0:T(1024)S(1)} %pad_clamp_fusion.1), kind=kCustom, calls=%fused_computation.17.clone | custom fusion | bytes 789504 | tf_op jit(solution)/shard_map/jit(_take)/gather | solution.py:89
  405.0 2.5 select_convert_fusion
  407.5 2.4 copy.58
  409.9 2.4 copy.59
  412.3 3.3 gather_fusion.6
  415.5 4.4 gather_fusion.8
  421.4 2.4 copy.40
  423.8 2.4 copy.41
  426.3 2.9 fusion.32
  429.5 3.1 fusion.36
  435.1 2.7 copy.61
  439.5 4.0 copy.62
  (217 shorter events, 135.4 us)
Async XLA Ops:
  6.5 328.4 %all-gather.3.cloned.1.call-start = ((), (), s32[]{:S(2)}) async-start(), calls=%async_computation | async-start | bytes 3538944 | tf_op jit(solution)/shard_map/all_gather | solution.py:77
  9.2 1.3 copy-start.1
  13.6 14.2 %copy-start.21 = (f32[1280]{0:T(1024)S(1)}, f32[1280]{0:T(1024)}, u32[]{:S(2)}) copy-start(f32[1280]{0:T(1024)} %param.18) | copy-start | bytes 15364
  31.2 4.0 copy-start.31
  36.5 12.3 %copy-start.29 = (pred[2]{0:T(512)(128)(4,1)}, pred[2]{0:T(512)(128)(4,1)S(1)}, u32[]{:S(2)}) copy-start(pred[2]{0:T(512)(128)(4,1)S(1)} %get-tuple-element.310) | copy-start | bytes 10
  50.8 288.6 %all-gather.5.cloned.1.call-start = ((), (), s32[]{:S(2)}) async-start(), calls=%async_computation.1 | async-start | bytes 3538944 | tf_op jit(solution)/shard_map/all_gather | solution.py:78
  54.4 3.5 copy-start.22
  62.5 1.9 copy-start.2
  70.4 87.1 %collective-permute-start.1 = (bf16[2,768,8,128]{3,1,2,0:T(8,128)(2,1)}, bf16[2,768,8,128]{3,1,2,0:T(8,128)(2,1)}, u32[]{:S(2)}, u32[]{:S(2)}) collective-permute-start(bf16[2,768,8,128]{3,1,2,0:T(8,128)(2,1)} %pad_maximum_fusion.1), channel_id=1, source_target_pairs={{4,0},{8,4},{12,8},{16,12},{20,16},{24,20},{28,24},{0,28},{5,1},{9... | collective-permute-start | bytes 9437192 | tf_op jit(solution)/shard_map/ppermute | solution.py:15
  70.4 90.5 %collective-permute-start = (bf16[2,768,8,128]{3,1,2,0:T(8,128)(2,1)}, bf16[2,768,8,128]{3,1,2,0:T(8,128)(2,1)}, u32[]{:S(2)}, u32[]{:S(2)}) collective-permute-start(bf16[2,768,8,128]{3,1,2,0:T(8,128)(2,1)} %pad_maximum_fusion.1), channel_id=1, source_target_pairs={{28,0},{0,4},{4,8},{8,12},{12,16},{16,20},{20,24},{24,28},{29,1},{... | collective-permute-start | bytes 9437192 | tf_op jit(solution)/shard_map/ppermute | solution.py:15
  168.2 166.7 %copy-start.15 = (s32[1024]{0:T(1024)S(1)}, s32[1024]{0:T(1024)}, u32[]{:S(2)}) copy-start(s32[1024]{0:T(1024)} %pad_clamp_fusion.2) | copy-start | bytes 12292
  339.3 4.4 copy-start.28
  345.1 4.7 %copy-start = (bf16[6144,256]{1,0:T(8,128)(2,1)S(1)}, bf16[6144,256]{1,0:T(8,128)(2,1)}, u32[]{:S(2)}) copy-start(bf16[6144,256]{1,0:T(8,128)(2,1)} %all-gather.3.cloned.1.call-done) | copy-start | bytes 9437188
  384.4 5.1 %copy-start.27 = (pred[768]{0:T(1024)(128)(4,1)S(1)}, pred[768]{0:T(1024)(128)(4,1)}, u32[]{:S(2)}) copy-start(pred[768]{0:T(1024)(128)(4,1)} %get-tuple-element.347) | copy-start | bytes 2308
  399.9 5.1 %copy-start.26 = (pred[768]{0:T(1024)(128)(4,1)S(1)}, pred[768]{0:T(1024)(128)(4,1)}, u32[]{:S(2)}) copy-start(pred[768]{0:T(1024)(128)(4,1)} %get-tuple-element.345) | copy-start | bytes 2308
  415.5 4.5 copy-start.14
  415.5 4.5 copy-start.25
  421.3 4.8 %copy-start.3 = (f32[768,2,128]{2,0,1:T(8,128)S(1)}, f32[768,2,128]{2,0,1:T(8,128)}, u32[]{:S(2)}) copy-start(f32[768,2,128]{2,0,1:T(8,128)} %copy.56) | copy-start | bytes 2359300
  421.3 4.8 %copy-start.4 = (f32[768,2,128]{2,0,1:T(8,128)S(1)}, f32[768,2,128]{2,0,1:T(8,128)}, u32[]{:S(2)}) copy-start(f32[768,2,128]{2,0,1:T(8,128)} %copy.47) | copy-start | bytes 2359300
  421.3 4.8 %copy-start.5 = (f32[768,2,128]{2,0,1:T(8,128)S(1)}, f32[768,2,128]{2,0,1:T(8,128)}, u32[]{:S(2)}) copy-start(f32[768,2,128]{2,0,1:T(8,128)} %copy.50) | copy-start | bytes 2359300
  421.3 4.8 %copy-start.6 = (f32[768,2,128]{2,0,1:T(8,128)S(1)}, f32[768,2,128]{2,0,1:T(8,128)}, u32[]{:S(2)}) copy-start(f32[768,2,128]{2,0,1:T(8,128)} %copy.53) | copy-start | bytes 2359300
  421.3 4.8 %copy-start.30 = (pred[2]{0:T(512)(128)(4,1)S(1)}, pred[2]{0:T(512)(128)(4,1)}, u32[]{:S(2)}) copy-start(pred[2]{0:T(512)(128)(4,1)} %copy-done.29) | copy-start | bytes 10
  426.2 3.0 copy-start.16
  426.2 3.0 copy-start.17
  426.2 3.0 copy-start.18
  426.2 3.0 copy-start.19
  426.2 3.1 copy-start.23
  426.2 3.1 copy-start.24
  426.3 3.2 copy-start.7
  426.3 3.2 copy-start.8
  426.3 3.2 copy-start.9
  426.3 3.2 copy-start.10
  426.3 3.2 copy-start.11
  426.3 3.2 copy-start.12
  429.5 3.1 copy-start.13
  435.1 2.7 copy-start.20
Sparse Core Ops, SparseCore 0:
  50.9 36.5 all-gather.2
  89.4 47.2 all-gather.4
where the time goes:
time: 454 us; the launch traced here: 450 us
  local copies, waits for them, and re-layouts  200 us (44%)
  waiting for transfers between devices  77.1 us (17%)
  matrix products  65.4 us (14%)
  other arithmetic  62.8 us (14%)
  loops' own time  16.4 us (4%)
  between operations  14 us (3%)
  blocking collectives  13.7 us (3%)
    ppermute x2, waiting for transfers between devices, passed_along(): return lax.ppermute(block, axis, route)  77.1 us
    slice x8, local copies, waits for them, and re-layouts, per_head(): value_one = lax.dynamic_index_in_dim(widened[1], which, 1, keepdims=False)  66.8 us
    dot_general x24, matrix products, per_head(): lax.dot_general(query_block, key_frame, (((1,), (1,)), ((), ())), preferr...  33.2 us
    dot_general x24, matrix products, per_head(): jnp.dot(weights, value_frame, preferred_element_type=jnp.float32)  32.2 us
    gather x6, local copies, waits for them, and re-layouts, temporal_folded(): jnp.take(value_piece, clipped, axis=0).reshape(rows, count, size)  29.6 us
    convert_element_type x12, local copies, waits for them, and re-layouts, temporal_folded(): jnp.take(key_piece, clipped, axis=0).reshape(rows, count, size)  28.1 us
    gather x6, local copies, waits for them, and re-layouts, temporal_folded(): jnp.take(key_piece, clipped, axis=0).reshape(rows, count, size)  20.9 us
    another operation x1, loops' own time, spatial_part(): results = lax.map(per_head, jnp.arange(count, dtype=jnp.int32))  16.4 us
  transfers between devices with their start and end apart: 4, of which 2 were waited for; matrix products, arithmetic and copies ran while one was open for 43% of the time, Pallas kernels for 0%

commit v1 on v0

v1 whole, which is shorter than its diff:
```python
import functools
import math

import jax
import jax.numpy as jnp
from jax import lax
from jax.experimental import pallas as pl
from jax.experimental.pallas import tpu as pltpu
from jax.sharding import PartitionSpec as P

HEAD_DIM = 128
D = 5120
FRAME = 1024
OFFSET = 512
CHUNKS = 2
VMEM = 48 * 1024 * 1024
LOW = -1e30
FACTOR = math.log2(math.e) / math.sqrt(HEAD_DIM)
F32 = jnp.float32
BF16 = jnp.bfloat16


def cost(flops, moved, exps=0):
    return pl.CostEstimate(flops=flops, bytes_accessed=moved, transcendentals=exps)


def params():
    return pltpu.CompilerParams(vmem_limit_bytes=VMEM)


def permuted(block, axis, route):
    return lax.ppermute(block, axis, route)


def shape(dims, dtype=BF16):
    return jax.ShapeDtypeStruct(dims, dtype)


def meta_of(head_kind, index, heads, spatial, temporal):
    is_temporal = head_kind == 1
    place = jnp.arange(heads, dtype=jnp.int32)
    before = jnp.sum(
        jnp.where((place[None, :] < place[:, None]) & is_temporal[None, :], 1, 0), axis=1
    ).astype(jnp.int32)
    turn = index % 2 if temporal == 2 else 0
    rank = jnp.where(is_temporal, spatial + (before ^ turn), place - before)
    order = jnp.sum(jnp.where(rank[None, :] == place[:, None], place[None, :], 0), axis=1)
    own = jnp.stack([index % 4, index % 2, index // 2])
    return jnp.concatenate([order, own]).astype(jnp.int32)


def cross_start(meta, heads, block):
    return pl.multiple_of(jnp.where(meta[heads] == 0, 0, block), block)


def sums_kernel(heads, spatial, block, meta, q_ref, k_ref, v_ref, sums_ref, vs_ref, vx_ref, sq_q, sq_k):
    h = pl.program_id(0)
    q = q_ref[...].astype(F32)
    k = k_ref[...].astype(F32)

    @pl.when(h == 0)
    def _():
        sq_q[...] = q * q
        sq_k[...] = k * k

    @pl.when(h > 0)
    def _():
        sq_q[...] += q * q
        sq_k[...] += k * k

    @pl.when(h < spatial)
    def _():
        vs_ref[0] = v_ref[...]
        vx_ref[0] = v_ref[pl.ds(cross_start(meta, heads, block), 2 * block), :]

    @pl.when(h == heads - 1)
    def _():
        ones = jnp.ones((8, HEAD_DIM), F32)
        for i, acc in enumerate((sq_q, sq_k)):
            total = lax.dot_general(
                ones,
                acc[...],
                (((1,), (1,)), ((), ())),
                precision=lax.Precision.HIGHEST,
                preferred_element_type=F32,
            )
            sums_ref[i : i + 1, :] = total[0:1, :]


def sums_call(meta, queries, keys, values, heads, spatial, block):
    rows = queries.shape[0]
    last = spatial - 1
    column = lambda h, m: (0, m[h])
    column_v = lambda h, m: (0, m[jnp.minimum(h, last)])
    by_head = lambda h, m: (jnp.minimum(h, last), 0, 0)
    one = (rows, HEAD_DIM)
    return pl.pallas_call(
        functools.partial(sums_kernel, heads, spatial, block),
        grid_spec=pltpu.PrefetchScalarGridSpec(
            num_scalar_prefetch=1,
            grid=(heads,),
            in_specs=[pl.BlockSpec(one, column), pl.BlockSpec(one, column), pl.BlockSpec(one, column_v)],
            out_specs=[
                pl.BlockSpec((2, rows), lambda h, m: (0, 0)),
                pl.BlockSpec((1,) + one, by_head),
                pl.BlockSpec((1, 2 * block, HEAD_DIM), by_head),
            ],
            scratch_shapes=[pltpu.VMEM(one, F32), pltpu.VMEM(one, F32)],
        ),
        out_shape=[
            shape((2, rows), F32),
            shape((spatial, rows, HEAD_DIM)),
            shape((spatial, 2 * block, HEAD_DIM)),
        ],
        compiler_params=params(),
        cost_estimate=cost(6 * queries.size, 10 * queries.size),
        name="sums",
    )(meta, queries, keys, values)


def norm_kernel(heads, spatial, block, parts, meta, q_ref, k_ref, v_ref, gq_ref, gk_ref, *refs):
    sums, refs = refs[:parts], refs[parts:]
    qs_ref, ks_ref = refs[:2]
    kx_refs = refs[2 : 2 + CHUNKS]
    t_refs = refs[2 + CHUNKS : -2]
    scale_q, scale_k = refs[-2:]
    h = pl.program_id(0)
    rows = q_ref.shape[0]

    @pl.when(h == 0)
    def _():
        total = sums[0][...]
        for other in sums[1:]:
            total = total + other[...]
        inverse = lax.rsqrt(total / D + 1e-06)
        for i, into in enumerate((scale_q, scale_k)):
            into[...] = jnp.transpose(jnp.broadcast_to(inverse[i : i + 1, :], (HEAD_DIM, rows)))

    q = (q_ref[...].astype(F32) * scale_q[...] * (gq_ref[...] * FACTOR)).astype(BF16)
    k = (k_ref[...].astype(F32) * scale_k[...] * gk_ref[...]).astype(BF16)

    @pl.when(h < spatial)
    def _():
        qs_ref[0] = q
        ks_ref[0] = k

    each = spatial // CHUNKS
    for c in range(CHUNKS):

        @pl.when((h >= c * each) & (h < (c + 1) * each))
        def _():
            kx_refs[c][0] = ks_ref[0, pl.ds(cross_start(meta, heads, block), 2 * block), :]

    for j, t_ref in enumerate(t_refs):

        @pl.when(h == spatial + j)
        def _():
            t_ref[0] = q
            t_ref[1] = k
            t_ref[2] = v_ref[...]


def norm_call(meta, queries, keys, values, query_gain, key_gain, sums, heads, spatial, block):
    rows = queries.shape[0]
    last = spatial - 1
    each = spatial // CHUNKS
    temporal = heads - spatial
    one = (rows, HEAD_DIM)
    column = lambda h, m: (0, m[h])
    column_v = lambda h, m: (0, m[jnp.maximum(h, spatial)])
    by_head = lambda h, m: (jnp.minimum(h, last), 0, 0)
    whole = lambda h, m: (0, 0)

    def by_chunk(c):
        return lambda h, m: (jnp.clip(h - c * each, 0, each - 1), 0, 0)

    return pl.pallas_call(
        functools.partial(norm_kernel, heads, spatial, block, len(sums)),
        grid_spec=pltpu.PrefetchScalarGridSpec(
            num_scalar_prefetch=1,
            grid=(heads,),
            in_specs=[
                pl.BlockSpec(one, column),
                pl.BlockSpec(one, column),
                pl.BlockSpec(one, column_v),
                pl.BlockSpec((1, HEAD_DIM), column),
                pl.BlockSpec((1, HEAD_DIM), column),
            ]
            + [pl.BlockSpec((2, rows), whole)] * len(sums),
            out_specs=[pl.BlockSpec((1,) + one, by_head)] * 2
            + [pl.BlockSpec((1, 2 * block, HEAD_DIM), by_chunk(c)) for c in range(CHUNKS)]
            + [pl.BlockSpec((3,) + one, lambda h, m: (0, 0, 0))] * temporal,
            scratch_shapes=[pltpu.VMEM(one, F32), pltpu.VMEM(one, F32)],
        ),
        out_shape=[shape((spatial,) + one)] * 2
        + [shape((each, 2 * block, HEAD_DIM))] * CHUNKS
        + [shape((3,) + one)] * temporal,
        compiler_params=params(),
        cost_estimate=cost(10 * queries.size, 12 * queries.size),
        name="norms",
    )(meta, queries, keys, values, query_gain.reshape(1, -1), key_gain.reshape(1, -1), *sums)


def attend(query, parts):
    scores = [
        lax.dot_general(query, k, (((1,), (1,)), ((), ())), preferred_element_type=F32)
        for k, _ in parts
    ]
    top = functools.reduce(jnp.maximum, [jnp.max(s, axis=1, keepdims=True) for s in scores])
    total = None
    for s, (_, v) in zip(scores, parts):
        wide = jnp.concatenate([v, jnp.ones_like(v)], axis=1)
        part = jnp.dot(jnp.exp2(s - top).astype(BF16), wide, preferred_element_type=F32)
        total = part if total is None else total + part
    return (total[:, :HEAD_DIM] / total[:, HEAD_DIM:]).astype(BF16)


def near_kernel(heads, block, meta, q_ref, k_ref, v_ref, kp_ref, vp_ref, o_ref):
    kind = meta[heads]
    apart = pl.multiple_of(jnp.where((kind == 0) | (kind == 1), 2 * block, 0), block)
    one = pl.ds(apart, block)

    @pl.when((kind == 1) | (kind == 2))
    def _():
        for part in range(3):
            rows = pl.ds(part * block, block)
            o_ref[rows, :] = attend(
                q_ref[0, rows, :],
                [(k_ref[0], v_ref[0]), (kp_ref[0, one, :], vp_ref[0, one, :])],
            )

    @pl.when((kind == 0) | (kind == 3))
    def _():
        o_ref[one, :] = attend(
            q_ref[0, one, :],
            [(kp_ref[0], vp_ref[0]), (k_ref[0, one, :], v_ref[0, one, :])],
        )


def near_call(meta, q, k, v, k_pair, v_pair, heads, block):
    spatial, rows, _ = q.shape
    by_head = pl.BlockSpec((1, rows, HEAD_DIM), lambda h, m: (h, 0, 0))
    pairs = spatial * rows * 4 * block
    return pl.pallas_call(
        functools.partial(near_kernel, heads, block),
        grid_spec=pltpu.PrefetchScalarGridSpec(
            num_scalar_prefetch=1,
            grid=(spatial,),
            in_specs=[by_head] * 5,
            out_specs=pl.BlockSpec((rows, HEAD_DIM), lambda h, m: (0, m[h])),
        ),
        out_shape=shape((rows, heads * HEAD_DIM)),
        compiler_params=params(),
        cost_estimate=cost(4 * pairs * HEAD_DIM, 12 * q.size, pairs),
        name="near",
    )(meta, q, k, v, k_pair, v_pair)


def far_kernel(heads, block, meta, q_ref, k_ref, v_ref, kx_ref, vx_ref, have_ref, o_ref):
    kind = meta[heads]
    start = cross_start(meta, heads, block)
    o_ref[...] = have_ref[...]

    @pl.when((kind == 0) | (kind == 3))
    def _():
        own = pl.ds(start, 2 * block)
        for part in range(2):
            rows = pl.ds(pl.multiple_of(start + part * block, block), block)
            o_ref[rows, :] = attend(
                q_ref[0, rows, :],
                [(k_ref[0, own, :], v_ref[0, own, :]), (kx_ref[0], vx_ref[0])],
            )


def far_call(meta, q, k, v, k_cross, v_cross, have, first, heads, block):
    rows = q.shape[1]
    count = k_cross.shape[0]
    by_head = pl.BlockSpec((1, rows, HEAD_DIM), lambda h, m: (h + first, 0, 0))
    column = pl.BlockSpec((rows, HEAD_DIM), lambda h, m: (0, m[h + first]))
    pairs = count * 2 * block * 4 * block
    return pl.pallas_call(
        functools.partial(far_kernel, heads, block),
        grid_spec=pltpu.PrefetchScalarGridSpec(
            num_scalar_prefetch=1,
            grid=(count,),
            in_specs=[
                by_head,
                by_head,
                by_head,
                pl.BlockSpec((1, 2 * block, HEAD_DIM), lambda h, m: (h, 0, 0)),
                pl.BlockSpec((1, 2 * block, HEAD_DIM), lambda h, m: (h + first, 0, 0)),
                column,
            ],
            out_specs=column,
        ),
        out_shape=shape(have.shape),
        input_output_aliases={6: 0},
        compiler_params=params(),
        cost_estimate=cost(4 * pairs * HEAD_DIM, 14 * count * rows * HEAD_DIM, pairs),
        name="far",
    )(meta, q, k, v, k_cross, v_cross, have)


def place_kernel(meta, *refs):
    parts, o_ref = refs[:-2], refs[-1]
    j = pl.program_id(0)
    for i, part in enumerate(parts):

        @pl.when(j == i)
        def _():
            o_ref[...] = part[...]


def place_call(meta, parts, have, spatial):
    rows = have.shape[0]
    count = len(parts)
    return pl.pallas_call(
        place_kernel,
        grid_spec=pltpu.PrefetchScalarGridSpec(
            num_scalar_prefetch=1,
            grid=(count,),
            in_specs=[pl.BlockSpec((rows, HEAD_DIM), lambda j, m: (0, 0))] * count
            + [pl.BlockSpec(memory_space=pl.ANY)],
            out_specs=pl.BlockSpec((rows, HEAD_DIM), lambda j, m: (0, m[spatial + j])),
        ),
        out_shape=shape(have.shape),
        input_output_aliases={1 + count: 0},
        compiler_params=params(),
        cost_estimate=cost(0, 4 * count * rows * HEAD_DIM),
        name="place",
    )(meta, *parts, have)


PIECE = 128
CHIPS = 4
TURNS = 3


def deal_kernel(heads, meta, keep_ref, got_ref, *refs):
    outs, held, sems = refs[:CHIPS], refs[CHIPS], refs[CHIPS + 1]
    core = meta[heads + 1]
    chip = meta[heads + 2]
    rows = keep_ref.shape[1]
    ins = [
        pltpu.make_async_copy(
            ref, held.at[:, pl.ds(pl.multiple_of(at * rows, rows), rows), :], sems.at[i]
        )
        for i, (ref, at) in enumerate(((keep_ref, core), (got_ref, 1 - core)))
    ]
    for copy in ins:
        copy.start()
    for copy in ins:
        copy.wait()
    copies = []
    for turn in range(CHIPS):
        owner = chip ^ turn
        for g in range(TURNS):
            at = pl.multiple_of((owner + CHIPS * g) * PIECE, PIECE)
            copies.append(
                pltpu.make_async_copy(
                    held.at[:, pl.ds(at, PIECE), :],
                    outs[turn].at[:, g],
                    sems.at[2 + turn * TURNS + g],
                )
            )
    for copy in copies:
        copy.start()
    for copy in copies:
        copy.wait()


def deal_call(meta, keep, got, heads):
    return pl.pallas_call(
        functools.partial(deal_kernel, heads),
        in_specs=[pl.BlockSpec(memory_space=pltpu.SMEM)] + [pl.BlockSpec(memory_space=pl.ANY)] * 2,
        out_specs=[pl.BlockSpec(memory_space=pl.ANY)] * CHIPS,
        out_shape=[shape((3, TURNS, PIECE, HEAD_DIM))] * CHIPS,
        scratch_shapes=[
            pltpu.VMEM((3, 2 * keep.shape[1], HEAD_DIM), BF16),
            pltpu.SemaphoreType.DMA((2 + CHIPS * TURNS,)),
        ],
        compiler_params=params(),
        cost_estimate=cost(0, 8 * keep.size),
        name="deal",
    )(meta, keep, got)


def gather_kernel(heads, meta, *refs):
    ins, (keep_ref, send_ref, held, sems) = refs[:CHIPS], refs[CHIPS:]
    core = meta[heads + 1]
    chip = meta[heads + 2]
    pieces = CHIPS * TURNS // 2
    copies = []
    for turn in range(CHIPS):
        owner = chip ^ turn
        for g in range(TURNS):
            copies.append(
                pltpu.make_async_copy(
                    ins[turn].at[g], held.at[owner + CHIPS * g], sems.at[turn * TURNS + g]
                )
            )
    for copy in copies:
        copy.start()
    for copy in copies:
        copy.wait()
    outs = [
        pltpu.make_async_copy(held.at[pl.ds(at * pieces, pieces)], ref, sems.at[i])
        for i, (ref, at) in enumerate(((keep_ref, core), (send_ref, 1 - core)))
    ]
    for copy in outs:
        copy.start()
    for copy in outs:
        copy.wait()


def gather_call(meta, parts, heads):
    pieces = CHIPS * TURNS // 2
    return pl.pallas_call(
        functools.partial(gather_kernel, heads),
        in_specs=[pl.BlockSpec(memory_space=pltpu.SMEM)]
        + [pl.BlockSpec(memory_space=pl.ANY)] * CHIPS,
        out_specs=[pl.BlockSpec(memory_space=pl.ANY)] * 2,
        out_shape=[shape((pieces, PIECE, HEAD_DIM))] * 2,
        scratch_shapes=[
            pltpu.VMEM((2 * pieces, PIECE, HEAD_DIM), BF16),
            pltpu.SemaphoreType.DMA((CHIPS * TURNS,)),
        ],
        compiler_params=params(),
        cost_estimate=cost(0, 8 * pieces * PIECE * HEAD_DIM),
        name="gather",
    )(meta, *parts)


GROUPS = (
    ((0, 1), (2, 1), (1, 0), (1, 2), (3, 0), (3, 2)),
    ((0, 0), (0, 2), (2, 0), (2, 2), (1, 1), (3, 1)),
)


def frames_kernel(*refs):
    ins, outs = refs[:CHIPS], refs[CHIPS:]
    row = lax.broadcasted_iota(jnp.int32, (PIECE, PIECE), 0)
    col = lax.broadcasted_iota(jnp.int32, (PIECE, PIECE), 1)
    off = jnp.where(row == col, 0.0, LOW)
    for group in GROUPS:
        key = jnp.concatenate([ins[s][1, g] for s, g in group], axis=0)
        value = jnp.concatenate([ins[s][2, g] for s, g in group], axis=0)
        wide = jnp.concatenate([value, jnp.ones_like(value)], axis=1)
        mask = jnp.concatenate([off] * len(group), axis=1)
        for s, g in group:
            scores = (
                lax.dot_general(
                    ins[s][0, g], key, (((1,), (1,)), ((), ())), preferred_element_type=F32
                )
            )
            scores = jnp.where(mask == 0.0, scores, LOW)
            top = jnp.max(scores, axis=1, keepdims=True)
            weights = jnp.exp2(scores - top).astype(BF16)
            total = jnp.dot(weights, wide, preferred_element_type=F32)
            outs[s][g] = (total[:, :HEAD_DIM] / total[:, HEAD_DIM:]).astype(BF16)


def frames_call(parts):
    size = TURNS * PIECE * HEAD_DIM
    return pl.pallas_call(
        frames_kernel,
        in_specs=[pl.BlockSpec(memory_space=pltpu.VMEM)] * CHIPS,
        out_specs=[pl.BlockSpec(memory_space=pltpu.VMEM)] * CHIPS,
        out_shape=[shape((TURNS, PIECE, HEAD_DIM))] * CHIPS,
        compiler_params=params(),
        cost_estimate=cost(4 * 12 * PIECE * 6 * PIECE * HEAD_DIM, 32 * size, 72 * PIECE * PIECE),
        name="frames",
    )(*parts)


def temporal_dealt(meta, keep, send, heads, devices):
    pair = [(i, i ^ 1) for i in range(devices)]
    routes = [[(i, i ^ (2 * turn)) for i in range(devices)] for turn in range(1, CHIPS)]
    got = permuted(send, "seq", pair)
    dealt = deal_call(meta, keep, got, heads)
    arrived = [dealt[0]] + [permuted(p, "seq", r) for p, r in zip(dealt[1:], routes)]
    results = frames_call(arrived)
    back = [results[0]] + [permuted(p, "seq", r) for p, r in zip(results[1:], routes)]
    own, other = gather_call(meta, back, heads)
    other = permuted(other, "seq", pair)
    return [own.reshape(-1, HEAD_DIM), other.reshape(-1, HEAD_DIM)]


def temporal_folded(parts, first):
    rows = parts[0].shape[1]
    stacked = jnp.stack(parts, axis=2).astype(F32)
    query = stacked[0]
    flat = jnp.stack(parts, axis=2).astype(BF16)
    count = len(parts)
    key_all = lax.all_gather(flat[1].reshape(rows, -1), "seq", axis=0, tiled=True)
    value_all = lax.all_gather(flat[2].reshape(rows, -1), "seq", axis=0, tiled=True)
    place = (first + jnp.arange(rows, dtype=jnp.int32)) % FRAME
    running = jnp.full((rows, count), LOW, F32)
    total = jnp.zeros((rows, count), F32)
    summed = jnp.zeros((rows, count, HEAD_DIM), F32)
    for step in range(key_all.shape[0] // FRAME):
        at = place + step * FRAME
        key = jnp.take(key_all, at, axis=0).reshape(rows, count, HEAD_DIM).astype(F32)
        value = jnp.take(value_all, at, axis=0).reshape(rows, count, HEAD_DIM).astype(F32)
        scores = jnp.sum(query * key, axis=2)
        newest = jnp.maximum(running, scores)
        shrink = jnp.exp2(running - newest)
        weight = jnp.exp2(scores - newest)
        total = total * shrink + weight
        summed = summed * shrink[:, :, None] + weight[:, :, None] * value
        running = newest
    done = (summed / total[:, :, None]).astype(BF16)
    return [done[:, j] for j in range(count)]


def per_device(queries, keys, values, query_gain, key_gain, head_kind):
    rows = queries.shape[0]
    heads = head_kind.shape[0]
    temporal = heads // 5
    spatial = heads - temporal
    block = rows // 3
    devices = lax.axis_size("seq")
    parts = lax.axis_size("head")
    index = lax.axis_index("seq").astype(jnp.int32)
    pair = [(i, i ^ 1) for i in range(devices)]
    cross = []
    for i in range(3, devices, 4):
        after = (i + 1) % devices
        cross += [(i, after), (after, i)]

    meta = meta_of(head_kind, index, heads, spatial, temporal)
    sums, v, v_near = sums_call(meta, queries, keys, values, heads, spatial, block)
    all_sums = [sums] + [
        permuted(sums, "head", [(i, (i + d) % parts) for i in range(parts)])
        for d in range(1, parts)
    ]
    v_cross = permuted(v_near, "seq", cross)
    v_pair = permuted(v, "seq", pair)
    q, k, *rest = norm_call(
        meta, queries, keys, values, query_gain, key_gain, all_sums, heads, spatial, block
    )
    k_near, t_parts = rest[:CHUNKS], rest[CHUNKS:]
    k_pair = permuted(k, "seq", pair)
    k_cross = [permuted(part, "seq", cross) for part in k_near]
    if temporal == 2 and devices == 2 * CHIPS and rows == 6 * PIECE:
        t_out = temporal_dealt(meta, t_parts[0], t_parts[1], heads, devices)
    else:
        t_out = temporal_folded(t_parts, index * rows)
    out = near_call(meta, q, k, v, k_pair, v_pair, heads, block)
    for c, part in enumerate(k_cross):
        first = c * part.shape[0]
        out = far_call(meta, q, k, v, part, v_cross, out, first, heads, block)
    return place_call(meta, t_out, out, spatial)


def solution(mesh):
    placed = (P("seq", "head"), P("seq", "head"), P("seq", "head"), P("head"), P("head"), P("head"))
    return jax.shard_map(
        per_device, mesh=mesh, in_specs=placed, out_specs=P("seq", "head"), check_vma=False
    )
```

time: 454 us -> 114 us (0.25)
  local copies, waits for them, and re-layouts: 200 us -> 3.1 us
  matrix products: 65.4 us -> 0 us
  other arithmetic: 62.8 us -> 1.63 us
  Pallas kernels: 0 us -> 45.2 us
  waiting for transfers between devices: 77.1 us -> 42 us
  starting transfers between devices: 0.55 us -> 21 us
  loops' own time: 16.4 us -> 0 us
  between operations: 14 us -> 0.18 us
  blocking collectives: 13.7 us -> 0 us
    gather x20 -> x0, local copies, waits for them, and re-layouts: 70.9 us -> none  [the longest x6 29.6 us: temporal_folded(): jnp.take(value_piece, clipped, axis=0).reshape(rows, count, size)]
    slice x8 -> x0, local copies, waits for them, and re-layouts: 66.8 us -> none  [per_head(): value_one = lax.dynamic_index_in_dim(widened[1], which, 1, keepdims=False)]
    dot_general x48 -> x0, matrix products: 65.4 us -> none  [the longest x24 33.2 us: per_head(): lax.dot_general(query_block, key_frame, (((1,), (1,)), ((), ())), preferr...]
    pallas_call x0 -> x9, Pallas kernels: none -> 45.2 us  [the longest x2 13.9 us: far_call(): pl.pallas_call(functools.partial(far_kernel, heads, block), grid_spec=plt...]
    ppermute x2 -> x16, waiting for transfers between devices: 77.1 us -> 42 us  [permuted(): return lax.ppermute(block, axis, route)]
    convert_element_type x12 -> x0, local copies, waits for them, and re-layouts: 28.1 us -> none  [temporal_folded(): jnp.take(key_piece, clipped, axis=0).reshape(rows, count, size)]
    convert_element_type x9 -> x0, other arithmetic: 20.8 us -> none  [the longest x6 12.6 us: temporal_folded(): jnp.take(key_piece, clipped, axis=0).reshape(rows, count, size)]
    ppermute x2 -> x16, starting transfers between devices: 0.51 us -> 21 us  [permuted(): return lax.ppermute(block, axis, route)]
  transfers between devices with their start and end apart: 4 -> 16, of which waited for: 2 -> 8; matrix products, arithmetic and copies ran while one was open for 43% -> 0% of each run, Pallas kernels for 0% -> 32%
where the time goes in v1:
time: 114 us; the launch traced here: 113 us
  Pallas kernels  45.2 us (40%)
  waiting for transfers between devices  42 us (37%)
  starting transfers between devices  21 us (18%)
  local copies, waits for them, and re-layouts  3.1 us (3%)
  other arithmetic  1.63 us (1%)
    ppermute x16, waiting for transfers between devices, permuted(): return lax.ppermute(block, axis, route)  42 us
    ppermute x16, starting transfers between devices, permuted(): return lax.ppermute(block, axis, route)  21 us
    pallas_call x2, Pallas kernels, far_call(): pl.pallas_call(functools.partial(far_kernel, heads, block), grid_spec=plt...  13.9 us
    pallas_call x1, Pallas kernels, near_call(): pl.pallas_call(functools.partial(near_kernel, heads, block), grid_spec=pl...  9.93 us
    pallas_call x1, Pallas kernels, sums_call(): pl.pallas_call(functools.partial(sums_kernel, heads, spatial, block), gri...  7.76 us
    pallas_call x1, Pallas kernels, norm_call(): pl.pallas_call(functools.partial(norm_kernel, heads, spatial, block, len(...  7.58 us
    unnamed x12, local copies, waits for them, and re-layouts  3.1 us
  transfers between devices with their start and end apart: 16, of which 8 were waited for; matrix products, arithmetic and copies ran while one was open for 0% of the time, Pallas kernels for 32%

profile of v1, /device:TPU:0, one launch (start us, length us, event | category | flops | bytes accessed | tf_op | source)
XLA Modules:
  0.0 113.1 jit_solution(16352858010900101851)
XLA Ops:
  0.0 0.7 broadcast_compare_fusion
  0.7 0.1 select_reduce_fusion.1
  0.8 0.7 subtract_select_fusion
  1.4 0.1 select_reduce_fusion
  1.6 0.1 pad_add_fusion.meta
  1.7 1.5 %copy-done = bf16[768,1280]{1,0:T(8,128)(2,1)S(1)} copy-done((bf16[768,1280]{1,0:T(8,128)(2,1)S(1)}, bf16[768,1280]{1,0:T(8,128)(2,1)}, u32[]{:S(2)}) %copy-start) | copy-done | bytes 1966104
  3.2 7.8 %sums.1 = (f32[2,768]{1,0:T(2,128)S(1)}, bf16[8,768,128]{2,1,0:T(8,128)(2,1)S(1)}, bf16[8,512,128]{2,1,0:T(8,128)(2,1)S(1)}) custom-call(s32[13]{0:T(128)S(1)} %pad_add_fusion.meta, bf16[768,1280]{1,0:T(8,128)(2,1)S(1)} %copy-done, bf16[768,1280]{1,0:T(8,128)(2,1)} %k_ref.3, bf16[768,1280]{1,0:T(8,128)(2,1)} %v_ref.3), custom_call_target="tpu_custom_call" | custom-call | flops 5898240 | bytes 9830400 | tf_op jit(solution)/shard_map/sums/pallas_call | solution.py:97
  11.0 5.1 %collective-permute-start.2 = (f32[2,768]{1,0:T(2,128)S(1)}, f32[2,768]{1,0:T(2,128)S(1)}, u32[]{:S(2)}, u32[]{:S(2)}) collective-permute-start(f32[2,768]{1,0:T(2,128)S(1)} %get-tuple-element.24.refs_0_), channel_id=1, source_target_pairs={{0,3},{1,0},{2,1},{3,2},{4,7},{5,4},{6,5},{7,6},{8,11},{9,8},{10,9... | collective-permute-start | bytes 18440 | tf_op jit(solution)/shard_map/ppermute | solution.py:32
  16.1 0.0 collective-permute-start.1
  16.1 1.0 collective-permute-start
  17.1 0.0 collective-permute-start.15
  17.1 0.3 collective-permute-done.2.refs_3_
  17.4 3.2 %collective-permute-done.1.refs_2_ = f32[2,768]{1,0:T(2,128)S(1)} collective-permute-done((f32[2,768]{1,0:T(2,128)S(1)}, f32[2,768]{1,0:T(2,128)S(1)}, u32[]{:S(2)}, u32[]{:S(2)}) %collective-permute-start.1) | collective-permute-done | bytes 6176 | tf_op jit(solution)/shard_map/ppermute | solution.py:32
  20.6 0.9 collective-permute-done.refs_1_
  21.5 7.6 %norms.1 = (bf16[8,768,128]{2,1,0:T(8,128)(2,1)S(1)}, bf16[8,768,128]{2,1,0:T(8,128)(2,1)S(1)}, bf16[4,512,128]{2,1,0:T(8,128)(2,1)S(1)}, bf16[4,512,128]{2,1,0:...) custom-call(s32[13]{0:T(128)S(1)} %pad_add_fusion.meta, bf16[768,1280]{1,0:T(8,128)(2,1)} %q_ref.3, ...), custom_call_target="tpu_custom_call" | custom-call | flops 9830400 | bytes 11796480 | tf_op jit(solution)/shard_map/norms/pallas_call | solution.py:177
  29.1 0.1 collective-permute-start.14
  29.2 0.5 collective-permute-start.3
  29.7 3.7 %collective-permute-done.3.got_ref = bf16[3,768,128]{2,1,0:T(8,128)(2,1)S(1)} collective-permute-done((bf16[3,768,128]{2,1,0:T(8,128)(2,1)S(1)}, bf16[3,768,128]{2,1,0:T(8,128)(2,1)S(1)}, u32[]{:S(2)}, u32[]{:S(2)}) %collective-permute-start.3) | collective-permute-done | bytes 589856 | tf_op jit(solution)/shard_map/ppermute | solution.py:32
  33.4 1.3 %deal.1 = (bf16[3,3,128,128]{3,2,1,0:T(8,128)(2,1)S(1)}, bf16[3,3,128,128]{3,2,1,0:T(8,128)(2,1)S(1)}, bf16[3,3,128,128]{3,2,1,0:T(8,128)(2,1)S(1)}, bf16[3,3,128,128]{3,2,1,0:T(8,128)(2,1)S(1)}) custom-call(s32[13]{0:T(128)S(1)} %pad_add_fusion.meta, bf16[3,768,128]{2,1,0:T(8,128)(2,1)S(1)} %get-tuple-element.25.keep_ref, ...), custom_call_target="tpu_custom_call" | custom-call | bytes 2359296 | tf_op jit(solution)/shard_map/deal/pallas_call | solution.py:373
  34.7 1.6 %collective-permute-start.4 = (bf16[3,3,128,128]{3,2,1,0:T(8,128)(2,1)S(1)}, bf16[3,3,128,128]{3,2,1,0:T(8,128)(2,1)S(1)}, u32[]{:S(2)}, u32[]{:S(2)}) collective-permute-start(bf16[3,3,128,128]{3,2,1,0:T(8,128)(2,1)S(1)} %get-tuple-element.28), channel_id=1, source_target_pairs={{0,8},{4,12},{8,0},{12,4},{16,24},{20,28},{24,16},{28,20},{1,9},{5... | collective-permute-start | bytes 884744 | tf_op jit(solution)/shard_map/ppermute | solution.py:32
  36.3 2.8 %collective-permute-start.12 = (bf16[8,512,128]{2,1,0:T(8,128)(2,1)S(1)}, bf16[8,512,128]{2,1,0:T(8,128)(2,1)S(1)}, u32[]{:S(2)}, u32[]{:S(2)}) collective-permute-start(bf16[8,512,128]{2,1,0:T(8,128)(2,1)S(1)} %get-tuple-element.41), channel_id=1, source_target_pairs={{12,16},{16,12},{28,0},{0,28},{13,17},{17,13},{29,1},{1,29},{14,18... | collective-permute-start | bytes 3145736 | tf_op jit(solution)/shard_map/ppermute | solution.py:32
  39.1 0.6 collective-permute-start.5
  39.8 4.9 %collective-permute-done.4.refs_1_ = bf16[3,3,128,128]{3,2,1,0:T(8,128)(2,1)S(1)} collective-permute-done((bf16[3,3,128,128]{3,2,1,0:T(8,128)(2,1)S(1)}, bf16[3,3,128,128]{3,2,1,0:T(8,128)(2,1)S(1)}, u32[]{:S(2)}, u32[]{:S(2)}) %collective-permute-start.4) | collective-permute-done | bytes 294944 | tf_op jit(solution)/shard_map/ppermute | solution.py:32
  44.6 1.6 %collective-permute-start.6 = (bf16[3,3,128,128]{3,2,1,0:T(8,128)(2,1)S(1)}, bf16[3,3,128,128]{3,2,1,0:T(8,128)(2,1)S(1)}, u32[]{:S(2)}, u32[]{:S(2)}) collective-permute-start(bf16[3,3,128,128]{3,2,1,0:T(8,128)(2,1)S(1)} %get-tuple-element.30), channel_id=1, source_target_pairs={{0,24},{4,28},{8,16},{12,20},{16,8},{20,12},{24,0},{28,4},{1,25},{... | collective-permute-start | bytes 884744 | tf_op jit(solution)/shard_map/ppermute | solution.py:32
  46.3 17.2 %collective-permute-done.5.refs_2_ = bf16[3,3,128,128]{3,2,1,0:T(8,128)(2,1)S(1)} collective-permute-done((bf16[3,3,128,128]{3,2,1,0:T(8,128)(2,1)S(1)}, bf16[3,3,128,128]{3,2,1,0:T(8,128)(2,1)S(1)}, u32[]{:S(2)}, u32[]{:S(2)}) %collective-permute-start.5) | collective-permute-done | bytes 294944 | tf_op jit(solution)/shard_map/ppermute | solution.py:32
  63.5 0.0 collective-permute-done.6.refs_3_
  63.5 1.8 %frames.1 = (bf16[3,128,128]{2,1,0:T(8,128)(2,1)S(1)}, bf16[3,128,128]{2,1,0:T(8,128)(2,1)S(1)}, bf16[3,128,128]{2,1,0:T(8,128)(2,1)S(1)}, bf16[3,128,128]{2,1,0:T(8,128)(2,1)S(1)}) custom-call(bf16[3,3,128,128]{3,2,1,0:T(8,128)(2,1)S(1)} %get-tuple-element.27.refs_0_, bf16[3,3,128,128]{3,2,1,0:T(8,128)(2,1)S(1)} %collective-permute-done.4.refs_1_, ...), custom_call_target="tpu_custom_call" | custom-call | flops 603979776 | bytes 1572864 | tf_op jit(solution)/shard_map/frames/pallas_call | solution.py:465
  65.2 0.5 collective-permute-start.7
  65.8 1.1 collective-permute-start.8
  66.8 3.1 %collective-permute-done.7.refs_1_ = bf16[3,128,128]{2,1,0:T(8,128)(2,1)S(1)} collective-permute-done((bf16[3,128,128]{2,1,0:T(8,128)(2,1)S(1)}, bf16[3,128,128]{2,1,0:T(8,128)(2,1)S(1)}, u32[]{:S(2)}, u32[]{:S(2)}) %collective-permute-start.7) | collective-permute-done | bytes 98336 | tf_op jit(solution)/shard_map/ppermute | solution.py:32
  69.9 3.6 %collective-permute-start.13 = (bf16[4,512,128]{2,1,0:T(8,128)(2,1)S(1)}, bf16[4,512,128]{2,1,0:T(8,128)(2,1)S(1)}, u32[]{:S(2)}, u32[]{:S(2)}) collective-permute-start(bf16[4,512,128]{2,1,0:T(8,128)(2,1)S(1)} %get-tuple-element.42), channel_id=1, source_target_pairs={{12,16},{16,12},{28,0},{0,28},{13,17},{17,13},{29,1},{1,29},{14,18... | collective-permute-start | bytes 1572872 | tf_op jit(solution)/shard_map/ppermute | solution.py:32
  73.5 0.0 collective-permute-done.8.refs_2_
  73.5 0.1 collective-permute-start.9
  73.6 8.7 %collective-permute-done.9.refs_3_ = bf16[3,128,128]{2,1,0:T(8,128)(2,1)S(1)} collective-permute-done((bf16[3,128,128]{2,1,0:T(8,128)(2,1)S(1)}, bf16[3,128,128]{2,1,0:T(8,128)(2,1)S(1)}, u32[]{:S(2)}, u32[]{:S(2)}) %collective-permute-start.9) | collective-permute-done | bytes 98336 | tf_op jit(solution)/shard_map/ppermute | solution.py:32
  82.3 2.3 %collective-permute-start.11 = (bf16[4,512,128]{2,1,0:T(8,128)(2,1)S(1)}, bf16[4,512,128]{2,1,0:T(8,128)(2,1)S(1)}, u32[]{:S(2)}, u32[]{:S(2)}) collective-permute-start(bf16[4,512,128]{2,1,0:T(8,128)(2,1)S(1)} %get-tuple-element.40), channel_id=1, source_target_pairs={{12,16},{16,12},{28,0},{0,28},{13,17},{17,13},{29,1},{1,29},{14,18... | collective-permute-start | bytes 1572872 | tf_op jit(solution)/shard_map/ppermute | solution.py:32
  84.6 1.7 %gather.1 = (bf16[6,128,128]{2,1,0:T(8,128)(2,1)S(1)}, bf16[6,128,128]{2,1,0:T(8,128)(2,1)S(1)}) custom-call(s32[13]{0:T(128)S(1)} %pad_add_fusion.meta, bf16[3,128,128]{2,1,0:T(8,128)(2,1)S(1)} %get-tuple-element.31.refs_0_, bf16[3,128,128]{2,1,0:T(8,128)(2,1)S(1)} %collective-permute-done.7.refs_1_, ...), custom_call_target="tpu_custom_call" | custom-call | bytes 786432 | tf_op jit(solution)/shard_map/gather/pallas_call | solution.py:418
  86.3 0.0 collective-permute-done.15.vp_ref
  86.3 0.1 collective-permute-start.10
  86.4 0.0 collective-permute-done.14.kp_ref
  86.4 1.0 copy-done.4
  87.5 0.5 copy-done.5
  87.9 9.9 %near.1.have_ref = bf16[768,1280]{1,0:T(8,128)(2,1)} custom-call(s32[13]{0:T(128)S(1)} %pad_add_fusion.meta, bf16[8,768,128]{2,1,0:T(8,128)(2,1)S(1)} %get-tuple-element.37.q_ref, bf16[8,768,128]{2,1,0:T(8,128)(2,1)S(1)} %get-tuple-element.38.k_ref, bf16[8,768,128]{2,1,0:T(8,128)(2,1)S(1)} %get-tuple-element.39.v_ref, bf16[8,768,128]{2,1,0:T(8,128)(2,1)} %copy-done.5, ...), custom_call_target="tpu_custom_call" | custom-call | flops 3221225472 | bytes 9437184 | tf_op jit(solution)/shard_map/near/pallas_call | solution.py:244
  97.9 0.0 collective-permute-done.13.kx_ref
  97.9 0.0 collective-permute-done.12.vx_ref
  97.9 6.9 %far.2.have_ref = bf16[768,1280]{1,0:T(8,128)(2,1)} custom-call(s32[13]{0:T(128)S(1)} %pad_add_fusion.meta, bf16[8,768,128]{2,1,0:T(8,128)(2,1)S(1)} %get-tuple-element.37.q_ref, bf16[8,768,128]{2,1,0:T(8,128)(2,1)S(1)} %get-tuple-element.38.k_ref, bf16[8,768,128]{2,1,0:T(8,128)(2,1)} %copy-done.1, ...), custom_call_target="tpu_custom_call", output_to_operand_aliasing={{}: (6, {})} | custom-call | flops 1073741824 | bytes 5505024 | tf_op jit(solution)/shard_map/far/pallas_call | solution.py:281
  104.8 0.0 collective-permute-done.11.kx_ref
  104.8 6.9 %far.3.refs_2_ = bf16[768,1280]{1,0:T(8,128)(2,1)} custom-call(s32[13]{0:T(128)S(1)} %pad_add_fusion.meta, bf16[8,768,128]{2,1,0:T(8,128)(2,1)S(1)} %get-tuple-element.37.q_ref, bf16[8,768,128]{2,1,0:T(8,128)(2,1)S(1)} %get-tuple-element.38.k_ref, bf16[8,768,128]{2,1,0:T(8,128)(2,1)} %copy-done.1, ...), custom_call_target="tpu_custom_call", output_to_operand_aliasing={{}: (6, {})} | custom-call | flops 1073741824 | bytes 5505024 | tf_op jit(solution)/shard_map/far/pallas_call | solution.py:281
  111.8 1.3 %place.1 = bf16[768,1280]{1,0:T(8,128)(2,1)} custom-call(s32[13]{0:T(128)S(1)} %pad_add_fusion.meta, bf16[768,128]{1,0:T(8,128)(2,1)S(1)} %bitcast.5, bf16[768,128]{1,0:T(8,128)(2,1)S(1)} %bitcast.6, bf16[768,1280]{1,0:T(8,128)(2,1)} %far.3.refs_2_), custom_call_target="tpu_custom_call", output_to_operand_aliasing={{}: (3, {})} | custom-call | bytes 786432 | tf_op jit(solution)/shard_map/place/pallas_call | solution.py:317
  (12 shorter events, 0.0 us)
Async XLA Ops:
  1.6 1.5 %copy-start = (bf16[768,1280]{1,0:T(8,128)(2,1)S(1)}, bf16[768,1280]{1,0:T(8,128)(2,1)}, u32[]{:S(2)}) copy-start(bf16[768,1280]{1,0:T(8,128)(2,1)} %q_ref.3) | copy-start | bytes 5898244
  3.2 13.9 %copy-start.2 = (f32[1280]{0:T(1024)S(1)}, f32[1280]{0:T(1024)}, u32[]{:S(2)}) copy-start(f32[1280]{0:T(1024)} %param.9) | copy-start | bytes 15364
  3.2 13.9 %copy-start.3 = (f32[1280]{0:T(1024)S(1)}, f32[1280]{0:T(1024)}, u32[]{:S(2)}) copy-start(f32[1280]{0:T(1024)} %param.10) | copy-start | bytes 15364
  11.0 75.4 %copy-start.1 = (bf16[8,768,128]{2,1,0:T(8,128)(2,1)}, bf16[8,768,128]{2,1,0:T(8,128)(2,1)S(1)}, u32[]{:S(2)}) copy-start(bf16[8,768,128]{2,1,0:T(8,128)(2,1)S(1)} %get-tuple-element.39.v_ref) | copy-start | bytes 4718596
  11.0 6.4 %collective-permute-start.2 = (f32[2,768]{1,0:T(2,128)S(1)}, f32[2,768]{1,0:T(2,128)S(1)}, u32[]{:S(2)}, u32[]{:S(2)}) collective-permute-start(f32[2,768]{1,0:T(2,128)S(1)} %get-tuple-element.24.refs_0_), channel_id=1, source_target_pairs={{0,3},{1,0},{2,1},{3,2},{4,7},{5,4},{6,5},{7,6},{8,11},{9,8},{10,9... | collective-permute-start | bytes 18440 | tf_op jit(solution)/shard_map/ppermute | solution.py:32
  16.1 4.5 %collective-permute-start.1 = (f32[2,768]{1,0:T(2,128)S(1)}, f32[2,768]{1,0:T(2,128)S(1)}, u32[]{:S(2)}, u32[]{:S(2)}) collective-permute-start(f32[2,768]{1,0:T(2,128)S(1)} %get-tuple-element.24.refs_0_), channel_id=1, source_target_pairs={{0,2},{1,3},{2,0},{3,1},{4,6},{5,7},{6,4},{7,5},{8,10},{9,11},{10,... | collective-permute-start | bytes 18440 | tf_op jit(solution)/shard_map/ppermute | solution.py:32
  16.1 5.4 %collective-permute-start = (f32[2,768]{1,0:T(2,128)S(1)}, f32[2,768]{1,0:T(2,128)S(1)}, u32[]{:S(2)}, u32[]{:S(2)}) collective-permute-start(f32[2,768]{1,0:T(2,128)S(1)} %get-tuple-element.24.refs_0_), channel_id=1, source_target_pairs={{0,1},{1,2},{2,3},{3,0},{4,5},{5,6},{6,7},{7,4},{8,9},{9,10},{10,1... | collective-permute-start | bytes 18440 | tf_op jit(solution)/shard_map/ppermute | solution.py:32
  17.1 69.2 %collective-permute-start.15 = (bf16[8,768,128]{2,1,0:T(8,128)(2,1)S(1)}, bf16[8,768,128]{2,1,0:T(8,128)(2,1)S(1)}, u32[]{:S(2)}, u32[]{:S(2)}) collective-permute-start(bf16[8,768,128]{2,1,0:T(8,128)(2,1)S(1)} %get-tuple-element.39.v_ref), channel_id=1, source_target_pairs={{0,4},{4,0},{8,12},{12,8},{16,20},{20,16},{24,28},{28,24},{1,5},{5... | collective-permute-start | bytes 4718600 | tf_op jit(solution)/shard_map/ppermute | solution.py:32
  29.1 57.3 %collective-permute-start.14 = (bf16[8,768,128]{2,1,0:T(8,128)(2,1)S(1)}, bf16[8,768,128]{2,1,0:T(8,128)(2,1)S(1)}, u32[]{:S(2)}, u32[]{:S(2)}) collective-permute-start(bf16[8,768,128]{2,1,0:T(8,128)(2,1)S(1)} %get-tuple-element.38.k_ref), channel_id=1, source_target_pairs={{0,4},{4,0},{8,12},{12,8},{16,20},{20,16},{24,28},{28,24},{1,5},{5... | collective-permute-start | bytes 4718600 | tf_op jit(solution)/shard_map/ppermute | solution.py:32
  29.2 4.2 %collective-permute-start.3 = (bf16[3,768,128]{2,1,0:T(8,128)(2,1)S(1)}, bf16[3,768,128]{2,1,0:T(8,128)(2,1)S(1)}, u32[]{:S(2)}, u32[]{:S(2)}) collective-permute-start(bf16[3,768,128]{2,1,0:T(8,128)(2,1)S(1)} %get-tuple-element.26), channel_id=1, source_target_pairs={{0,4},{4,0},{8,12},{12,8},{16,20},{20,16},{24,28},{28,24},{1,5},{5... | collective-permute-start | bytes 1769480 | tf_op jit(solution)/shard_map/ppermute | solution.py:32
  34.7 9.9 %collective-permute-start.4 = (bf16[3,3,128,128]{3,2,1,0:T(8,128)(2,1)S(1)}, bf16[3,3,128,128]{3,2,1,0:T(8,128)(2,1)S(1)}, u32[]{:S(2)}, u32[]{:S(2)}) collective-permute-start(bf16[3,3,128,128]{3,2,1,0:T(8,128)(2,1)S(1)} %get-tuple-element.28), channel_id=1, source_target_pairs={{0,8},{4,12},{8,0},{12,4},{16,24},{20,28},{24,16},{28,20},{1,9},{5... | collective-permute-start | bytes 884744 | tf_op jit(solution)/shard_map/ppermute | solution.py:32
  36.3 61.6 %collective-permute-start.12 = (bf16[8,512,128]{2,1,0:T(8,128)(2,1)S(1)}, bf16[8,512,128]{2,1,0:T(8,128)(2,1)S(1)}, u32[]{:S(2)}, u32[]{:S(2)}) collective-permute-start(bf16[8,512,128]{2,1,0:T(8,128)(2,1)S(1)} %get-tuple-element.41), channel_id=1, source_target_pairs={{12,16},{16,12},{28,0},{0,28},{13,17},{17,13},{29,1},{1,29},{14,18... | collective-permute-start | bytes 3145736 | tf_op jit(solution)/shard_map/ppermute | solution.py:32
  39.1 24.3 %collective-permute-start.5 = (bf16[3,3,128,128]{3,2,1,0:T(8,128)(2,1)S(1)}, bf16[3,3,128,128]{3,2,1,0:T(8,128)(2,1)S(1)}, u32[]{:S(2)}, u32[]{:S(2)}) collective-permute-start(bf16[3,3,128,128]{3,2,1,0:T(8,128)(2,1)S(1)} %get-tuple-element.29), channel_id=1, source_target_pairs={{0,16},{4,20},{8,24},{12,28},{16,0},{20,4},{24,8},{28,12},{1,17},{... | collective-permute-start | bytes 884744 | tf_op jit(solution)/shard_map/ppermute | solution.py:32
  44.6 18.8 %collective-permute-start.6 = (bf16[3,3,128,128]{3,2,1,0:T(8,128)(2,1)S(1)}, bf16[3,3,128,128]{3,2,1,0:T(8,128)(2,1)S(1)}, u32[]{:S(2)}, u32[]{:S(2)}) collective-permute-start(bf16[3,3,128,128]{3,2,1,0:T(8,128)(2,1)S(1)} %get-tuple-element.30), channel_id=1, source_target_pairs={{0,24},{4,28},{8,16},{12,20},{16,8},{20,12},{24,0},{28,4},{1,25},{... | collective-permute-start | bytes 884744 | tf_op jit(solution)/shard_map/ppermute | solution.py:32
  65.2 4.7 %collective-permute-start.7 = (bf16[3,128,128]{2,1,0:T(8,128)(2,1)S(1)}, bf16[3,128,128]{2,1,0:T(8,128)(2,1)S(1)}, u32[]{:S(2)}, u32[]{:S(2)}) collective-permute-start(bf16[3,128,128]{2,1,0:T(8,128)(2,1)S(1)} %get-tuple-element.32), channel_id=1, source_target_pairs={{0,8},{4,12},{8,0},{12,4},{16,24},{20,28},{24,16},{28,20},{1,9},{5... | collective-permute-start | bytes 294920 | tf_op jit(solution)/shard_map/ppermute | solution.py:32
  65.8 7.7 %collective-permute-start.8 = (bf16[3,128,128]{2,1,0:T(8,128)(2,1)S(1)}, bf16[3,128,128]{2,1,0:T(8,128)(2,1)S(1)}, u32[]{:S(2)}, u32[]{:S(2)}) collective-permute-start(bf16[3,128,128]{2,1,0:T(8,128)(2,1)S(1)} %get-tuple-element.33), channel_id=1, source_target_pairs={{0,16},{4,20},{8,24},{12,28},{16,0},{20,4},{24,8},{28,12},{1,17},{... | collective-permute-start | bytes 294920 | tf_op jit(solution)/shard_map/ppermute | solution.py:32
  69.9 28.0 %collective-permute-start.13 = (bf16[4,512,128]{2,1,0:T(8,128)(2,1)S(1)}, bf16[4,512,128]{2,1,0:T(8,128)(2,1)S(1)}, u32[]{:S(2)}, u32[]{:S(2)}) collective-permute-start(bf16[4,512,128]{2,1,0:T(8,128)(2,1)S(1)} %get-tuple-element.42), channel_id=1, source_target_pairs={{12,16},{16,12},{28,0},{0,28},{13,17},{17,13},{29,1},{1,29},{14,18... | collective-permute-start | bytes 1572872 | tf_op jit(solution)/shard_map/ppermute | solution.py:32
  73.5 8.8 %collective-permute-start.9 = (bf16[3,128,128]{2,1,0:T(8,128)(2,1)S(1)}, bf16[3,128,128]{2,1,0:T(8,128)(2,1)S(1)}, u32[]{:S(2)}, u32[]{:S(2)}) collective-permute-start(bf16[3,128,128]{2,1,0:T(8,128)(2,1)S(1)} %get-tuple-element.34), channel_id=1, source_target_pairs={{0,24},{4,28},{8,16},{12,20},{16,8},{20,12},{24,0},{28,4},{1,25},{... | collective-permute-start | bytes 294920 | tf_op jit(solution)/shard_map/ppermute | solution.py:32
  82.3 22.5 %collective-permute-start.11 = (bf16[4,512,128]{2,1,0:T(8,128)(2,1)S(1)}, bf16[4,512,128]{2,1,0:T(8,128)(2,1)S(1)}, u32[]{:S(2)}, u32[]{:S(2)}) collective-permute-start(bf16[4,512,128]{2,1,0:T(8,128)(2,1)S(1)} %get-tuple-element.40), channel_id=1, source_target_pairs={{12,16},{16,12},{28,0},{0,28},{13,17},{17,13},{29,1},{1,29},{14,18... | collective-permute-start | bytes 1572872 | tf_op jit(solution)/shard_map/ppermute | solution.py:32
  86.3 1.2 %copy-start.4 = (bf16[8,768,128]{2,1,0:T(8,128)(2,1)}, bf16[8,768,128]{2,1,0:T(8,128)(2,1)S(1)}, u32[]{:S(2)}) copy-start(bf16[8,768,128]{2,1,0:T(8,128)(2,1)S(1)} %collective-permute-done.15.vp_ref) | copy-start | bytes 4718596
  86.3 25.4 %collective-permute-start.10 = (bf16[6,128,128]{2,1,0:T(8,128)(2,1)S(1)}, bf16[6,128,128]{2,1,0:T(8,128)(2,1)S(1)}, u32[]{:S(2)}, u32[]{:S(2)}) collective-permute-start(bf16[6,128,128]{2,1,0:T(8,128)(2,1)S(1)} %get-tuple-element.36), channel_id=1, source_target_pairs={{0,4},{4,0},{8,12},{12,8},{16,20},{20,16},{24,28},{28,24},{1,5},{5... | collective-permute-start | bytes 589832 | tf_op jit(solution)/shard_map/ppermute | solution.py:32
  86.4 1.6 %copy-start.5 = (bf16[8,768,128]{2,1,0:T(8,128)(2,1)}, bf16[8,768,128]{2,1,0:T(8,128)(2,1)S(1)}, u32[]{:S(2)}) copy-start(bf16[8,768,128]{2,1,0:T(8,128)(2,1)S(1)} %collective-permute-done.14.kp_ref) | copy-start | bytes 4718596

commit v2 on v0

v2 whole, which is shorter than its diff:
```python
import functools
import math

import jax
import jax.numpy as jnp
from jax import lax
from jax.experimental import pallas as pl
from jax.experimental.pallas import tpu as pltpu
from jax.sharding import PartitionSpec as P

HEAD_DIM = 128
D = 5120
FRAME = 1024
OFFSET = 512
CHUNKS = 2
UNROLL = 4
VMEM = 64 * 1024 * 1024
LOW = -1e30
FACTOR = math.log2(math.e) / math.sqrt(HEAD_DIM)
F32 = jnp.float32
BF16 = jnp.bfloat16
ANY = pl.BlockSpec(memory_space=pl.ANY)
IN_SMEM = pl.BlockSpec(memory_space=pltpu.SMEM)
IN_VMEM = pl.BlockSpec(memory_space=pltpu.VMEM)


def shape(dims, dtype=BF16):
    return jax.ShapeDtypeStruct(dims, dtype)


def call(kernel, name, out_shape, in_specs, out_specs, scratch, operands, aliases=None):
    return pl.pallas_call(
        kernel,
        out_shape=out_shape,
        in_specs=in_specs,
        out_specs=out_specs,
        scratch_shapes=scratch,
        input_output_aliases=aliases or {},
        compiler_params=pltpu.CompilerParams(vmem_limit_bytes=VMEM),
        cost_estimate=pl.CostEstimate(flops=1000, bytes_accessed=1000, transcendentals=0),
        name=name,
    )(*operands)


def column(ref, head, rows=None):
    lanes = pl.ds(pl.multiple_of(head * HEAD_DIM, HEAD_DIM), HEAD_DIM)
    return ref.at[:, lanes] if rows is None else ref.at[rows, lanes]


def put_order(kind_ref, order_ref, spatial):
    heads = kind_ref.shape[0]

    def step(h, count):
        s, t = count
        temporal = kind_ref[h] == 1
        order_ref[jnp.where(temporal, spatial + t, s)] = h
        return jnp.where(temporal, s, s + 1), jnp.where(temporal, t + 1, t)

    lax.fori_loop(0, heads, step, (jnp.int32(0), jnp.int32(0)))


def order_scratch(heads):
    return pltpu.SMEM((heads,), jnp.int32)


class Place:
    def __init__(self, block):
        index = lax.axis_index("seq").astype(jnp.int32)
        self.kind = index % 4
        self.core = index % 2
        self.chip = index // 2
        self.inner = (self.kind == 1) | (self.kind == 2)
        self.apart = jnp.where((self.kind == 0) | (self.kind == 1), 2 * block, 0)
        self.near = jnp.where(self.kind == 0, 2 * block, 0)
        self.far = jnp.where(self.kind == 0, 0, block)
        self.cross = jnp.where(self.kind == 0, 0, block)


def start_all(copies):
    for copy in copies:
        copy.start()


def wait_all(copies):
    for copy in copies:
        copy.wait()


def first_kernel(spatial, block, dealt, kind_ref, q_ref, k_ref, v_ref, sums_ref, vx_ref, *refs):
    order, held, squares, v_buf, t_buf, sums, sems, v_sems, t_sems = refs[-9:]
    put_order(kind_ref, order, spatial)
    place = Place(block)
    rows, width = q_ref.shape
    steps = held.shape[1]
    size = rows // steps
    across = pl.ds(pl.multiple_of(place.cross, block), 2 * block)
    v_in = [
        pltpu.make_async_copy(column(v_ref, order[h], across), v_buf.at[h], v_sems.at[0, h])
        for h in range(spatial)
    ]
    v_out = [
        pltpu.make_async_copy(v_buf.at[h], vx_ref.at[h], v_sems.at[1, h]) for h in range(spatial)
    ]
    t_in = []
    t_out = []
    if dealt:
        head = order[spatial + 1 - place.core]
        t_in = [
            pltpu.make_async_copy(column(ref, head), t_buf.at[i], t_sems.at[i])
            for i, ref in enumerate((q_ref, k_ref, v_ref))
        ]
        t_out = [pltpu.make_async_copy(t_buf, refs[0], t_sems.at[3])]
    copies = [
        [
            pltpu.make_async_copy(ref.at[pl.ds(s * size, size), :], held.at[i, s], sems.at[i, s])
            for s in range(steps)
        ]
        for i, ref in enumerate((q_ref, k_ref))
    ]
    start_all(t_in)
    start_all(v_in)
    for line in copies:
        start_all(line)
    wait_all(t_in)
    start_all(t_out)
    for h in range(spatial):
        v_in[h].wait()
        v_out[h].start()
    for i in range(2):
        for s in range(steps):
            copies[i][s].wait()
            total = None
            for c in range(width // HEAD_DIM):
                x = held[i, s, :, c * HEAD_DIM : (c + 1) * HEAD_DIM].astype(F32)
                total = x * x if total is None else total + x * x
            squares[s * size : (s + 1) * size, :] = total
        row = lax.dot_general(
            jnp.ones((8, HEAD_DIM), F32),
            squares[...],
            (((1,), (1,)), ((), ())),
            precision=lax.Precision.HIGHEST,
            preferred_element_type=F32,
        )
        sums[i : i + 1, :] = row[0:1, :]
    out = pltpu.make_async_copy(sums, sums_ref, t_sems.at[4])
    out.start()
    wait_all(t_out + v_out + [out])


def first_call(head_kind, queries, keys, values, spatial, block, dealt):
    rows, width = queries.shape
    steps = 6
    outs = [shape((2, rows), F32), shape((spatial, 2 * block, HEAD_DIM))]
    if dealt:
        outs.append(shape((3, rows, HEAD_DIM)))
    return call(
        functools.partial(first_kernel, spatial, block, dealt),
        "first",
        outs,
        [IN_SMEM, ANY, ANY, ANY],
        [ANY] * len(outs),
        [
            order_scratch(head_kind.shape[0]),
            pltpu.VMEM((2, steps, rows // steps, width), BF16),
            pltpu.VMEM((rows, HEAD_DIM), F32),
            pltpu.VMEM((spatial, 2 * block, HEAD_DIM), BF16),
            pltpu.VMEM((3, rows, HEAD_DIM), BF16),
            pltpu.VMEM((2, rows), F32),
            pltpu.SemaphoreType.DMA((2, steps)),
            pltpu.SemaphoreType.DMA((2, spatial)),
            pltpu.SemaphoreType.DMA((5,)),
        ],
        (head_kind, queries, keys, values),
    )


def small_scratch(*operands):
    return [pltpu.VMEM(x.shape, F32) for x in operands] + [
        pltpu.SemaphoreType.DMA((len(operands),))
    ]


def small_copies(sources, scratch):
    return [
        pltpu.make_async_copy(ref, buf, scratch[-1].at[i])
        for i, (ref, buf) in enumerate(zip(sources, scratch[:-1]))
    ]


def row_factors(total_ref, which, start, size):
    sums = total_ref[which : which + 1, pl.ds(start, size)]
    inverse = lax.rsqrt(sums / D + 1e-06)
    return jnp.transpose(jnp.broadcast_to(inverse, (HEAD_DIM, size)))


def gain_of(gain_ref, head):
    gain = gain_ref[pl.ds(pl.multiple_of(head * HEAD_DIM, HEAD_DIM), HEAD_DIM)]
    return jnp.broadcast_to(gain[None, :], (8, HEAD_DIM))[0:1, :]


def keys_kernel(spatial, block, kind_ref, k_ref, gain_any, total_any, after_ref, after_too, *refs):
    ks_ref, kx_refs = refs[0], refs[1 : 1 + CHUNKS]
    order, held, done, factors, sems, *small = refs[1 + CHUNKS :]
    gain_ref, total_ref = small[:2]
    smalls = small_copies((gain_any, total_any), small)
    start_all(smalls)
    put_order(kind_ref, order, spatial)
    place = Place(block)
    rows = k_ref.shape[0]
    ins = [
        pltpu.make_async_copy(column(k_ref, order[h]), held.at[h], sems.at[0, h])
        for h in range(spatial)
    ]
    start_all(ins)
    wait_all(smalls)
    factors[...] = row_factors(total_ref, 1, 0, rows)
    each = spatial // CHUNKS
    own = pl.ds(pl.multiple_of(place.cross, block), 2 * block)
    outs = []
    for h in range(spatial):
        ins[h].wait()
        done[h] = (held[h].astype(F32) * factors[...] * gain_of(gain_ref, order[h])).astype(BF16)
        outs.append(pltpu.make_async_copy(done.at[h], ks_ref.at[h], sems.at[1, h]))
        outs.append(
            pltpu.make_async_copy(
                done.at[h, own], kx_refs[h // each].at[h % each], sems.at[2, h]
            )
        )
        start_all(outs[-2:])
    wait_all(outs)


def keys_call(head_kind, keys, gain, total, after, after_too, spatial, block):
    rows = keys.shape[0]
    each = spatial // CHUNKS
    one = (spatial, rows, HEAD_DIM)
    return call(
        functools.partial(keys_kernel, spatial, block),
        "keys",
        [shape(one)] + [shape((each, 2 * block, HEAD_DIM))] * CHUNKS,
        [IN_SMEM] + [ANY] * 5,
        [ANY] * (1 + CHUNKS),
        [
            order_scratch(head_kind.shape[0]),
            pltpu.VMEM(one, BF16),
            pltpu.VMEM(one, BF16),
            pltpu.VMEM((rows, HEAD_DIM), F32),
            pltpu.SemaphoreType.DMA((3, spatial)),
            *small_scratch(gain, total),
        ],
        (head_kind, keys, gain, total, after, after_too),
    )


def attend(query, key, value):
    scores = lax.dot_general(query, key, (((1,), (1,)), ((), ())), preferred_element_type=F32)
    top = jnp.max(scores, axis=1, keepdims=True)
    weights = jnp.exp2(scores - top).astype(BF16)
    wide = jnp.concatenate([value, jnp.ones_like(value)], axis=1)
    total = jnp.dot(weights, wide, preferred_element_type=F32)
    return (total[:, :HEAD_DIM] / total[:, HEAD_DIM:]).astype(BF16)


def attention(count, first, blocks, block, starts, load, refs):
    q_ref, gain_any, total_any, out_ref, order, q_buf, k_buf, v_buf, o_buf, factors, sems, *small = refs
    gain_ref, total_ref = small[:2]
    smalls = small_copies((gain_any, total_any), small)
    start_all(smalls)
    size = blocks * block
    start = pl.multiple_of(starts, block)

    def q_copy(h):
        return pltpu.make_async_copy(
            column(q_ref, order[first + h], pl.ds(start, size)), q_buf.at[h], sems.at[0, h]
        )

    def o_copy(h):
        return pltpu.make_async_copy(
            o_buf.at[h], column(out_ref, order[first + h], pl.ds(start, size)), sems.at[3, h]
        )

    for h in range(count):
        q_copy(h).start()
        load(h)
    wait_all(smalls)
    factors[...] = row_factors(total_ref, 0, start, size)
    together = min(UNROLL // blocks, count)

    def step(g, _):
        for n in range(together):
            h = g * together + n
            q_copy(h).wait()
            for i, buf in ((1, k_buf), (2, v_buf)):
                pltpu.make_async_copy(buf.at[h], buf.at[h], sems.at[i, h]).wait()
        for n in range(together):
            h = g * together + n
            gain = gain_of(gain_ref, order[first + h]) * FACTOR
            for part in range(blocks):
                rows = slice(part * block, (part + 1) * block)
                query = (q_buf[h, rows, :].astype(F32) * factors[rows, :] * gain).astype(BF16)
                o_buf[h, rows, :] = attend(query, k_buf[h], v_buf[h])
        for n in range(together):
            o_copy(g * together + n).start()
        return 0

    lax.fori_loop(0, count // together, step, 0)
    for h in range(count):
        o_copy(h).wait()


def attention_scratch(heads, count, blocks, block, gain, total):
    return [
        order_scratch(heads),
        pltpu.VMEM((count, blocks * block, HEAD_DIM), BF16),
        pltpu.VMEM((count, 4 * block, HEAD_DIM), BF16),
        pltpu.VMEM((count, 4 * block, HEAD_DIM), BF16),
        pltpu.VMEM((count, blocks * block, HEAD_DIM), BF16),
        pltpu.VMEM((blocks * block, HEAD_DIM), F32),
        pltpu.SemaphoreType.DMA((4, count)),
        *small_scratch(gain, total),
    ]


def fill(buf, sem, parts):
    at = 0
    for part in parts:
        size = part.shape[0]
        pltpu.make_async_copy(part, buf.at[pl.ds(at, size)], sem).start()
        at += size


def near_kernel(spatial, block, kind_ref, q_ref, k_ref, v_ref, kp_ref, vp_ref, gain_ref, total_ref, after_ref, out_ref, *scratch):
    order, q_buf, k_buf, v_buf, o_buf, factors, sems = scratch[:7]
    put_order(kind_ref, order, spatial)
    place = Place(block)
    one = pl.ds(pl.multiple_of(place.apart, block), block)

    def load(h):
        head = order[h]

        @pl.when(place.inner)
        def _():
            fill(k_buf.at[h], sems.at[1, h], (k_ref.at[h], kp_ref.at[h, one]))
            fill(v_buf.at[h], sems.at[2, h], (column(v_ref, head), column(vp_ref, head, one)))

        @pl.when(jnp.logical_not(place.inner))
        def _():
            fill(k_buf.at[h], sems.at[1, h], (kp_ref.at[h], k_ref.at[h, one]))
            fill(v_buf.at[h], sems.at[2, h], (column(vp_ref, head), column(v_ref, head, one)))

    refs = (q_ref, gain_ref, total_ref, out_ref) + scratch
    attention(spatial, 0, 1, block, place.near, load, refs)


def near_call(head_kind, q, k, v, k_pair, v_pair, gain, total, after, spatial, block):
    heads = head_kind.shape[0]
    return call(
        functools.partial(near_kernel, spatial, block),
        "near",
        shape(q.shape),
        [IN_SMEM] + [ANY] * 8,
        ANY,
        attention_scratch(heads, spatial, 1, block, gain, total),
        (head_kind, q, k, v, k_pair, v_pair, gain, total, after),
    )


def far_kernel(spatial, first, count, block, kind_ref, q_ref, k_ref, v_ref, kp_ref, vp_ref, kx_ref, vx_ref, gain_ref, total_ref, after_ref, have_ref, out_ref, *scratch):
    order, q_buf, k_buf, v_buf, o_buf, factors, sems = scratch[:7]
    put_order(kind_ref, order, spatial)
    place = Place(block)
    one = pl.ds(pl.multiple_of(place.apart, block), block)
    two = pl.ds(pl.multiple_of(place.far, block), 2 * block)

    def load(h):
        n = first + h
        head = order[n]

        @pl.when(place.inner)
        def _():
            fill(k_buf.at[h], sems.at[1, h], (k_ref.at[n], kp_ref.at[n, one]))
            fill(v_buf.at[h], sems.at[2, h], (column(v_ref, head), column(vp_ref, head, one)))

        @pl.when(jnp.logical_not(place.inner))
        def _():
            fill(k_buf.at[h], sems.at[1, h], (k_ref.at[n, two], kx_ref.at[h]))
            fill(v_buf.at[h], sems.at[2, h], (column(v_ref, head, two), vx_ref.at[n]))

    refs = (q_ref, gain_ref, total_ref, out_ref) + scratch
    attention(count, first, 2, block, place.far, load, refs)


def far_call(head_kind, q, k, v, k_pair, v_pair, k_cross, v_cross, gain, total, after, have, first, spatial, block):
    heads = head_kind.shape[0]
    count = k_cross.shape[0]
    return call(
        functools.partial(far_kernel, spatial, first, count, block),
        "far",
        shape(q.shape),
        [IN_SMEM] + [ANY] * 11,
        ANY,
        attention_scratch(heads, count, 2, block, gain, total),
        (head_kind, q, k, v, k_pair, v_pair, k_cross, v_cross, gain, total, after, have),
        aliases={11: 0},
    )


def place_kernel(spatial, firsts, kind_ref, *refs):
    count = len(firsts)
    parts, (out_ref, order, held, sems) = refs[:count], refs[-4:]
    copies = [pltpu.make_async_copy(x, held.at[i], sems.at[0, i]) for i, x in enumerate(parts)]
    start_all(copies)
    put_order(kind_ref, order, spatial)
    core = lax.axis_index("seq").astype(jnp.int32) % 2
    wait_all(copies)
    copies = [
        pltpu.make_async_copy(
            held.at[i],
            column(out_ref, order[spatial + (1 - core if at is None else at)]),
            sems.at[1, i],
        )
        for i, at in enumerate(firsts)
    ]
    start_all(copies)
    wait_all(copies)


def place_call(head_kind, parts, firsts, have, spatial):
    count = len(parts)
    return call(
        functools.partial(place_kernel, spatial, firsts),
        "place",
        shape(have.shape),
        [IN_SMEM] + [ANY] * (count + 1),
        ANY,
        [
            order_scratch(head_kind.shape[0]),
            pltpu.VMEM((count,) + parts[0].shape, BF16),
            pltpu.SemaphoreType.DMA((2, count)),
        ],
        (head_kind, *parts, have),
        aliases={1 + count: 0},
    )


PIECE = 128
CHIPS = 4
TURNS = 3


def deal_kernel(spatial, block, kind_ref, q_ref, k_ref, v_ref, got_ref, *refs):
    small_any, outs = refs[:4], refs[5 : 5 + CHIPS]
    order, held, sems, *small = refs[5 + CHIPS :]
    gq_ref, gk_ref, total_ref, pair_ref = small[:4]
    smalls = small_copies(small_any, small)
    start_all(smalls)
    put_order(kind_ref, order, spatial)
    place = Place(block)
    rows = q_ref.shape[0]
    head = order[spatial + place.core]
    own = pl.ds(pl.multiple_of(place.core * rows, rows), rows)
    other = pl.ds(pl.multiple_of((1 - place.core) * rows, rows), rows)
    ins = [
        pltpu.make_async_copy(column(ref, head), held.at[i, own], sems.at[i])
        for i, ref in enumerate((q_ref, k_ref, v_ref))
    ]
    ins.append(pltpu.make_async_copy(got_ref, held.at[:, other], sems.at[3]))
    start_all(ins)
    wait_all(smalls)
    gains = (gain_of(gq_ref, head) * FACTOR, gain_of(gk_ref, head))
    factors = [
        [row_factors(ref, i, 0, rows) for i in range(2)] for ref in (total_ref, pair_ref)
    ]
    wait_all(ins)
    for half, factor in zip((own, other), factors):
        for i in range(2):
            held[i, half, :] = (held[i, half, :].astype(F32) * factor[i] * gains[i]).astype(BF16)
    copies = []
    for turn in (1, 2, 3, 0):
        owner = place.chip ^ turn
        for g in range(TURNS):
            at = pl.multiple_of((owner + CHIPS * g) * PIECE, PIECE)
            copies.append(
                pltpu.make_async_copy(
                    held.at[:, pl.ds(at, PIECE), :],
                    outs[turn].at[:, g],
                    sems.at[4 + turn * TURNS + g],
                )
            )
    start_all(copies)
    wait_all(copies)


def deal_call(head_kind, queries, keys, values, got, query_gain, key_gain, total, pair, after, spatial, block):
    return call(
        functools.partial(deal_kernel, spatial, block),
        "deal",
        [shape((3, TURNS, PIECE, HEAD_DIM))] * CHIPS,
        [IN_SMEM] + [ANY] * 9,
        [ANY] * CHIPS,
        [
            order_scratch(head_kind.shape[0]),
            pltpu.VMEM((3, 2 * queries.shape[0], HEAD_DIM), BF16),
            pltpu.SemaphoreType.DMA((4 + CHIPS * TURNS,)),
            *small_scratch(query_gain, key_gain, total, pair),
        ],
        (head_kind, queries, keys, values, got, query_gain, key_gain, total, pair, after),
    )


def gather_kernel(spatial, kind_ref, *refs):
    ins = refs[:CHIPS]
    out_ref, send_ref, order, held, sems = refs[-5:]
    put_order(kind_ref, order, spatial)
    index = lax.axis_index("seq").astype(jnp.int32)
    core, chip = index % 2, index // 2
    rows = send_ref.shape[0]
    copies = []
    for turn in range(CHIPS):
        owner = chip ^ turn
        for g in range(TURNS):
            at = pl.multiple_of((owner + CHIPS * g) * PIECE, PIECE)
            copies.append(
                pltpu.make_async_copy(
                    ins[turn].at[g], held.at[pl.ds(at, PIECE)], sems.at[turn * TURNS + g]
                )
            )
    start_all(copies)
    wait_all(copies)
    own = held.at[pl.ds(pl.multiple_of(core * rows, rows), rows)]
    other = held.at[pl.ds(pl.multiple_of((1 - core) * rows, rows), rows)]
    outs = [
        pltpu.make_async_copy(other, send_ref, sems.at[0]),
        pltpu.make_async_copy(own, column(out_ref, order[spatial + core]), sems.at[1]),
    ]
    start_all(outs)
    wait_all(outs)


def gather_call(head_kind, parts, have, spatial):
    rows = have.shape[0]
    return call(
        functools.partial(gather_kernel, spatial),
        "gather",
        [shape(have.shape), shape((rows, HEAD_DIM))],
        [IN_SMEM] + [ANY] * (CHIPS + 1),
        [ANY] * 2,
        [
            order_scratch(head_kind.shape[0]),
            pltpu.VMEM((2 * rows, HEAD_DIM), BF16),
            pltpu.SemaphoreType.DMA((CHIPS * TURNS,)),
        ],
        (head_kind, *parts, have),
        aliases={1 + CHIPS: 0},
    )


GROUPS = (
    ((0, 1), (2, 1), (1, 0), (1, 2), (3, 0), (3, 2)),
    ((0, 0), (0, 2), (2, 0), (2, 2), (1, 1), (3, 1)),
)


def frames_kernel(*refs):
    anys, outs, ins, sems = refs[:CHIPS], refs[CHIPS + 1 : 2 * CHIPS + 1], refs[2 * CHIPS + 1 : -1], refs[-1]
    copies = [pltpu.make_async_copy(a, b, sems.at[i]) for i, (a, b) in enumerate(zip(anys, ins))]
    start_all(copies)
    wait_all(copies)
    row = lax.broadcasted_iota(jnp.int32, (PIECE, PIECE), 0)
    col = lax.broadcasted_iota(jnp.int32, (PIECE, PIECE), 1)
    for group in GROUPS:
        key = jnp.concatenate([ins[s][1, g] for s, g in group], axis=0)
        value = jnp.concatenate([ins[s][2, g] for s, g in group], axis=0)
        wide = jnp.concatenate([value, jnp.ones_like(value)], axis=1)
        same = jnp.concatenate([row == col] * len(group), axis=1)
        for s, g in group:
            scores = lax.dot_general(
                ins[s][0, g], key, (((1,), (1,)), ((), ())), preferred_element_type=F32
            )
            scores = jnp.where(same, scores, LOW)
            top = jnp.max(scores, axis=1, keepdims=True)
            weights = jnp.exp2(scores - top).astype(BF16)
            total = jnp.dot(weights, wide, preferred_element_type=F32)
            outs[s][g] = (total[:, :HEAD_DIM] / total[:, HEAD_DIM:]).astype(BF16)


def frames_call(parts, after):
    return call(
        frames_kernel,
        "frames",
        [shape((TURNS, PIECE, HEAD_DIM))] * CHIPS,
        [ANY] * (CHIPS + 1),
        [IN_VMEM] * CHIPS,
        [pltpu.VMEM(parts[0].shape, BF16) for _ in parts] + [pltpu.SemaphoreType.DMA((CHIPS,))],
        (*parts, after),
    )


def temporal_folded(queries, keys, values, query_gain, key_gain, head_kind, total, spatial, first):
    rows = queries.shape[0]
    heads = head_kind.shape[0]
    count = heads - spatial
    ids = jnp.argsort(head_kind, stable=True)[spatial:]
    take = lambda x: jnp.take(x.reshape(-1, heads, HEAD_DIM), ids, axis=1)
    inverse = lax.rsqrt(total / D + 1e-06)[:, :, None, None]
    norm = lambda x, i, gain: (take(x).astype(F32) * inverse[i] * take(gain)).astype(BF16)
    query = norm(queries, 0, query_gain * FACTOR).astype(F32)
    flat = lambda x: lax.all_gather(x.reshape(rows, -1), "seq", axis=0, tiled=True)
    key_all = flat(norm(keys, 1, key_gain))
    value_all = flat(take(values))
    place = (first + jnp.arange(rows, dtype=jnp.int32)) % FRAME
    running = jnp.full((rows, count), LOW, F32)
    summed = jnp.zeros((rows, count), F32)
    result = jnp.zeros((rows, count, HEAD_DIM), F32)
    for step in range(key_all.shape[0] // FRAME):
        at = place + step * FRAME
        key = jnp.take(key_all, at, axis=0).reshape(rows, count, HEAD_DIM).astype(F32)
        value = jnp.take(value_all, at, axis=0).reshape(rows, count, HEAD_DIM).astype(F32)
        scores = jnp.sum(query * key, axis=2)
        newest = jnp.maximum(running, scores)
        shrink = jnp.exp2(running - newest)
        weight = jnp.exp2(scores - newest)
        summed = summed * shrink + weight
        result = result * shrink[:, :, None] + weight[:, :, None] * value
        running = newest
    done = (result / summed[:, :, None]).astype(BF16)
    return [done[:, j] for j in range(count)]


def per_device(queries, keys, values, query_gain, key_gain, head_kind):
    rows = queries.shape[0]
    heads = head_kind.shape[0]
    temporal = heads // 5
    spatial = heads - temporal
    block = rows // 3
    devices = lax.axis_size("seq")
    parts = lax.axis_size("head")
    dealt = temporal == 2 and devices == 2 * CHIPS and rows == 6 * PIECE
    pair = [(i, i ^ 1) for i in range(devices)]
    cross = []
    for i in range(3, devices, 4):
        after = (i + 1) % devices
        cross += [(i, after), (after, i)]
    turned = [[(i, i ^ (2 * turn)) for i in range(devices)] for turn in range(1, CHIPS)]
    send = lambda x, route: lax.ppermute(x, "seq", route)
    gq, gk = query_gain, key_gain

    v_pair = send(values, pair)
    sums, v_near, *t_send = first_call(head_kind, queries, keys, values, spatial, block, dealt)
    v_cross = send(v_near, cross)
    total = sums
    for d in range(1, parts):
        total = total + lax.ppermute(sums, "head", [(i, (i + d) % parts) for i in range(parts)])
    last = total
    if dealt:
        t_got = send(t_send[0], pair)
        pair_total = send(total, pair)
        pieces = deal_call(
            head_kind, queries, keys, values, t_got, gq, gk, total, pair_total, v_pair,
            spatial, block,
        )
        arrived = [pieces[0]] + [send(p, r) for p, r in zip(pieces[1:], turned)]
        last = pieces[0]
    k, *k_near = keys_call(head_kind, keys, gk, total, last, v_cross, spatial, block)
    k_pair = send(k, pair)
    k_cross = [send(part, cross) for part in k_near]
    out = near_call(head_kind, queries, k, values, k_pair, v_pair, gq, total, total, spatial, block)
    last = total
    if dealt:
        results = frames_call(arrived, out)
        back = [results[0]] + [send(p, r) for p, r in zip(results[1:], turned)]
        last = results[0]
    each = spatial // CHUNKS
    for c, part in enumerate(k_cross):
        out = far_call(
            head_kind, queries, k, values, k_pair, v_pair, part, v_cross, gq, total, last, out,
            c * each, spatial, block,
        )
        if dealt and c == 0:
            out, t_other = gather_call(head_kind, back, out, spatial)
            t_other = send(t_other, pair)
    if dealt:
        return place_call(head_kind, [t_other], [None], out, spatial)
    index = lax.axis_index("seq").astype(jnp.int32)
    t_out = temporal_folded(
        queries, keys, values, query_gain, key_gain, head_kind, total, spatial, index * rows
    )
    return place_call(head_kind, t_out, list(range(temporal)), out, spatial)


def solution(mesh):
    placed = (P("seq", "head"), P("seq", "head"), P("seq", "head"), P("head"), P("head"), P("head"))
    return jax.shard_map(
        per_device, mesh=mesh, in_specs=placed, out_specs=P("seq", "head"), check_vma=False
    )
```

time: 454 us -> 83.3 us (0.18)
  local copies, waits for them, and re-layouts: 200 us -> 1.19 us
  matrix products: 65.4 us -> 0 us
  waiting for transfers between devices: 77.1 us -> 13.6 us
  other arithmetic: 62.8 us -> 0.7 us
  Pallas kernels: 0 us -> 42.6 us
  starting transfers between devices: 0.55 us -> 24.4 us
  loops' own time: 16.4 us -> 0 us
  between operations: 14 us -> 0.18 us
  blocking collectives: 13.7 us -> 0 us
    gather x20 -> x0, local copies, waits for them, and re-layouts: 70.9 us -> none  [the longest x6 29.6 us: temporal_folded(): jnp.take(value_piece, clipped, axis=0).reshape(rows, count, size)]
    slice x8 -> x0, local copies, waits for them, and re-layouts: 66.8 us -> none  [per_head(): value_one = lax.dynamic_index_in_dim(widened[1], which, 1, keepdims=False)]
    dot_general x48 -> x0, matrix products: 65.4 us -> none  [the longest x24 33.2 us: per_head(): lax.dot_general(query_block, key_frame, (((1,), (1,)), ((), ())), preferr...]
    ppermute x2 -> x17, waiting for transfers between devices: 77.1 us -> 13.6 us  [the longest x3 7.19 us: per_device(): lax.ppermute(sums, 'head', [(i, (i + d) % parts) for i in range(parts)])]
    pallas_call x0 -> x9, Pallas kernels: none -> 42.6 us  [call(): pl.pallas_call(kernel, out_shape=out_shape, in_specs=in_specs, out_specs=...]
    convert_element_type x12 -> x0, local copies, waits for them, and re-layouts: 28.1 us -> none  [temporal_folded(): jnp.take(key_piece, clipped, axis=0).reshape(rows, count, size)]
    ppermute x2 -> x17, starting transfers between devices: 0.51 us -> 24.4 us  [the longest x14 20.5 us: per_device(): send = lambda x, route: lax.ppermute(x, 'seq', route)]
    convert_element_type x9 -> x0, other arithmetic: 20.8 us -> none  [the longest x6 12.6 us: temporal_folded(): jnp.take(key_piece, clipped, axis=0).reshape(rows, count, size)]
  transfers between devices with their start and end apart: 4 -> 17, of which waited for: 2 -> 7; matrix products, arithmetic and copies ran while one was open for 43% -> 1% of each run, Pallas kernels for 0% -> 45%
where the time goes in v2:
time: 83.3 us; the launch traced here: 82.7 us
  Pallas kernels  42.6 us (51%)
  starting transfers between devices  24.4 us (29%)
  waiting for transfers between devices  13.6 us (16%)
  local copies, waits for them, and re-layouts  1.19 us (1%)
    pallas_call x9, Pallas kernels, call(): pl.pallas_call(kernel, out_shape=out_shape, in_specs=in_specs, out_specs=...  42.6 us
    ppermute x14, starting transfers between devices, per_device(): send = lambda x, route: lax.ppermute(x, 'seq', route)  20.5 us
    ppermute x3, waiting for transfers between devices, per_device(): lax.ppermute(sums, 'head', [(i, (i + d) % parts) for i in range(parts)])  7.19 us
    ppermute x14, waiting for transfers between devices, per_device(): send = lambda x, route: lax.ppermute(x, 'seq', route)  6.4 us
    ppermute x3, starting transfers between devices, per_device(): lax.ppermute(sums, 'head', [(i, (i + d) % parts) for i in range(parts)])  3.87 us
  transfers between devices with their start and end apart: 17, of which 7 were waited for; matrix products, arithmetic and copies ran while one was open for 1% of the time, Pallas kernels for 45%

profile of v2, /device:TPU:0, one launch (start us, length us, event | category | flops | bytes accessed | tf_op | source)
XLA Modules:
  0.0 82.7 jit_solution(12052137280776344679)
XLA Ops:
  0.0 0.5 collective-permute-start.5
  0.5 5.9 %first.1 = (f32[2,768]{1,0:T(2,128)}, bf16[8,512,128]{2,1,0:T(8,128)(2,1)}, bf16[3,768,128]{2,1,0:T(8,128)(2,1)}) custom-call(s32[10]{0:T(128)} %kind_ref.15, bf16[768,1280]{1,0:T(8,128)(2,1)} %q_ref.9, bf16[768,1280]{1,0:T(8,128)(2,1)} %k_ref.5, bf16[768,1280]{1,0:T(8,128)(2,1)} %v_ref.9), custom_call_target="tpu_custom_call" | custom-call | flops 1000 | bytes 1000 | tf_op jit(solution)/shard_map/first/pallas_call | solution.py:32
  6.3 5.5 %collective-permute-start.9 = (bf16[8,512,128]{2,1,0:T(8,128)(2,1)}, bf16[8,512,128]{2,1,0:T(8,128)(2,1)}, u32[]{:S(2)}, u32[]{:S(2)}) collective-permute-start(bf16[8,512,128]{2,1,0:T(8,128)(2,1)} %get-tuple-element.27), channel_id=1, source_target_pairs={{12,16},{16,12},{28,0},{0,28},{13,17},{17,13},{29,1},{1,29},{14,18... | collective-permute-start | bytes 3145736 | tf_op jit(solution)/shard_map/ppermute | solution.py:645
  11.8 0.1 collective-permute-start
  11.9 3.6 %collective-permute-start.3 = (f32[2,768]{1,0:T(2,128)}, f32[2,768]{1,0:T(2,128)S(1)}, u32[]{:S(2)}, u32[]{:S(2)}) collective-permute-start(f32[2,768]{1,0:T(2,128)} %get-tuple-element.22), channel_id=1, source_target_pairs={{0,3},{1,0},{2,1},{3,2},{4,7},{5,4},{6,5},{7,6},{8,11},{9,8},{10,9... | collective-permute-start | bytes 18440 | tf_op jit(solution)/shard_map/ppermute | solution.py:653
  15.5 0.0 collective-permute-start.2
  15.5 1.6 %collective-permute-done.3 = f32[2,768]{1,0:T(2,128)S(1)} collective-permute-done((f32[2,768]{1,0:T(2,128)}, f32[2,768]{1,0:T(2,128)S(1)}, u32[]{:S(2)}, u32[]{:S(2)}) %collective-permute-start.3) | collective-permute-done | bytes 6176 | tf_op jit(solution)/shard_map/ppermute | solution.py:653
  17.1 0.3 collective-permute-start.1
  17.3 2.9 %collective-permute-done.2 = f32[2,768]{1,0:T(2,128)S(1)} collective-permute-done((f32[2,768]{1,0:T(2,128)}, f32[2,768]{1,0:T(2,128)S(1)}, u32[]{:S(2)}, u32[]{:S(2)}) %collective-permute-start.2) | collective-permute-done | bytes 6176 | tf_op jit(solution)/shard_map/ppermute | solution.py:653
  20.3 2.7 %collective-permute-done.1 = f32[2,768]{1,0:T(2,128)S(1)} collective-permute-done((f32[2,768]{1,0:T(2,128)}, f32[2,768]{1,0:T(2,128)S(1)}, u32[]{:S(2)}, u32[]{:S(2)}) %collective-permute-start.1) | collective-permute-done | bytes 6176 | tf_op jit(solution)/shard_map/ppermute | solution.py:653
  23.0 0.7 add_add_fusion.refs_2_.total_any.total_ref.after_ref
  23.7 0.0 copy-start
  23.7 0.6 copy-done
  24.3 0.0 collective-permute-start.4
  24.3 1.2 %collective-permute-done.4.refs_3_ = f32[2,768]{1,0:T(2,128)S(1)} collective-permute-done((f32[2,768]{1,0:T(2,128)S(1)}, f32[2,768]{1,0:T(2,128)S(1)}, u32[]{:S(2)}, u32[]{:S(2)}) %collective-permute-start.4) | collective-permute-done | bytes 6176 | tf_op jit(solution)/shard_map/ppermute | solution.py:645
  25.4 0.0 copy-start.1
  25.4 0.6 copy-done.1
  26.0 0.0 collective-permute-done.got_ref
  26.0 0.0 collective-permute-done.5.refs_4_.vp_ref
  26.0 3.7 %deal.1 = (bf16[3,3,128,128]{3,2,1,0:T(8,128)(2,1)}, bf16[3,3,128,128]{3,2,1,0:T(8,128)(2,1)}, bf16[3,3,128,128]{3,2,1,0:T(8,128)(2,1)}, bf16[3,3,128,128]{3,2,1,0:T(8,128)(2,1)}) custom-call(s32[10]{0:T(128)} %kind_ref.15, bf16[768,1280]{1,0:T(8,128)(2,1)} %q_ref.9, bf16[768,1280]{1,0:T(8,128)(2,1)} %k_ref.5, bf16[768,1280]{1,0:T(8,128)(2,1)} %v_ref.9, ...), custom_call_target="tpu_custom_call" | custom-call | flops 1000 | bytes 1000 | tf_op jit(solution)/shard_map/deal/pallas_call | solution.py:32
  29.8 0.0 collective-permute-done.9.after_too.vx_ref
  29.8 3.5 %keys.1 = (bf16[8,768,128]{2,1,0:T(8,128)(2,1)}, bf16[4,512,128]{2,1,0:T(8,128)(2,1)}, bf16[4,512,128]{2,1,0:T(8,128)(2,1)}) custom-call(s32[10]{0:T(128)} %kind_ref.15, bf16[768,1280]{1,0:T(8,128)(2,1)} %k_ref.5, f32[1280]{0:T(1024)} %gain_any.1, f32[2,768]{1,0:T(2,128)} %copy-done, bf16[3,3,128,128]{3,2,1,0:T(8,128)(2,1)} %get-tuple-element.23.after_ref.refs_0_, ...), custom_call_target="tpu_custom_call" | custom-call | flops 1000 | bytes 1000 | tf_op jit(solution)/shard_map/keys/pallas_call | solution.py:32
  33.3 0.2 collective-permute-start.10
  33.5 2.3 %collective-permute-start.14 = (bf16[4,512,128]{2,1,0:T(8,128)(2,1)}, bf16[4,512,128]{2,1,0:T(8,128)(2,1)}, u32[]{:S(2)}, u32[]{:S(2)}) collective-permute-start(bf16[4,512,128]{2,1,0:T(8,128)(2,1)} %get-tuple-element.33), channel_id=1, source_target_pairs={{12,16},{16,12},{28,0},{0,28},{13,17},{17,13},{29,1},{1,29},{14,18... | collective-permute-start | bytes 1572872 | tf_op jit(solution)/shard_map/ppermute | solution.py:645
  35.8 0.1 collective-permute-start.6
  35.9 1.6 %collective-permute-start.7 = (bf16[3,3,128,128]{3,2,1,0:T(8,128)(2,1)}, bf16[3,3,128,128]{3,2,1,0:T(8,128)(2,1)}, u32[]{:S(2)}, u32[]{:S(2)}) collective-permute-start(bf16[3,3,128,128]{3,2,1,0:T(8,128)(2,1)} %get-tuple-element.25), channel_id=1, source_target_pairs={{0,16},{4,20},{8,24},{12,28},{16,0},{20,4},{24,8},{28,12},{1,17},{... | collective-permute-start | bytes 884744 | tf_op jit(solution)/shard_map/ppermute | solution.py:645
  37.4 1.9 %collective-permute-start.8 = (bf16[3,3,128,128]{3,2,1,0:T(8,128)(2,1)}, bf16[3,3,128,128]{3,2,1,0:T(8,128)(2,1)}, u32[]{:S(2)}, u32[]{:S(2)}) collective-permute-start(bf16[3,3,128,128]{3,2,1,0:T(8,128)(2,1)} %get-tuple-element.26), channel_id=1, source_target_pairs={{0,24},{4,28},{8,16},{12,20},{16,8},{20,12},{24,0},{28,4},{1,25},{... | collective-permute-start | bytes 884744 | tf_op jit(solution)/shard_map/ppermute | solution.py:645
  39.3 0.0 collective-permute-done.10.kp_ref
  39.3 3.3 %collective-permute-start.16 = (bf16[4,512,128]{2,1,0:T(8,128)(2,1)}, bf16[4,512,128]{2,1,0:T(8,128)(2,1)}, u32[]{:S(2)}, u32[]{:S(2)}) collective-permute-start(bf16[4,512,128]{2,1,0:T(8,128)(2,1)} %get-tuple-element.35), channel_id=1, source_target_pairs={{12,16},{16,12},{28,0},{0,28},{13,17},{17,13},{29,1},{1,29},{14,18... | collective-permute-start | bytes 1572872 | tf_op jit(solution)/shard_map/ppermute | solution.py:645
  42.7 7.6 %near.1.refs_4_.have_ref = bf16[768,1280]{1,0:T(8,128)(2,1)} custom-call(s32[10]{0:T(128)} %kind_ref.15, bf16[768,1280]{1,0:T(8,128)(2,1)} %q_ref.9, bf16[8,768,128]{2,1,0:T(8,128)(2,1)} %get-tuple-element.28.k_ref, bf16[768,1280]{1,0:T(8,128)(2,1)} %v_ref.9, bf16[8,768,128]{2,1,0:T(8,128)(2,1)} %collective-permute-done.10.kp_ref, ...), custom_call_target="tpu_custom_call" | custom-call | flops 1000 | bytes 1000 | tf_op jit(solution)/shard_map/near/pallas_call | solution.py:32
  50.3 2.0 %collective-permute-done.6.refs_1_ = bf16[3,3,128,128]{3,2,1,0:T(8,128)(2,1)} collective-permute-done((bf16[3,3,128,128]{3,2,1,0:T(8,128)(2,1)}, bf16[3,3,128,128]{3,2,1,0:T(8,128)(2,1)}, u32[]{:S(2)}, u32[]{:S(2)}) %collective-permute-start.6) | collective-permute-done | bytes 294944 | tf_op jit(solution)/shard_map/ppermute | solution.py:645
  52.3 2.4 %collective-permute-done.7.refs_2_ = bf16[3,3,128,128]{3,2,1,0:T(8,128)(2,1)} collective-permute-done((bf16[3,3,128,128]{3,2,1,0:T(8,128)(2,1)}, bf16[3,3,128,128]{3,2,1,0:T(8,128)(2,1)}, u32[]{:S(2)}, u32[]{:S(2)}) %collective-permute-start.7) | collective-permute-done | bytes 294944 | tf_op jit(solution)/shard_map/ppermute | solution.py:645
  54.7 0.8 collective-permute-done.8.refs_3_
  55.5 3.7 %frames.1 = (bf16[3,128,128]{2,1,0:T(8,128)(2,1)}, bf16[3,128,128]{2,1,0:T(8,128)(2,1)}, bf16[3,128,128]{2,1,0:T(8,128)(2,1)}, bf16[3,128,128]{2,1,0:T(8,128)(2,1)}) custom-call(bf16[3,3,128,128]{3,2,1,0:T(8,128)(2,1)} %get-tuple-element.23.after_ref.refs_0_, bf16[3,3,128,128]{3,2,1,0:T(8,128)(2,1)} %collective-permute-done.6.refs_1_, ...), custom_call_target="tpu_custom_call" | custom-call | flops 1000 | bytes 1000 | tf_op jit(solution)/shard_map/frames/pallas_call | solution.py:32
  59.1 3.5 %collective-permute-start.11 = (bf16[3,128,128]{2,1,0:T(8,128)(2,1)}, bf16[3,128,128]{2,1,0:T(8,128)(2,1)}, u32[]{:S(2)}, u32[]{:S(2)}) collective-permute-start(bf16[3,128,128]{2,1,0:T(8,128)(2,1)} %get-tuple-element.30), channel_id=1, source_target_pairs={{0,8},{4,12},{8,0},{12,4},{16,24},{20,28},{24,16},{28,20},{1,9},{5... | collective-permute-start | bytes 294920 | tf_op jit(solution)/shard_map/ppermute | solution.py:645
  62.6 0.6 collective-permute-start.12
  63.2 1.0 %collective-permute-start.13 = (bf16[3,128,128]{2,1,0:T(8,128)(2,1)}, bf16[3,128,128]{2,1,0:T(8,128)(2,1)}, u32[]{:S(2)}, u32[]{:S(2)}) collective-permute-start(bf16[3,128,128]{2,1,0:T(8,128)(2,1)} %get-tuple-element.32), channel_id=1, source_target_pairs={{0,24},{4,28},{8,16},{12,20},{16,8},{20,12},{24,0},{28,4},{1,25},{... | collective-permute-start | bytes 294920 | tf_op jit(solution)/shard_map/ppermute | solution.py:645
  64.1 0.0 collective-permute-done.14.kx_ref
  64.1 6.7 %far.2.refs_4_ = bf16[768,1280]{1,0:T(8,128)(2,1)} custom-call(s32[10]{0:T(128)} %kind_ref.15, bf16[768,1280]{1,0:T(8,128)(2,1)} %q_ref.9, bf16[8,768,128]{2,1,0:T(8,128)(2,1)} %get-tuple-element.28.k_ref, bf16[768,1280]{1,0:T(8,128)(2,1)} %v_ref.9, bf16[8,768,128]{2,1,0:T(8,128)(2,1)} %collective-permute-done.10.kp_ref, ...), custom_call_target="tpu_custom_call", output_to_operand_aliasing={{}: (11, {})} | custom-call | flops 1000 | bytes 1000 | tf_op jit(solution)/shard_map/far/pallas_call | solution.py:32
  70.9 0.0 collective-permute-done.11.refs_1_
  70.9 0.0 collective-permute-done.12.refs_2_
  70.9 0.0 collective-permute-done.13.refs_3_
  70.9 2.6 %gather.1 = (bf16[768,1280]{1,0:T(8,128)(2,1)}, bf16[768,128]{1,0:T(8,128)(2,1)}) custom-call(s32[10]{0:T(128)} %kind_ref.15, bf16[3,128,128]{2,1,0:T(8,128)(2,1)} %get-tuple-element.29.after_ref.refs_0_, bf16[3,128,128]{2,1,0:T(8,128)(2,1)} %collective-permute-done.11.refs_1_, ...), custom_call_target="tpu_custom_call", output_to_operand_aliasing={{0}: (5, {})} | custom-call | flops 1000 | bytes 1000 | tf_op jit(solution)/shard_map/gather/pallas_call | solution.py:32
  73.5 0.1 collective-permute-start.15
  73.6 0.0 collective-permute-done.16.kx_ref
  73.6 6.8 %far.3.refs_1_ = bf16[768,1280]{1,0:T(8,128)(2,1)} custom-call(s32[10]{0:T(128)} %kind_ref.15, bf16[768,1280]{1,0:T(8,128)(2,1)} %q_ref.9, bf16[8,768,128]{2,1,0:T(8,128)(2,1)} %get-tuple-element.28.k_ref, bf16[768,1280]{1,0:T(8,128)(2,1)} %v_ref.9, bf16[8,768,128]{2,1,0:T(8,128)(2,1)} %collective-permute-done.10.kp_ref, ...), custom_call_target="tpu_custom_call", output_to_operand_aliasing={{}: (11, {})} | custom-call | flops 1000 | bytes 1000 | tf_op jit(solution)/shard_map/far/pallas_call | solution.py:32
  80.4 0.0 collective-permute-done.15.refs_0_
  80.4 2.3 %place.1 = bf16[768,1280]{1,0:T(8,128)(2,1)} custom-call(s32[10]{0:T(128)} %kind_ref.15, bf16[768,128]{1,0:T(8,128)(2,1)} %collective-permute-done.15.refs_0_, bf16[768,1280]{1,0:T(8,128)(2,1)} %far.3.refs_1_), custom_call_target="tpu_custom_call", output_to_operand_aliasing={{}: (2, {})} | custom-call | flops 1000 | bytes 1000 | tf_op jit(solution)/shard_map/place/pallas_call | solution.py:32
Async XLA Ops:
  0.0 26.0 %collective-permute-start.5 = (bf16[768,1280]{1,0:T(8,128)(2,1)}, bf16[768,1280]{1,0:T(8,128)(2,1)}, u32[]{:S(2)}, u32[]{:S(2)}) collective-permute-start(bf16[768,1280]{1,0:T(8,128)(2,1)} %v_ref.9), channel_id=1, source_target_pairs={{0,4},{4,0},{8,12},{12,8},{16,20},{20,16},{24,28},{28,24},{1,5},{5... | collective-permute-start | bytes 5898248 | tf_op jit(solution)/shard_map/ppermute | solution.py:645
  6.3 23.5 %collective-permute-start.9 = (bf16[8,512,128]{2,1,0:T(8,128)(2,1)}, bf16[8,512,128]{2,1,0:T(8,128)(2,1)}, u32[]{:S(2)}, u32[]{:S(2)}) collective-permute-start(bf16[8,512,128]{2,1,0:T(8,128)(2,1)} %get-tuple-element.27), channel_id=1, source_target_pairs={{12,16},{16,12},{28,0},{0,28},{13,17},{17,13},{29,1},{1,29},{14,18... | collective-permute-start | bytes 3145736 | tf_op jit(solution)/shard_map/ppermute | solution.py:645
  11.8 14.2 %collective-permute-start = (bf16[3,768,128]{2,1,0:T(8,128)(2,1)}, bf16[3,768,128]{2,1,0:T(8,128)(2,1)}, u32[]{:S(2)}, u32[]{:S(2)}) collective-permute-start(bf16[3,768,128]{2,1,0:T(8,128)(2,1)} %get-tuple-element.21), channel_id=1, source_target_pairs={{0,4},{4,0},{8,12},{12,8},{16,20},{20,16},{24,28},{28,24},{1,5},{5... | collective-permute-start | bytes 1769480 | tf_op jit(solution)/shard_map/ppermute | solution.py:645
  11.9 5.2 %collective-permute-start.3 = (f32[2,768]{1,0:T(2,128)}, f32[2,768]{1,0:T(2,128)S(1)}, u32[]{:S(2)}, u32[]{:S(2)}) collective-permute-start(f32[2,768]{1,0:T(2,128)} %get-tuple-element.22), channel_id=1, source_target_pairs={{0,3},{1,0},{2,1},{3,2},{4,7},{5,4},{6,5},{7,6},{8,11},{9,8},{10,9... | collective-permute-start | bytes 18440 | tf_op jit(solution)/shard_map/ppermute | solution.py:653
  15.5 4.7 %collective-permute-start.2 = (f32[2,768]{1,0:T(2,128)}, f32[2,768]{1,0:T(2,128)S(1)}, u32[]{:S(2)}, u32[]{:S(2)}) collective-permute-start(f32[2,768]{1,0:T(2,128)} %get-tuple-element.22), channel_id=1, source_target_pairs={{0,2},{1,3},{2,0},{3,1},{4,6},{5,7},{6,4},{7,5},{8,10},{9,11},{10,... | collective-permute-start | bytes 18440 | tf_op jit(solution)/shard_map/ppermute | solution.py:653
  17.1 5.9 %collective-permute-start.1 = (f32[2,768]{1,0:T(2,128)}, f32[2,768]{1,0:T(2,128)S(1)}, u32[]{:S(2)}, u32[]{:S(2)}) collective-permute-start(f32[2,768]{1,0:T(2,128)} %get-tuple-element.22), channel_id=1, source_target_pairs={{0,1},{1,2},{2,3},{3,0},{4,5},{5,6},{6,7},{7,4},{8,9},{9,10},{10,1... | collective-permute-start | bytes 18440 | tf_op jit(solution)/shard_map/ppermute | solution.py:653
  23.7 0.6 copy-start
  24.3 1.2 %collective-permute-start.4 = (f32[2,768]{1,0:T(2,128)S(1)}, f32[2,768]{1,0:T(2,128)S(1)}, u32[]{:S(2)}, u32[]{:S(2)}) collective-permute-start(f32[2,768]{1,0:T(2,128)S(1)} %add_add_fusion.refs_2_.total_any.total_ref.after_ref), channel_id=1, source_target_pairs={{0,4},{4,0},{8,12},{12,8},{16,20},{20,16},{24,28},{28,24},{1,5},{5... | collective-permute-start | bytes 18440 | tf_op jit(solution)/shard_map/ppermute | solution.py:645
  25.4 0.6 copy-start.1
  33.3 6.1 %collective-permute-start.10 = (bf16[8,768,128]{2,1,0:T(8,128)(2,1)}, bf16[8,768,128]{2,1,0:T(8,128)(2,1)}, u32[]{:S(2)}, u32[]{:S(2)}) collective-permute-start(bf16[8,768,128]{2,1,0:T(8,128)(2,1)} %get-tuple-element.28.k_ref), channel_id=1, source_target_pairs={{0,4},{4,0},{8,12},{12,8},{16,20},{20,16},{24,28},{28,24},{1,5},{5... | collective-permute-start | bytes 4718600 | tf_op jit(solution)/shard_map/ppermute | solution.py:645
  33.5 30.6 %collective-permute-start.14 = (bf16[4,512,128]{2,1,0:T(8,128)(2,1)}, bf16[4,512,128]{2,1,0:T(8,128)(2,1)}, u32[]{:S(2)}, u32[]{:S(2)}) collective-permute-start(bf16[4,512,128]{2,1,0:T(8,128)(2,1)} %get-tuple-element.33), channel_id=1, source_target_pairs={{12,16},{16,12},{28,0},{0,28},{13,17},{17,13},{29,1},{1,29},{14,18... | collective-permute-start | bytes 1572872 | tf_op jit(solution)/shard_map/ppermute | solution.py:645
  35.8 16.5 %collective-permute-start.6 = (bf16[3,3,128,128]{3,2,1,0:T(8,128)(2,1)}, bf16[3,3,128,128]{3,2,1,0:T(8,128)(2,1)}, u32[]{:S(2)}, u32[]{:S(2)}) collective-permute-start(bf16[3,3,128,128]{3,2,1,0:T(8,128)(2,1)} %get-tuple-element.24), channel_id=1, source_target_pairs={{0,8},{4,12},{8,0},{12,4},{16,24},{20,28},{24,16},{28,20},{1,9},{5... | collective-permute-start | bytes 884744 | tf_op jit(solution)/shard_map/ppermute | solution.py:645
  35.9 18.8 %collective-permute-start.7 = (bf16[3,3,128,128]{3,2,1,0:T(8,128)(2,1)}, bf16[3,3,128,128]{3,2,1,0:T(8,128)(2,1)}, u32[]{:S(2)}, u32[]{:S(2)}) collective-permute-start(bf16[3,3,128,128]{3,2,1,0:T(8,128)(2,1)} %get-tuple-element.25), channel_id=1, source_target_pairs={{0,16},{4,20},{8,24},{12,28},{16,0},{20,4},{24,8},{28,12},{1,17},{... | collective-permute-start | bytes 884744 | tf_op jit(solution)/shard_map/ppermute | solution.py:645
  37.4 18.0 %collective-permute-start.8 = (bf16[3,3,128,128]{3,2,1,0:T(8,128)(2,1)}, bf16[3,3,128,128]{3,2,1,0:T(8,128)(2,1)}, u32[]{:S(2)}, u32[]{:S(2)}) collective-permute-start(bf16[3,3,128,128]{3,2,1,0:T(8,128)(2,1)} %get-tuple-element.26), channel_id=1, source_target_pairs={{0,24},{4,28},{8,16},{12,20},{16,8},{20,12},{24,0},{28,4},{1,25},{... | collective-permute-start | bytes 884744 | tf_op jit(solution)/shard_map/ppermute | solution.py:645
  39.3 34.3 %collective-permute-start.16 = (bf16[4,512,128]{2,1,0:T(8,128)(2,1)}, bf16[4,512,128]{2,1,0:T(8,128)(2,1)}, u32[]{:S(2)}, u32[]{:S(2)}) collective-permute-start(bf16[4,512,128]{2,1,0:T(8,128)(2,1)} %get-tuple-element.35), channel_id=1, source_target_pairs={{12,16},{16,12},{28,0},{0,28},{13,17},{17,13},{29,1},{1,29},{14,18... | collective-permute-start | bytes 1572872 | tf_op jit(solution)/shard_map/ppermute | solution.py:645
  59.1 11.8 %collective-permute-start.11 = (bf16[3,128,128]{2,1,0:T(8,128)(2,1)}, bf16[3,128,128]{2,1,0:T(8,128)(2,1)}, u32[]{:S(2)}, u32[]{:S(2)}) collective-permute-start(bf16[3,128,128]{2,1,0:T(8,128)(2,1)} %get-tuple-element.30), channel_id=1, source_target_pairs={{0,8},{4,12},{8,0},{12,4},{16,24},{20,28},{24,16},{28,20},{1,9},{5... | collective-permute-start | bytes 294920 | tf_op jit(solution)/shard_map/ppermute | solution.py:645
  62.6 8.3 %collective-permute-start.12 = (bf16[3,128,128]{2,1,0:T(8,128)(2,1)}, bf16[3,128,128]{2,1,0:T(8,128)(2,1)}, u32[]{:S(2)}, u32[]{:S(2)}) collective-permute-start(bf16[3,128,128]{2,1,0:T(8,128)(2,1)} %get-tuple-element.31), channel_id=1, source_target_pairs={{0,16},{4,20},{8,24},{12,28},{16,0},{20,4},{24,8},{28,12},{1,17},{... | collective-permute-start | bytes 294920 | tf_op jit(solution)/shard_map/ppermute | solution.py:645
  63.2 7.7 %collective-permute-start.13 = (bf16[3,128,128]{2,1,0:T(8,128)(2,1)}, bf16[3,128,128]{2,1,0:T(8,128)(2,1)}, u32[]{:S(2)}, u32[]{:S(2)}) collective-permute-start(bf16[3,128,128]{2,1,0:T(8,128)(2,1)} %get-tuple-element.32), channel_id=1, source_target_pairs={{0,24},{4,28},{8,16},{12,20},{16,8},{20,12},{24,0},{28,4},{1,25},{... | collective-permute-start | bytes 294920 | tf_op jit(solution)/shard_map/ppermute | solution.py:645
  73.5 6.9 %collective-permute-start.15 = (bf16[768,128]{1,0:T(8,128)(2,1)}, bf16[768,128]{1,0:T(8,128)(2,1)}, u32[]{:S(2)}, u32[]{:S(2)}) collective-permute-start(bf16[768,128]{1,0:T(8,128)(2,1)} %get-tuple-element.34), channel_id=1, source_target_pairs={{0,4},{4,0},{8,12},{12,8},{16,20},{20,16},{24,28},{28,24},{1,5},{5... | collective-permute-start | bytes 589832 | tf_op jit(solution)/shard_map/ppermute | solution.py:645

commit v3 on v0

v3 whole, which is shorter than its diff:
```python
import functools
import math

import jax
import jax.numpy as jnp
from jax import lax
from jax.experimental import pallas as pl
from jax.experimental.pallas import tpu as pltpu
from jax.sharding import PartitionSpec as P

HEAD_DIM = 128
D = 5120
FRAME = 1024
OFFSET = 512
VMEM = 24 * 1024 * 1024
VMEM_FIRST = 61 * 1024 * 1024
LOW = -1e30
FACTOR = math.log2(math.e) / math.sqrt(HEAD_DIM)
F32 = jnp.float32
BF16 = jnp.bfloat16
CHUNKS = 4
ANY = pl.BlockSpec(memory_space=pltpu.HBM)
LOOSE = pl.BlockSpec(memory_space=pl.ANY)
IN_SMEM = pl.BlockSpec(memory_space=pltpu.SMEM)
IN_VMEM = pl.BlockSpec(memory_space=pltpu.VMEM)


def shape(dims, dtype=BF16):
    return jax.ShapeDtypeStruct(dims, dtype)


def call(kernel, name, out_shape, in_specs, out_specs, scratch, operands, aliases=None, cycles=1000, vmem=VMEM):
    return pl.pallas_call(
        kernel,
        out_shape=out_shape,
        in_specs=in_specs,
        out_specs=out_specs,
        scratch_shapes=scratch,
        input_output_aliases=aliases or {},
        compiler_params=pltpu.CompilerParams(vmem_limit_bytes=vmem),
        cost_estimate=pl.CostEstimate(flops=1000 * cycles, bytes_accessed=1000, transcendentals=0),
        name=name,
    )(*operands)


def column(ref, head, rows=None):
    lanes = pl.ds(pl.multiple_of(head * HEAD_DIM, HEAD_DIM), HEAD_DIM)
    return ref.at[:, lanes] if rows is None else ref.at[rows, lanes]


def put_order(kind_ref, order_ref, spatial):
    heads = kind_ref.shape[0]

    def step(h, count):
        s, t = count
        temporal = kind_ref[h] == 1
        order_ref[jnp.where(temporal, spatial + t, s)] = h
        return jnp.where(temporal, s, s + 1), jnp.where(temporal, t + 1, t)

    lax.fori_loop(0, heads, step, (jnp.int32(0), jnp.int32(0)))


def order_scratch(heads):
    return pltpu.SMEM((heads,), jnp.int32)


class Place:
    def __init__(self, block=1):
        index = lax.axis_index("seq").astype(jnp.int32)
        self.kind = index % 4
        self.core = index % 2
        self.chip = index // 2
        self.inner = (self.kind == 1) | (self.kind == 2)
        self.apart = jnp.where((self.kind == 0) | (self.kind == 1), 2 * block, 0)
        self.near = jnp.where(self.kind == 0, 2 * block, 0)
        self.far = jnp.where(self.kind == 0, 0, block)
        self.cross = jnp.where(self.kind == 0, 0, block)


def lanes(head):
    return pl.ds(pl.multiple_of(head * HEAD_DIM, HEAD_DIM), HEAD_DIM)


def start_all(copies):
    for copy in copies:
        copy.start()


def wait_all(copies):
    for copy in copies:
        copy.wait()


def first_kernel(spatial, block, dealt, kind_ref, q_any, k_any, v_any, sums_ref, vx_ref, *refs):
    order, held, squares, sems = refs[-4:]
    rows, width = q_any.shape
    steps = (sems.shape[0] - 1) // 2
    size = rows // steps
    copies = [
        [
            pltpu.make_async_copy(
                source.at[pl.ds(s * size, size), :],
                held.at[i, pl.ds(s * size, size), :],
                sems.at[i * steps + s],
            )
            for s in range(steps)
        ]
        for i, source in enumerate((q_any, k_any))
    ]
    v_copy = pltpu.make_async_copy(v_any, held.at[2], sems.at[2 * steps])
    start_all(copies[0] + copies[1] + [v_copy])
    put_order(kind_ref, order, spatial)
    place = Place(block)
    across = pl.ds(pl.multiple_of(place.cross, block), 2 * block)
    for i in range(2):
        for s in range(steps):
            copies[i][s].wait()
            total = None
            for c in range(width // HEAD_DIM):
                x = held[i, s * size : (s + 1) * size, c * HEAD_DIM : (c + 1) * HEAD_DIM].astype(F32)
                total = x * x if total is None else total + x * x
            squares[s * size : (s + 1) * size, :] = total
        sums_ref[i : i + 1, :] = jnp.sum(jnp.transpose(squares[...]), axis=0, keepdims=True)
    v_copy.wait()
    for h in range(spatial):
        vx_ref[h] = held[2, across, lanes(order[h])]
    if dealt:
        for j, ref in enumerate(refs[:2]):
            one = lanes(order[spatial + (1 - place.core if j == 0 else place.core)])
            for i in range(3):
                ref[i] = held[i, :, one]


def first_call(head_kind, queries, keys, values, spatial, block, dealt):
    rows, width = queries.shape
    steps = 6
    outs = [
        shape((2, rows), F32),
        shape((spatial, 2 * block, HEAD_DIM)),
    ]
    if dealt:
        outs += [shape((3, rows, HEAD_DIM))] * 2
    return call(
        functools.partial(first_kernel, spatial, block, dealt),
        "first",
        outs,
        [IN_SMEM] + [ANY] * 3,
        [IN_VMEM] * len(outs),
        [
            order_scratch(head_kind.shape[0]),
            pltpu.VMEM((3, rows, width), BF16),
            pltpu.VMEM((rows, HEAD_DIM), F32),
            pltpu.SemaphoreType.DMA((2 * steps + 1,)),
        ],
        (head_kind, queries, keys, values),
        vmem=VMEM_FIRST,
    )


def row_factors(sums, which, start, size):
    total = None
    for part in sums:
        row = part[which : which + 1, pl.ds(start, size)]
        total = row if total is None else total + row
    inverse = lax.rsqrt(total / D + 1e-06)
    return jnp.transpose(jnp.broadcast_to(inverse, (HEAD_DIM, size)))


def gain_of(gain_ref, head):
    gain = gain_ref[lanes(head)]
    return jnp.broadcast_to(gain[None, :], (8, HEAD_DIM))[0:1, :]


def keys_kernel(spatial, block, kind_ref, k_ref, k_pair_ref, gain_ref, total_ref, pair_ref, after_ref, ks_ref, kp_ref, *refs):
    kx_refs, (order, factors) = refs[:-2], refs[-2:]
    each = kx_refs[0].shape[0]
    rows = k_ref.shape[0]
    put_order(kind_ref, order, spatial)
    place = Place(block)
    factors[0] = row_factors([total_ref], 1, 0, rows)
    factors[1] = row_factors([pair_ref], 1, 0, rows)
    across = pl.ds(pl.multiple_of(place.cross, block), 2 * block)
    for h in range(spatial):
        gain = gain_of(gain_ref, order[h])
        one = lanes(order[h])
        ks_ref[h] = (k_ref[:, one].astype(F32) * factors[0] * gain).astype(BF16)
        kp_ref[h] = (k_pair_ref[:, one].astype(F32) * factors[1] * gain).astype(BF16)
        kx_refs[h // each][h % each] = ks_ref[h, across, :]


def keys_call(head_kind, keys, k_pair, gain, total, pair, after, spatial, block):
    rows = keys.shape[0]
    each = spatial // CHUNKS
    return call(
        functools.partial(keys_kernel, spatial, block),
        "keys",
        [shape((spatial, rows, HEAD_DIM))] * 2
        + [shape((each, 2 * block, HEAD_DIM))] * CHUNKS,
        [IN_SMEM] + [IN_VMEM] * 5 + [LOOSE],
        [IN_VMEM] * (2 + CHUNKS),
        [order_scratch(head_kind.shape[0]), pltpu.VMEM((2, rows, HEAD_DIM), F32)],
        (head_kind, keys, k_pair, gain, total, pair, after),
    )


def attend_all(work, query_of, keys_of, values_of, put):
    def scores_of(item):
        parts = [
            lax.dot_general(query_of(*item), k, (((1,), (1,)), ((), ())), preferred_element_type=F32)
            for k in keys_of(*item)
        ]
        return jnp.concatenate(parts, axis=1)

    scores = scores_of(work[0])
    for n, item in enumerate(work):
        ahead = scores_of(work[n + 1]) if n + 1 < len(work) else None
        top = jnp.max(scores, axis=1, keepdims=True)
        weights = jnp.exp2(scores - top).astype(BF16)
        value = jnp.concatenate(values_of(*item), axis=0)
        wide = jnp.concatenate([value, jnp.ones_like(value)], axis=1)
        total = jnp.dot(weights, wide, preferred_element_type=F32)
        put(item, (total[:, :HEAD_DIM] / total[:, HEAD_DIM:]).astype(BF16))
        scores = ahead


def query_part(q_ref, gain_ref, factors, head, start, size, part):
    rows = pl.ds(pl.multiple_of(start + part * size, size), size)
    gain = gain_of(gain_ref, head) * FACTOR
    scale = factors[part * size : (part + 1) * size, :]
    return (q_ref[rows, lanes(head)].astype(F32) * scale * gain).astype(BF16)


def near_kernel(spatial, block, kind_ref, q_ref, k_ref, v_ref, kp_ref, v_pair_ref, gain_ref, total_ref, after_ref, out_ref, order, factors):
    put_order(kind_ref, order, spatial)
    place = Place(block)
    one = pl.ds(pl.multiple_of(place.apart, block), block)
    factors[...] = row_factors([total_ref], 0, pl.multiple_of(place.near, block), block)

    def both(own_ref, pair_ref):
        return (
            jnp.where(place.inner, own_ref[...], pair_ref[...]),
            jnp.where(place.inner, pair_ref[one, :], own_ref[one, :]),
        )

    def values_of(h):
        head = lanes(order[h])
        return both(v_ref.at[:, head], v_pair_ref.at[:, head])

    def put(item, result):
        out_ref[item[0]] = result

    attend_all(
        [(h,) for h in range(spatial)],
        lambda h: query_part(q_ref, gain_ref, factors, order[h], place.near, block, 0),
        lambda h: both(k_ref.at[h], kp_ref.at[h]),
        values_of,
        put,
    )


def near_call(head_kind, q, k, v, k_pair, v_pair, gain, total, after, spatial, block):
    return call(
        functools.partial(near_kernel, spatial, block),
        "near",
        shape((spatial, block, HEAD_DIM)),
        [IN_SMEM] + [IN_VMEM] * 7 + [LOOSE],
        IN_VMEM,
        [order_scratch(head_kind.shape[0]), pltpu.VMEM((block, HEAD_DIM), F32)],
        (head_kind, q, k, v, k_pair, v_pair, gain, total, after),
    )


def far_attention(first, count, block, place, order, refs, put):
    q_ref, k_ref, v_ref, kp_ref, v_pair_ref, vx_ref, gain_ref, total_ref, factors, *kx_refs = refs
    each = kx_refs[0].shape[0]
    one = pl.ds(pl.multiple_of(place.apart, block), block)
    start = jnp.where(place.inner, 0, place.far)
    two = pl.ds(pl.multiple_of(start, block), 2 * block)
    factors[...] = row_factors([total_ref], 0, pl.multiple_of(place.far, block), 2 * block)

    def three(own_ref, pair_ref, cross_ref):
        return (
            own_ref[two, :],
            jnp.where(place.inner, own_ref[2 * block :, :], cross_ref[:block, :]),
            jnp.where(place.inner, pair_ref[one, :], cross_ref[block:, :]),
        )

    def values_of(h, part):
        head = lanes(order[first + h])
        return three(v_ref.at[:, head], v_pair_ref.at[:, head], vx_ref.at[first + h])

    attend_all(
        [(h, part) for h in range(count) for part in range(2)],
        lambda h, part: query_part(q_ref, gain_ref, factors, order[first + h], place.far, block, part),
        lambda h, part: three(k_ref.at[first + h], kp_ref.at[first + h], kx_refs[h // each].at[h % each]),
        values_of,
        put,
    )


def far_kernel(spatial, first, count, block, chunks, kind_ref, *refs):
    operands, kx_refs, (out_ref, order, factors) = refs[:8], refs[8 : 8 + chunks], refs[-3:]
    put_order(kind_ref, order, spatial)
    place = Place(block)

    def put(item, result):
        h, part = item
        out_ref[h, part * block : (part + 1) * block, :] = result

    far_attention(first, count, block, place, order, operands + (factors,) + kx_refs, put)


def far_call(head_kind, operands, k_cross, after, first, count, spatial, block):
    return call(
        functools.partial(far_kernel, spatial, first, count, block, len(k_cross)),
        "far",
        shape((count, 2 * block, HEAD_DIM)),
        [IN_SMEM] + [IN_VMEM] * (len(operands) + len(k_cross)) + [LOOSE],
        IN_VMEM,
        [order_scratch(head_kind.shape[0]), pltpu.VMEM((2 * block, HEAD_DIM), F32)],
        (head_kind, *operands, *k_cross, after),
    )


def last_kernel(spatial, first, count, block, parts, chunks, kind_ref, *refs):
    operands, kx_refs, refs = refs[:8], refs[8 : 8 + chunks], refs[8 + chunks :]
    near_ref, far_ref, t_refs = refs[0], refs[1], refs[2 : 2 + parts]
    out_ref, order, factors, done, held, sems = refs[2 + parts :]
    put_order(kind_ref, order, spatial)
    place = Place(block)
    near_rows = pl.ds(pl.multiple_of(place.near, block), block)
    far_rows = pl.ds(pl.multiple_of(place.far, block), 2 * block)
    copies = []

    def send(source, head, rows):
        copies.append(
            pltpu.make_async_copy(source, column(out_ref, head, rows), sems.at[len(copies)])
        )
        copies[-1].start()

    for h in range(spatial):
        send(near_ref.at[h], order[h], near_rows)
    for h in range(first):
        send(far_ref.at[h], order[h], far_rows)
    rows = 3 * block
    if parts == 2 * CHIPS:
        for j in range(2):
            for turn in range(CHIPS):
                for g in range(TURNS):
                    piece = (place.chip ^ turn) + CHIPS * g
                    into = pl.ds(pl.multiple_of(piece * PIECE, PIECE), PIECE)
                    held[j, into, :] = t_refs[j * CHIPS + turn][g]
            own = pl.ds(pl.multiple_of(place.core * rows, block), rows)
            send(held.at[j, own], order[spatial + (place.core ^ j)], pl.ds(0, rows))
    else:
        for j in range(parts):
            send(t_refs[j], order[spatial + j], pl.ds(0, rows))

    def put(item, result):
        h, part = item
        done[h, part * block : (part + 1) * block, :] = result
        if part == 1:
            send(done.at[h], order[first + h], far_rows)

    far_attention(first, count, block, place, order, operands + (factors,) + kx_refs, put)
    wait_all(copies)


def last_call(head_kind, operands, k_cross, near, far, parts, first, count, spatial, block):
    rows, width = operands[0].shape
    heads = head_kind.shape[0]
    return call(
        functools.partial(last_kernel, spatial, first, count, block, len(parts), len(k_cross)),
        "last",
        shape((rows, width)),
        [IN_SMEM] + [IN_VMEM] * (len(operands) + len(k_cross) + 2 + len(parts)),
        ANY,
        [
            order_scratch(heads),
            pltpu.VMEM((2 * block, HEAD_DIM), F32),
            pltpu.VMEM((count, 2 * block, HEAD_DIM), BF16),
            pltpu.VMEM((2, 2 * rows, HEAD_DIM), BF16),
            pltpu.SemaphoreType.DMA((2 * spatial + heads - spatial,)),
        ],
        (head_kind, *operands, *k_cross, near, far, *parts),
    )


PIECE = 128
CHIPS = 4
TURNS = 3


def deal_kernel(spatial, block, kind_ref, own_ref, got_ref, gq_ref, gk_ref, total_ref, pair_ref, *refs):
    outs, (order, held) = refs[:CHIPS], refs[CHIPS:]
    put_order(kind_ref, order, spatial)
    place = Place(block)
    rows = own_ref.shape[1]
    head = order[spatial + place.core]
    own = pl.ds(pl.multiple_of(place.core * rows, rows), rows)
    other = pl.ds(pl.multiple_of((1 - place.core) * rows, rows), rows)
    gains = (gain_of(gq_ref, head) * FACTOR, gain_of(gk_ref, head))
    for half, source, sums in ((own, own_ref, total_ref), (other, got_ref, pair_ref)):
        for i in range(2):
            factors = row_factors([sums], i, 0, rows)
            held[i, half, :] = (source[i].astype(F32) * factors * gains[i]).astype(BF16)
        held[2, half, :] = source[2]
    for turn in range(CHIPS):
        owner = place.chip ^ turn
        for g in range(TURNS):
            at = pl.multiple_of((owner + CHIPS * g) * PIECE, PIECE)
            for i in range(3):
                outs[turn][i, g] = held[i, pl.ds(at, PIECE), :]


def deal_call(head_kind, own, got, query_gain, key_gain, total, pair, spatial, block):
    return call(
        functools.partial(deal_kernel, spatial, block),
        "deal",
        [shape((3, TURNS, PIECE, HEAD_DIM))] * CHIPS,
        [IN_SMEM] + [IN_VMEM] * 6,
        [IN_VMEM] * CHIPS,
        [
            order_scratch(head_kind.shape[0]),
            pltpu.VMEM((3, 2 * own.shape[1], HEAD_DIM), BF16),
        ],
        (head_kind, own, got, query_gain, key_gain, total, pair),
    )


GROUPS = (
    ((0, 1), (2, 1), (1, 0), (1, 2), (3, 0), (3, 2)),
    ((0, 0), (0, 2), (2, 0), (2, 2), (1, 1), (3, 1)),
)


def frames_kernel(*refs):
    ins, outs = refs[:CHIPS], refs[-CHIPS:]
    side = len(GROUPS[0]) * PIECE
    row = lax.broadcasted_iota(jnp.int32, (PIECE, PIECE), 0)
    col = lax.broadcasted_iota(jnp.int32, (PIECE, PIECE), 1)
    same = jnp.tile(row == col, (1, len(GROUPS[0])))
    half = side // 2
    work = [(n, part) for n in range(len(GROUPS)) for part in range(2)]
    query, key, value = (
        [jnp.concatenate([ins[s][i, g] for s, g in group], axis=0) for group in GROUPS]
        for i in range(3)
    )
    same = jnp.concatenate([same] * (half // PIECE), axis=0)

    def scores_of(n, part):
        return lax.dot_general(
            query[n][part * half : (part + 1) * half],
            key[n],
            (((1,), (1,)), ((), ())),
            preferred_element_type=F32,
        )

    scores = scores_of(*work[0])
    for at, (n, part) in enumerate(work):
        ahead = scores_of(*work[at + 1]) if at + 1 < len(work) else None
        scores = jnp.where(same, scores, LOW)
        top = jnp.max(scores, axis=1, keepdims=True)
        weights = jnp.exp2(scores - top).astype(BF16)
        wide = jnp.concatenate([value[n], jnp.ones_like(value[n])], axis=1)
        total = jnp.dot(weights, wide, preferred_element_type=F32)
        done = (total[:, :HEAD_DIM] / total[:, HEAD_DIM:]).astype(BF16)
        for i in range(half // PIECE):
            s, g = GROUPS[n][part * (half // PIECE) + i]
            outs[s][g] = done[i * PIECE : (i + 1) * PIECE]
        scores = ahead


def frames_call(parts, after):
    return call(
        frames_kernel,
        "frames",
        [shape((TURNS, PIECE, HEAD_DIM))] * CHIPS,
        [IN_VMEM] * CHIPS + [LOOSE],
        [IN_VMEM] * CHIPS,
        [],
        (*parts, after),
    )


def temporal_folded(queries, keys, values, query_gain, key_gain, head_kind, total, spatial, first):
    rows = queries.shape[0]
    heads = head_kind.shape[0]
    count = heads - spatial
    ids = jnp.argsort(head_kind, stable=True)[spatial:]
    take = lambda x: jnp.take(x.reshape(-1, heads, HEAD_DIM), ids, axis=1)
    inverse = lax.rsqrt(total / D + 1e-06)[:, :, None, None]
    norm = lambda x, i, gain: (take(x).astype(F32) * inverse[i] * take(gain)).astype(BF16)
    query = norm(queries, 0, query_gain * FACTOR).astype(F32)
    flat = lambda x: lax.all_gather(x.reshape(rows, -1), "seq", axis=0, tiled=True)
    key_all = flat(norm(keys, 1, key_gain))
    value_all = flat(take(values))
    place = (first + jnp.arange(rows, dtype=jnp.int32)) % FRAME
    running = jnp.full((rows, count), LOW, F32)
    summed = jnp.zeros((rows, count), F32)
    result = jnp.zeros((rows, count, HEAD_DIM), F32)
    for step in range(key_all.shape[0] // FRAME):
        at = place + step * FRAME
        key = jnp.take(key_all, at, axis=0).reshape(rows, count, HEAD_DIM).astype(F32)
        value = jnp.take(value_all, at, axis=0).reshape(rows, count, HEAD_DIM).astype(F32)
        scores = jnp.sum(query * key, axis=2)
        newest = jnp.maximum(running, scores)
        shrink = jnp.exp2(running - newest)
        weight = jnp.exp2(scores - newest)
        summed = summed * shrink + weight
        result = result * shrink[:, :, None] + weight[:, :, None] * value
        running = newest
    done = (result / summed[:, :, None]).astype(BF16)
    return [done[:, j] for j in range(count)]


def per_device(queries, keys, values, query_gain, key_gain, head_kind):
    rows = queries.shape[0]
    heads = head_kind.shape[0]
    temporal = heads // 5
    spatial = heads - temporal
    block = rows // 3
    devices = lax.axis_size("seq")
    planes = lax.axis_size("head")
    dealt = temporal == 2 and devices == 2 * CHIPS and rows == 6 * PIECE
    pair = [(i, i ^ 1) for i in range(devices)]
    cross = []
    for i in range(3, devices, 4):
        after = (i + 1) % devices
        cross += [(i, after), (after, i)]
    turned = [[(i, i ^ (2 * turn)) for i in range(devices)] for turn in range(1, CHIPS)]
    send = lambda x, route: lax.ppermute(x, "seq", route)

    sums, v_near, *t_parts = first_call(
        head_kind, queries, keys, values, spatial, block, dealt
    )
    k_pair = send(lax.optimization_barrier((keys, sums))[0], pair)
    v_pair = send(lax.optimization_barrier((values, sums))[0], pair)
    v_cross = send(v_near, cross)
    total = sums
    if planes & (planes - 1) == 0:
        for d in [1 << n for n in range(planes.bit_length() - 1)]:
            total = total + lax.ppermute(total, "head", [(i, i ^ d) for i in range(planes)])
    else:
        total = lax.psum(sums, "head")
    pair_total = send(total, pair)
    last = total
    if dealt:
        t_got = send(t_parts[0], pair)
        pieces = deal_call(
            head_kind, t_parts[1], t_got, query_gain, key_gain, total, pair_total, spatial, block
        )
        arrived = [pieces[0]] + [send(p, r) for p, r in zip(pieces[1:], turned)]
        last = pieces[0]
    k, kp, *k_near = keys_call(
        head_kind, keys, k_pair, key_gain, total, pair_total, last, spatial, block
    )
    near = near_call(
        head_kind, queries, k, values, kp, v_pair, query_gain, total, v_cross, spatial, block
    )
    k_cross = [send(lax.optimization_barrier((part, near))[0], cross) for part in k_near]
    last = near
    if dealt:
        results = frames_call(arrived, near)
        own = [results[0]] + [send(p, r) for p, r in zip(results[1:], turned)]
        last = results[0]
    else:
        index = lax.axis_index("seq").astype(jnp.int32)
        parts = temporal_folded(
            queries, keys, values, query_gain, key_gain, head_kind, total, spatial, index * rows
        )
    operands = (queries, k, values, kp, v_pair, v_cross, query_gain, total)
    half = spatial // 2
    far = far_call(
        head_kind, operands, k_cross[: CHUNKS // 2], last, 0, half, spatial, block
    )
    if dealt:
        parts = own + [send(lax.optimization_barrier((p, far))[0], pair) for p in own]
    return last_call(
        head_kind, operands, k_cross[CHUNKS // 2 :], near, far, parts, half, spatial - half,
        spatial, block,
    )


def solution(mesh):
    placed = (P("seq", "head"), P("seq", "head"), P("seq", "head"), P("head"), P("head"), P("head"))
    return jax.shard_map(
        per_device, mesh=mesh, in_specs=placed, out_specs=P("seq", "head"), check_vma=False
    )
```

time: 454 us -> 64.4 us (0.14)
  local copies, waits for them, and re-layouts: 200 us -> 2.62 us
  waiting for transfers between devices: 77.1 us -> 6.34 us
  matrix products: 65.4 us -> 0 us
  other arithmetic: 62.8 us -> 0.7 us
  starting transfers between devices: 0.55 us -> 31.7 us
  Pallas kernels: 0 us -> 22.3 us
  loops' own time: 16.4 us -> 0 us
  blocking collectives: 13.7 us -> 0 us
  between operations: 14 us -> 0.39 us
    gather x20 -> x0, local copies, waits for them, and re-layouts: 70.9 us -> none  [the longest x6 29.6 us: temporal_folded(): jnp.take(value_piece, clipped, axis=0).reshape(rows, count, size)]
    ppermute x2 -> x21, waiting for transfers between devices: 77.1 us -> 6.34 us  [the longest x2 4.2 us: per_device(): lax.ppermute(total, 'head', [(i, i ^ d) for i in range(planes)])]
    slice x8 -> x0, local copies, waits for them, and re-layouts: 66.8 us -> none  [per_head(): value_one = lax.dynamic_index_in_dim(widened[1], which, 1, keepdims=False)]
    dot_general x48 -> x0, matrix products: 65.4 us -> none  [the longest x24 33.2 us: per_head(): lax.dot_general(query_block, key_frame, (((1,), (1,)), ((), ())), preferr...]
    ppermute x2 -> x21, starting transfers between devices: 0.51 us -> 31.7 us  [the longest x19 27.4 us: per_device(): send = lambda x, route: lax.ppermute(x, 'seq', route)]
    convert_element_type x12 -> x0, local copies, waits for them, and re-layouts: 28.1 us -> none  [temporal_folded(): jnp.take(key_piece, clipped, axis=0).reshape(rows, count, size)]
    pallas_call x0 -> x7, Pallas kernels: none -> 22.3 us  [call(): pl.pallas_call(kernel, out_shape=out_shape, in_specs=in_specs, out_specs=...]
    convert_element_type x9 -> x0, other arithmetic: 20.8 us -> none  [the longest x6 12.6 us: temporal_folded(): jnp.take(key_piece, clipped, axis=0).reshape(rows, count, size)]
  transfers between devices with their start and end apart: 4 -> 21, of which waited for: 2 -> 7; matrix products, arithmetic and copies ran while one was open for 43% -> 1% of each run, Pallas kernels for 0% -> 19%
where the time goes in v3:
time: 64.4 us; the launch traced here: 64 us
  starting transfers between devices  31.7 us (49%)
  Pallas kernels  22.3 us (35%)
  waiting for transfers between devices  6.34 us (10%)
  local copies, waits for them, and re-layouts  2.62 us (4%)
  other arithmetic  0.7 us (1%)
    ppermute x19, starting transfers between devices, per_device(): send = lambda x, route: lax.ppermute(x, 'seq', route)  27.4 us
    pallas_call x7, Pallas kernels, call(): pl.pallas_call(kernel, out_shape=out_shape, in_specs=in_specs, out_specs=...  22.3 us
    ppermute x2, starting transfers between devices, per_device(): lax.ppermute(total, 'head', [(i, i ^ d) for i in range(planes)])  4.23 us
    ppermute x2, waiting for transfers between devices, per_device(): lax.ppermute(total, 'head', [(i, i ^ d) for i in range(planes)])  4.2 us
    unnamed x14, local copies, waits for them, and re-layouts  2.62 us
    ppermute x19, waiting for transfers between devices, per_device(): send = lambda x, route: lax.ppermute(x, 'seq', route)  2.14 us
  transfers between devices with their start and end apart: 21, of which 7 were waited for; matrix products, arithmetic and copies ran while one was open for 1% of the time, Pallas kernels for 19%

profile of v3, /device:TPU:0, one launch (start us, length us, event | category | flops | bytes accessed | tf_op | source)
XLA Modules:
  0.0 64.0 jit_solution(9730323688716304381)
XLA Ops:
  0.0 5.3 %first.1 = (f32[2,768]{1,0:T(2,128)}, bf16[8,512,128]{2,1,0:T(8,128)(2,1)}, bf16[3,768,128]{2,1,0:T(8,128)(2,1)}, bf16[3,768,128]{2,1,0:T(8,128)(2,1)}) custom-call(s32[10]{0:T(128)} %kind_ref.11, bf16[768,1280]{1,0:T(8,128)(2,1)} %refs_0_.3, bf16[768,1280]{1,0:T(8,128)(2,1)} %k_ref.1, bf16[768,1280]{1,0:T(8,128)(2,1)} %refs_2_.3), custom_call_target="tpu_custom_call" | custom-call | flops 1000000 | bytes 1000 | tf_op jit(solution)/shard_map/first/pallas_call | solution.py:33
  5.4 0.5 collective-permute-start
  5.9 0.1 collective-permute-start.5
  6.0 5.5 %collective-permute-start.6 = (bf16[8,512,128]{2,1,0:T(8,128)(2,1)}, bf16[8,512,128]{2,1,0:T(8,128)(2,1)S(1)}, u32[]{:S(2)}, u32[]{:S(2)}) collective-permute-start(bf16[8,512,128]{2,1,0:T(8,128)(2,1)} %get-tuple-element.41), channel_id=1, source_target_pairs={{12,16},{16,12},{28,0},{0,28},{13,17},{17,13},{29,1},{1,29},{14,18... | collective-permute-start | bytes 3145736 | tf_op jit(solution)/shard_map/ppermute | solution.py:532
  11.4 0.1 collective-permute-start.4
  11.5 1.6 %collective-permute-start.1 = (f32[2,768]{1,0:T(2,128)}, f32[2,768]{1,0:T(2,128)S(1)}, u32[]{:S(2)}, u32[]{:S(2)}) collective-permute-start(f32[2,768]{1,0:T(2,128)} %get-tuple-element.33), channel_id=1, source_target_pairs={{0,1},{1,0},{2,3},{3,2},{4,5},{5,4},{6,7},{7,6},{8,9},{9,8},{10,11... | collective-permute-start | bytes 18440 | tf_op jit(solution)/shard_map/ppermute | solution.py:543
  13.2 2.3 %collective-permute-done.1 = f32[2,768]{1,0:T(2,128)S(1)} collective-permute-done((f32[2,768]{1,0:T(2,128)}, f32[2,768]{1,0:T(2,128)S(1)}, u32[]{:S(2)}, u32[]{:S(2)}) %collective-permute-start.1) | collective-permute-done | bytes 6176 | tf_op jit(solution)/shard_map/ppermute | solution.py:543
  15.4 0.7 %add.6 = f32[2,768]{1,0:T(2,128)S(1)} add(f32[2,768]{1,0:T(2,128)} %get-tuple-element.33, f32[2,768]{1,0:T(2,128)S(1)} %collective-permute-done.1) | non-fusion elementwise | flops 1536 | bytes 18432 | tf_op jit(solution)/shard_map/add | solution.py:543
  16.1 2.6 %collective-permute-start.2 = (f32[2,768]{1,0:T(2,128)S(1)}, f32[2,768]{1,0:T(2,128)S(1)}, u32[]{:S(2)}, u32[]{:S(2)}) collective-permute-start(f32[2,768]{1,0:T(2,128)S(1)} %add.6), channel_id=1, source_target_pairs={{0,2},{1,3},{2,0},{3,1},{4,6},{5,7},{6,4},{7,5},{8,10},{9,11},{10,... | collective-permute-start | bytes 18440 | tf_op jit(solution)/shard_map/ppermute | solution.py:543
  18.7 1.9 %collective-permute-done.2 = f32[2,768]{1,0:T(2,128)S(1)} collective-permute-done((f32[2,768]{1,0:T(2,128)S(1)}, f32[2,768]{1,0:T(2,128)S(1)}, u32[]{:S(2)}, u32[]{:S(2)}) %collective-permute-start.2) | collective-permute-done | bytes 6176 | tf_op jit(solution)/shard_map/ppermute | solution.py:543
  20.7 0.0 collective-permute-start.3
  20.7 1.2 %collective-permute-done.3.pair_ref = f32[2,768]{1,0:T(2,128)S(1)} collective-permute-done((f32[2,768]{1,0:T(2,128)S(1)}, f32[2,768]{1,0:T(2,128)S(1)}, u32[]{:S(2)}, u32[]{:S(2)}) %collective-permute-start.3) | collective-permute-done | bytes 6176 | tf_op jit(solution)/shard_map/ppermute | solution.py:532
  21.8 0.0 collective-permute-done.4.got_ref
  21.9 1.1 %copy-done.3 = bf16[3,768,128]{2,1,0:T(8,128)(2,1)S(1)} copy-done((bf16[3,768,128]{2,1,0:T(8,128)(2,1)S(1)}, bf16[3,768,128]{2,1,0:T(8,128)(2,1)}, u32[]{:S(2)}) %copy-start.3) | copy-done | bytes 589848
  22.9 1.2 %deal.1 = (bf16[3,3,128,128]{3,2,1,0:T(8,128)(2,1)S(1)}, bf16[3,3,128,128]{3,2,1,0:T(8,128)(2,1)S(1)}, bf16[3,3,128,128]{3,2,1,0:T(8,128)(2,1)S(1)}, bf16[3,3,128,128]{3,2,1,0:T(8,128)(2,1)S(1)}) custom-call(s32[10]{0:T(128)S(1)} %copy-done.6, bf16[3,768,128]{2,1,0:T(8,128)(2,1)S(1)} %copy-done.3, bf16[3,768,128]{2,1,0:T(8,128)(2,1)S(1)} %collective-permute-done.4.got_ref, ...), custom_call_target="tpu_custom_call" | custom-call | flops 1000000 | bytes 1000 | tf_op jit(solution)/shard_map/deal/pallas_call | solution.py:33
  24.1 0.9 %collective-permute-start.11 = (bf16[3,3,128,128]{3,2,1,0:T(8,128)(2,1)S(1)}, bf16[3,3,128,128]{3,2,1,0:T(8,128)(2,1)S(1)}, u32[]{:S(2)}, u32[]{:S(2)}) collective-permute-start(bf16[3,3,128,128]{3,2,1,0:T(8,128)(2,1)S(1)} %get-tuple-element.50), channel_id=1, source_target_pairs={{0,8},{4,12},{8,0},{12,4},{16,24},{20,28},{24,16},{28,20},{1,9},{5... | collective-permute-start | bytes 884744 | tf_op jit(solution)/shard_map/ppermute | solution.py:532
  25.1 0.2 collective-permute-start.12
  25.2 0.0 collective-permute-done.k_pair_ref
  25.3 2.4 %collective-permute-start.13 = (bf16[3,3,128,128]{3,2,1,0:T(8,128)(2,1)S(1)}, bf16[3,3,128,128]{3,2,1,0:T(8,128)(2,1)S(1)}, u32[]{:S(2)}, u32[]{:S(2)}) collective-permute-start(bf16[3,3,128,128]{3,2,1,0:T(8,128)(2,1)S(1)} %get-tuple-element.52), channel_id=1, source_target_pairs={{0,24},{4,28},{8,16},{12,20},{16,8},{20,12},{24,0},{28,4},{1,25},{... | collective-permute-start | bytes 884744 | tf_op jit(solution)/shard_map/ppermute | solution.py:532
  27.7 1.5 %copy-done.2 = bf16[768,1280]{1,0:T(8,128)(2,1)S(1)} copy-done((bf16[768,1280]{1,0:T(8,128)(2,1)S(1)}, bf16[768,1280]{1,0:T(8,128)(2,1)}, u32[]{:S(2)}) %copy-start.2) | copy-done | bytes 1966104
  29.2 1.7 %keys.1 = (bf16[8,768,128]{2,1,0:T(8,128)(2,1)S(1)}, bf16[8,768,128]{2,1,0:T(8,128)(2,1)S(1)}, bf16[2,512,128]{2,1,0:T(8,128)(2,1)S(1)}, bf16[2,512,128]{2,1,0:T...) custom-call(s32[10]{0:T(128)S(1)} %copy-done.6, bf16[768,1280]{1,0:T(8,128)(2,1)S(1)} %copy-done.2, ...), custom_call_target="tpu_custom_call" | custom-call | flops 1000000 | bytes 1000 | tf_op jit(solution)/shard_map/keys/pallas_call | solution.py:33
  30.9 0.0 collective-permute-done.6.after_ref.refs_5_
  30.9 0.0 collective-permute-done.5.v_pair_ref.refs_4_
  30.9 4.0 %near.1.refs_4_.refs_10_ = bf16[8,256,128]{2,1,0:T(8,128)(2,1)S(1)} custom-call(s32[10]{0:T(128)S(1)} %copy-done.6, bf16[768,1280]{1,0:T(8,128)(2,1)S(1)} %copy-done, bf16[8,768,128]{2,1,0:T(8,128)(2,1)S(1)} %get-tuple-element.38.k_ref.refs_1_, bf16[768,1280]{1,0:T(8,128)(2,1)S(1)} %copy-done.1, bf16[8,768,128]{2,1,0:T(8,128)(2,1)S(1)} %get-tuple-element.39.kp_ref.refs_3_, ...), custom_call_target="tpu_custom_call" | custom-call | flops 1000000 | bytes 1000 | tf_op jit(solution)/shard_map/near/pallas_call | solution.py:33
  35.0 1.9 %collective-permute-start.9 = (bf16[2,512,128]{2,1,0:T(8,128)(2,1)S(1)}, bf16[2,512,128]{2,1,0:T(8,128)(2,1)S(1)}, u32[]{:S(2)}, u32[]{:S(2)}) collective-permute-start(bf16[2,512,128]{2,1,0:T(8,128)(2,1)S(1)} %get-tuple-element.47), channel_id=1, source_target_pairs={{12,16},{16,12},{28,0},{0,28},{13,17},{17,13},{29,1},{1,29},{14,18... | collective-permute-start | bytes 786440 | tf_op jit(solution)/shard_map/ppermute | solution.py:532
  36.9 4.5 %collective-permute-start.10 = (bf16[2,512,128]{2,1,0:T(8,128)(2,1)S(1)}, bf16[2,512,128]{2,1,0:T(8,128)(2,1)S(1)}, u32[]{:S(2)}, u32[]{:S(2)}) collective-permute-start(bf16[2,512,128]{2,1,0:T(8,128)(2,1)S(1)} %get-tuple-element.49), channel_id=1, source_target_pairs={{12,16},{16,12},{28,0},{0,28},{13,17},{17,13},{29,1},{1,29},{14,18... | collective-permute-start | bytes 786440 | tf_op jit(solution)/shard_map/ppermute | solution.py:532
  41.4 0.0 collective-permute-done.11.refs_1_
  41.5 1.9 %collective-permute-start.7 = (bf16[2,512,128]{2,1,0:T(8,128)(2,1)S(1)}, bf16[2,512,128]{2,1,0:T(8,128)(2,1)S(1)}, u32[]{:S(2)}, u32[]{:S(2)}) collective-permute-start(bf16[2,512,128]{2,1,0:T(8,128)(2,1)S(1)} %get-tuple-element.43), channel_id=1, source_target_pairs={{12,16},{16,12},{28,0},{0,28},{13,17},{17,13},{29,1},{1,29},{14,18... | collective-permute-start | bytes 786440 | tf_op jit(solution)/shard_map/ppermute | solution.py:532
  43.4 0.0 collective-permute-done.12.refs_2_
  43.4 4.7 %collective-permute-start.8 = (bf16[2,512,128]{2,1,0:T(8,128)(2,1)S(1)}, bf16[2,512,128]{2,1,0:T(8,128)(2,1)S(1)}, u32[]{:S(2)}, u32[]{:S(2)}) collective-permute-start(bf16[2,512,128]{2,1,0:T(8,128)(2,1)S(1)} %get-tuple-element.45), channel_id=1, source_target_pairs={{12,16},{16,12},{28,0},{0,28},{13,17},{17,13},{29,1},{1,29},{14,18... | collective-permute-start | bytes 786440 | tf_op jit(solution)/shard_map/ppermute | solution.py:532
  48.1 0.0 collective-permute-done.13.refs_3_
  48.1 1.8 %frames.1 = (bf16[3,128,128]{2,1,0:T(8,128)(2,1)S(1)}, bf16[3,128,128]{2,1,0:T(8,128)(2,1)S(1)}, bf16[3,128,128]{2,1,0:T(8,128)(2,1)S(1)}, bf16[3,128,128]{2,1,0:T(8,128)(2,1)S(1)}) custom-call(bf16[3,3,128,128]{3,2,1,0:T(8,128)(2,1)S(1)} %get-tuple-element.37.after_ref.refs_0_, bf16[3,3,128,128]{3,2,1,0:T(8,128)(2,1)S(1)} %collective-permute-done.11.refs_1_, ...), custom_call_target="tpu_custom_call" | custom-call | flops 1000000 | bytes 1000 | tf_op jit(solution)/shard_map/frames/pallas_call | solution.py:33
  50.0 0.1 collective-permute-start.16
  50.1 0.6 collective-permute-start.15
  50.6 2.9 %collective-permute-start.14 = (bf16[3,128,128]{2,1,0:T(8,128)(2,1)S(1)}, bf16[3,128,128]{2,1,0:T(8,128)(2,1)S(1)}, u32[]{:S(2)}, u32[]{:S(2)}) collective-permute-start(bf16[3,128,128]{2,1,0:T(8,128)(2,1)S(1)} %get-tuple-element.54), channel_id=1, source_target_pairs={{0,8},{4,12},{8,0},{12,4},{16,24},{20,28},{24,16},{28,20},{1,9},{5... | collective-permute-start | bytes 294920 | tf_op jit(solution)/shard_map/ppermute | solution.py:532
  53.5 3.7 %far.1.refs_11_ = bf16[4,512,128]{2,1,0:T(8,128)(2,1)S(1)} custom-call(s32[10]{0:T(128)S(1)} %copy-done.6, bf16[768,1280]{1,0:T(8,128)(2,1)S(1)} %copy-done, bf16[8,768,128]{2,1,0:T(8,128)(2,1)S(1)} %get-tuple-element.38.k_ref.refs_1_, bf16[768,1280]{1,0:T(8,128)(2,1)S(1)} %copy-done.1, bf16[8,768,128]{2,1,0:T(8,128)(2,1)S(1)} %get-tuple-element.39.kp_ref.refs_3_, ...), custom_call_target="tpu_custom_call" | custom-call | flops 1000000 | bytes 1000 | tf_op jit(solution)/shard_map/far/pallas_call | solution.py:33
  57.2 0.0 collective-permute-done.16.refs_15_
  57.2 0.0 collective-permute-done.14.refs_13_
  57.2 0.1 collective-permute-start.17
  57.3 0.5 collective-permute-start.18
  57.8 0.1 collective-permute-start.19
  57.9 0.4 collective-permute-start.20
  58.3 0.0 collective-permute-done.8.refs_9_
  58.3 0.3 collective-permute-done.17.refs_16_
  58.6 0.2 collective-permute-done.18.refs_17_
  58.8 0.4 collective-permute-done.19.refs_18_
  59.1 0.2 collective-permute-done.20.refs_19_
  59.3 4.6 %last.1 = bf16[768,1280]{1,0:T(8,128)(2,1)} custom-call(s32[10]{0:T(128)S(1)} %copy-done.6, bf16[768,1280]{1,0:T(8,128)(2,1)S(1)} %copy-done, bf16[8,768,128]{2,1,0:T(8,128)(2,1)S(1)} %get-tuple-element.38.k_ref.refs_1_, bf16[768,1280]{1,0:T(8,128)(2,1)S(1)} %copy-done.1, bf16[8,768,128]{2,1,0:T(8,128)(2,1)S(1)} %get-tuple-element.39.kp_ref.refs_3_, ...), custom_call_target="tpu_custom_call" | custom-call | flops 1000000 | bytes 1000 | tf_op jit(solution)/shard_map/last/pallas_call | solution.py:33
  (17 shorter events, 0.0 us)
Async XLA Ops:
  0.0 21.8 %copy-start.6 = (s32[10]{0:T(128)S(1)}, s32[10]{0:T(128)}, u32[]{:S(2)}) copy-start(s32[10]{0:T(128)} %kind_ref.11) | copy-start | bytes 124
  0.0 5.9 %copy-start.1 = (bf16[768,1280]{1,0:T(8,128)(2,1)S(1)}, bf16[768,1280]{1,0:T(8,128)(2,1)}, u32[]{:S(2)}) copy-start(bf16[768,1280]{1,0:T(8,128)(2,1)} %refs_2_.3) | copy-start | bytes 5898244
  0.0 21.8 %copy-start.4 = (f32[1280]{0:T(1024)S(1)}, f32[1280]{0:T(1024)}, u32[]{:S(2)}) copy-start(f32[1280]{0:T(1024)} %refs_6_.3) | copy-start | bytes 15364
  0.0 21.8 %copy-start.5 = (f32[1280]{0:T(1024)S(1)}, f32[1280]{0:T(1024)}, u32[]{:S(2)}) copy-start(f32[1280]{0:T(1024)} %gain_ref.2) | copy-start | bytes 15364
  5.4 19.9 %collective-permute-start = (bf16[768,1280]{1,0:T(8,128)(2,1)}, bf16[768,1280]{1,0:T(8,128)(2,1)S(1)}, u32[]{:S(2)}, u32[]{:S(2)}) collective-permute-start(bf16[768,1280]{1,0:T(8,128)(2,1)} %k_ref.1), channel_id=1, source_target_pairs={{0,4},{4,0},{8,12},{12,8},{16,20},{20,16},{24,28},{28,24},{1,5},{5... | collective-permute-start | bytes 5898248 | tf_op jit(solution)/shard_map/ppermute | solution.py:532
  5.9 25.0 %collective-permute-start.5 = (bf16[768,1280]{1,0:T(8,128)(2,1)S(1)}, bf16[768,1280]{1,0:T(8,128)(2,1)S(1)}, u32[]{:S(2)}, u32[]{:S(2)}) collective-permute-start(bf16[768,1280]{1,0:T(8,128)(2,1)S(1)} %copy-done.1), channel_id=1, source_target_pairs={{0,4},{4,0},{8,12},{12,8},{16,20},{20,16},{24,28},{28,24},{1,5},{5... | collective-permute-start | bytes 5898248 | tf_op jit(solution)/shard_map/ppermute | solution.py:532
  6.0 24.9 %collective-permute-start.6 = (bf16[8,512,128]{2,1,0:T(8,128)(2,1)}, bf16[8,512,128]{2,1,0:T(8,128)(2,1)S(1)}, u32[]{:S(2)}, u32[]{:S(2)}) collective-permute-start(bf16[8,512,128]{2,1,0:T(8,128)(2,1)} %get-tuple-element.41), channel_id=1, source_target_pairs={{12,16},{16,12},{28,0},{0,28},{13,17},{17,13},{29,1},{1,29},{14,18... | collective-permute-start | bytes 3145736 | tf_op jit(solution)/shard_map/ppermute | solution.py:532
  11.4 10.4 %collective-permute-start.4 = (bf16[3,768,128]{2,1,0:T(8,128)(2,1)}, bf16[3,768,128]{2,1,0:T(8,128)(2,1)S(1)}, u32[]{:S(2)}, u32[]{:S(2)}) collective-permute-start(bf16[3,768,128]{2,1,0:T(8,128)(2,1)} %get-tuple-element.36), channel_id=1, source_target_pairs={{0,4},{4,0},{8,12},{12,8},{16,20},{20,16},{24,28},{28,24},{1,5},{5... | collective-permute-start | bytes 1769480 | tf_op jit(solution)/shard_map/ppermute | solution.py:532
  11.5 3.9 %collective-permute-start.1 = (f32[2,768]{1,0:T(2,128)}, f32[2,768]{1,0:T(2,128)S(1)}, u32[]{:S(2)}, u32[]{:S(2)}) collective-permute-start(f32[2,768]{1,0:T(2,128)} %get-tuple-element.33), channel_id=1, source_target_pairs={{0,1},{1,0},{2,3},{3,2},{4,5},{5,4},{6,7},{7,6},{8,9},{9,8},{10,11... | collective-permute-start | bytes 18440 | tf_op jit(solution)/shard_map/ppermute | solution.py:543
  16.1 4.5 %collective-permute-start.2 = (f32[2,768]{1,0:T(2,128)S(1)}, f32[2,768]{1,0:T(2,128)S(1)}, u32[]{:S(2)}, u32[]{:S(2)}) collective-permute-start(f32[2,768]{1,0:T(2,128)S(1)} %add.6), channel_id=1, source_target_pairs={{0,2},{1,3},{2,0},{3,1},{4,6},{5,7},{6,4},{7,5},{8,10},{9,11},{10,... | collective-permute-start | bytes 18440 | tf_op jit(solution)/shard_map/ppermute | solution.py:543
  20.7 1.2 %collective-permute-start.3 = (f32[2,768]{1,0:T(2,128)S(1)}, f32[2,768]{1,0:T(2,128)S(1)}, u32[]{:S(2)}, u32[]{:S(2)}) collective-permute-start(f32[2,768]{1,0:T(2,128)S(1)} %add.7.total_ref.refs_7_), channel_id=1, source_target_pairs={{0,4},{4,0},{8,12},{12,8},{16,20},{20,16},{24,28},{28,24},{1,5},{5... | collective-permute-start | bytes 18440 | tf_op jit(solution)/shard_map/ppermute | solution.py:532
  21.9 1.1 %copy-start.3 = (bf16[3,768,128]{2,1,0:T(8,128)(2,1)S(1)}, bf16[3,768,128]{2,1,0:T(8,128)(2,1)}, u32[]{:S(2)}) copy-start(bf16[3,768,128]{2,1,0:T(8,128)(2,1)} %get-tuple-element.35.own_ref) | copy-start | bytes 1769476
  24.1 17.3 %collective-permute-start.11 = (bf16[3,3,128,128]{3,2,1,0:T(8,128)(2,1)S(1)}, bf16[3,3,128,128]{3,2,1,0:T(8,128)(2,1)S(1)}, u32[]{:S(2)}, u32[]{:S(2)}) collective-permute-start(bf16[3,3,128,128]{3,2,1,0:T(8,128)(2,1)S(1)} %get-tuple-element.50), channel_id=1, source_target_pairs={{0,8},{4,12},{8,0},{12,4},{16,24},{20,28},{24,16},{28,20},{1,9},{5... | collective-permute-start | bytes 884744 | tf_op jit(solution)/shard_map/ppermute | solution.py:532
  25.1 18.3 %collective-permute-start.12 = (bf16[3,3,128,128]{3,2,1,0:T(8,128)(2,1)S(1)}, bf16[3,3,128,128]{3,2,1,0:T(8,128)(2,1)S(1)}, u32[]{:S(2)}, u32[]{:S(2)}) collective-permute-start(bf16[3,3,128,128]{3,2,1,0:T(8,128)(2,1)S(1)} %get-tuple-element.51), channel_id=1, source_target_pairs={{0,16},{4,20},{8,24},{12,28},{16,0},{20,4},{24,8},{28,12},{1,17},{... | collective-permute-start | bytes 884744 | tf_op jit(solution)/shard_map/ppermute | solution.py:532
  25.3 22.9 %collective-permute-start.13 = (bf16[3,3,128,128]{3,2,1,0:T(8,128)(2,1)S(1)}, bf16[3,3,128,128]{3,2,1,0:T(8,128)(2,1)S(1)}, u32[]{:S(2)}, u32[]{:S(2)}) collective-permute-start(bf16[3,3,128,128]{3,2,1,0:T(8,128)(2,1)S(1)} %get-tuple-element.52), channel_id=1, source_target_pairs={{0,24},{4,28},{8,16},{12,20},{16,8},{20,12},{24,0},{28,4},{1,25},{... | collective-permute-start | bytes 884744 | tf_op jit(solution)/shard_map/ppermute | solution.py:532
  27.7 1.5 %copy-start.2 = (bf16[768,1280]{1,0:T(8,128)(2,1)S(1)}, bf16[768,1280]{1,0:T(8,128)(2,1)}, u32[]{:S(2)}) copy-start(bf16[768,1280]{1,0:T(8,128)(2,1)} %k_ref.1) | copy-start | bytes 5898244
  29.2 1.7 %copy-start = (bf16[768,1280]{1,0:T(8,128)(2,1)S(1)}, bf16[768,1280]{1,0:T(8,128)(2,1)}, u32[]{:S(2)}) copy-start(bf16[768,1280]{1,0:T(8,128)(2,1)} %refs_0_.3) | copy-start | bytes 5898244
  35.0 15.1 %collective-permute-start.9 = (bf16[2,512,128]{2,1,0:T(8,128)(2,1)S(1)}, bf16[2,512,128]{2,1,0:T(8,128)(2,1)S(1)}, u32[]{:S(2)}, u32[]{:S(2)}) collective-permute-start(bf16[2,512,128]{2,1,0:T(8,128)(2,1)S(1)} %get-tuple-element.47), channel_id=1, source_target_pairs={{12,16},{16,12},{28,0},{0,28},{13,17},{17,13},{29,1},{1,29},{14,18... | collective-permute-start | bytes 786440 | tf_op jit(solution)/shard_map/ppermute | solution.py:532
  36.9 13.7 %collective-permute-start.10 = (bf16[2,512,128]{2,1,0:T(8,128)(2,1)S(1)}, bf16[2,512,128]{2,1,0:T(8,128)(2,1)S(1)}, u32[]{:S(2)}, u32[]{:S(2)}) collective-permute-start(bf16[2,512,128]{2,1,0:T(8,128)(2,1)S(1)} %get-tuple-element.49), channel_id=1, source_target_pairs={{12,16},{16,12},{28,0},{0,28},{13,17},{17,13},{29,1},{1,29},{14,18... | collective-permute-start | bytes 786440 | tf_op jit(solution)/shard_map/ppermute | solution.py:532
  41.5 16.4 %collective-permute-start.7 = (bf16[2,512,128]{2,1,0:T(8,128)(2,1)S(1)}, bf16[2,512,128]{2,1,0:T(8,128)(2,1)S(1)}, u32[]{:S(2)}, u32[]{:S(2)}) collective-permute-start(bf16[2,512,128]{2,1,0:T(8,128)(2,1)S(1)} %get-tuple-element.43), channel_id=1, source_target_pairs={{12,16},{16,12},{28,0},{0,28},{13,17},{17,13},{29,1},{1,29},{14,18... | collective-permute-start | bytes 786440 | tf_op jit(solution)/shard_map/ppermute | solution.py:532
  43.4 14.9 %collective-permute-start.8 = (bf16[2,512,128]{2,1,0:T(8,128)(2,1)S(1)}, bf16[2,512,128]{2,1,0:T(8,128)(2,1)S(1)}, u32[]{:S(2)}, u32[]{:S(2)}) collective-permute-start(bf16[2,512,128]{2,1,0:T(8,128)(2,1)S(1)} %get-tuple-element.45), channel_id=1, source_target_pairs={{12,16},{16,12},{28,0},{0,28},{13,17},{17,13},{29,1},{1,29},{14,18... | collective-permute-start | bytes 786440 | tf_op jit(solution)/shard_map/ppermute | solution.py:532
  50.0 7.2 %collective-permute-start.16 = (bf16[3,128,128]{2,1,0:T(8,128)(2,1)S(1)}, bf16[3,128,128]{2,1,0:T(8,128)(2,1)S(1)}, u32[]{:S(2)}, u32[]{:S(2)}) collective-permute-start(bf16[3,128,128]{2,1,0:T(8,128)(2,1)S(1)} %get-tuple-element.56), channel_id=1, source_target_pairs={{0,24},{4,28},{8,16},{12,20},{16,8},{20,12},{24,0},{28,4},{1,25},{... | collective-permute-start | bytes 294920 | tf_op jit(solution)/shard_map/ppermute | solution.py:532
  50.1 7.2 %collective-permute-start.15 = (bf16[3,128,128]{2,1,0:T(8,128)(2,1)S(1)}, bf16[3,128,128]{2,1,0:T(8,128)(2,1)S(1)}, u32[]{:S(2)}, u32[]{:S(2)}) collective-permute-start(bf16[3,128,128]{2,1,0:T(8,128)(2,1)S(1)} %get-tuple-element.55), channel_id=1, source_target_pairs={{0,16},{4,20},{8,24},{12,28},{16,0},{20,4},{24,8},{28,12},{1,17},{... | collective-permute-start | bytes 294920 | tf_op jit(solution)/shard_map/ppermute | solution.py:532
  50.6 6.6 %collective-permute-start.14 = (bf16[3,128,128]{2,1,0:T(8,128)(2,1)S(1)}, bf16[3,128,128]{2,1,0:T(8,128)(2,1)S(1)}, u32[]{:S(2)}, u32[]{:S(2)}) collective-permute-start(bf16[3,128,128]{2,1,0:T(8,128)(2,1)S(1)} %get-tuple-element.54), channel_id=1, source_target_pairs={{0,8},{4,12},{8,0},{12,4},{16,24},{20,28},{24,16},{28,20},{1,9},{5... | collective-permute-start | bytes 294920 | tf_op jit(solution)/shard_map/ppermute | solution.py:532
  57.2 1.4 %collective-permute-start.17 = (bf16[3,128,128]{2,1,0:T(8,128)(2,1)S(1)}, bf16[3,128,128]{2,1,0:T(8,128)(2,1)S(1)}, u32[]{:S(2)}, u32[]{:S(2)}) collective-permute-start(bf16[3,128,128]{2,1,0:T(8,128)(2,1)S(1)} %get-tuple-element.57.refs_10_.refs_12_), channel_id=1, source_target_pairs={{0,4},{4,0},{8,12},{12,8},{16,20},{20,16},{24,28},{28,24},{1,5},{5... | collective-permute-start | bytes 294920 | tf_op jit(solution)/shard_map/ppermute | solution.py:532
  57.3 1.4 %collective-permute-start.18 = (bf16[3,128,128]{2,1,0:T(8,128)(2,1)S(1)}, bf16[3,128,128]{2,1,0:T(8,128)(2,1)S(1)}, u32[]{:S(2)}, u32[]{:S(2)}) collective-permute-start(bf16[3,128,128]{2,1,0:T(8,128)(2,1)S(1)} %collective-permute-done.14.refs_13_), channel_id=1, source_target_pairs={{0,4},{4,0},{8,12},{12,8},{16,20},{20,16},{24,28},{28,24},{1,5},{5... | collective-permute-start | bytes 294920 | tf_op jit(solution)/shard_map/ppermute | solution.py:532
  57.8 1.3 %collective-permute-start.19 = (bf16[3,128,128]{2,1,0:T(8,128)(2,1)S(1)}, bf16[3,128,128]{2,1,0:T(8,128)(2,1)S(1)}, u32[]{:S(2)}, u32[]{:S(2)}) collective-permute-start(bf16[3,128,128]{2,1,0:T(8,128)(2,1)S(1)} %collective-permute-done.15.refs_14_), channel_id=1, source_target_pairs={{0,4},{4,0},{8,12},{12,8},{16,20},{20,16},{24,28},{28,24},{1,5},{5... | collective-permute-start | bytes 294920 | tf_op jit(solution)/shard_map/ppermute | solution.py:532
  57.9 1.4 %collective-permute-start.20 = (bf16[3,128,128]{2,1,0:T(8,128)(2,1)S(1)}, bf16[3,128,128]{2,1,0:T(8,128)(2,1)S(1)}, u32[]{:S(2)}, u32[]{:S(2)}) collective-permute-start(bf16[3,128,128]{2,1,0:T(8,128)(2,1)S(1)} %collective-permute-done.16.refs_15_), channel_id=1, source_target_pairs={{0,4},{4,0},{8,12},{12,8},{16,20},{20,16},{24,28},{28,24},{1,5},{5... | collective-permute-start | bytes 294920 | tf_op jit(solution)/shard_map/ppermute | solution.py:532

commit v4 on v3

--- a/solution.py
+++ b/solution.py
@@ -13,12 +13,12 @@
 FRAME = 1024
 OFFSET = 512
 VMEM = 24 * 1024 * 1024
-VMEM_FIRST = 61 * 1024 * 1024
+VMEM_PACK = 57 * 1024 * 1024
+VMEM_SUMS = 53 * 1024 * 1024
 LOW = -1e30
 FACTOR = math.log2(math.e) / math.sqrt(HEAD_DIM)
 F32 = jnp.float32
 BF16 = jnp.bfloat16
-CHUNKS = 4
 ANY = pl.BlockSpec(memory_space=pltpu.HBM)
 LOOSE = pl.BlockSpec(memory_space=pl.ANY)
 IN_SMEM = pl.BlockSpec(memory_space=pltpu.SMEM)
@@ -38,7 +38,7 @@
         scratch_shapes=scratch,
         input_output_aliases=aliases or {},
         compiler_params=pltpu.CompilerParams(vmem_limit_bytes=vmem),
-        cost_estimate=pl.CostEstimate(flops=1000 * cycles, bytes_accessed=1000, transcendentals=0),
+        cost_estimate=pl.CostEstimate(flops=cycles, bytes_accessed=1000, transcendentals=0),
         name=name,
     )(*operands)
 
@@ -91,8 +91,61 @@
         copy.wait()
 
 
-def first_kernel(spatial, block, dealt, kind_ref, q_any, k_any, v_any, sums_ref, vx_ref, *refs):
-    order, held, squares, sems = refs[-4:]
+def pack_kernel(spatial, block, dealt, kind_ref, q_any, k_any, v_any, *refs):
+    outs, (order, packed, t_buf, sems) = refs[:-4], refs[-4:]
+    put_order(kind_ref, order, spatial)
+    place = Place(block)
+    across = pl.ds(pl.multiple_of(place.cross, block), 2 * block)
+    moves = []
+
+    def move(source, held, into):
+        n = len(moves)
+        moves.append(
+            (
+                pltpu.make_async_copy(source, held, sems.at[0, n]),
+                pltpu.make_async_copy(held, into, sems.at[1, n]),
+            )
+        )
+        moves[-1][0].start()
+
+    for h in range(spatial):
+        for i, ref in enumerate((k_any, v_any)):
+            move(column(ref, order[h], across), packed.at[i, h], outs[0].at[i, h])
+    if dealt:
+        head = order[spatial + 1 - place.core]
+        for i, ref in enumerate((q_any, k_any, v_any)):
+            move(column(ref, head), t_buf.at[i], outs[1].at[i])
+    for came, goes in moves:
+        came.wait()
+        goes.start()
+    for _, goes in moves:
+        goes.wait()
+
+
+def pack_call(head_kind, queries, keys, values, spatial, block, dealt):
+    rows = queries.shape[0]
+    both = (2, spatial, 2 * block, HEAD_DIM)
+    outs = [shape(both)]
+    if dealt:
+        outs.append(shape((3, rows, HEAD_DIM)))
+    return call(
+        functools.partial(pack_kernel, spatial, block, dealt),
+        "pack",
+        outs,
+        [IN_SMEM] + [ANY] * 3,
+        [ANY] * len(outs),
+        [
+            order_scratch(head_kind.shape[0]),
+            pltpu.VMEM(both, BF16),
+            pltpu.VMEM((3, rows, HEAD_DIM), BF16),
+            pltpu.SemaphoreType.DMA((2, 2 * spatial + 3)),
+        ],
+        (head_kind, queries, keys, values),
+        vmem=VMEM_PACK,
+    )
+
+
+def sums_kernel(q_any, k_any, after_ref, sums_any, held, squares, sums, sems):
     rows, width = q_any.shape
     steps = (sems.shape[0] - 1) // 2
     size = rows // steps
@@ -107,11 +160,7 @@
         ]
         for i, source in enumerate((q_any, k_any))
     ]
-    v_copy = pltpu.make_async_copy(v_any, held.at[2], sems.at[2 * steps])
-    start_all(copies[0] + copies[1] + [v_copy])
-    put_order(kind_ref, order, spatial)
-    place = Place(block)
-    across = pl.ds(pl.multiple_of(place.cross, block), 2 * block)
+    start_all(copies[0] + copies[1])
     for i in range(2):
         for s in range(steps):
             copies[i][s].wait()
@@ -120,40 +169,29 @@
                 x = held[i, s * size : (s + 1) * size, c * HEAD_DIM : (c + 1) * HEAD_DIM].astype(F32)
                 total = x * x if total is None else total + x * x
             squares[s * size : (s + 1) * size, :] = total
-        sums_ref[i : i + 1, :] = jnp.sum(jnp.transpose(squares[...]), axis=0, keepdims=True)
-    v_copy.wait()
-    for h in range(spatial):
-        vx_ref[h] = held[2, across, lanes(order[h])]
-    if dealt:
-        for j, ref in enumerate(refs[:2]):
-            one = lanes(order[spatial + (1 - place.core if j == 0 else place.core)])
-            for i in range(3):
-                ref[i] = held[i, :, one]
-
-
-def first_call(head_kind, queries, keys, values, spatial, block, dealt):
+        sums[i : i + 1, :] = jnp.sum(jnp.transpose(squares[...]), axis=0, keepdims=True)
+    out = pltpu.make_async_copy(sums, sums_any, sems.at[2 * steps])
+    out.start()
+    out.wait()
+
+
+def sums_call(queries, keys, after):
     rows, width = queries.shape
-    steps = 6
-    outs = [
+    steps = 4
+    return call(
+        sums_kernel,
+        "sums",
         shape((2, rows), F32),
-        shape((spatial, 2 * block, HEAD_DIM)),
-    ]
-    if dealt:
-        outs += [shape((3, rows, HEAD_DIM))] * 2
-    return call(
-        functools.partial(first_kernel, spatial, block, dealt),
-        "first",
-        outs,
-        [IN_SMEM] + [ANY] * 3,
-        [IN_VMEM] * len(outs),
+        [ANY] * 2 + [LOOSE],
+        ANY,
         [
-            order_scratch(head_kind.shape[0]),
-            pltpu.VMEM((3, rows, width), BF16),
+            pltpu.VMEM((2, rows, width), BF16),
             pltpu.VMEM((rows, HEAD_DIM), F32),
+            pltpu.VMEM((2, rows), F32),
             pltpu.SemaphoreType.DMA((2 * steps + 1,)),
         ],
-        (head_kind, queries, keys, values),
-        vmem=VMEM_FIRST,
+        (queries, keys, after),
+        vmem=VMEM_SUMS,
     )
 
 
@@ -171,35 +209,59 @@
     return jnp.broadcast_to(gain[None, :], (8, HEAD_DIM))[0:1, :]
 
 
-def keys_kernel(spatial, block, kind_ref, k_ref, k_pair_ref, gain_ref, total_ref, pair_ref, after_ref, ks_ref, kp_ref, *refs):
-    kx_refs, (order, factors) = refs[:-2], refs[-2:]
-    each = kx_refs[0].shape[0]
+def own_kernel(spatial, dealt, afters, kind_ref, q_ref, k_ref, v_ref, gq_ref, gk_ref, total_ref, *refs):
+    ks_ref, (order, factors) = refs[afters], refs[-2:]
     rows = k_ref.shape[0]
     put_order(kind_ref, order, spatial)
-    place = Place(block)
-    factors[0] = row_factors([total_ref], 1, 0, rows)
-    factors[1] = row_factors([pair_ref], 1, 0, rows)
-    across = pl.ds(pl.multiple_of(place.cross, block), 2 * block)
+    place = Place()
+    factors[...] = row_factors([total_ref], 1, 0, rows)
+    for h in range(spatial):
+        gain = gain_of(gk_ref, order[h])
+        ks_ref[h] = (k_ref[:, lanes(order[h])].astype(F32) * factors[...] * gain).astype(BF16)
+    if dealt:
+        t_ref = refs[afters + 1]
+        head = order[spatial + place.core]
+        one = lanes(head)
+        scale = row_factors([total_ref], 0, 0, rows)
+        t_ref[0] = (q_ref[:, one].astype(F32) * scale * (gain_of(gq_ref, head) * FACTOR)).astype(BF16)
+        t_ref[1] = (k_ref[:, one].astype(F32) * factors[...] * gain_of(gk_ref, head)).astype(BF16)
+        t_ref[2] = v_ref[:, one]
+
+
+def own_call(head_kind, queries, keys, values, query_gain, key_gain, total, afters, spatial, dealt):
+    rows = keys.shape[0]
+    outs = [shape((spatial, rows, HEAD_DIM))]
+    if dealt:
+        outs.append(shape((3, rows, HEAD_DIM)))
+    return call(
+        functools.partial(own_kernel, spatial, dealt, len(afters)),
+        "own",
+        outs,
+        [IN_SMEM] + [IN_VMEM] * 6 + [LOOSE] * len(afters),
+        [IN_VMEM] * len(outs),
+        [order_scratch(head_kind.shape[0]), pltpu.VMEM((rows, HEAD_DIM), F32)],
+        (head_kind, queries, keys, values, query_gain, key_gain, total, *afters),
+    )
+
+
+def pair_kernel(spatial, kind_ref, k_ref, gain_ref, sums_ref, after_ref, kp_ref, order, factors):
+    put_order(kind_ref, order, spatial)
+    factors[...] = row_factors([sums_ref], 1, 0, k_ref.shape[0])
     for h in range(spatial):
         gain = gain_of(gain_ref, order[h])
-        one = lanes(order[h])
-        ks_ref[h] = (k_ref[:, one].astype(F32) * factors[0] * gain).astype(BF16)
-        kp_ref[h] = (k_pair_ref[:, one].astype(F32) * factors[1] * gain).astype(BF16)
-        kx_refs[h // each][h % each] = ks_ref[h, across, :]
-
-
-def keys_call(head_kind, keys, k_pair, gain, total, pair, after, spatial, block):
+        kp_ref[h] = (k_ref[:, lanes(order[h])].astype(F32) * factors[...] * gain).astype(BF16)
+
+
+def pair_call(head_kind, keys, gain, sums, after, spatial):
     rows = keys.shape[0]
-    each = spatial // CHUNKS
-    return call(
-        functools.partial(keys_kernel, spatial, block),
-        "keys",
-        [shape((spatial, rows, HEAD_DIM))] * 2
-        + [shape((each, 2 * block, HEAD_DIM))] * CHUNKS,
-        [IN_SMEM] + [IN_VMEM] * 5 + [LOOSE],
-        [IN_VMEM] * (2 + CHUNKS),
-        [order_scratch(head_kind.shape[0]), pltpu.VMEM((2, rows, HEAD_DIM), F32)],
-        (head_kind, keys, k_pair, gain, total, pair, after),
+    return call(
+        functools.partial(pair_kernel, spatial),
+        "pair",
+        shape((spatial, rows, HEAD_DIM)),
+        [IN_SMEM] + [IN_VMEM] * 3 + [LOOSE],
+        IN_VMEM,
+        [order_scratch(head_kind.shape[0]), pltpu.VMEM((rows, HEAD_DIM), F32)],
+        (head_kind, keys, gain, sums, after),
     )
 
 
@@ -230,7 +292,7 @@
     return (q_ref[rows, lanes(head)].astype(F32) * scale * gain).astype(BF16)
 
 
-def near_kernel(spatial, block, kind_ref, q_ref, k_ref, v_ref, kp_ref, v_pair_ref, gain_ref, total_ref, after_ref, out_ref, order, factors):
+def near_kernel(spatial, block, kind_ref, q_ref, k_ref, v_ref, kp_ref, v_pair_ref, gain_ref, total_ref, out_ref, order, factors):
     put_order(kind_ref, order, spatial)
     place = Place(block)
     one = pl.ds(pl.multiple_of(place.apart, block), block)
@@ -258,48 +320,56 @@
     )
 
 
-def near_call(head_kind, q, k, v, k_pair, v_pair, gain, total, after, spatial, block):
+def near_call(head_kind, q, k, v, k_pair, v_pair, gain, total, spatial, block):
     return call(
         functools.partial(near_kernel, spatial, block),
         "near",
         shape((spatial, block, HEAD_DIM)),
-        [IN_SMEM] + [IN_VMEM] * 7 + [LOOSE],
+        [IN_SMEM] + [IN_VMEM] * 7,
         IN_VMEM,
         [order_scratch(head_kind.shape[0]), pltpu.VMEM((block, HEAD_DIM), F32)],
-        (head_kind, q, k, v, k_pair, v_pair, gain, total, after),
+        (head_kind, q, k, v, k_pair, v_pair, gain, total),
     )
 
 
 def far_attention(first, count, block, place, order, refs, put):
-    q_ref, k_ref, v_ref, kp_ref, v_pair_ref, vx_ref, gain_ref, total_ref, factors, *kx_refs = refs
-    each = kx_refs[0].shape[0]
+    q_ref, k_ref, v_ref, kp_ref, v_pair_ref, kvx_ref, gq_ref, gk_ref, total_ref, cross_ref, factors, x_factors, x_keys = refs
     one = pl.ds(pl.multiple_of(place.apart, block), block)
     start = jnp.where(place.inner, 0, place.far)
     two = pl.ds(pl.multiple_of(start, block), 2 * block)
     factors[...] = row_factors([total_ref], 0, pl.multiple_of(place.far, block), 2 * block)
-
-    def three(own_ref, pair_ref, cross_ref):
+    sent = pl.multiple_of(jnp.where(place.kind == 0, block, 0), block)
+    x_factors[...] = row_factors([cross_ref], 1, sent, 2 * block)
+
+    def three(own_ref, pair_ref, cross):
         return (
             own_ref[two, :],
-            jnp.where(place.inner, own_ref[2 * block :, :], cross_ref[:block, :]),
-            jnp.where(place.inner, pair_ref[one, :], cross_ref[block:, :]),
+            jnp.where(place.inner, own_ref[2 * block :, :], cross[:block]),
+            jnp.where(place.inner, pair_ref[one, :], cross[block:]),
         )
+
+    def keys_of(h, part):
+        n = first + h
+        if part == 0:
+            gain = gain_of(gk_ref, order[n])
+            x_keys[h % 2] = (kvx_ref[0, n].astype(F32) * x_factors[...] * gain).astype(BF16)
+        return three(k_ref.at[n], kp_ref.at[n], x_keys[h % 2])
 
     def values_of(h, part):
         head = lanes(order[first + h])
-        return three(v_ref.at[:, head], v_pair_ref.at[:, head], vx_ref.at[first + h])
+        return three(v_ref.at[:, head], v_pair_ref.at[:, head], kvx_ref[1, first + h])
 
     attend_all(
         [(h, part) for h in range(count) for part in range(2)],
-        lambda h, part: query_part(q_ref, gain_ref, factors, order[first + h], place.far, block, part),
-        lambda h, part: three(k_ref.at[first + h], kp_ref.at[first + h], kx_refs[h // each].at[h % each]),
+        lambda h, part: query_part(q_ref, gq_ref, factors, order[first + h], place.far, block, part),
+        keys_of,
         values_of,
         put,
     )
 
 
-def far_kernel(spatial, first, count, block, chunks, kind_ref, *refs):
-    operands, kx_refs, (out_ref, order, factors) = refs[:8], refs[8 : 8 + chunks], refs[-3:]
+def far_kernel(spatial, first, count, block, kind_ref, *refs):
+    operands, (out_ref, order, factors, x_factors, x_keys) = refs[:10], refs[-5:]
     put_order(kind_ref, order, spatial)
     place = Place(block)
 
@@ -307,25 +377,27 @@
         h, part = item
         out_ref[h, part * block : (part + 1) * block, :] = result
 
-    far_attention(first, count, block, place, order, operands + (factors,) + kx_refs, put)
-
-
-def far_call(head_kind, operands, k_cross, after, first, count, spatial, block):
-    return call(
-        functools.partial(far_kernel, spatial, first, count, block, len(k_cross)),
+    far_attention(first, count, block, place, order, operands + (factors, x_factors, x_keys), put)
+
+
+def far_call(head_kind, operands, after, first, count, spatial, block):
+    return call(
+        functools.partial(far_kernel, spatial, first, count, block),
         "far",
         shape((count, 2 * block, HEAD_DIM)),
-        [IN_SMEM] + [IN_VMEM] * (len(operands) + len(k_cross)) + [LOOSE],
+        [IN_SMEM] + [IN_VMEM] * len(operands) + [LOOSE],
         IN_VMEM,
-        [order_scratch(head_kind.shape[0]), pltpu.VMEM((2 * block, HEAD_DIM), F32)],
-        (head_kind, *operands, *k_cross, after),
-    )
-
-
-def last_kernel(spatial, first, count, block, parts, chunks, kind_ref, *refs):
-    operands, kx_refs, refs = refs[:8], refs[8 : 8 + chunks], refs[8 + chunks :]
-    near_ref, far_ref, t_refs = refs[0], refs[1], refs[2 : 2 + parts]
-    out_ref, order, factors, done, held, sems = refs[2 + parts :]
+        [order_scratch(head_kind.shape[0])]
+        + [pltpu.VMEM((2 * block, HEAD_DIM), F32)] * 2
+        + [pltpu.VMEM((2, 2 * block, HEAD_DIM), BF16)],
+        (head_kind, *operands, after),
+    )
+
+
+def rest_kernel(spatial, first, count, block, kind_ref, *refs):
+    operands, refs = refs[:10], refs[10:]
+    near_ref, far_ref, _, out_ref, token_ref, order, factors, x_factors, x_keys, done, sems = refs
+    token_ref[...] = jnp.zeros_like(token_ref)
     put_order(kind_ref, order, spatial)
     place = Place(block)
     near_rows = pl.ds(pl.multiple_of(place.near, block), block)
@@ -342,7 +414,51 @@
         send(near_ref.at[h], order[h], near_rows)
     for h in range(first):
         send(far_ref.at[h], order[h], far_rows)
+
+    def put(item, result):
+        h, part = item
+        done[h, part * block : (part + 1) * block, :] = result
+        if part == 1:
+            send(done.at[h], order[first + h], far_rows)
+
+    far_attention(first, count, block, place, order, operands + (factors, x_factors, x_keys), put)
+    wait_all(copies)
+
+
+def rest_call(head_kind, operands, near, far, after, first, count, spatial, block):
+    rows, width = operands[0].shape
+    heads = head_kind.shape[0]
+    return call(
+        functools.partial(rest_kernel, spatial, first, count, block),
+        "rest",
+        [shape((rows, width)), shape((8, HEAD_DIM), F32)],
+        [IN_SMEM] + [IN_VMEM] * (len(operands) + 2) + [LOOSE],
+        [ANY, IN_VMEM],
+        [
+            order_scratch(heads),
+            pltpu.VMEM((2 * block, HEAD_DIM), F32),
+            pltpu.VMEM((2 * block, HEAD_DIM), F32),
+            pltpu.VMEM((2, 2 * block, HEAD_DIM), BF16),
+            pltpu.VMEM((count, 2 * block, HEAD_DIM), BF16),
+            pltpu.SemaphoreType.DMA((2 * spatial,)),
+        ],
+        (head_kind, *operands, near, far, after),
+    )
+
+
+def place_kernel(spatial, block, parts, kind_ref, *refs):
+    t_refs, (_, out_ref, order, held, sems) = refs[:parts], refs[parts:]
+    put_order(kind_ref, order, spatial)
+    place = Place(block)
     rows = 3 * block
+    copies = []
+
+    def send(source, head):
+        copies.append(
+            pltpu.make_async_copy(source, column(out_ref, head), sems.at[len(copies)])
+        )
+        copies[-1].start()
+
     if parts == 2 * CHIPS:
         for j in range(2):
             for turn in range(CHIPS):
@@ -351,38 +467,28 @@
                     into = pl.ds(pl.multiple_of(piece * PIECE, PIECE), PIECE)
                     held[j, into, :] = t_refs[j * CHIPS + turn][g]
             own = pl.ds(pl.multiple_of(place.core * rows, block), rows)
-            send(held.at[j, own], order[spatial + (place.core ^ j)], pl.ds(0, rows))
+            send(held.at[j, own], order[spatial + (place.core ^ j)])
     else:
         for j in range(parts):
-            send(t_refs[j], order[spatial + j], pl.ds(0, rows))
-
-    def put(item, result):
-        h, part = item
-        done[h, part * block : (part + 1) * block, :] = result
-        if part == 1:
-            send(done.at[h], order[first + h], far_rows)
-
-    far_attention(first, count, block, place, order, operands + (factors,) + kx_refs, put)
+            send(t_refs[j], order[spatial + j])
     wait_all(copies)
 
 
-def last_call(head_kind, operands, k_cross, near, far, parts, first, count, spatial, block):
-    rows, width = operands[0].shape
+def place_call(head_kind, parts, have, spatial, block):
     heads = head_kind.shape[0]
     return call(
-        functools.partial(last_kernel, spatial, first, count, block, len(parts), len(k_cross)),
-        "last",
-        shape((rows, width)),
-        [IN_SMEM] + [IN_VMEM] * (len(operands) + len(k_cross) + 2 + len(parts)),
+        functools.partial(place_kernel, spatial, block, len(parts)),
+        "place",
+        shape(have.shape),
+        [IN_SMEM] + [IN_VMEM] * len(parts) + [ANY],
         ANY,
         [
             order_scratch(heads),
-            pltpu.VMEM((2 * block, HEAD_DIM), F32),
-            pltpu.VMEM((count, 2 * block, HEAD_DIM), BF16),
-            pltpu.VMEM((2, 2 * rows, HEAD_DIM), BF16),
-            pltpu.SemaphoreType.DMA((2 * spatial + heads - spatial,)),
+            pltpu.VMEM((2, 2 * have.shape[0], HEAD_DIM), BF16),
+            pltpu.SemaphoreType.DMA((heads - spatial,)),
         ],
-        (head_kind, *operands, *k_cross, near, far, *parts),
+        (head_kind, *parts, have),
+        aliases={1 + len(parts): 0},
     )
 
 
@@ -391,7 +497,7 @@
 TURNS = 3
 
 
-def deal_kernel(spatial, block, kind_ref, own_ref, got_ref, gq_ref, gk_ref, total_ref, pair_ref, *refs):
+def deal_kernel(spatial, block, kind_ref, own_ref, got_ref, gq_ref, gk_ref, sums_ref, *refs):
     outs, (order, held) = refs[:CHIPS], refs[CHIPS:]
     put_order(kind_ref, order, spatial)
     place = Place(block)
@@ -400,11 +506,12 @@
     own = pl.ds(pl.multiple_of(place.core * rows, rows), rows)
     other = pl.ds(pl.multiple_of((1 - place.core) * rows, rows), rows)
     gains = (gain_of(gq_ref, head) * FACTOR, gain_of(gk_ref, head))
-    for half, source, sums in ((own, own_ref, total_ref), (other, got_ref, pair_ref)):
-        for i in range(2):
-            factors = row_factors([sums], i, 0, rows)
-            held[i, half, :] = (source[i].astype(F32) * factors * gains[i]).astype(BF16)
-        held[2, half, :] = source[2]
+    for i in range(2):
+        factors = row_factors([sums_ref], i, 0, rows)
+        held[i, other, :] = (got_ref[i].astype(F32) * factors * gains[i]).astype(BF16)
+    held[2, other, :] = got_ref[2]
+    for i in range(3):
+        held[i, own, :] = own_ref[i]
     for turn in range(CHIPS):
         owner = place.chip ^ turn
         for g in range(TURNS):
@@ -413,18 +520,18 @@
                 outs[turn][i, g] = held[i, pl.ds(at, PIECE), :]
 
 
-def deal_call(head_kind, own, got, query_gain, key_gain, total, pair, spatial, block):
+def deal_call(head_kind, own, got, query_gain, key_gain, sums, spatial, block):
     return call(
         functools.partial(deal_kernel, spatial, block),
         "deal",
         [shape((3, TURNS, PIECE, HEAD_DIM))] * CHIPS,
-        [IN_SMEM] + [IN_VMEM] * 6,
+        [IN_SMEM] + [IN_VMEM] * 5,
         [IN_VMEM] * CHIPS,
         [
             order_scratch(head_kind.shape[0]),
             pltpu.VMEM((3, 2 * own.shape[1], HEAD_DIM), BF16),
         ],
-        (head_kind, own, got, query_gain, key_gain, total, pair),
+        (head_kind, own, got, query_gain, key_gain, sums),
     )
 
 
@@ -531,12 +638,12 @@
     turned = [[(i, i ^ (2 * turn)) for i in range(devices)] for turn in range(1, CHIPS)]
     send = lambda x, route: lax.ppermute(x, "seq", route)
 
-    sums, v_near, *t_parts = first_call(
-        head_kind, queries, keys, values, spatial, block, dealt
-    )
-    k_pair = send(lax.optimization_barrier((keys, sums))[0], pair)
-    v_pair = send(lax.optimization_barrier((values, sums))[0], pair)
-    v_cross = send(v_near, cross)
+    kv_near, *t_send = pack_call(head_kind, queries, keys, values, spatial, block, dealt)
+    kv_cross = send(kv_near, cross)
+    sums = sums_call(queries, keys, t_send[0] if t_send else kv_near)
+    k_pair = send(lax.optimization_barrier((keys, kv_near))[0], pair)
+    v_pair = send(lax.optimization_barrier((values, kv_near))[0], pair)
+    t_got = [send(part, pair) for part in t_send]
     total = sums
     if planes & (planes - 1) == 0:
         for d in [1 << n for n in range(planes.bit_length() - 1)]:
@@ -544,42 +651,46 @@
     else:
         total = lax.psum(sums, "head")
     pair_total = send(total, pair)
-    last = total
+    cross_total = lax.ppermute(
+        total,
+        ("seq", "head"),
+        [(i * planes + p, j * planes + (p ^ 1)) for i, j in cross for p in range(planes)],
+    )
+    k, *t_own = own_call(
+        head_kind, queries, keys, values, query_gain, key_gain, total, t_got, spatial, dealt
+    )
+    last = k
     if dealt:
-        t_got = send(t_parts[0], pair)
         pieces = deal_call(
-            head_kind, t_parts[1], t_got, query_gain, key_gain, total, pair_total, spatial, block
+            head_kind, t_own[0], t_got[0], query_gain, key_gain, pair_total, spatial, block
         )
         arrived = [pieces[0]] + [send(p, r) for p, r in zip(pieces[1:], turned)]
         last = pieces[0]
-    k, kp, *k_near = keys_call(
-        head_kind, keys, k_pair, key_gain, total, pair_total, last, spatial, block
-    )
+    kp = pair_call(head_kind, k_pair, key_gain, pair_total, last, spatial)
     near = near_call(
-        head_kind, queries, k, values, kp, v_pair, query_gain, total, v_cross, spatial, block
-    )
-    k_cross = [send(lax.optimization_barrier((part, near))[0], cross) for part in k_near]
-    last = near
+        head_kind, queries, k, values, kp, v_pair, query_gain, total, spatial, block
+    )
+    operands = (
+        queries, k, values, kp, v_pair, kv_cross, query_gain, key_gain, total, cross_total
+    )
+    half = spatial // 2
+    far = far_call(head_kind, operands, near, 0, half, spatial, block)
+    last = far
     if dealt:
-        results = frames_call(arrived, near)
-        own = [results[0]] + [send(p, r) for p, r in zip(results[1:], turned)]
+        results = frames_call(arrived, far)
+        parts = [results[0]] + [send(p, r) for p, r in zip(results[1:], turned)]
         last = results[0]
+    out, token = rest_call(
+        head_kind, operands, near, far, last, half, spatial - half, spatial, block
+    )
+    if dealt:
+        parts += [send(lax.optimization_barrier((p, token))[0], pair) for p in parts]
     else:
         index = lax.axis_index("seq").astype(jnp.int32)
         parts = temporal_folded(
             queries, keys, values, query_gain, key_gain, head_kind, total, spatial, index * rows
         )
-    operands = (queries, k, values, kp, v_pair, v_cross, query_gain, total)
-    half = spatial // 2
-    far = far_call(
-        head_kind, operands, k_cross[: CHUNKS // 2], last, 0, half, spatial, block
-    )
-    if dealt:
-        parts = own + [send(lax.optimization_barrier((p, far))[0], pair) for p in own]
-    return last_call(
-        head_kind, operands, k_cross[CHUNKS // 2 :], near, far, parts, half, spatial - half,
-        spatial, block,
-    )
+    return place_call(head_kind, parts, out, spatial, block)
 
 
 def solution(mesh):

time: 64.4 us -> 62.1 us (0.964)
  starting transfers between devices: 31.7 us -> 22.7 us
  Pallas kernels: 22.3 us -> 27.9 us
  waiting for transfers between devices: 6.34 us -> 9.58 us
  local copies, waits for them, and re-layouts: 2.62 us -> 1.18 us
  other arithmetic: 0.7 us -> 0.01 us
    ppermute x19 -> x15, starting transfers between devices: 27.4 us -> 15.8 us  [per_device(): send = lambda x, route: lax.ppermute(x, 'seq', route)]
    pallas_call x7 -> x10, Pallas kernels: 22.3 us -> 27.9 us  [call(): pl.pallas_call(kernel, out_shape=out_shape, in_specs=in_specs, out_specs=...]
    ppermute x19 -> x15, waiting for transfers between devices: 2.14 us -> 5.59 us  [per_device(): send = lambda x, route: lax.ppermute(x, 'seq', route)]
    ppermute x0 -> x1, starting transfers between devices: none -> 2.65 us  [per_device(): lax.ppermute(total, ('seq', 'head'), [(i * planes + p, j * planes + (p ^...]
    unnamed x14 -> x12, local copies, waits for them, and re-layouts: 2.62 us -> 1.18 us
    add x2, other arithmetic: 0.7 us -> 0.01 us  [per_device(): total + lax.ppermute(total, 'head', [(i, i ^ d) for i in range(planes)])]
  transfers between devices with their start and end apart: 21 -> 18, of which waited for: 7 -> 8; matrix products, arithmetic and copies ran while one was open for 1% -> 0% of each run, Pallas kernels for 19% -> 33%
where the time goes in v4:
time: 62.1 us; the launch traced here: 61.8 us
  Pallas kernels  27.9 us (45%)
  starting transfers between devices  22.7 us (37%)
  waiting for transfers between devices  9.58 us (15%)
  local copies, waits for them, and re-layouts  1.18 us (2%)
    pallas_call x10, Pallas kernels, call(): pl.pallas_call(kernel, out_shape=out_shape, in_specs=in_specs, out_specs=...  27.9 us
    ppermute x15, starting transfers between devices, per_device(): send = lambda x, route: lax.ppermute(x, 'seq', route)  15.8 us
    ppermute x15, waiting for transfers between devices, per_device(): send = lambda x, route: lax.ppermute(x, 'seq', route)  5.59 us
    ppermute x2, starting transfers between devices, per_device(): lax.ppermute(total, 'head', [(i, i ^ d) for i in range(planes)])  4.23 us
    ppermute x2, waiting for transfers between devices, per_device(): lax.ppermute(total, 'head', [(i, i ^ d) for i in range(planes)])  3.99 us
    ppermute x1, starting transfers between devices, per_device(): lax.ppermute(total, ('seq', 'head'), [(i * planes + p, j * planes + (p ^...  2.65 us
  transfers between devices with their start and end apart: 18, of which 8 were waited for; matrix products, arithmetic and copies ran while one was open for 0% of the time, Pallas kernels for 33%

profile of v4, /device:TPU:0, one launch (start us, length us, event | category | flops | bytes accessed | tf_op | source)
XLA Modules:
  0.0 61.8 jit_solution(2103930610578503009)
XLA Ops:
  0.0 3.9 %pack.1 = (bf16[2,8,512,128]{3,2,1,0:T(8,128)(2,1)}, bf16[3,768,128]{2,1,0:T(8,128)(2,1)}) custom-call(s32[10]{0:T(128)} %kind_ref.15, bf16[768,1280]{1,0:T(8,128)(2,1)} %refs_0_.3, bf16[768,1280]{1,0:T(8,128)(2,1)} %k_ref.1, bf16[768,1280]{1,0:T(8,128)(2,1)} %refs_2_.3), custom_call_target="tpu_custom_call" | custom-call | flops 1000 | bytes 1000 | tf_op jit(solution)/shard_map/pack/pallas_call | solution.py:33
  3.9 0.5 collective-permute-start.7
  4.5 5.5 %collective-permute-start.9 = (bf16[2,8,512,128]{3,2,1,0:T(8,128)(2,1)}, bf16[2,8,512,128]{3,2,1,0:T(8,128)(2,1)S(1)}, u32[]{:S(2)}, u32[]{:S(2)}) collective-permute-start(bf16[2,8,512,128]{3,2,1,0:T(8,128)(2,1)} %get-tuple-element.32), channel_id=1, source_target_pairs={{12,16},{16,12},{28,0},{0,28},{13,17},{17,13},{29,1},{1,29},{14,18... | collective-permute-start | bytes 6291464 | tf_op jit(solution)/shard_map/ppermute | solution.py:639
  9.9 0.1 collective-permute-start.8
  10.0 0.0 copy-start
  10.0 0.5 collective-permute-start.2
  10.5 1.2 %copy-done.2 = bf16[3,768,128]{2,1,0:T(8,128)(2,1)S(1)} copy-done((bf16[3,768,128]{2,1,0:T(8,128)(2,1)S(1)}, bf16[3,768,128]{2,1,0:T(8,128)(2,1)}, u32[]{:S(2)}) %copy-start.2) | copy-done | bytes 589848
  11.7 2.4 %sums.1 = f32[2,768]{1,0:T(2,128)S(1)} custom-call(bf16[768,1280]{1,0:T(8,128)(2,1)} %refs_0_.3, bf16[768,1280]{1,0:T(8,128)(2,1)} %k_ref.1, bf16[3,768,128]{2,1,0:T(8,128)(2,1)S(1)} %copy-done.2), custom_call_target="tpu_custom_call" | custom-call | flops 1000 | bytes 1000 | tf_op jit(solution)/shard_map/sums/pallas_call | solution.py:33
  14.1 1.6 %collective-permute-start = (f32[2,768]{1,0:T(2,128)S(1)}, f32[2,768]{1,0:T(2,128)S(1)}, u32[]{:S(2)}, u32[]{:S(2)}) collective-permute-start(f32[2,768]{1,0:T(2,128)S(1)} %sums.1), channel_id=1, source_target_pairs={{0,1},{1,0},{2,3},{3,2},{4,5},{5,4},{6,7},{7,6},{8,9},{9,8},{10,11... | collective-permute-start | bytes 18440 | tf_op jit(solution)/shard_map/ppermute | solution.py:650
  15.7 2.1 %collective-permute-done = f32[2,768]{1,0:T(2,128)S(1)} collective-permute-done((f32[2,768]{1,0:T(2,128)S(1)}, f32[2,768]{1,0:T(2,128)S(1)}, u32[]{:S(2)}, u32[]{:S(2)}) %collective-permute-start) | collective-permute-done | bytes 6176 | tf_op jit(solution)/shard_map/ppermute | solution.py:650
  17.8 2.6 %collective-permute-start.1 = (f32[2,768]{1,0:T(2,128)S(1)}, f32[2,768]{1,0:T(2,128)S(1)}, u32[]{:S(2)}, u32[]{:S(2)}) collective-permute-start(f32[2,768]{1,0:T(2,128)S(1)} %add.6), channel_id=1, source_target_pairs={{0,2},{1,3},{2,0},{3,1},{4,6},{5,7},{6,4},{7,5},{8,10},{9,11},{10,... | collective-permute-start | bytes 18440 | tf_op jit(solution)/shard_map/ppermute | solution.py:650
  20.3 1.9 %collective-permute-done.1 = f32[2,768]{1,0:T(2,128)S(1)} collective-permute-done((f32[2,768]{1,0:T(2,128)S(1)}, f32[2,768]{1,0:T(2,128)S(1)}, u32[]{:S(2)}, u32[]{:S(2)}) %collective-permute-start.1) | collective-permute-done | bytes 6176 | tf_op jit(solution)/shard_map/ppermute | solution.py:650
  22.3 0.0 collective-permute-start.3
  22.3 0.0 collective-permute-done.2.refs_0_.got_ref
  22.3 2.3 %own.1 = (bf16[8,768,128]{2,1,0:T(8,128)(2,1)S(1)}, bf16[3,768,128]{2,1,0:T(8,128)(2,1)S(1)}) custom-call(s32[10]{0:T(128)S(1)} %copy-done.5, bf16[768,1280]{1,0:T(8,128)(2,1)S(1)} %copy-done, bf16[768,1280]{1,0:T(8,128)(2,1)} %k_ref.1, bf16[768,1280]{1,0:T(8,128)(2,1)S(1)} %copy-done.1, f32[1280]{0:T(1024)S(1)} %copy-done.4, f32[1280]{0:T(1024)S(1)} %copy-done.3, ...), custom_call_target="tpu_custom_call" | custom-call | flops 1000 | bytes 1000 | tf_op jit(solution)/shard_map/own/pallas_call | solution.py:33
  24.7 0.0 collective-permute-done.3.sums_ref
  24.7 1.0 %deal.1 = (bf16[3,3,128,128]{3,2,1,0:T(8,128)(2,1)S(1)}, bf16[3,3,128,128]{3,2,1,0:T(8,128)(2,1)S(1)}, bf16[3,3,128,128]{3,2,1,0:T(8,128)(2,1)S(1)}, bf16[3,3,128,128]{3,2,1,0:T(8,128)(2,1)S(1)}) custom-call(s32[10]{0:T(128)S(1)} %copy-done.5, bf16[3,768,128]{2,1,0:T(8,128)(2,1)S(1)} %get-tuple-element.26.own_ref, ...), custom_call_target="tpu_custom_call" | custom-call | flops 1000 | bytes 1000 | tf_op jit(solution)/shard_map/deal/pallas_call | solution.py:33
  25.7 0.3 collective-permute-start.4
  26.0 0.4 collective-permute-start.5
  26.4 0.0 collective-permute-done.7.k_ref
  26.4 2.9 %collective-permute-start.6 = (bf16[3,3,128,128]{3,2,1,0:T(8,128)(2,1)S(1)}, bf16[3,3,128,128]{3,2,1,0:T(8,128)(2,1)S(1)}, u32[]{:S(2)}, u32[]{:S(2)}) collective-permute-start(bf16[3,3,128,128]{3,2,1,0:T(8,128)(2,1)S(1)} %get-tuple-element.30), channel_id=1, source_target_pairs={{0,24},{4,28},{8,16},{12,20},{16,8},{20,12},{24,0},{28,4},{1,25},{... | collective-permute-start | bytes 884744 | tf_op jit(solution)/shard_map/ppermute | solution.py:639
  29.2 0.0 collective-permute-done.8.v_pair_ref.refs_4_
  29.3 2.6 %collective-permute-start.10 = (f32[2,768]{1,0:T(2,128)S(1)}, f32[2,768]{1,0:T(2,128)S(1)}, u32[]{:S(2)}, u32[]{:S(2)}) collective-permute-start(f32[2,768]{1,0:T(2,128)S(1)} %add.7.total_ref.refs_8_), channel_id=1, source_target_pairs={{12,17},{13,16},{14,19},{15,18},{16,13},{17,12},{18,15},{19,14},{2... | collective-permute-start | bytes 18440 | tf_op jit(solution)/shard_map/ppermute | solution.py:654
  31.9 2.2 %pair.1.kp_ref.refs_3_ = bf16[8,768,128]{2,1,0:T(8,128)(2,1)S(1)} custom-call(s32[10]{0:T(128)S(1)} %copy-done.5, bf16[768,1280]{1,0:T(8,128)(2,1)} %collective-permute-done.7.k_ref, f32[1280]{0:T(1024)S(1)} %copy-done.3, f32[2,768]{1,0:T(2,128)S(1)} %collective-permute-done.3.sums_ref, bf16[3,3,128,128]{3,2,1,0:T(8,128)(2,1)S(1)} %get-tuple-element.27.after_ref.refs_0_), custom_call_target="tpu_custom_call" | custom-call | flops 1000 | bytes 1000 | tf_op jit(solution)/shard_map/pair/pallas_call | solution.py:33
  34.1 4.0 %near.1.refs_10_ = bf16[8,256,128]{2,1,0:T(8,128)(2,1)S(1)} custom-call(s32[10]{0:T(128)S(1)} %copy-done.5, bf16[768,1280]{1,0:T(8,128)(2,1)S(1)} %copy-done, bf16[8,768,128]{2,1,0:T(8,128)(2,1)S(1)} %get-tuple-element.31.k_ref.refs_1_, bf16[768,1280]{1,0:T(8,128)(2,1)S(1)} %copy-done.1, bf16[8,768,128]{2,1,0:T(8,128)(2,1)S(1)} %pair.1.kp_ref.refs_3_, ...), custom_call_target="tpu_custom_call" | custom-call | flops 1000 | bytes 1000 | tf_op jit(solution)/shard_map/near/pallas_call | solution.py:33
  38.0 0.0 collective-permute-done.10.refs_9_
  38.1 2.1 %collective-permute-done.9.refs_5_ = bf16[2,8,512,128]{3,2,1,0:T(8,128)(2,1)S(1)} collective-permute-done((bf16[2,8,512,128]{3,2,1,0:T(8,128)(2,1)}, bf16[2,8,512,128]{3,2,1,0:T(8,128)(2,1)S(1)}, u32[]{:S(2)}, u32[]{:S(2)}) %collective-permute-start.9) | collective-permute-done | bytes 2097184 | tf_op jit(solution)/shard_map/ppermute | solution.py:639
  40.2 3.7 %far.1.refs_4_.refs_11_ = bf16[4,512,128]{2,1,0:T(8,128)(2,1)S(1)} custom-call(s32[10]{0:T(128)S(1)} %copy-done.5, bf16[768,1280]{1,0:T(8,128)(2,1)S(1)} %copy-done, bf16[8,768,128]{2,1,0:T(8,128)(2,1)S(1)} %get-tuple-element.31.k_ref.refs_1_, bf16[768,1280]{1,0:T(8,128)(2,1)S(1)} %copy-done.1, bf16[8,768,128]{2,1,0:T(8,128)(2,1)S(1)} %pair.1.kp_ref.refs_3_, ...), custom_call_target="tpu_custom_call" | custom-call | flops 1000 | bytes 1000 | tf_op jit(solution)/shard_map/far/pallas_call | solution.py:33
  43.9 0.0 collective-permute-done.4.refs_1_
  44.0 0.0 collective-permute-done.5.refs_2_
  44.0 2.5 %collective-permute-done.6.refs_3_ = bf16[3,3,128,128]{3,2,1,0:T(8,128)(2,1)S(1)} collective-permute-done((bf16[3,3,128,128]{3,2,1,0:T(8,128)(2,1)S(1)}, bf16[3,3,128,128]{3,2,1,0:T(8,128)(2,1)S(1)}, u32[]{:S(2)}, u32[]{:S(2)}) %collective-permute-start.6) | collective-permute-done | bytes 294944 | tf_op jit(solution)/shard_map/ppermute | solution.py:639
  46.5 1.8 %frames.1 = (bf16[3,128,128]{2,1,0:T(8,128)(2,1)S(1)}, bf16[3,128,128]{2,1,0:T(8,128)(2,1)S(1)}, bf16[3,128,128]{2,1,0:T(8,128)(2,1)S(1)}, bf16[3,128,128]{2,1,0:T(8,128)(2,1)S(1)}) custom-call(bf16[3,3,128,128]{3,2,1,0:T(8,128)(2,1)S(1)} %get-tuple-element.27.after_ref.refs_0_, bf16[3,3,128,128]{3,2,1,0:T(8,128)(2,1)S(1)} %collective-permute-done.4.refs_1_, ...), custom_call_target="tpu_custom_call" | custom-call | flops 1000 | bytes 1000 | tf_op jit(solution)/shard_map/frames/pallas_call | solution.py:33
  48.3 3.1 %collective-permute-start.11 = (bf16[3,128,128]{2,1,0:T(8,128)(2,1)S(1)}, bf16[3,128,128]{2,1,0:T(8,128)(2,1)S(1)}, u32[]{:S(2)}, u32[]{:S(2)}) collective-permute-start(bf16[3,128,128]{2,1,0:T(8,128)(2,1)S(1)} %get-tuple-element.36), channel_id=1, source_target_pairs={{0,8},{4,12},{8,0},{12,4},{16,24},{20,28},{24,16},{28,20},{1,9},{5... | collective-permute-start | bytes 294920 | tf_op jit(solution)/shard_map/ppermute | solution.py:639
  51.4 1.0 %collective-permute-start.12 = (bf16[3,128,128]{2,1,0:T(8,128)(2,1)S(1)}, bf16[3,128,128]{2,1,0:T(8,128)(2,1)S(1)}, u32[]{:S(2)}, u32[]{:S(2)}) collective-permute-start(bf16[3,128,128]{2,1,0:T(8,128)(2,1)S(1)} %get-tuple-element.37), channel_id=1, source_target_pairs={{0,16},{4,20},{8,24},{12,28},{16,0},{20,4},{24,8},{28,12},{1,17},{... | collective-permute-start | bytes 294920 | tf_op jit(solution)/shard_map/ppermute | solution.py:639
  52.4 0.5 collective-permute-start.13
  53.0 5.1 %rest.1 = (bf16[768,1280]{1,0:T(8,128)(2,1)}, f32[8,128]{1,0:T(8,128)}) custom-call(s32[10]{0:T(128)S(1)} %copy-done.5, bf16[768,1280]{1,0:T(8,128)(2,1)S(1)} %copy-done, bf16[8,768,128]{2,1,0:T(8,128)(2,1)S(1)} %get-tuple-element.31.k_ref.refs_1_, bf16[768,1280]{1,0:T(8,128)(2,1)S(1)} %copy-done.1, bf16[8,768,128]{2,1,0:T(8,128)(2,1)S(1)} %pair.1.kp_ref.refs_3_, ...), custom_call_target="tpu_custom_call" | custom-call | flops 1000 | bytes 1000 | tf_op jit(solution)/shard_map/rest/pallas_call | solution.py:33
  58.1 0.1 collective-permute-start.14
  58.2 0.0 collective-permute-done.11.refs_1_
  58.2 0.5 collective-permute-start.15
  58.7 0.0 collective-permute-done.12.refs_2_
  58.7 0.1 collective-permute-start.16
  58.8 0.0 collective-permute-done.13.refs_3_
  58.8 0.4 collective-permute-start.17
  59.2 0.3 collective-permute-done.14.refs_4_
  59.5 0.2 collective-permute-done.15.refs_5_
  59.6 0.4 collective-permute-done.16.refs_6_
  60.0 0.2 collective-permute-done.17.refs_7_
  60.1 1.5 %place.1 = bf16[768,1280]{1,0:T(8,128)(2,1)} custom-call(s32[10]{0:T(128)S(1)} %copy-done.5, bf16[3,128,128]{2,1,0:T(8,128)(2,1)S(1)} %get-tuple-element.40.refs_12_.refs_0_, bf16[3,128,128]{2,1,0:T(8,128)(2,1)S(1)} %collective-permute-done.11.refs_1_, bf16[3,128,128]{2,1,0:T(8,128)(2,1)S(1)} %collective-permute-done.12.refs_2_, ...), custom_call_target="tpu_custom_call", output_to_operand_aliasing={{}: (9, {})} | custom-call | flops 1000 | bytes 1000 | tf_op jit(solution)/shard_map/place/pallas_call | solution.py:33
  (12 shorter events, 0.0 us)
Async XLA Ops:
  0.0 9.9 %copy-start.1 = (bf16[768,1280]{1,0:T(8,128)(2,1)S(1)}, bf16[768,1280]{1,0:T(8,128)(2,1)}, u32[]{:S(2)}) copy-start(bf16[768,1280]{1,0:T(8,128)(2,1)} %refs_2_.3) | copy-start | bytes 5898244
  3.9 22.4 %collective-permute-start.7 = (bf16[768,1280]{1,0:T(8,128)(2,1)}, bf16[768,1280]{1,0:T(8,128)(2,1)}, u32[]{:S(2)}, u32[]{:S(2)}) collective-permute-start(bf16[768,1280]{1,0:T(8,128)(2,1)} %k_ref.1), channel_id=1, source_target_pairs={{0,4},{4,0},{8,12},{12,8},{16,20},{20,16},{24,28},{28,24},{1,5},{5... | collective-permute-start | bytes 5898248 | tf_op jit(solution)/shard_map/ppermute | solution.py:639
  4.5 35.7 %collective-permute-start.9 = (bf16[2,8,512,128]{3,2,1,0:T(8,128)(2,1)}, bf16[2,8,512,128]{3,2,1,0:T(8,128)(2,1)S(1)}, u32[]{:S(2)}, u32[]{:S(2)}) collective-permute-start(bf16[2,8,512,128]{3,2,1,0:T(8,128)(2,1)} %get-tuple-element.32), channel_id=1, source_target_pairs={{12,16},{16,12},{28,0},{0,28},{13,17},{17,13},{29,1},{1,29},{14,18... | collective-permute-start | bytes 6291464 | tf_op jit(solution)/shard_map/ppermute | solution.py:639
  9.9 19.3 %collective-permute-start.8 = (bf16[768,1280]{1,0:T(8,128)(2,1)S(1)}, bf16[768,1280]{1,0:T(8,128)(2,1)S(1)}, u32[]{:S(2)}, u32[]{:S(2)}) collective-permute-start(bf16[768,1280]{1,0:T(8,128)(2,1)S(1)} %copy-done.1), channel_id=1, source_target_pairs={{0,4},{4,0},{8,12},{12,8},{16,20},{20,16},{24,28},{28,24},{1,5},{5... | collective-permute-start | bytes 5898248 | tf_op jit(solution)/shard_map/ppermute | solution.py:639
  10.0 12.3 %copy-start = (bf16[768,1280]{1,0:T(8,128)(2,1)S(1)}, bf16[768,1280]{1,0:T(8,128)(2,1)}, u32[]{:S(2)}) copy-start(bf16[768,1280]{1,0:T(8,128)(2,1)} %refs_0_.3) | copy-start | bytes 5898244
  10.0 12.3 %collective-permute-start.2 = (bf16[3,768,128]{2,1,0:T(8,128)(2,1)}, bf16[3,768,128]{2,1,0:T(8,128)(2,1)S(1)}, u32[]{:S(2)}, u32[]{:S(2)}) collective-permute-start(bf16[3,768,128]{2,1,0:T(8,128)(2,1)} %get-tuple-element.25.after_ref), channel_id=1, source_target_pairs={{0,4},{4,0},{8,12},{12,8},{16,20},{20,16},{24,28},{28,24},{1,5},{5... | collective-permute-start | bytes 1769480 | tf_op jit(solution)/shard_map/ppermute | solution.py:639
  10.5 1.2 %copy-start.2 = (bf16[3,768,128]{2,1,0:T(8,128)(2,1)S(1)}, bf16[3,768,128]{2,1,0:T(8,128)(2,1)}, u32[]{:S(2)}) copy-start(bf16[3,768,128]{2,1,0:T(8,128)(2,1)} %get-tuple-element.25.after_ref) | copy-start | bytes 1769476
  11.7 10.6 %copy-start.3 = (f32[1280]{0:T(1024)S(1)}, f32[1280]{0:T(1024)}, u32[]{:S(2)}) copy-start(f32[1280]{0:T(1024)} %refs_7_.3) | copy-start | bytes 15364
  11.7 10.7 %copy-start.4 = (f32[1280]{0:T(1024)S(1)}, f32[1280]{0:T(1024)}, u32[]{:S(2)}) copy-start(f32[1280]{0:T(1024)} %refs_6_.3) | copy-start | bytes 15364
  11.7 10.7 %copy-start.5 = (s32[10]{0:T(128)S(1)}, s32[10]{0:T(128)}, u32[]{:S(2)}) copy-start(s32[10]{0:T(128)} %kind_ref.15) | copy-start | bytes 124
  14.1 3.7 %collective-permute-start = (f32[2,768]{1,0:T(2,128)S(1)}, f32[2,768]{1,0:T(2,128)S(1)}, u32[]{:S(2)}, u32[]{:S(2)}) collective-permute-start(f32[2,768]{1,0:T(2,128)S(1)} %sums.1), channel_id=1, source_target_pairs={{0,1},{1,0},{2,3},{3,2},{4,5},{5,4},{6,7},{7,6},{8,9},{9,8},{10,11... | collective-permute-start | bytes 18440 | tf_op jit(solution)/shard_map/ppermute | solution.py:650
  17.8 4.5 %collective-permute-start.1 = (f32[2,768]{1,0:T(2,128)S(1)}, f32[2,768]{1,0:T(2,128)S(1)}, u32[]{:S(2)}, u32[]{:S(2)}) collective-permute-start(f32[2,768]{1,0:T(2,128)S(1)} %add.6), channel_id=1, source_target_pairs={{0,2},{1,3},{2,0},{3,1},{4,6},{5,7},{6,4},{7,5},{8,10},{9,11},{10,... | collective-permute-start | bytes 18440 | tf_op jit(solution)/shard_map/ppermute | solution.py:650
  22.3 2.4 %collective-permute-start.3 = (f32[2,768]{1,0:T(2,128)S(1)}, f32[2,768]{1,0:T(2,128)S(1)}, u32[]{:S(2)}, u32[]{:S(2)}) collective-permute-start(f32[2,768]{1,0:T(2,128)S(1)} %add.7.total_ref.refs_8_), channel_id=1, source_target_pairs={{0,4},{4,0},{8,12},{12,8},{16,20},{20,16},{24,28},{28,24},{1,5},{5... | collective-permute-start | bytes 18440 | tf_op jit(solution)/shard_map/ppermute | solution.py:639
  25.7 18.3 %collective-permute-start.4 = (bf16[3,3,128,128]{3,2,1,0:T(8,128)(2,1)S(1)}, bf16[3,3,128,128]{3,2,1,0:T(8,128)(2,1)S(1)}, u32[]{:S(2)}, u32[]{:S(2)}) collective-permute-start(bf16[3,3,128,128]{3,2,1,0:T(8,128)(2,1)S(1)} %get-tuple-element.28), channel_id=1, source_target_pairs={{0,8},{4,12},{8,0},{12,4},{16,24},{20,28},{24,16},{28,20},{1,9},{5... | collective-permute-start | bytes 884744 | tf_op jit(solution)/shard_map/ppermute | solution.py:639
  26.0 18.0 %collective-permute-start.5 = (bf16[3,3,128,128]{3,2,1,0:T(8,128)(2,1)S(1)}, bf16[3,3,128,128]{3,2,1,0:T(8,128)(2,1)S(1)}, u32[]{:S(2)}, u32[]{:S(2)}) collective-permute-start(bf16[3,3,128,128]{3,2,1,0:T(8,128)(2,1)S(1)} %get-tuple-element.29), channel_id=1, source_target_pairs={{0,16},{4,20},{8,24},{12,28},{16,0},{20,4},{24,8},{28,12},{1,17},{... | collective-permute-start | bytes 884744 | tf_op jit(solution)/shard_map/ppermute | solution.py:639
  26.4 20.1 %collective-permute-start.6 = (bf16[3,3,128,128]{3,2,1,0:T(8,128)(2,1)S(1)}, bf16[3,3,128,128]{3,2,1,0:T(8,128)(2,1)S(1)}, u32[]{:S(2)}, u32[]{:S(2)}) collective-permute-start(bf16[3,3,128,128]{3,2,1,0:T(8,128)(2,1)S(1)} %get-tuple-element.30), channel_id=1, source_target_pairs={{0,24},{4,28},{8,16},{12,20},{16,8},{20,12},{24,0},{28,4},{1,25},{... | collective-permute-start | bytes 884744 | tf_op jit(solution)/shard_map/ppermute | solution.py:639
  29.3 8.8 %collective-permute-start.10 = (f32[2,768]{1,0:T(2,128)S(1)}, f32[2,768]{1,0:T(2,128)S(1)}, u32[]{:S(2)}, u32[]{:S(2)}) collective-permute-start(f32[2,768]{1,0:T(2,128)S(1)} %add.7.total_ref.refs_8_), channel_id=1, source_target_pairs={{12,17},{13,16},{14,19},{15,18},{16,13},{17,12},{18,15},{19,14},{2... | collective-permute-start | bytes 18440 | tf_op jit(solution)/shard_map/ppermute | solution.py:654
  48.3 9.9 %collective-permute-start.11 = (bf16[3,128,128]{2,1,0:T(8,128)(2,1)S(1)}, bf16[3,128,128]{2,1,0:T(8,128)(2,1)S(1)}, u32[]{:S(2)}, u32[]{:S(2)}) collective-permute-start(bf16[3,128,128]{2,1,0:T(8,128)(2,1)S(1)} %get-tuple-element.36), channel_id=1, source_target_pairs={{0,8},{4,12},{8,0},{12,4},{16,24},{20,28},{24,16},{28,20},{1,9},{5... | collective-permute-start | bytes 294920 | tf_op jit(solution)/shard_map/ppermute | solution.py:639
  51.4 7.3 %collective-permute-start.12 = (bf16[3,128,128]{2,1,0:T(8,128)(2,1)S(1)}, bf16[3,128,128]{2,1,0:T(8,128)(2,1)S(1)}, u32[]{:S(2)}, u32[]{:S(2)}) collective-permute-start(bf16[3,128,128]{2,1,0:T(8,128)(2,1)S(1)} %get-tuple-element.37), channel_id=1, source_target_pairs={{0,16},{4,20},{8,24},{12,28},{16,0},{20,4},{24,8},{28,12},{1,17},{... | collective-permute-start | bytes 294920 | tf_op jit(solution)/shard_map/ppermute | solution.py:639
  52.4 6.3 %collective-permute-start.13 = (bf16[3,128,128]{2,1,0:T(8,128)(2,1)S(1)}, bf16[3,128,128]{2,1,0:T(8,128)(2,1)S(1)}, u32[]{:S(2)}, u32[]{:S(2)}) collective-permute-start(bf16[3,128,128]{2,1,0:T(8,128)(2,1)S(1)} %get-tuple-element.38), channel_id=1, source_target_pairs={{0,24},{4,28},{8,16},{12,20},{16,8},{20,12},{24,0},{28,4},{1,25},{... | collective-permute-start | bytes 294920 | tf_op jit(solution)/shard_map/ppermute | solution.py:639
  58.1 1.4 %collective-permute-start.14 = (bf16[3,128,128]{2,1,0:T(8,128)(2,1)S(1)}, bf16[3,128,128]{2,1,0:T(8,128)(2,1)S(1)}, u32[]{:S(2)}, u32[]{:S(2)}) collective-permute-start(bf16[3,128,128]{2,1,0:T(8,128)(2,1)S(1)} %get-tuple-element.40.refs_12_.refs_0_), channel_id=1, source_target_pairs={{0,4},{4,0},{8,12},{12,8},{16,20},{20,16},{24,28},{28,24},{1,5},{5... | collective-permute-start | bytes 294920 | tf_op jit(solution)/shard_map/ppermute | solution.py:639
  58.2 1.4 %collective-permute-start.15 = (bf16[3,128,128]{2,1,0:T(8,128)(2,1)S(1)}, bf16[3,128,128]{2,1,0:T(8,128)(2,1)S(1)}, u32[]{:S(2)}, u32[]{:S(2)}) collective-permute-start(bf16[3,128,128]{2,1,0:T(8,128)(2,1)S(1)} %collective-permute-done.11.refs_1_), channel_id=1, source_target_pairs={{0,4},{4,0},{8,12},{12,8},{16,20},{20,16},{24,28},{28,24},{1,5},{5... | collective-permute-start | bytes 294920 | tf_op jit(solution)/shard_map/ppermute | solution.py:639
  58.7 1.3 %collective-permute-start.16 = (bf16[3,128,128]{2,1,0:T(8,128)(2,1)S(1)}, bf16[3,128,128]{2,1,0:T(8,128)(2,1)S(1)}, u32[]{:S(2)}, u32[]{:S(2)}) collective-permute-start(bf16[3,128,128]{2,1,0:T(8,128)(2,1)S(1)} %collective-permute-done.12.refs_2_), channel_id=1, source_target_pairs={{0,4},{4,0},{8,12},{12,8},{16,20},{20,16},{24,28},{28,24},{1,5},{5... | collective-permute-start | bytes 294920 | tf_op jit(solution)/shard_map/ppermute | solution.py:639
  58.8 1.4 %collective-permute-start.17 = (bf16[3,128,128]{2,1,0:T(8,128)(2,1)S(1)}, bf16[3,128,128]{2,1,0:T(8,128)(2,1)S(1)}, u32[]{:S(2)}, u32[]{:S(2)}) collective-permute-start(bf16[3,128,128]{2,1,0:T(8,128)(2,1)S(1)} %collective-permute-done.13.refs_3_), channel_id=1, source_target_pairs={{0,4},{4,0},{8,12},{12,8},{16,20},{20,16},{24,28},{28,24},{1,5},{5... | collective-permute-start | bytes 294920 | tf_op jit(solution)/shard_map/ppermute | solution.py:639

commit v5 on v4

--- a/solution.py
+++ b/solution.py
@@ -13,9 +13,11 @@
 FRAME = 1024
 OFFSET = 512
 VMEM = 24 * 1024 * 1024
-VMEM_PACK = 57 * 1024 * 1024
-VMEM_SUMS = 53 * 1024 * 1024
+VMEM_PACK = 58 * 1024 * 1024
+VMEM_SUMS = 32 * 1024 * 1024
 LOW = -1e30
+LATE = 1
+FRAMES_COST = 10000000000
 FACTOR = math.log2(math.e) / math.sqrt(HEAD_DIM)
 F32 = jnp.float32
 BF16 = jnp.bfloat16
@@ -91,106 +93,77 @@
         copy.wait()
 
 
-def pack_kernel(spatial, block, dealt, kind_ref, q_any, k_any, v_any, *refs):
-    outs, (order, packed, t_buf, sems) = refs[:-4], refs[-4:]
+def pack_kernel(spatial, block, kind_ref, k_any, v_any, early_any, late_any, order, packed, sems):
     put_order(kind_ref, order, spatial)
     place = Place(block)
     across = pl.ds(pl.multiple_of(place.cross, block), 2 * block)
-    moves = []
-
-    def move(source, held, into):
-        n = len(moves)
-        moves.append(
-            (
-                pltpu.make_async_copy(source, held, sems.at[0, n]),
-                pltpu.make_async_copy(held, into, sems.at[1, n]),
-            )
-        )
-        moves[-1][0].start()
-
-    for h in range(spatial):
-        for i, ref in enumerate((k_any, v_any)):
-            move(column(ref, order[h], across), packed.at[i, h], outs[0].at[i, h])
+    early = early_any.shape[1]
+    each = [(h, i) for h in range(spatial) for i in range(2)]
+    ins = [
+        pltpu.make_async_copy(
+            column((k_any, v_any)[i], order[h], across), packed.at[i, h], sems.at[0, h, i]
+        )
+        for h, i in each
+    ]
+    start_all(ins)
+    outs = []
+    for (h, i), came in zip(each, ins):
+        into = early_any.at[i, h] if h < early else late_any.at[i, h - early]
+        came.wait()
+        outs.append(pltpu.make_async_copy(packed.at[i, h], into, sems.at[1, h, i]))
+        outs[-1].start()
+    wait_all(outs)
+
+
+def pack_call(head_kind, keys, values, spatial, late, block):
+    return call(
+        functools.partial(pack_kernel, spatial, block),
+        "pack",
+        [shape((2, n, 2 * block, HEAD_DIM)) for n in (spatial - late, late)],
+        [IN_SMEM] + [ANY] * 2,
+        [ANY] * 2,
+        [
+            order_scratch(head_kind.shape[0]),
+            pltpu.VMEM((2, spatial, 2 * block, HEAD_DIM), BF16),
+            pltpu.SemaphoreType.DMA((2, spatial, 2)),
+        ],
+        (head_kind, keys, values),
+        vmem=VMEM_PACK,
+    )
+
+
+def sums_kernel(spatial, dealt, kind_ref, q_ref, k_ref, v_ref, after_ref, sums_ref, *refs):
+    order, squares = refs[-2:]
+    rows, width = q_ref.shape
+    size = HEAD_DIM
+    put_order(kind_ref, order, spatial)
+    for i, ref in enumerate((q_ref, k_ref)):
+        for s in range(rows // size):
+            total = None
+            for c in range(width // HEAD_DIM):
+                x = ref[s * size : (s + 1) * size, c * HEAD_DIM : (c + 1) * HEAD_DIM].astype(F32)
+                total = x * x if total is None else total + x * x
+            squares[s * size : (s + 1) * size, :] = total
+        sums_ref[i : i + 1, :] = jnp.sum(jnp.transpose(squares[...]), axis=0, keepdims=True)
     if dealt:
-        head = order[spatial + 1 - place.core]
-        for i, ref in enumerate((q_any, k_any, v_any)):
-            move(column(ref, head), t_buf.at[i], outs[1].at[i])
-    for came, goes in moves:
-        came.wait()
-        goes.start()
-    for _, goes in moves:
-        goes.wait()
-
-
-def pack_call(head_kind, queries, keys, values, spatial, block, dealt):
-    rows = queries.shape[0]
-    both = (2, spatial, 2 * block, HEAD_DIM)
-    outs = [shape(both)]
+        one = lanes(order[spatial + 1 - Place().core])
+        for i, ref in enumerate((q_ref, k_ref, v_ref)):
+            refs[0][i] = ref[:, one]
+
+
+def sums_call(head_kind, queries, keys, values, after, spatial, dealt):
+    rows, width = queries.shape
+    outs = [shape((2, rows), F32)]
     if dealt:
         outs.append(shape((3, rows, HEAD_DIM)))
     return call(
-        functools.partial(pack_kernel, spatial, block, dealt),
-        "pack",
+        functools.partial(sums_kernel, spatial, dealt),
+        "sums",
         outs,
-        [IN_SMEM] + [ANY] * 3,
-        [ANY] * len(outs),
-        [
-            order_scratch(head_kind.shape[0]),
-            pltpu.VMEM(both, BF16),
-            pltpu.VMEM((3, rows, HEAD_DIM), BF16),
-            pltpu.SemaphoreType.DMA((2, 2 * spatial + 3)),
-        ],
-        (head_kind, queries, keys, values),
-        vmem=VMEM_PACK,
-    )
-
-
-def sums_kernel(q_any, k_any, after_ref, sums_any, held, squares, sums, sems):
-    rows, width = q_any.shape
-    steps = (sems.shape[0] - 1) // 2
-    size = rows // steps
-    copies = [
-        [
-            pltpu.make_async_copy(
-                source.at[pl.ds(s * size, size), :],
-                held.at[i, pl.ds(s * size, size), :],
-                sems.at[i * steps + s],
-            )
-            for s in range(steps)
-        ]
-        for i, source in enumerate((q_any, k_any))
-    ]
-    start_all(copies[0] + copies[1])
-    for i in range(2):
-        for s in range(steps):
-            copies[i][s].wait()
-            total = None
-            for c in range(width // HEAD_DIM):
-                x = held[i, s * size : (s + 1) * size, c * HEAD_DIM : (c + 1) * HEAD_DIM].astype(F32)
-                total = x * x if total is None else total + x * x
-            squares[s * size : (s + 1) * size, :] = total
-        sums[i : i + 1, :] = jnp.sum(jnp.transpose(squares[...]), axis=0, keepdims=True)
-    out = pltpu.make_async_copy(sums, sums_any, sems.at[2 * steps])
-    out.start()
-    out.wait()
-
-
-def sums_call(queries, keys, after):
-    rows, width = queries.shape
-    steps = 4
-    return call(
-        sums_kernel,
-        "sums",
-        shape((2, rows), F32),
-        [ANY] * 2 + [LOOSE],
-        ANY,
-        [
-            pltpu.VMEM((2, rows, width), BF16),
-            pltpu.VMEM((rows, HEAD_DIM), F32),
-            pltpu.VMEM((2, rows), F32),
-            pltpu.SemaphoreType.DMA((2 * steps + 1,)),
-        ],
-        (queries, keys, after),
+        [IN_SMEM] + [IN_VMEM] * 3 + [LOOSE],
+        [IN_VMEM] * len(outs),
+        [order_scratch(head_kind.shape[0]), pltpu.VMEM((rows, HEAD_DIM), F32)],
+        (head_kind, queries, keys, values, after),
         vmem=VMEM_SUMS,
     )
 
@@ -333,7 +306,13 @@
 
 
 def far_attention(first, count, block, place, order, refs, put):
-    q_ref, k_ref, v_ref, kp_ref, v_pair_ref, kvx_ref, gq_ref, gk_ref, total_ref, cross_ref, factors, x_factors, x_keys = refs
+    q_ref, k_ref, v_ref, kp_ref, v_pair_ref, gq_ref, gk_ref, total_ref, cross_ref, *refs = refs
+    kvx_refs, (factors, x_factors, x_keys) = refs[:-3], refs[-3:]
+    early = kvx_refs[0].shape[1]
+
+    def crossed(i, n):
+        return kvx_refs[0][i, n] if n < early else kvx_refs[1][i, n - early]
+
     one = pl.ds(pl.multiple_of(place.apart, block), block)
     start = jnp.where(place.inner, 0, place.far)
     two = pl.ds(pl.multiple_of(start, block), 2 * block)
@@ -352,12 +331,12 @@
         n = first + h
         if part == 0:
             gain = gain_of(gk_ref, order[n])
-            x_keys[h % 2] = (kvx_ref[0, n].astype(F32) * x_factors[...] * gain).astype(BF16)
+            x_keys[h % 2] = (crossed(0, n).astype(F32) * x_factors[...] * gain).astype(BF16)
         return three(k_ref.at[n], kp_ref.at[n], x_keys[h % 2])
 
     def values_of(h, part):
         head = lanes(order[first + h])
-        return three(v_ref.at[:, head], v_pair_ref.at[:, head], kvx_ref[1, first + h])
+        return three(v_ref.at[:, head], v_pair_ref.at[:, head], crossed(1, first + h))
 
     attend_all(
         [(h, part) for h in range(count) for part in range(2)],
@@ -369,7 +348,7 @@
 
 
 def far_kernel(spatial, first, count, block, kind_ref, *refs):
-    operands, (out_ref, order, factors, x_factors, x_keys) = refs[:10], refs[-5:]
+    operands, (out_ref, order, factors, x_factors, x_keys) = refs[:-6], refs[-5:]
     put_order(kind_ref, order, spatial)
     place = Place(block)
 
@@ -394,8 +373,8 @@
     )
 
 
-def rest_kernel(spatial, first, count, block, kind_ref, *refs):
-    operands, refs = refs[:10], refs[10:]
+def rest_kernel(spatial, first, count, block, given, kind_ref, *refs):
+    operands, refs = refs[:given], refs[given:]
     near_ref, far_ref, _, out_ref, token_ref, order, factors, x_factors, x_keys, done, sems = refs
     token_ref[...] = jnp.zeros_like(token_ref)
     put_order(kind_ref, order, spatial)
@@ -429,7 +408,7 @@
     rows, width = operands[0].shape
     heads = head_kind.shape[0]
     return call(
-        functools.partial(rest_kernel, spatial, first, count, block),
+        functools.partial(rest_kernel, spatial, first, count, block, len(operands)),
         "rest",
         [shape((rows, width)), shape((8, HEAD_DIM), F32)],
         [IN_SMEM] + [IN_VMEM] * (len(operands) + 2) + [LOOSE],
@@ -587,6 +566,7 @@
         [IN_VMEM] * CHIPS,
         [],
         (*parts, after),
+        cycles=FRAMES_COST,
     )
 
 
@@ -638,9 +618,10 @@
     turned = [[(i, i ^ (2 * turn)) for i in range(devices)] for turn in range(1, CHIPS)]
     send = lambda x, route: lax.ppermute(x, "seq", route)
 
-    kv_near, *t_send = pack_call(head_kind, queries, keys, values, spatial, block, dealt)
+    late = LATE
+    kv_near, kv_late = pack_call(head_kind, keys, values, spatial, late, block)
     kv_cross = send(kv_near, cross)
-    sums = sums_call(queries, keys, t_send[0] if t_send else kv_near)
+    sums, *t_send = sums_call(head_kind, queries, keys, values, kv_late, spatial, dealt)
     k_pair = send(lax.optimization_barrier((keys, kv_near))[0], pair)
     v_pair = send(lax.optimization_barrier((values, kv_near))[0], pair)
     t_got = [send(part, pair) for part in t_send]
@@ -670,18 +651,18 @@
     near = near_call(
         head_kind, queries, k, values, kp, v_pair, query_gain, total, spatial, block
     )
-    operands = (
-        queries, k, values, kp, v_pair, kv_cross, query_gain, key_gain, total, cross_total
-    )
+    operands = (queries, k, values, kp, v_pair, query_gain, key_gain, total, cross_total, kv_cross)
     half = spatial // 2
     far = far_call(head_kind, operands, near, 0, half, spatial, block)
+    late_cross = send(lax.optimization_barrier((kv_late, far))[0], cross)
     last = far
     if dealt:
         results = frames_call(arrived, far)
-        parts = [results[0]] + [send(p, r) for p, r in zip(results[1:], turned)]
+        parts = [send(p, r) for p, r in zip(results[:0:-1], turned[::-1])]
+        parts = [results[0]] + parts[::-1]
         last = results[0]
     out, token = rest_call(
-        head_kind, operands, near, far, last, half, spatial - half, spatial, block
+        head_kind, operands + (late_cross,), near, far, last, half, spatial - half, spatial, block
     )
     if dealt:
         parts += [send(lax.optimization_barrier((p, token))[0], pair) for p in parts]

time: 62.1 us -> 59.3 us (0.955)
  waiting for transfers between devices: 9.58 us -> 4.97 us
  starting transfers between devices: 22.7 us -> 26.2 us
  Pallas kernels: 27.9 us -> 24.9 us
  local copies, waits for them, and re-layouts: 1.18 us -> 2.51 us
    ppermute x15 -> x16, waiting for transfers between devices: 5.59 us -> 0.97 us  [per_device(): send = lambda x, route: lax.ppermute(x, 'seq', route)]
    ppermute x15 -> x16, starting transfers between devices: 15.8 us -> 19 us  [per_device(): send = lambda x, route: lax.ppermute(x, 'seq', route)]
    pallas_call x10, Pallas kernels: 27.9 us -> 24.9 us  [call(): pl.pallas_call(kernel, out_shape=out_shape, in_specs=in_specs, out_specs=...]
    unnamed x12 -> x16, local copies, waits for them, and re-layouts: 1.18 us -> 2.51 us
  transfers between devices with their start and end apart: 18 -> 19, of which waited for: 8 -> 6; matrix products, arithmetic and copies ran while one was open for 0% -> 0% of each run, Pallas kernels for 33% -> 34%
where the time goes in v5:
time: 59.3 us; the launch traced here: 59 us
  starting transfers between devices  26.2 us (44%)
  Pallas kernels  24.9 us (42%)
  waiting for transfers between devices  4.97 us (8%)
  local copies, waits for them, and re-layouts  2.51 us (4%)
    pallas_call x10, Pallas kernels, call(): pl.pallas_call(kernel, out_shape=out_shape, in_specs=in_specs, out_specs=...  24.9 us
    ppermute x16, starting transfers between devices, per_device(): send = lambda x, route: lax.ppermute(x, 'seq', route)  19 us
    ppermute x2, starting transfers between devices, per_device(): lax.ppermute(total, 'head', [(i, i ^ d) for i in range(planes)])  4.23 us
    ppermute x2, waiting for transfers between devices, per_device(): lax.ppermute(total, 'head', [(i, i ^ d) for i in range(planes)])  3.99 us
    ppermute x1, starting transfers between devices, per_device(): lax.ppermute(total, ('seq', 'head'), [(i * planes + p, j * planes + (p ^...  2.98 us
    unnamed x16, local copies, waits for them, and re-layouts  2.51 us
  transfers between devices with their start and end apart: 19, of which 6 were waited for; matrix products, arithmetic and copies ran while one was open for 0% of the time, Pallas kernels for 34%

profile of v5, /device:TPU:0, one launch (start us, length us, event | category | flops | bytes accessed | tf_op | source)
XLA Modules:
  0.0 59.0 jit_solution(11848357585812431649)
XLA Ops:
  0.0 3.7 %pack.1 = (bf16[2,7,512,128]{3,2,1,0:T(8,128)(2,1)}, bf16[2,1,512,128]{3,2,1,0:T(8,128)(2,1)}) custom-call(s32[10]{0:T(128)} %kind_ref.17, bf16[768,1280]{1,0:T(8,128)(2,1)} %k_ref.3, bf16[768,1280]{1,0:T(8,128)(2,1)} %refs_2_.3), custom_call_target="tpu_custom_call" | custom-call | flops 1000 | bytes 1000 | tf_op jit(solution)/shard_map/pack/pallas_call | solution.py:35
  3.7 0.5 collective-permute-start.7
  4.2 0.1 collective-permute-start.8
  4.3 5.5 %collective-permute-start.10 = (bf16[2,7,512,128]{3,2,1,0:T(8,128)(2,1)}, bf16[2,7,512,128]{3,2,1,0:T(8,128)(2,1)S(1)}, u32[]{:S(2)}, u32[]{:S(2)}) collective-permute-start(bf16[2,7,512,128]{3,2,1,0:T(8,128)(2,1)} %get-tuple-element.37), channel_id=1, source_target_pairs={{12,16},{16,12},{28,0},{0,28},{13,17},{17,13},{29,1},{1,29},{14,18... | collective-permute-start | bytes 5505032 | tf_op jit(solution)/shard_map/ppermute | solution.py:619
  9.8 0.0 copy-start.2
  9.8 1.5 %copy-done.2 = bf16[768,1280]{1,0:T(8,128)(2,1)S(1)} copy-done((bf16[768,1280]{1,0:T(8,128)(2,1)S(1)}, bf16[768,1280]{1,0:T(8,128)(2,1)}, u32[]{:S(2)}) %copy-start.2) | copy-done | bytes 1966104
  11.3 0.9 %copy-done.4 = bf16[2,1,512,128]{3,2,1,0:T(8,128)(2,1)S(1)} copy-done((bf16[2,1,512,128]{3,2,1,0:T(8,128)(2,1)S(1)}, bf16[2,1,512,128]{3,2,1,0:T(8,128)(2,1)}, u32[]{:S(2)}) %copy-start.4) | copy-done | bytes 262168
  12.3 1.5 %sums.1 = (f32[2,768]{1,0:T(2,128)S(1)}, bf16[3,768,128]{2,1,0:T(8,128)(2,1)S(1)}) custom-call(s32[10]{0:T(128)S(1)} %copy-done.7, bf16[768,1280]{1,0:T(8,128)(2,1)S(1)} %copy-done.1, bf16[768,1280]{1,0:T(8,128)(2,1)S(1)} %copy-done.2, bf16[768,1280]{1,0:T(8,128)(2,1)S(1)} %copy-done, bf16[2,1,512,128]{3,2,1,0:T(8,128)(2,1)S(1)} %copy-done.4), custom_call_target="tpu_custom_call" | custom-call | flops 1000 | bytes 1000 | tf_op jit(solution)/shard_map/sums/pallas_call | solution.py:35
  13.8 0.1 collective-permute-start.2
  13.9 1.6 %collective-permute-start = (f32[2,768]{1,0:T(2,128)S(1)}, f32[2,768]{1,0:T(2,128)S(1)}, u32[]{:S(2)}, u32[]{:S(2)}) collective-permute-start(f32[2,768]{1,0:T(2,128)S(1)} %get-tuple-element.29), channel_id=1, source_target_pairs={{0,1},{1,0},{2,3},{3,2},{4,5},{5,4},{6,7},{7,6},{8,9},{9,8},{10,11... | collective-permute-start | bytes 18440 | tf_op jit(solution)/shard_map/ppermute | solution.py:631
  15.5 2.1 %collective-permute-done = f32[2,768]{1,0:T(2,128)S(1)} collective-permute-done((f32[2,768]{1,0:T(2,128)S(1)}, f32[2,768]{1,0:T(2,128)S(1)}, u32[]{:S(2)}, u32[]{:S(2)}) %collective-permute-start) | collective-permute-done | bytes 6176 | tf_op jit(solution)/shard_map/ppermute | solution.py:631
  17.6 2.6 %collective-permute-start.1 = (f32[2,768]{1,0:T(2,128)S(1)}, f32[2,768]{1,0:T(2,128)S(1)}, u32[]{:S(2)}, u32[]{:S(2)}) collective-permute-start(f32[2,768]{1,0:T(2,128)S(1)} %add.6), channel_id=1, source_target_pairs={{0,2},{1,3},{2,0},{3,1},{4,6},{5,7},{6,4},{7,5},{8,10},{9,11},{10,... | collective-permute-start | bytes 18440 | tf_op jit(solution)/shard_map/ppermute | solution.py:631
  20.2 1.9 %collective-permute-done.1 = f32[2,768]{1,0:T(2,128)S(1)} collective-permute-done((f32[2,768]{1,0:T(2,128)S(1)}, f32[2,768]{1,0:T(2,128)S(1)}, u32[]{:S(2)}, u32[]{:S(2)}) %collective-permute-start.1) | collective-permute-done | bytes 6176 | tf_op jit(solution)/shard_map/ppermute | solution.py:631
  22.1 0.0 collective-permute-start.3
  22.1 0.0 collective-permute-done.2.refs_0_.got_ref
  22.2 1.3 %own.1 = (bf16[8,768,128]{2,1,0:T(8,128)(2,1)S(1)}, bf16[3,768,128]{2,1,0:T(8,128)(2,1)S(1)}) custom-call(s32[10]{0:T(128)S(1)} %copy-done.7, bf16[768,1280]{1,0:T(8,128)(2,1)S(1)} %copy-done.1, bf16[768,1280]{1,0:T(8,128)(2,1)S(1)} %copy-done.3, bf16[768,1280]{1,0:T(8,128)(2,1)S(1)} %copy-done, f32[1280]{0:T(1024)S(1)} %copy-done.6, f32[1280]{0:T(1024)S(1)} %copy-done.5, ...), custom_call_target="tpu_custom_call" | custom-call | flops 1000 | bytes 1000 | tf_op jit(solution)/shard_map/own/pallas_call | solution.py:35
  23.5 0.0 collective-permute-done.3.sums_ref
  23.5 1.0 %deal.1 = (bf16[3,3,128,128]{3,2,1,0:T(8,128)(2,1)S(1)}, bf16[3,3,128,128]{3,2,1,0:T(8,128)(2,1)S(1)}, bf16[3,3,128,128]{3,2,1,0:T(8,128)(2,1)S(1)}, bf16[3,3,128,128]{3,2,1,0:T(8,128)(2,1)S(1)}) custom-call(s32[10]{0:T(128)S(1)} %copy-done.7, bf16[3,768,128]{2,1,0:T(8,128)(2,1)S(1)} %get-tuple-element.31.own_ref, ...), custom_call_target="tpu_custom_call" | custom-call | flops 1000 | bytes 1000 | tf_op jit(solution)/shard_map/deal/pallas_call | solution.py:35
  24.5 0.9 %collective-permute-start.4 = (bf16[3,3,128,128]{3,2,1,0:T(8,128)(2,1)S(1)}, bf16[3,3,128,128]{3,2,1,0:T(8,128)(2,1)S(1)}, u32[]{:S(2)}, u32[]{:S(2)}) collective-permute-start(bf16[3,3,128,128]{3,2,1,0:T(8,128)(2,1)S(1)} %get-tuple-element.33), channel_id=1, source_target_pairs={{0,8},{4,12},{8,0},{12,4},{16,24},{20,28},{24,16},{28,20},{1,9},{5... | collective-permute-start | bytes 884744 | tf_op jit(solution)/shard_map/ppermute | solution.py:619
  25.4 0.2 collective-permute-start.5
  25.6 0.0 collective-permute-done.7.k_ref
  25.6 2.4 %collective-permute-start.6 = (bf16[3,3,128,128]{3,2,1,0:T(8,128)(2,1)S(1)}, bf16[3,3,128,128]{3,2,1,0:T(8,128)(2,1)S(1)}, u32[]{:S(2)}, u32[]{:S(2)}) collective-permute-start(bf16[3,3,128,128]{3,2,1,0:T(8,128)(2,1)S(1)} %get-tuple-element.35), channel_id=1, source_target_pairs={{0,24},{4,28},{8,16},{12,20},{16,8},{20,12},{24,0},{28,4},{1,25},{... | collective-permute-start | bytes 884744 | tf_op jit(solution)/shard_map/ppermute | solution.py:619
  28.1 3.0 %collective-permute-start.9 = (f32[2,768]{1,0:T(2,128)S(1)}, f32[2,768]{1,0:T(2,128)S(1)}, u32[]{:S(2)}, u32[]{:S(2)}) collective-permute-start(f32[2,768]{1,0:T(2,128)S(1)} %add.7.total_ref.refs_7_), channel_id=1, source_target_pairs={{12,17},{13,16},{14,19},{15,18},{16,13},{17,12},{18,15},{19,14},{2... | collective-permute-start | bytes 18440 | tf_op jit(solution)/shard_map/ppermute | solution.py:635
  31.0 1.1 %pair.1.kp_ref.refs_3_ = bf16[8,768,128]{2,1,0:T(8,128)(2,1)S(1)} custom-call(s32[10]{0:T(128)S(1)} %copy-done.7, bf16[768,1280]{1,0:T(8,128)(2,1)S(1)} %collective-permute-done.7.k_ref, f32[1280]{0:T(1024)S(1)} %copy-done.5, f32[2,768]{1,0:T(2,128)S(1)} %collective-permute-done.3.sums_ref, bf16[3,3,128,128]{3,2,1,0:T(8,128)(2,1)S(1)} %get-tuple-element.32.after_ref.refs_0_), custom_call_target="tpu_custom_call" | custom-call | flops 1000 | bytes 1000 | tf_op jit(solution)/shard_map/pair/pallas_call | solution.py:35
  32.2 4.0 %near.1.refs_10_.refs_11_ = bf16[8,256,128]{2,1,0:T(8,128)(2,1)S(1)} custom-call(s32[10]{0:T(128)S(1)} %copy-done.7, bf16[768,1280]{1,0:T(8,128)(2,1)S(1)} %copy-done.1, bf16[8,768,128]{2,1,0:T(8,128)(2,1)S(1)} %get-tuple-element.36.k_ref.refs_1_, bf16[768,1280]{1,0:T(8,128)(2,1)S(1)} %copy-done, bf16[8,768,128]{2,1,0:T(8,128)(2,1)S(1)} %pair.1.kp_ref.refs_3_, ...), custom_call_target="tpu_custom_call" | custom-call | flops 1000 | bytes 1000 | tf_op jit(solution)/shard_map/near/pallas_call | solution.py:35
  36.2 0.0 collective-permute-done.9.refs_8_
  36.2 0.0 collective-permute-done.10.refs_9_
  36.3 3.8 %far.1.refs_4_.refs_12_ = bf16[4,512,128]{2,1,0:T(8,128)(2,1)S(1)} custom-call(s32[10]{0:T(128)S(1)} %copy-done.7, bf16[768,1280]{1,0:T(8,128)(2,1)S(1)} %copy-done.1, bf16[8,768,128]{2,1,0:T(8,128)(2,1)S(1)} %get-tuple-element.36.k_ref.refs_1_, bf16[768,1280]{1,0:T(8,128)(2,1)S(1)} %copy-done, bf16[8,768,128]{2,1,0:T(8,128)(2,1)S(1)} %pair.1.kp_ref.refs_3_, ...), custom_call_target="tpu_custom_call" | custom-call | flops 1000 | bytes 1000 | tf_op jit(solution)/shard_map/far/pallas_call | solution.py:35
  40.1 4.7 %collective-permute-start.14 = (bf16[2,1,512,128]{3,2,1,0:T(8,128)(2,1)S(1)}, bf16[2,1,512,128]{3,2,1,0:T(8,128)(2,1)S(1)}, u32[]{:S(2)}, u32[]{:S(2)}) collective-permute-start(bf16[2,1,512,128]{3,2,1,0:T(8,128)(2,1)S(1)} %copy-done.4), channel_id=1, source_target_pairs={{12,16},{16,12},{28,0},{0,28},{13,17},{17,13},{29,1},{1,29},{14,18... | collective-permute-start | bytes 786440 | tf_op jit(solution)/shard_map/ppermute | solution.py:619
  44.8 0.0 collective-permute-done.5.refs_2_
  44.8 0.0 collective-permute-done.6.refs_3_
  44.8 1.8 %frames.1 = (bf16[3,128,128]{2,1,0:T(8,128)(2,1)S(1)}, bf16[3,128,128]{2,1,0:T(8,128)(2,1)S(1)}, bf16[3,128,128]{2,1,0:T(8,128)(2,1)S(1)}, bf16[3,128,128]{2,1,0:T(8,128)(2,1)S(1)}) custom-call(bf16[3,3,128,128]{3,2,1,0:T(8,128)(2,1)S(1)} %get-tuple-element.32.after_ref.refs_0_, bf16[3,3,128,128]{3,2,1,0:T(8,128)(2,1)S(1)} %collective-permute-done.4.refs_1_, ...), custom_call_target="tpu_custom_call" | custom-call | flops 10000000000 | bytes 1000 | tf_op jit(solution)/shard_map/frames/pallas_call | solution.py:35
  46.6 2.1 %collective-permute-start.13 = (bf16[3,128,128]{2,1,0:T(8,128)(2,1)S(1)}, bf16[3,128,128]{2,1,0:T(8,128)(2,1)S(1)}, u32[]{:S(2)}, u32[]{:S(2)}) collective-permute-start(bf16[3,128,128]{2,1,0:T(8,128)(2,1)S(1)} %get-tuple-element.43), channel_id=1, source_target_pairs={{0,24},{4,28},{8,16},{12,20},{16,8},{20,12},{24,0},{28,4},{1,25},{... | collective-permute-start | bytes 294920 | tf_op jit(solution)/shard_map/ppermute | solution.py:619
  48.7 1.1 %collective-permute-start.12 = (bf16[3,128,128]{2,1,0:T(8,128)(2,1)S(1)}, bf16[3,128,128]{2,1,0:T(8,128)(2,1)S(1)}, u32[]{:S(2)}, u32[]{:S(2)}) collective-permute-start(bf16[3,128,128]{2,1,0:T(8,128)(2,1)S(1)} %get-tuple-element.42), channel_id=1, source_target_pairs={{0,16},{4,20},{8,24},{12,28},{16,0},{20,4},{24,8},{28,12},{1,17},{... | collective-permute-start | bytes 294920 | tf_op jit(solution)/shard_map/ppermute | solution.py:619
  49.8 0.4 collective-permute-start.11
  50.2 0.0 collective-permute-done.14.refs_10_
  50.2 5.2 %rest.1 = (bf16[768,1280]{1,0:T(8,128)(2,1)}, f32[8,128]{1,0:T(8,128)}) custom-call(s32[10]{0:T(128)S(1)} %copy-done.7, bf16[768,1280]{1,0:T(8,128)(2,1)S(1)} %copy-done.1, bf16[8,768,128]{2,1,0:T(8,128)(2,1)S(1)} %get-tuple-element.36.k_ref.refs_1_, bf16[768,1280]{1,0:T(8,128)(2,1)S(1)} %copy-done, bf16[8,768,128]{2,1,0:T(8,128)(2,1)S(1)} %pair.1.kp_ref.refs_3_, ...), custom_call_target="tpu_custom_call" | custom-call | flops 1000 | bytes 1000 | tf_op jit(solution)/shard_map/rest/pallas_call | solution.py:35
  55.4 0.0 collective-permute-done.12.refs_2_
  55.4 0.0 collective-permute-done.11.refs_1_
  55.4 0.1 collective-permute-start.15
  55.5 0.5 collective-permute-start.16
  56.0 0.1 collective-permute-start.17
  56.0 0.4 collective-permute-start.18
  56.5 0.3 collective-permute-done.15.refs_4_
  56.7 0.2 collective-permute-done.16.refs_5_
  56.9 0.4 collective-permute-done.17.refs_6_
  57.3 0.2 collective-permute-done.18.refs_7_
  57.4 1.5 %place.1 = bf16[768,1280]{1,0:T(8,128)(2,1)} custom-call(s32[10]{0:T(128)S(1)} %copy-done.7, bf16[3,128,128]{2,1,0:T(8,128)(2,1)S(1)} %get-tuple-element.46.refs_13_.refs_0_, bf16[3,128,128]{2,1,0:T(8,128)(2,1)S(1)} %collective-permute-done.11.refs_1_, bf16[3,128,128]{2,1,0:T(8,128)(2,1)S(1)} %collective-permute-done.12.refs_2_, ...), custom_call_target="tpu_custom_call", output_to_operand_aliasing={{}: (9, {})} | custom-call | flops 1000 | bytes 1000 | tf_op jit(solution)/shard_map/place/pallas_call | solution.py:35
  (18 shorter events, 0.0 us)
Async XLA Ops:
  0.0 9.8 %copy-start.7 = (s32[10]{0:T(128)S(1)}, s32[10]{0:T(128)}, u32[]{:S(2)}) copy-start(s32[10]{0:T(128)} %kind_ref.17) | copy-start | bytes 124
  0.0 4.2 %copy-start = (bf16[768,1280]{1,0:T(8,128)(2,1)S(1)}, bf16[768,1280]{1,0:T(8,128)(2,1)}, u32[]{:S(2)}) copy-start(bf16[768,1280]{1,0:T(8,128)(2,1)} %refs_2_.3) | copy-start | bytes 5898244
  0.0 9.8 %copy-start.1 = (bf16[768,1280]{1,0:T(8,128)(2,1)S(1)}, bf16[768,1280]{1,0:T(8,128)(2,1)}, u32[]{:S(2)}) copy-start(bf16[768,1280]{1,0:T(8,128)(2,1)} %refs_0_.3) | copy-start | bytes 5898244
  3.7 21.9 %collective-permute-start.7 = (bf16[768,1280]{1,0:T(8,128)(2,1)}, bf16[768,1280]{1,0:T(8,128)(2,1)S(1)}, u32[]{:S(2)}, u32[]{:S(2)}) collective-permute-start(bf16[768,1280]{1,0:T(8,128)(2,1)} %k_ref.3), channel_id=1, source_target_pairs={{0,4},{4,0},{8,12},{12,8},{16,20},{20,16},{24,28},{28,24},{1,5},{5... | collective-permute-start | bytes 5898248 | tf_op jit(solution)/shard_map/ppermute | solution.py:619
  4.2 23.8 %collective-permute-start.8 = (bf16[768,1280]{1,0:T(8,128)(2,1)S(1)}, bf16[768,1280]{1,0:T(8,128)(2,1)S(1)}, u32[]{:S(2)}, u32[]{:S(2)}) collective-permute-start(bf16[768,1280]{1,0:T(8,128)(2,1)S(1)} %copy-done), channel_id=1, source_target_pairs={{0,4},{4,0},{8,12},{12,8},{16,20},{20,16},{24,28},{28,24},{1,5},{5... | collective-permute-start | bytes 5898248 | tf_op jit(solution)/shard_map/ppermute | solution.py:619
  4.3 32.0 %collective-permute-start.10 = (bf16[2,7,512,128]{3,2,1,0:T(8,128)(2,1)}, bf16[2,7,512,128]{3,2,1,0:T(8,128)(2,1)S(1)}, u32[]{:S(2)}, u32[]{:S(2)}) collective-permute-start(bf16[2,7,512,128]{3,2,1,0:T(8,128)(2,1)} %get-tuple-element.37), channel_id=1, source_target_pairs={{12,16},{16,12},{28,0},{0,28},{13,17},{17,13},{29,1},{1,29},{14,18... | collective-permute-start | bytes 5505032 | tf_op jit(solution)/shard_map/ppermute | solution.py:619
  9.8 1.5 %copy-start.2 = (bf16[768,1280]{1,0:T(8,128)(2,1)S(1)}, bf16[768,1280]{1,0:T(8,128)(2,1)}, u32[]{:S(2)}) copy-start(bf16[768,1280]{1,0:T(8,128)(2,1)} %k_ref.3) | copy-start | bytes 5898244
  11.3 0.9 %copy-start.4 = (bf16[2,1,512,128]{3,2,1,0:T(8,128)(2,1)S(1)}, bf16[2,1,512,128]{3,2,1,0:T(8,128)(2,1)}, u32[]{:S(2)}) copy-start(bf16[2,1,512,128]{3,2,1,0:T(8,128)(2,1)} %get-tuple-element.44.after_ref) | copy-start | bytes 786436
  12.3 9.9 %copy-start.3 = (bf16[768,1280]{1,0:T(8,128)(2,1)S(1)}, bf16[768,1280]{1,0:T(8,128)(2,1)}, u32[]{:S(2)}) copy-start(bf16[768,1280]{1,0:T(8,128)(2,1)} %k_ref.3) | copy-start | bytes 5898244
  12.3 9.9 %copy-start.5 = (f32[1280]{0:T(1024)S(1)}, f32[1280]{0:T(1024)}, u32[]{:S(2)}) copy-start(f32[1280]{0:T(1024)} %refs_6_.3) | copy-start | bytes 15364
  12.3 9.9 %copy-start.6 = (f32[1280]{0:T(1024)S(1)}, f32[1280]{0:T(1024)}, u32[]{:S(2)}) copy-start(f32[1280]{0:T(1024)} %refs_5_.3) | copy-start | bytes 15364
  13.8 8.3 %collective-permute-start.2 = (bf16[3,768,128]{2,1,0:T(8,128)(2,1)S(1)}, bf16[3,768,128]{2,1,0:T(8,128)(2,1)S(1)}, u32[]{:S(2)}, u32[]{:S(2)}) collective-permute-start(bf16[3,768,128]{2,1,0:T(8,128)(2,1)S(1)} %get-tuple-element.30), channel_id=1, source_target_pairs={{0,4},{4,0},{8,12},{12,8},{16,20},{20,16},{24,28},{28,24},{1,5},{5... | collective-permute-start | bytes 1769480 | tf_op jit(solution)/shard_map/ppermute | solution.py:619
  13.9 3.7 %collective-permute-start = (f32[2,768]{1,0:T(2,128)S(1)}, f32[2,768]{1,0:T(2,128)S(1)}, u32[]{:S(2)}, u32[]{:S(2)}) collective-permute-start(f32[2,768]{1,0:T(2,128)S(1)} %get-tuple-element.29), channel_id=1, source_target_pairs={{0,1},{1,0},{2,3},{3,2},{4,5},{5,4},{6,7},{7,6},{8,9},{9,8},{10,11... | collective-permute-start | bytes 18440 | tf_op jit(solution)/shard_map/ppermute | solution.py:631
  17.6 4.5 %collective-permute-start.1 = (f32[2,768]{1,0:T(2,128)S(1)}, f32[2,768]{1,0:T(2,128)S(1)}, u32[]{:S(2)}, u32[]{:S(2)}) collective-permute-start(f32[2,768]{1,0:T(2,128)S(1)} %add.6), channel_id=1, source_target_pairs={{0,2},{1,3},{2,0},{3,1},{4,6},{5,7},{6,4},{7,5},{8,10},{9,11},{10,... | collective-permute-start | bytes 18440 | tf_op jit(solution)/shard_map/ppermute | solution.py:631
  22.1 1.3 %collective-permute-start.3 = (f32[2,768]{1,0:T(2,128)S(1)}, f32[2,768]{1,0:T(2,128)S(1)}, u32[]{:S(2)}, u32[]{:S(2)}) collective-permute-start(f32[2,768]{1,0:T(2,128)S(1)} %add.7.total_ref.refs_7_), channel_id=1, source_target_pairs={{0,4},{4,0},{8,12},{12,8},{16,20},{20,16},{24,28},{28,24},{1,5},{5... | collective-permute-start | bytes 18440 | tf_op jit(solution)/shard_map/ppermute | solution.py:619
  24.5 20.3 %collective-permute-start.4 = (bf16[3,3,128,128]{3,2,1,0:T(8,128)(2,1)S(1)}, bf16[3,3,128,128]{3,2,1,0:T(8,128)(2,1)S(1)}, u32[]{:S(2)}, u32[]{:S(2)}) collective-permute-start(bf16[3,3,128,128]{3,2,1,0:T(8,128)(2,1)S(1)} %get-tuple-element.33), channel_id=1, source_target_pairs={{0,8},{4,12},{8,0},{12,4},{16,24},{20,28},{24,16},{28,20},{1,9},{5... | collective-permute-start | bytes 884744 | tf_op jit(solution)/shard_map/ppermute | solution.py:619
  25.4 19.3 %collective-permute-start.5 = (bf16[3,3,128,128]{3,2,1,0:T(8,128)(2,1)S(1)}, bf16[3,3,128,128]{3,2,1,0:T(8,128)(2,1)S(1)}, u32[]{:S(2)}, u32[]{:S(2)}) collective-permute-start(bf16[3,3,128,128]{3,2,1,0:T(8,128)(2,1)S(1)} %get-tuple-element.34), channel_id=1, source_target_pairs={{0,16},{4,20},{8,24},{12,28},{16,0},{20,4},{24,8},{28,12},{1,17},{... | collective-permute-start | bytes 884744 | tf_op jit(solution)/shard_map/ppermute | solution.py:619
  25.6 19.2 %collective-permute-start.6 = (bf16[3,3,128,128]{3,2,1,0:T(8,128)(2,1)S(1)}, bf16[3,3,128,128]{3,2,1,0:T(8,128)(2,1)S(1)}, u32[]{:S(2)}, u32[]{:S(2)}) collective-permute-start(bf16[3,3,128,128]{3,2,1,0:T(8,128)(2,1)S(1)} %get-tuple-element.35), channel_id=1, source_target_pairs={{0,24},{4,28},{8,16},{12,20},{16,8},{20,12},{24,0},{28,4},{1,25},{... | collective-permute-start | bytes 884744 | tf_op jit(solution)/shard_map/ppermute | solution.py:619
  28.1 8.2 %collective-permute-start.9 = (f32[2,768]{1,0:T(2,128)S(1)}, f32[2,768]{1,0:T(2,128)S(1)}, u32[]{:S(2)}, u32[]{:S(2)}) collective-permute-start(f32[2,768]{1,0:T(2,128)S(1)} %add.7.total_ref.refs_7_), channel_id=1, source_target_pairs={{12,17},{13,16},{14,19},{15,18},{16,13},{17,12},{18,15},{19,14},{2... | collective-permute-start | bytes 18440 | tf_op jit(solution)/shard_map/ppermute | solution.py:635
  40.1 10.1 %collective-permute-start.14 = (bf16[2,1,512,128]{3,2,1,0:T(8,128)(2,1)S(1)}, bf16[2,1,512,128]{3,2,1,0:T(8,128)(2,1)S(1)}, u32[]{:S(2)}, u32[]{:S(2)}) collective-permute-start(bf16[2,1,512,128]{3,2,1,0:T(8,128)(2,1)S(1)} %copy-done.4), channel_id=1, source_target_pairs={{12,16},{16,12},{28,0},{0,28},{13,17},{17,13},{29,1},{1,29},{14,18... | collective-permute-start | bytes 786440 | tf_op jit(solution)/shard_map/ppermute | solution.py:619
  46.6 8.7 %collective-permute-start.13 = (bf16[3,128,128]{2,1,0:T(8,128)(2,1)S(1)}, bf16[3,128,128]{2,1,0:T(8,128)(2,1)S(1)}, u32[]{:S(2)}, u32[]{:S(2)}) collective-permute-start(bf16[3,128,128]{2,1,0:T(8,128)(2,1)S(1)} %get-tuple-element.43), channel_id=1, source_target_pairs={{0,24},{4,28},{8,16},{12,20},{16,8},{20,12},{24,0},{28,4},{1,25},{... | collective-permute-start | bytes 294920 | tf_op jit(solution)/shard_map/ppermute | solution.py:619
  48.7 6.7 %collective-permute-start.12 = (bf16[3,128,128]{2,1,0:T(8,128)(2,1)S(1)}, bf16[3,128,128]{2,1,0:T(8,128)(2,1)S(1)}, u32[]{:S(2)}, u32[]{:S(2)}) collective-permute-start(bf16[3,128,128]{2,1,0:T(8,128)(2,1)S(1)} %get-tuple-element.42), channel_id=1, source_target_pairs={{0,16},{4,20},{8,24},{12,28},{16,0},{20,4},{24,8},{28,12},{1,17},{... | collective-permute-start | bytes 294920 | tf_op jit(solution)/shard_map/ppermute | solution.py:619
  49.8 5.6 %collective-permute-start.11 = (bf16[3,128,128]{2,1,0:T(8,128)(2,1)S(1)}, bf16[3,128,128]{2,1,0:T(8,128)(2,1)S(1)}, u32[]{:S(2)}, u32[]{:S(2)}) collective-permute-start(bf16[3,128,128]{2,1,0:T(8,128)(2,1)S(1)} %get-tuple-element.41), channel_id=1, source_target_pairs={{0,8},{4,12},{8,0},{12,4},{16,24},{20,28},{24,16},{28,20},{1,9},{5... | collective-permute-start | bytes 294920 | tf_op jit(solution)/shard_map/ppermute | solution.py:619
  55.4 1.4 %collective-permute-start.15 = (bf16[3,128,128]{2,1,0:T(8,128)(2,1)S(1)}, bf16[3,128,128]{2,1,0:T(8,128)(2,1)S(1)}, u32[]{:S(2)}, u32[]{:S(2)}) collective-permute-start(bf16[3,128,128]{2,1,0:T(8,128)(2,1)S(1)} %get-tuple-element.46.refs_13_.refs_0_), channel_id=1, source_target_pairs={{0,4},{4,0},{8,12},{12,8},{16,20},{20,16},{24,28},{28,24},{1,5},{5... | collective-permute-start | bytes 294920 | tf_op jit(solution)/shard_map/ppermute | solution.py:619
  55.5 1.4 %collective-permute-start.16 = (bf16[3,128,128]{2,1,0:T(8,128)(2,1)S(1)}, bf16[3,128,128]{2,1,0:T(8,128)(2,1)S(1)}, u32[]{:S(2)}, u32[]{:S(2)}) collective-permute-start(bf16[3,128,128]{2,1,0:T(8,128)(2,1)S(1)} %collective-permute-done.11.refs_1_), channel_id=1, source_target_pairs={{0,4},{4,0},{8,12},{12,8},{16,20},{20,16},{24,28},{28,24},{1,5},{5... | collective-permute-start | bytes 294920 | tf_op jit(solution)/shard_map/ppermute | solution.py:619
  56.0 1.3 %collective-permute-start.17 = (bf16[3,128,128]{2,1,0:T(8,128)(2,1)S(1)}, bf16[3,128,128]{2,1,0:T(8,128)(2,1)S(1)}, u32[]{:S(2)}, u32[]{:S(2)}) collective-permute-start(bf16[3,128,128]{2,1,0:T(8,128)(2,1)S(1)} %collective-permute-done.12.refs_2_), channel_id=1, source_target_pairs={{0,4},{4,0},{8,12},{12,8},{16,20},{20,16},{24,28},{28,24},{1,5},{5... | collective-permute-start | bytes 294920 | tf_op jit(solution)/shard_map/ppermute | solution.py:619
  56.0 1.4 %collective-permute-start.18 = (bf16[3,128,128]{2,1,0:T(8,128)(2,1)S(1)}, bf16[3,128,128]{2,1,0:T(8,128)(2,1)S(1)}, u32[]{:S(2)}, u32[]{:S(2)}) collective-permute-start(bf16[3,128,128]{2,1,0:T(8,128)(2,1)S(1)} %collective-permute-done.13.refs_3_), channel_id=1, source_target_pairs={{0,4},{4,0},{8,12},{12,8},{16,20},{20,16},{24,28},{28,24},{1,5},{5... | collective-permute-start | bytes 294920 | tf_op jit(solution)/shard_map/ppermute | solution.py:619

commit v6 on v5

--- a/solution.py
+++ b/solution.py
@@ -93,25 +93,28 @@
         copy.wait()
 
 
-def pack_kernel(spatial, block, kind_ref, k_any, v_any, early_any, late_any, order, packed, sems):
-    put_order(kind_ref, order, spatial)
+def pack_kernel(spatial, block, kind_any, k_any, v_any, early_any, late_any, kind_ref, order, held, sems, in_sems):
     place = Place(block)
     across = pl.ds(pl.multiple_of(place.cross, block), 2 * block)
+    ins = [
+        pltpu.make_async_copy(ref.at[across, :], held.at[i], in_sems.at[i])
+        for i, ref in enumerate((k_any, v_any))
+    ]
+    kinds = pltpu.make_async_copy(kind_any, kind_ref, in_sems.at[2])
+    kinds.start()
+    start_all(ins)
+    kinds.wait()
+    put_order(kind_ref, order, spatial)
     early = early_any.shape[1]
-    each = [(h, i) for h in range(spatial) for i in range(2)]
-    ins = [
-        pltpu.make_async_copy(
-            column((k_any, v_any)[i], order[h], across), packed.at[i, h], sems.at[0, h, i]
-        )
-        for h, i in each
-    ]
-    start_all(ins)
     outs = []
-    for (h, i), came in zip(each, ins):
-        into = early_any.at[i, h] if h < early else late_any.at[i, h - early]
-        came.wait()
-        outs.append(pltpu.make_async_copy(packed.at[i, h], into, sems.at[1, h, i]))
-        outs[-1].start()
+    for i in range(2):
+        ins[i].wait()
+        for h in range(spatial):
+            into = early_any.at[i, h] if h < early else late_any.at[i, h - early]
+            outs.append(
+                pltpu.make_async_copy(held.at[i, :, lanes(order[h])], into, sems.at[i, h])
+            )
+            outs[-1].start()
     wait_all(outs)
 
 
@@ -120,19 +123,21 @@
         functools.partial(pack_kernel, spatial, block),
         "pack",
         [shape((2, n, 2 * block, HEAD_DIM)) for n in (spatial - late, late)],
-        [IN_SMEM] + [ANY] * 2,
+        [ANY] * 3,
         [ANY] * 2,
         [
+            pltpu.SMEM(head_kind.shape, jnp.int32),
             order_scratch(head_kind.shape[0]),
-            pltpu.VMEM((2, spatial, 2 * block, HEAD_DIM), BF16),
-            pltpu.SemaphoreType.DMA((2, spatial, 2)),
+            pltpu.VMEM((2, 2 * block, keys.shape[1]), BF16),
+            pltpu.SemaphoreType.DMA((2, spatial)),
+            pltpu.SemaphoreType.DMA((3,)),
         ],
         (head_kind, keys, values),
         vmem=VMEM_PACK,
     )
 
 
-def sums_kernel(spatial, dealt, kind_ref, q_ref, k_ref, v_ref, after_ref, sums_ref, *refs):
+def sums_kernel(spatial, dealt, kind_ref, q_ref, k_ref, v_ref, sums_ref, *refs):
     order, squares = refs[-2:]
     rows, width = q_ref.shape
     size = HEAD_DIM
@@ -151,7 +156,7 @@
             refs[0][i] = ref[:, one]
 
 
-def sums_call(head_kind, queries, keys, values, after, spatial, dealt):
+def sums_call(head_kind, queries, keys, values, spatial, dealt):
     rows, width = queries.shape
     outs = [shape((2, rows), F32)]
     if dealt:
@@ -160,10 +165,10 @@
         functools.partial(sums_kernel, spatial, dealt),
         "sums",
         outs,
-        [IN_SMEM] + [IN_VMEM] * 3 + [LOOSE],
+        [IN_SMEM] + [IN_VMEM] * 3,
         [IN_VMEM] * len(outs),
         [order_scratch(head_kind.shape[0]), pltpu.VMEM((rows, HEAD_DIM), F32)],
-        (head_kind, queries, keys, values, after),
+        (head_kind, queries, keys, values),
         vmem=VMEM_SUMS,
     )
 
@@ -375,8 +380,7 @@
 
 def rest_kernel(spatial, first, count, block, given, kind_ref, *refs):
     operands, refs = refs[:given], refs[given:]
-    near_ref, far_ref, _, out_ref, token_ref, order, factors, x_factors, x_keys, done, sems = refs
-    token_ref[...] = jnp.zeros_like(token_ref)
+    near_ref, far_ref, _, out_ref, order, factors, x_factors, x_keys, done, sems = refs
     put_order(kind_ref, order, spatial)
     place = Place(block)
     near_rows = pl.ds(pl.multiple_of(place.near, block), block)
@@ -389,16 +393,17 @@
         )
         copies[-1].start()
 
-    for h in range(spatial):
-        send(near_ref.at[h], order[h], near_rows)
-    for h in range(first):
-        send(far_ref.at[h], order[h], far_rows)
+    waiting = [(near_ref.at[h], order[h], near_rows) for h in range(spatial)]
+    waiting += [(far_ref.at[h], order[h], far_rows) for h in range(first)]
+    some = -(-len(waiting) // (2 * count - 1))
 
     def put(item, result):
         h, part = item
         done[h, part * block : (part + 1) * block, :] = result
         if part == 1:
             send(done.at[h], order[first + h], far_rows)
+        for _ in range(min(some, len(waiting))):
+            send(*waiting.pop(0))
 
     far_attention(first, count, block, place, order, operands + (factors, x_factors, x_keys), put)
     wait_all(copies)
@@ -410,9 +415,9 @@
     return call(
         functools.partial(rest_kernel, spatial, first, count, block, len(operands)),
         "rest",
-        [shape((rows, width)), shape((8, HEAD_DIM), F32)],
+        shape((rows, width)),
         [IN_SMEM] + [IN_VMEM] * (len(operands) + 2) + [LOOSE],
-        [ANY, IN_VMEM],
+        ANY,
         [
             order_scratch(heads),
             pltpu.VMEM((2 * block, HEAD_DIM), F32),
@@ -621,7 +626,7 @@
     late = LATE
     kv_near, kv_late = pack_call(head_kind, keys, values, spatial, late, block)
     kv_cross = send(kv_near, cross)
-    sums, *t_send = sums_call(head_kind, queries, keys, values, kv_late, spatial, dealt)
+    sums, *t_send = sums_call(head_kind, queries, keys, values, spatial, dealt)
     k_pair = send(lax.optimization_barrier((keys, kv_near))[0], pair)
     v_pair = send(lax.optimization_barrier((values, kv_near))[0], pair)
     t_got = [send(part, pair) for part in t_send]
@@ -661,11 +666,11 @@
         parts = [send(p, r) for p, r in zip(results[:0:-1], turned[::-1])]
         parts = [results[0]] + parts[::-1]
         last = results[0]
-    out, token = rest_call(
+    out = rest_call(
         head_kind, operands + (late_cross,), near, far, last, half, spatial - half, spatial, block
     )
     if dealt:
-        parts += [send(lax.optimization_barrier((p, token))[0], pair) for p in parts]
+        parts += [send(lax.optimization_barrier((p, out))[0], pair) for p in parts]
     else:
         index = lax.axis_index("seq").astype(jnp.int32)
         parts = temporal_folded(

time: 59.3 us -> 58.3 us (0.983)
  Pallas kernels: 24.9 us -> 23.7 us
  waiting for transfers between devices: 4.97 us -> 6.03 us
  local copies, waits for them, and re-layouts: 2.51 us -> 1.57 us
    pallas_call x10, Pallas kernels: 24.9 us -> 23.7 us  [call(): pl.pallas_call(kernel, out_shape=out_shape, in_specs=in_specs, out_specs=...]
    ppermute x16, waiting for transfers between devices: 0.97 us -> 2.04 us  [per_device(): send = lambda x, route: lax.ppermute(x, 'seq', route)]
    unnamed x16, local copies, waits for them, and re-layouts: 2.51 us -> 1.57 us
  transfers between devices with their start and end apart: 19 -> 19, of which waited for: 6 -> 7; matrix products, arithmetic and copies ran while one was open for 0% -> 0% of each run, Pallas kernels for 34% -> 33%
where the time goes in v6:
time: 58.3 us; the launch traced here: 58.1 us
  starting transfers between devices  26.4 us (45%)
  Pallas kernels  23.7 us (41%)
  waiting for transfers between devices  6.03 us (10%)
  local copies, waits for them, and re-layouts  1.57 us (3%)
    pallas_call x10, Pallas kernels, call(): pl.pallas_call(kernel, out_shape=out_shape, in_specs=in_specs, out_specs=...  23.7 us
    ppermute x16, starting transfers between devices, per_device(): send = lambda x, route: lax.ppermute(x, 'seq', route)  19.2 us
    ppermute x2, starting transfers between devices, per_device(): lax.ppermute(total, 'head', [(i, i ^ d) for i in range(planes)])  4.23 us
    ppermute x2, waiting for transfers between devices, per_device(): lax.ppermute(total, 'head', [(i, i ^ d) for i in range(planes)])  3.99 us
    ppermute x1, starting transfers between devices, per_device(): lax.ppermute(total, ('seq', 'head'), [(i * planes + p, j * planes + (p ^...  2.98 us
    ppermute x16, waiting for transfers between devices, per_device(): send = lambda x, route: lax.ppermute(x, 'seq', route)  2.04 us
    unnamed x16, local copies, waits for them, and re-layouts  1.57 us
  transfers between devices with their start and end apart: 19, of which 7 were waited for; matrix products, arithmetic and copies ran while one was open for 0% of the time, Pallas kernels for 33%

profile of v6, /device:TPU:0, one launch (start us, length us, event | category | flops | bytes accessed | tf_op | source)
XLA Modules:
  0.0 58.1 jit_solution(17233422839185741830)
XLA Ops:
  0.0 3.0 %pack.1 = (bf16[2,7,512,128]{3,2,1,0:T(8,128)(2,1)}, bf16[2,1,512,128]{3,2,1,0:T(8,128)(2,1)}) custom-call(s32[10]{0:T(128)} %kind_ref.15, bf16[768,1280]{1,0:T(8,128)(2,1)} %k_any.1, bf16[768,1280]{1,0:T(8,128)(2,1)} %refs_2_.3), custom_call_target="tpu_custom_call" | custom-call | flops 1000 | bytes 1000 | tf_op jit(solution)/shard_map/pack/pallas_call | solution.py:35
  3.0 0.5 collective-permute-start.7
  3.5 0.1 collective-permute-start.8
  3.6 5.5 %collective-permute-start.10 = (bf16[2,7,512,128]{3,2,1,0:T(8,128)(2,1)}, bf16[2,7,512,128]{3,2,1,0:T(8,128)(2,1)S(1)}, u32[]{:S(2)}, u32[]{:S(2)}) collective-permute-start(bf16[2,7,512,128]{3,2,1,0:T(8,128)(2,1)} %get-tuple-element.34), channel_id=1, source_target_pairs={{12,16},{16,12},{28,0},{0,28},{13,17},{17,13},{29,1},{1,29},{14,18... | collective-permute-start | bytes 5505032 | tf_op jit(solution)/shard_map/ppermute | solution.py:624
  9.1 0.0 copy-start.2
  9.1 1.5 %copy-done.2 = bf16[768,1280]{1,0:T(8,128)(2,1)S(1)} copy-done((bf16[768,1280]{1,0:T(8,128)(2,1)S(1)}, bf16[768,1280]{1,0:T(8,128)(2,1)}, u32[]{:S(2)}) %copy-start.2) | copy-done | bytes 1966104
  10.6 1.5 %sums.1 = (f32[2,768]{1,0:T(2,128)S(1)}, bf16[3,768,128]{2,1,0:T(8,128)(2,1)S(1)}) custom-call(s32[10]{0:T(128)S(1)} %copy-done.6, bf16[768,1280]{1,0:T(8,128)(2,1)S(1)} %copy-done.1, bf16[768,1280]{1,0:T(8,128)(2,1)S(1)} %copy-done.2, bf16[768,1280]{1,0:T(8,128)(2,1)S(1)} %copy-done), custom_call_target="tpu_custom_call" | custom-call | flops 1000 | bytes 1000 | tf_op jit(solution)/shard_map/sums/pallas_call | solution.py:35
  12.2 0.1 collective-permute-start.2
  12.2 1.6 %collective-permute-start = (f32[2,768]{1,0:T(2,128)S(1)}, f32[2,768]{1,0:T(2,128)S(1)}, u32[]{:S(2)}, u32[]{:S(2)}) collective-permute-start(f32[2,768]{1,0:T(2,128)S(1)} %get-tuple-element.26), channel_id=1, source_target_pairs={{0,1},{1,0},{2,3},{3,2},{4,5},{5,4},{6,7},{7,6},{8,9},{9,8},{10,11... | collective-permute-start | bytes 18440 | tf_op jit(solution)/shard_map/ppermute | solution.py:636
  13.9 2.1 %collective-permute-done = f32[2,768]{1,0:T(2,128)S(1)} collective-permute-done((f32[2,768]{1,0:T(2,128)S(1)}, f32[2,768]{1,0:T(2,128)S(1)}, u32[]{:S(2)}, u32[]{:S(2)}) %collective-permute-start) | collective-permute-done | bytes 6176 | tf_op jit(solution)/shard_map/ppermute | solution.py:636
  15.9 2.6 %collective-permute-start.1 = (f32[2,768]{1,0:T(2,128)S(1)}, f32[2,768]{1,0:T(2,128)S(1)}, u32[]{:S(2)}, u32[]{:S(2)}) collective-permute-start(f32[2,768]{1,0:T(2,128)S(1)} %add.6), channel_id=1, source_target_pairs={{0,2},{1,3},{2,0},{3,1},{4,6},{5,7},{6,4},{7,5},{8,10},{9,11},{10,... | collective-permute-start | bytes 18440 | tf_op jit(solution)/shard_map/ppermute | solution.py:636
  18.5 1.9 %collective-permute-done.1 = f32[2,768]{1,0:T(2,128)S(1)} collective-permute-done((f32[2,768]{1,0:T(2,128)S(1)}, f32[2,768]{1,0:T(2,128)S(1)}, u32[]{:S(2)}, u32[]{:S(2)}) %collective-permute-start.1) | collective-permute-done | bytes 6176 | tf_op jit(solution)/shard_map/ppermute | solution.py:636
  20.5 0.0 collective-permute-start.3
  20.5 0.0 collective-permute-done.2.refs_0_.got_ref
  20.5 1.3 %own.1 = (bf16[8,768,128]{2,1,0:T(8,128)(2,1)S(1)}, bf16[3,768,128]{2,1,0:T(8,128)(2,1)S(1)}) custom-call(s32[10]{0:T(128)S(1)} %copy-done.6, bf16[768,1280]{1,0:T(8,128)(2,1)S(1)} %copy-done.1, bf16[768,1280]{1,0:T(8,128)(2,1)S(1)} %copy-done.3, bf16[768,1280]{1,0:T(8,128)(2,1)S(1)} %copy-done, f32[1280]{0:T(1024)S(1)} %copy-done.5, f32[1280]{0:T(1024)S(1)} %copy-done.4, ...), custom_call_target="tpu_custom_call" | custom-call | flops 1000 | bytes 1000 | tf_op jit(solution)/shard_map/own/pallas_call | solution.py:35
  21.8 0.0 collective-permute-done.3.sums_ref
  21.8 1.0 %deal.1 = (bf16[3,3,128,128]{3,2,1,0:T(8,128)(2,1)S(1)}, bf16[3,3,128,128]{3,2,1,0:T(8,128)(2,1)S(1)}, bf16[3,3,128,128]{3,2,1,0:T(8,128)(2,1)S(1)}, bf16[3,3,128,128]{3,2,1,0:T(8,128)(2,1)S(1)}) custom-call(s32[10]{0:T(128)S(1)} %copy-done.6, bf16[3,768,128]{2,1,0:T(8,128)(2,1)S(1)} %get-tuple-element.28.own_ref, ...), custom_call_target="tpu_custom_call" | custom-call | flops 1000 | bytes 1000 | tf_op jit(solution)/shard_map/deal/pallas_call | solution.py:35
  22.9 0.9 %collective-permute-start.4 = (bf16[3,3,128,128]{3,2,1,0:T(8,128)(2,1)S(1)}, bf16[3,3,128,128]{3,2,1,0:T(8,128)(2,1)S(1)}, u32[]{:S(2)}, u32[]{:S(2)}) collective-permute-start(bf16[3,3,128,128]{3,2,1,0:T(8,128)(2,1)S(1)} %get-tuple-element.30), channel_id=1, source_target_pairs={{0,8},{4,12},{8,0},{12,4},{16,24},{20,28},{24,16},{28,20},{1,9},{5... | collective-permute-start | bytes 884744 | tf_op jit(solution)/shard_map/ppermute | solution.py:624
  23.8 0.2 collective-permute-start.5
  24.0 0.0 collective-permute-done.7.k_ref
  24.0 2.4 %collective-permute-start.6 = (bf16[3,3,128,128]{3,2,1,0:T(8,128)(2,1)S(1)}, bf16[3,3,128,128]{3,2,1,0:T(8,128)(2,1)S(1)}, u32[]{:S(2)}, u32[]{:S(2)}) collective-permute-start(bf16[3,3,128,128]{3,2,1,0:T(8,128)(2,1)S(1)} %get-tuple-element.32), channel_id=1, source_target_pairs={{0,24},{4,28},{8,16},{12,20},{16,8},{20,12},{24,0},{28,4},{1,25},{... | collective-permute-start | bytes 884744 | tf_op jit(solution)/shard_map/ppermute | solution.py:624
  26.4 0.0 collective-permute-done.8.v_pair_ref.refs_4_
  26.4 3.0 %collective-permute-start.9 = (f32[2,768]{1,0:T(2,128)S(1)}, f32[2,768]{1,0:T(2,128)S(1)}, u32[]{:S(2)}, u32[]{:S(2)}) collective-permute-start(f32[2,768]{1,0:T(2,128)S(1)} %add.7.total_ref.refs_7_), channel_id=1, source_target_pairs={{12,17},{13,16},{14,19},{15,18},{16,13},{17,12},{18,15},{19,14},{2... | collective-permute-start | bytes 18440 | tf_op jit(solution)/shard_map/ppermute | solution.py:640
  29.4 1.1 %pair.1.kp_ref.refs_3_ = bf16[8,768,128]{2,1,0:T(8,128)(2,1)S(1)} custom-call(s32[10]{0:T(128)S(1)} %copy-done.6, bf16[768,1280]{1,0:T(8,128)(2,1)S(1)} %collective-permute-done.7.k_ref, f32[1280]{0:T(1024)S(1)} %copy-done.4, f32[2,768]{1,0:T(2,128)S(1)} %collective-permute-done.3.sums_ref, bf16[3,3,128,128]{3,2,1,0:T(8,128)(2,1)S(1)} %get-tuple-element.29.after_ref.refs_0_), custom_call_target="tpu_custom_call" | custom-call | flops 1000 | bytes 1000 | tf_op jit(solution)/shard_map/pair/pallas_call | solution.py:35
  30.5 4.1 %near.1.refs_10_.refs_11_ = bf16[8,256,128]{2,1,0:T(8,128)(2,1)S(1)} custom-call(s32[10]{0:T(128)S(1)} %copy-done.6, bf16[768,1280]{1,0:T(8,128)(2,1)S(1)} %copy-done.1, bf16[8,768,128]{2,1,0:T(8,128)(2,1)S(1)} %get-tuple-element.33.k_ref.refs_1_, bf16[768,1280]{1,0:T(8,128)(2,1)S(1)} %copy-done, bf16[8,768,128]{2,1,0:T(8,128)(2,1)S(1)} %pair.1.kp_ref.refs_3_, ...), custom_call_target="tpu_custom_call" | custom-call | flops 1000 | bytes 1000 | tf_op jit(solution)/shard_map/near/pallas_call | solution.py:35
  34.6 0.0 collective-permute-done.9.refs_8_
  34.6 1.1 %collective-permute-done.10.refs_9_ = bf16[2,7,512,128]{3,2,1,0:T(8,128)(2,1)S(1)} collective-permute-done((bf16[2,7,512,128]{3,2,1,0:T(8,128)(2,1)}, bf16[2,7,512,128]{3,2,1,0:T(8,128)(2,1)S(1)}, u32[]{:S(2)}, u32[]{:S(2)}) %collective-permute-start.10) | collective-permute-done | bytes 1835040 | tf_op jit(solution)/shard_map/ppermute | solution.py:624
  35.7 3.8 %far.1.refs_4_.refs_12_ = bf16[4,512,128]{2,1,0:T(8,128)(2,1)S(1)} custom-call(s32[10]{0:T(128)S(1)} %copy-done.6, bf16[768,1280]{1,0:T(8,128)(2,1)S(1)} %copy-done.1, bf16[8,768,128]{2,1,0:T(8,128)(2,1)S(1)} %get-tuple-element.33.k_ref.refs_1_, bf16[768,1280]{1,0:T(8,128)(2,1)S(1)} %copy-done, bf16[8,768,128]{2,1,0:T(8,128)(2,1)S(1)} %pair.1.kp_ref.refs_3_, ...), custom_call_target="tpu_custom_call" | custom-call | flops 1000 | bytes 1000 | tf_op jit(solution)/shard_map/far/pallas_call | solution.py:35
  39.5 4.8 %collective-permute-start.14 = (bf16[2,1,512,128]{3,2,1,0:T(8,128)(2,1)S(1)}, bf16[2,1,512,128]{3,2,1,0:T(8,128)(2,1)S(1)}, u32[]{:S(2)}, u32[]{:S(2)}) collective-permute-start(bf16[2,1,512,128]{3,2,1,0:T(8,128)(2,1)S(1)} %copy-done.7), channel_id=1, source_target_pairs={{12,16},{16,12},{28,0},{0,28},{13,17},{17,13},{29,1},{1,29},{14,18... | collective-permute-start | bytes 786440 | tf_op jit(solution)/shard_map/ppermute | solution.py:624
  44.4 0.0 collective-permute-done.4.refs_1_
  44.4 0.0 collective-permute-done.5.refs_2_
  44.4 0.0 collective-permute-done.6.refs_3_
  44.4 1.8 %frames.1 = (bf16[3,128,128]{2,1,0:T(8,128)(2,1)S(1)}, bf16[3,128,128]{2,1,0:T(8,128)(2,1)S(1)}, bf16[3,128,128]{2,1,0:T(8,128)(2,1)S(1)}, bf16[3,128,128]{2,1,0:T(8,128)(2,1)S(1)}) custom-call(bf16[3,3,128,128]{3,2,1,0:T(8,128)(2,1)S(1)} %get-tuple-element.29.after_ref.refs_0_, bf16[3,3,128,128]{3,2,1,0:T(8,128)(2,1)S(1)} %collective-permute-done.4.refs_1_, ...), custom_call_target="tpu_custom_call" | custom-call | flops 10000000000 | bytes 1000 | tf_op jit(solution)/shard_map/frames/pallas_call | solution.py:35
  46.2 1.7 %collective-permute-start.13 = (bf16[3,128,128]{2,1,0:T(8,128)(2,1)S(1)}, bf16[3,128,128]{2,1,0:T(8,128)(2,1)S(1)}, u32[]{:S(2)}, u32[]{:S(2)}) collective-permute-start(bf16[3,128,128]{2,1,0:T(8,128)(2,1)S(1)} %get-tuple-element.40), channel_id=1, source_target_pairs={{0,24},{4,28},{8,16},{12,20},{16,8},{20,12},{24,0},{28,4},{1,25},{... | collective-permute-start | bytes 294920 | tf_op jit(solution)/shard_map/ppermute | solution.py:624
  48.0 1.1 %collective-permute-start.12 = (bf16[3,128,128]{2,1,0:T(8,128)(2,1)S(1)}, bf16[3,128,128]{2,1,0:T(8,128)(2,1)S(1)}, u32[]{:S(2)}, u32[]{:S(2)}) collective-permute-start(bf16[3,128,128]{2,1,0:T(8,128)(2,1)S(1)} %get-tuple-element.39), channel_id=1, source_target_pairs={{0,16},{4,20},{8,24},{12,28},{16,0},{20,4},{24,8},{28,12},{1,17},{... | collective-permute-start | bytes 294920 | tf_op jit(solution)/shard_map/ppermute | solution.py:624
  49.1 0.7 %collective-permute-start.11 = (bf16[3,128,128]{2,1,0:T(8,128)(2,1)S(1)}, bf16[3,128,128]{2,1,0:T(8,128)(2,1)S(1)}, u32[]{:S(2)}, u32[]{:S(2)}) collective-permute-start(bf16[3,128,128]{2,1,0:T(8,128)(2,1)S(1)} %get-tuple-element.38), channel_id=1, source_target_pairs={{0,8},{4,12},{8,0},{12,4},{16,24},{20,28},{24,16},{28,20},{1,9},{5... | collective-permute-start | bytes 294920 | tf_op jit(solution)/shard_map/ppermute | solution.py:624
  49.8 4.6 %rest.1.refs_8_ = bf16[768,1280]{1,0:T(8,128)(2,1)} custom-call(s32[10]{0:T(128)S(1)} %copy-done.6, bf16[768,1280]{1,0:T(8,128)(2,1)S(1)} %copy-done.1, bf16[8,768,128]{2,1,0:T(8,128)(2,1)S(1)} %get-tuple-element.33.k_ref.refs_1_, bf16[768,1280]{1,0:T(8,128)(2,1)S(1)} %copy-done, bf16[8,768,128]{2,1,0:T(8,128)(2,1)S(1)} %pair.1.kp_ref.refs_3_, ...), custom_call_target="tpu_custom_call" | custom-call | flops 1000 | bytes 1000 | tf_op jit(solution)/shard_map/rest/pallas_call | solution.py:35
  54.4 0.0 collective-permute-done.13.refs_3_
  54.5 0.0 collective-permute-done.11.refs_1_
  54.5 0.1 collective-permute-start.15
  54.6 0.5 collective-permute-start.16
  55.1 0.1 collective-permute-start.17
  55.1 0.4 collective-permute-start.18
  55.6 0.3 collective-permute-done.15.refs_4_
  55.8 0.2 collective-permute-done.16.refs_5_
  56.0 0.4 collective-permute-done.17.refs_6_
  56.4 0.2 collective-permute-done.18.refs_7_
  56.5 1.5 %place.1 = bf16[768,1280]{1,0:T(8,128)(2,1)} custom-call(s32[10]{0:T(128)S(1)} %copy-done.6, bf16[3,128,128]{2,1,0:T(8,128)(2,1)S(1)} %get-tuple-element.43.refs_13_.refs_0_, bf16[3,128,128]{2,1,0:T(8,128)(2,1)S(1)} %collective-permute-done.11.refs_1_, bf16[3,128,128]{2,1,0:T(8,128)(2,1)S(1)} %collective-permute-done.12.refs_2_, ...), custom_call_target="tpu_custom_call", output_to_operand_aliasing={{}: (9, {})} | custom-call | flops 1000 | bytes 1000 | tf_op jit(solution)/shard_map/place/pallas_call | solution.py:35
  (18 shorter events, 0.0 us)
Async XLA Ops:
  0.0 9.1 %copy-start.6 = (s32[10]{0:T(128)S(1)}, s32[10]{0:T(128)}, u32[]{:S(2)}) copy-start(s32[10]{0:T(128)} %kind_ref.15) | copy-start | bytes 124
  0.0 3.5 %copy-start = (bf16[768,1280]{1,0:T(8,128)(2,1)S(1)}, bf16[768,1280]{1,0:T(8,128)(2,1)}, u32[]{:S(2)}) copy-start(bf16[768,1280]{1,0:T(8,128)(2,1)} %refs_2_.3) | copy-start | bytes 5898244
  0.0 9.1 %copy-start.1 = (bf16[768,1280]{1,0:T(8,128)(2,1)S(1)}, bf16[768,1280]{1,0:T(8,128)(2,1)}, u32[]{:S(2)}) copy-start(bf16[768,1280]{1,0:T(8,128)(2,1)} %refs_0_.3) | copy-start | bytes 5898244
  3.0 21.0 %collective-permute-start.7 = (bf16[768,1280]{1,0:T(8,128)(2,1)}, bf16[768,1280]{1,0:T(8,128)(2,1)S(1)}, u32[]{:S(2)}, u32[]{:S(2)}) collective-permute-start(bf16[768,1280]{1,0:T(8,128)(2,1)} %k_any.1), channel_id=1, source_target_pairs={{0,4},{4,0},{8,12},{12,8},{16,20},{20,16},{24,28},{28,24},{1,5},{5... | collective-permute-start | bytes 5898248 | tf_op jit(solution)/shard_map/ppermute | solution.py:624
  3.5 22.9 %collective-permute-start.8 = (bf16[768,1280]{1,0:T(8,128)(2,1)S(1)}, bf16[768,1280]{1,0:T(8,128)(2,1)S(1)}, u32[]{:S(2)}, u32[]{:S(2)}) collective-permute-start(bf16[768,1280]{1,0:T(8,128)(2,1)S(1)} %copy-done), channel_id=1, source_target_pairs={{0,4},{4,0},{8,12},{12,8},{16,20},{20,16},{24,28},{28,24},{1,5},{5... | collective-permute-start | bytes 5898248 | tf_op jit(solution)/shard_map/ppermute | solution.py:624
  3.6 32.1 %collective-permute-start.10 = (bf16[2,7,512,128]{3,2,1,0:T(8,128)(2,1)}, bf16[2,7,512,128]{3,2,1,0:T(8,128)(2,1)S(1)}, u32[]{:S(2)}, u32[]{:S(2)}) collective-permute-start(bf16[2,7,512,128]{3,2,1,0:T(8,128)(2,1)} %get-tuple-element.34), channel_id=1, source_target_pairs={{12,16},{16,12},{28,0},{0,28},{13,17},{17,13},{29,1},{1,29},{14,18... | collective-permute-start | bytes 5505032 | tf_op jit(solution)/shard_map/ppermute | solution.py:624
  9.1 1.5 %copy-start.2 = (bf16[768,1280]{1,0:T(8,128)(2,1)S(1)}, bf16[768,1280]{1,0:T(8,128)(2,1)}, u32[]{:S(2)}) copy-start(bf16[768,1280]{1,0:T(8,128)(2,1)} %k_any.1) | copy-start | bytes 5898244
  10.6 9.9 %copy-start.3 = (bf16[768,1280]{1,0:T(8,128)(2,1)S(1)}, bf16[768,1280]{1,0:T(8,128)(2,1)}, u32[]{:S(2)}) copy-start(bf16[768,1280]{1,0:T(8,128)(2,1)} %k_any.1) | copy-start | bytes 5898244
  10.6 9.9 %copy-start.4 = (f32[1280]{0:T(1024)S(1)}, f32[1280]{0:T(1024)}, u32[]{:S(2)}) copy-start(f32[1280]{0:T(1024)} %refs_6_.3) | copy-start | bytes 15364
  10.6 9.9 %copy-start.5 = (f32[1280]{0:T(1024)S(1)}, f32[1280]{0:T(1024)}, u32[]{:S(2)}) copy-start(f32[1280]{0:T(1024)} %refs_5_.3) | copy-start | bytes 15364
  12.2 8.3 %collective-permute-start.2 = (bf16[3,768,128]{2,1,0:T(8,128)(2,1)S(1)}, bf16[3,768,128]{2,1,0:T(8,128)(2,1)S(1)}, u32[]{:S(2)}, u32[]{:S(2)}) collective-permute-start(bf16[3,768,128]{2,1,0:T(8,128)(2,1)S(1)} %get-tuple-element.27), channel_id=1, source_target_pairs={{0,4},{4,0},{8,12},{12,8},{16,20},{20,16},{24,28},{28,24},{1,5},{5... | collective-permute-start | bytes 1769480 | tf_op jit(solution)/shard_map/ppermute | solution.py:624
  12.2 3.7 %collective-permute-start = (f32[2,768]{1,0:T(2,128)S(1)}, f32[2,768]{1,0:T(2,128)S(1)}, u32[]{:S(2)}, u32[]{:S(2)}) collective-permute-start(f32[2,768]{1,0:T(2,128)S(1)} %get-tuple-element.26), channel_id=1, source_target_pairs={{0,1},{1,0},{2,3},{3,2},{4,5},{5,4},{6,7},{7,6},{8,9},{9,8},{10,11... | collective-permute-start | bytes 18440 | tf_op jit(solution)/shard_map/ppermute | solution.py:636
  15.9 4.5 %collective-permute-start.1 = (f32[2,768]{1,0:T(2,128)S(1)}, f32[2,768]{1,0:T(2,128)S(1)}, u32[]{:S(2)}, u32[]{:S(2)}) collective-permute-start(f32[2,768]{1,0:T(2,128)S(1)} %add.6), channel_id=1, source_target_pairs={{0,2},{1,3},{2,0},{3,1},{4,6},{5,7},{6,4},{7,5},{8,10},{9,11},{10,... | collective-permute-start | bytes 18440 | tf_op jit(solution)/shard_map/ppermute | solution.py:636
  20.5 1.3 %collective-permute-start.3 = (f32[2,768]{1,0:T(2,128)S(1)}, f32[2,768]{1,0:T(2,128)S(1)}, u32[]{:S(2)}, u32[]{:S(2)}) collective-permute-start(f32[2,768]{1,0:T(2,128)S(1)} %add.7.total_ref.refs_7_), channel_id=1, source_target_pairs={{0,4},{4,0},{8,12},{12,8},{16,20},{20,16},{24,28},{28,24},{1,5},{5... | collective-permute-start | bytes 18440 | tf_op jit(solution)/shard_map/ppermute | solution.py:624
  22.9 21.5 %collective-permute-start.4 = (bf16[3,3,128,128]{3,2,1,0:T(8,128)(2,1)S(1)}, bf16[3,3,128,128]{3,2,1,0:T(8,128)(2,1)S(1)}, u32[]{:S(2)}, u32[]{:S(2)}) collective-permute-start(bf16[3,3,128,128]{3,2,1,0:T(8,128)(2,1)S(1)} %get-tuple-element.30), channel_id=1, source_target_pairs={{0,8},{4,12},{8,0},{12,4},{16,24},{20,28},{24,16},{28,20},{1,9},{5... | collective-permute-start | bytes 884744 | tf_op jit(solution)/shard_map/ppermute | solution.py:624
  23.8 20.6 %collective-permute-start.5 = (bf16[3,3,128,128]{3,2,1,0:T(8,128)(2,1)S(1)}, bf16[3,3,128,128]{3,2,1,0:T(8,128)(2,1)S(1)}, u32[]{:S(2)}, u32[]{:S(2)}) collective-permute-start(bf16[3,3,128,128]{3,2,1,0:T(8,128)(2,1)S(1)} %get-tuple-element.31), channel_id=1, source_target_pairs={{0,16},{4,20},{8,24},{12,28},{16,0},{20,4},{24,8},{28,12},{1,17},{... | collective-permute-start | bytes 884744 | tf_op jit(solution)/shard_map/ppermute | solution.py:624
  24.0 20.4 %collective-permute-start.6 = (bf16[3,3,128,128]{3,2,1,0:T(8,128)(2,1)S(1)}, bf16[3,3,128,128]{3,2,1,0:T(8,128)(2,1)S(1)}, u32[]{:S(2)}, u32[]{:S(2)}) collective-permute-start(bf16[3,3,128,128]{3,2,1,0:T(8,128)(2,1)S(1)} %get-tuple-element.32), channel_id=1, source_target_pairs={{0,24},{4,28},{8,16},{12,20},{16,8},{20,12},{24,0},{28,4},{1,25},{... | collective-permute-start | bytes 884744 | tf_op jit(solution)/shard_map/ppermute | solution.py:624
  26.4 8.2 %collective-permute-start.9 = (f32[2,768]{1,0:T(2,128)S(1)}, f32[2,768]{1,0:T(2,128)S(1)}, u32[]{:S(2)}, u32[]{:S(2)}) collective-permute-start(f32[2,768]{1,0:T(2,128)S(1)} %add.7.total_ref.refs_7_), channel_id=1, source_target_pairs={{12,17},{13,16},{14,19},{15,18},{16,13},{17,12},{18,15},{19,14},{2... | collective-permute-start | bytes 18440 | tf_op jit(solution)/shard_map/ppermute | solution.py:640
  34.6 4.9 %copy-start.7 = (bf16[2,1,512,128]{3,2,1,0:T(8,128)(2,1)S(1)}, bf16[2,1,512,128]{3,2,1,0:T(8,128)(2,1)}, u32[]{:S(2)}) copy-start(bf16[2,1,512,128]{3,2,1,0:T(8,128)(2,1)} %get-tuple-element.42) | copy-start | bytes 786436
  39.5 10.3 %collective-permute-start.14 = (bf16[2,1,512,128]{3,2,1,0:T(8,128)(2,1)S(1)}, bf16[2,1,512,128]{3,2,1,0:T(8,128)(2,1)S(1)}, u32[]{:S(2)}, u32[]{:S(2)}) collective-permute-start(bf16[2,1,512,128]{3,2,1,0:T(8,128)(2,1)S(1)} %copy-done.7), channel_id=1, source_target_pairs={{12,16},{16,12},{28,0},{0,28},{13,17},{17,13},{29,1},{1,29},{14,18... | collective-permute-start | bytes 786440 | tf_op jit(solution)/shard_map/ppermute | solution.py:624
  46.2 8.2 %collective-permute-start.13 = (bf16[3,128,128]{2,1,0:T(8,128)(2,1)S(1)}, bf16[3,128,128]{2,1,0:T(8,128)(2,1)S(1)}, u32[]{:S(2)}, u32[]{:S(2)}) collective-permute-start(bf16[3,128,128]{2,1,0:T(8,128)(2,1)S(1)} %get-tuple-element.40), channel_id=1, source_target_pairs={{0,24},{4,28},{8,16},{12,20},{16,8},{20,12},{24,0},{28,4},{1,25},{... | collective-permute-start | bytes 294920 | tf_op jit(solution)/shard_map/ppermute | solution.py:624
  48.0 6.5 %collective-permute-start.12 = (bf16[3,128,128]{2,1,0:T(8,128)(2,1)S(1)}, bf16[3,128,128]{2,1,0:T(8,128)(2,1)S(1)}, u32[]{:S(2)}, u32[]{:S(2)}) collective-permute-start(bf16[3,128,128]{2,1,0:T(8,128)(2,1)S(1)} %get-tuple-element.39), channel_id=1, source_target_pairs={{0,16},{4,20},{8,24},{12,28},{16,0},{20,4},{24,8},{28,12},{1,17},{... | collective-permute-start | bytes 294920 | tf_op jit(solution)/shard_map/ppermute | solution.py:624
  49.1 5.4 %collective-permute-start.11 = (bf16[3,128,128]{2,1,0:T(8,128)(2,1)S(1)}, bf16[3,128,128]{2,1,0:T(8,128)(2,1)S(1)}, u32[]{:S(2)}, u32[]{:S(2)}) collective-permute-start(bf16[3,128,128]{2,1,0:T(8,128)(2,1)S(1)} %get-tuple-element.38), channel_id=1, source_target_pairs={{0,8},{4,12},{8,0},{12,4},{16,24},{20,28},{24,16},{28,20},{1,9},{5... | collective-permute-start | bytes 294920 | tf_op jit(solution)/shard_map/ppermute | solution.py:624
  54.5 1.4 %collective-permute-start.15 = (bf16[3,128,128]{2,1,0:T(8,128)(2,1)S(1)}, bf16[3,128,128]{2,1,0:T(8,128)(2,1)S(1)}, u32[]{:S(2)}, u32[]{:S(2)}) collective-permute-start(bf16[3,128,128]{2,1,0:T(8,128)(2,1)S(1)} %get-tuple-element.43.refs_13_.refs_0_), channel_id=1, source_target_pairs={{0,4},{4,0},{8,12},{12,8},{16,20},{20,16},{24,28},{28,24},{1,5},{5... | collective-permute-start | bytes 294920 | tf_op jit(solution)/shard_map/ppermute | solution.py:624
  54.6 1.4 %collective-permute-start.16 = (bf16[3,128,128]{2,1,0:T(8,128)(2,1)S(1)}, bf16[3,128,128]{2,1,0:T(8,128)(2,1)S(1)}, u32[]{:S(2)}, u32[]{:S(2)}) collective-permute-start(bf16[3,128,128]{2,1,0:T(8,128)(2,1)S(1)} %collective-permute-done.11.refs_1_), channel_id=1, source_target_pairs={{0,4},{4,0},{8,12},{12,8},{16,20},{20,16},{24,28},{28,24},{1,5},{5... | collective-permute-start | bytes 294920 | tf_op jit(solution)/shard_map/ppermute | solution.py:624
  55.1 1.3 %collective-permute-start.17 = (bf16[3,128,128]{2,1,0:T(8,128)(2,1)S(1)}, bf16[3,128,128]{2,1,0:T(8,128)(2,1)S(1)}, u32[]{:S(2)}, u32[]{:S(2)}) collective-permute-start(bf16[3,128,128]{2,1,0:T(8,128)(2,1)S(1)} %collective-permute-done.12.refs_2_), channel_id=1, source_target_pairs={{0,4},{4,0},{8,12},{12,8},{16,20},{20,16},{24,28},{28,24},{1,5},{5... | collective-permute-start | bytes 294920 | tf_op jit(solution)/shard_map/ppermute | solution.py:624
  55.1 1.4 %collective-permute-start.18 = (bf16[3,128,128]{2,1,0:T(8,128)(2,1)S(1)}, bf16[3,128,128]{2,1,0:T(8,128)(2,1)S(1)}, u32[]{:S(2)}, u32[]{:S(2)}) collective-permute-start(bf16[3,128,128]{2,1,0:T(8,128)(2,1)S(1)} %collective-permute-done.13.refs_3_), channel_id=1, source_target_pairs={{0,4},{4,0},{8,12},{12,8},{16,20},{20,16},{24,28},{28,24},{1,5},{5... | collective-permute-start | bytes 294920 | tf_op jit(solution)/shard_map/ppermute | solution.py:624

commit v7 on v6

--- a/solution.py
+++ b/solution.py
@@ -16,7 +16,7 @@
 VMEM_PACK = 58 * 1024 * 1024
 VMEM_SUMS = 32 * 1024 * 1024
 LOW = -1e30
-LATE = 1
+LATE = 4
 FRAMES_COST = 10000000000
 FACTOR = math.log2(math.e) / math.sqrt(HEAD_DIM)
 F32 = jnp.float32
@@ -137,19 +137,27 @@
     )
 
 
-def sums_kernel(spatial, dealt, kind_ref, q_ref, k_ref, v_ref, sums_ref, *refs):
+def row_sums(ref, squares):
+    rows, width = ref.shape
+    size = HEAD_DIM
+    for s in range(rows // size):
+        total = None
+        for c in range(width // HEAD_DIM):
+            x = ref[s * size : (s + 1) * size, c * HEAD_DIM : (c + 1) * HEAD_DIM].astype(F32)
+            total = x * x if total is None else total + x * x
+        squares[s * size : (s + 1) * size, :] = total
+    return jnp.sum(jnp.transpose(squares[...]), axis=0, keepdims=True)
+
+
+def key_sums_kernel(k_ref, sums_ref, squares):
+    sums_ref[...] = row_sums(k_ref, squares)
+
+
+def sums_kernel(spatial, dealt, kind_ref, q_ref, k_ref, v_ref, key_sums_ref, sums_ref, *refs):
     order, squares = refs[-2:]
-    rows, width = q_ref.shape
-    size = HEAD_DIM
-    put_order(kind_ref, order, spatial)
-    for i, ref in enumerate((q_ref, k_ref)):
-        for s in range(rows // size):
-            total = None
-            for c in range(width // HEAD_DIM):
-                x = ref[s * size : (s + 1) * size, c * HEAD_DIM : (c + 1) * HEAD_DIM].astype(F32)
-                total = x * x if total is None else total + x * x
-            squares[s * size : (s + 1) * size, :] = total
-        sums_ref[i : i + 1, :] = jnp.sum(jnp.transpose(squares[...]), axis=0, keepdims=True)
+    put_order(kind_ref, order, spatial)
+    sums_ref[0:1, :] = row_sums(q_ref, squares)
+    sums_ref[1:2, :] = key_sums_ref[...]
     if dealt:
         one = lanes(order[spatial + 1 - Place().core])
         for i, ref in enumerate((q_ref, k_ref, v_ref)):
@@ -158,6 +166,16 @@
 
 def sums_call(head_kind, queries, keys, values, spatial, dealt):
     rows, width = queries.shape
+    key_sums = call(
+        key_sums_kernel,
+        "key_sums",
+        shape((1, rows), F32),
+        [IN_VMEM],
+        IN_VMEM,
+        [pltpu.VMEM((rows, HEAD_DIM), F32)],
+        (keys,),
+        vmem=VMEM_SUMS,
+    )
     outs = [shape((2, rows), F32)]
     if dealt:
         outs.append(shape((3, rows, HEAD_DIM)))
@@ -165,10 +183,10 @@
         functools.partial(sums_kernel, spatial, dealt),
         "sums",
         outs,
-        [IN_SMEM] + [IN_VMEM] * 3,
+        [IN_SMEM] + [IN_VMEM] * 4,
         [IN_VMEM] * len(outs),
         [order_scratch(head_kind.shape[0]), pltpu.VMEM((rows, HEAD_DIM), F32)],
-        (head_kind, queries, keys, values),
+        (head_kind, queries, keys, values, key_sums),
         vmem=VMEM_SUMS,
     )
 
@@ -380,7 +398,7 @@
 
 def rest_kernel(spatial, first, count, block, given, kind_ref, *refs):
     operands, refs = refs[:given], refs[given:]
-    near_ref, far_ref, _, out_ref, order, factors, x_factors, x_keys, done, sems = refs
+    near_ref, far_ref, mid_ref, out_ref, order, factors, x_factors, x_keys, done, sems = refs
     put_order(kind_ref, order, spatial)
     place = Place(block)
     near_rows = pl.ds(pl.multiple_of(place.near, block), block)
@@ -394,7 +412,8 @@
         copies[-1].start()
 
     waiting = [(near_ref.at[h], order[h], near_rows) for h in range(spatial)]
-    waiting += [(far_ref.at[h], order[h], far_rows) for h in range(first)]
+    for at, ref in ((0, far_ref), (far_ref.shape[0], mid_ref)):
+        waiting += [(ref.at[h], order[at + h], far_rows) for h in range(ref.shape[0])]
     some = -(-len(waiting) // (2 * count - 1))
 
     def put(item, result):
@@ -409,14 +428,14 @@
     wait_all(copies)
 
 
-def rest_call(head_kind, operands, near, far, after, first, count, spatial, block):
+def rest_call(head_kind, operands, near, far, mid, first, count, spatial, block):
     rows, width = operands[0].shape
     heads = head_kind.shape[0]
     return call(
         functools.partial(rest_kernel, spatial, first, count, block, len(operands)),
         "rest",
         shape((rows, width)),
-        [IN_SMEM] + [IN_VMEM] * (len(operands) + 2) + [LOOSE],
+        [IN_SMEM] + [IN_VMEM] * (len(operands) + 3),
         ANY,
         [
             order_scratch(heads),
@@ -426,7 +445,7 @@
             pltpu.VMEM((count, 2 * block, HEAD_DIM), BF16),
             pltpu.SemaphoreType.DMA((2 * spatial,)),
         ],
-        (head_kind, *operands, near, far, after),
+        (head_kind, *operands, near, far, mid),
     )
 
 
@@ -623,7 +642,7 @@
     turned = [[(i, i ^ (2 * turn)) for i in range(devices)] for turn in range(1, CHIPS)]
     send = lambda x, route: lax.ppermute(x, "seq", route)
 
-    late = LATE
+    late = spatial // LATE
     kv_near, kv_late = pack_call(head_kind, keys, values, spatial, late, block)
     kv_cross = send(kv_near, cross)
     sums, *t_send = sums_call(head_kind, queries, keys, values, spatial, dealt)
@@ -666,11 +685,14 @@
         parts = [send(p, r) for p, r in zip(results[:0:-1], turned[::-1])]
         parts = [results[0]] + parts[::-1]
         last = results[0]
+    mid = far_call(head_kind, operands, last, half, half - late, spatial, block)
     out = rest_call(
-        head_kind, operands + (late_cross,), near, far, last, half, spatial - half, spatial, block
+        head_kind, operands + (late_cross,), near, far, mid, spatial - late, late, spatial, block
     )
     if dealt:
-        parts += [send(lax.optimization_barrier((p, out))[0], pair) for p in parts]
+        parts += [send(parts[0], pair)] + [
+            send(lax.optimization_barrier((p, out))[0], pair) for p in parts[1:]
+        ]
     else:
         index = lax.axis_index("seq").astype(jnp.int32)
         parts = temporal_folded(

time: 58.3 us -> 58 us (level)
  Pallas kernels: 23.7 us -> 25.2 us
  local copies, waits for them, and re-layouts: 1.57 us -> 0.16 us
    pallas_call x10 -> x12, Pallas kernels: 23.7 us -> 25.2 us  [call(): pl.pallas_call(kernel, out_shape=out_shape, in_specs=in_specs, out_specs=...]
    unnamed x16 -> x14, local copies, waits for them, and re-layouts: 1.57 us -> 0.16 us
  transfers between devices with their start and end apart: 19 -> 19, of which waited for: 7 -> 6; matrix products, arithmetic and copies ran while one was open for 0% -> 0% of each run, Pallas kernels for 33% -> 36%
where the time goes in v7:
time: 58 us; the launch traced here: 57.9 us
  starting transfers between devices  26.1 us (45%)
  Pallas kernels  25.2 us (43%)
  waiting for transfers between devices  5.96 us (10%)
    pallas_call x12, Pallas kernels, call(): pl.pallas_call(kernel, out_shape=out_shape, in_specs=in_specs, out_specs=...  25.2 us
    ppermute x16, starting transfers between devices, per_device(): send = lambda x, route: lax.ppermute(x, 'seq', route)  19.3 us
    ppermute x2, starting transfers between devices, per_device(): lax.ppermute(total, 'head', [(i, i ^ d) for i in range(planes)])  4.23 us
    ppermute x2, waiting for transfers between devices, per_device(): lax.ppermute(total, 'head', [(i, i ^ d) for i in range(planes)])  3.99 us
    ppermute x1, starting transfers between devices, per_device(): lax.ppermute(total, ('seq', 'head'), [(i * planes + p, j * planes + (p ^...  2.56 us
    ppermute x16, waiting for transfers between devices, per_device(): send = lambda x, route: lax.ppermute(x, 'seq', route)  1.96 us
  transfers between devices with their start and end apart: 19, of which 6 were waited for; matrix products, arithmetic and copies ran while one was open for 0% of the time, Pallas kernels for 36%

profile of v7, /device:TPU:0, one launch (start us, length us, event | category | flops | bytes accessed | tf_op | source)
XLA Modules:
  0.0 57.9 jit_solution(10605323432241977412)
XLA Ops:
  0.0 3.0 %pack.1 = (bf16[2,6,512,128]{3,2,1,0:T(8,128)(2,1)}, bf16[2,2,512,128]{3,2,1,0:T(8,128)(2,1)}) custom-call(s32[10]{0:T(128)} %kind_ref.17, bf16[768,1280]{1,0:T(8,128)(2,1)} %k_any.1, bf16[768,1280]{1,0:T(8,128)(2,1)} %refs_2_.5), custom_call_target="tpu_custom_call" | custom-call | flops 1000 | bytes 1000 | tf_op jit(solution)/shard_map/pack/pallas_call | solution.py:35
  3.0 0.0 copy-start.1
  3.0 0.0 copy-start.5
  3.0 0.5 collective-permute-start.7
  3.5 0.1 copy-done
  3.7 0.5 collective-permute-start.8
  4.1 5.5 %collective-permute-start.10 = (bf16[2,6,512,128]{3,2,1,0:T(8,128)(2,1)}, bf16[2,6,512,128]{3,2,1,0:T(8,128)(2,1)S(1)}, u32[]{:S(2)}, u32[]{:S(2)}) collective-permute-start(bf16[2,6,512,128]{3,2,1,0:T(8,128)(2,1)} %get-tuple-element.33), channel_id=1, source_target_pairs={{12,16},{16,12},{28,0},{0,28},{13,17},{17,13},{29,1},{1,29},{14,18... | collective-permute-start | bytes 4718600 | tf_op jit(solution)/shard_map/ppermute | solution.py:643
  9.6 0.5 key_sums.1.key_sums_ref
  10.1 0.0 copy-start.3
  10.1 0.0 copy-start.4
  10.1 1.1 %sums.1 = (f32[2,768]{1,0:T(2,128)S(1)}, bf16[3,768,128]{2,1,0:T(8,128)(2,1)S(1)}) custom-call(s32[10]{0:T(128)S(1)} %copy-done.5, bf16[768,1280]{1,0:T(8,128)(2,1)S(1)} %copy-done.1, bf16[768,1280]{1,0:T(8,128)(2,1)S(1)} %copy-done.2, bf16[768,1280]{1,0:T(8,128)(2,1)S(1)} %copy-done, f32[1,768]{1,0:T(1,128)S(1)} %key_sums.1.key_sums_ref), custom_call_target="tpu_custom_call" | custom-call | flops 1000 | bytes 1000 | tf_op jit(solution)/shard_map/sums/pallas_call | solution.py:35
  11.2 0.1 collective-permute-start.2
  11.3 1.6 %collective-permute-start = (f32[2,768]{1,0:T(2,128)S(1)}, f32[2,768]{1,0:T(2,128)S(1)}, u32[]{:S(2)}, u32[]{:S(2)}) collective-permute-start(f32[2,768]{1,0:T(2,128)S(1)} %get-tuple-element.25), channel_id=1, source_target_pairs={{0,1},{1,0},{2,3},{3,2},{4,5},{5,4},{6,7},{7,6},{8,9},{9,8},{10,11... | collective-permute-start | bytes 18440 | tf_op jit(solution)/shard_map/ppermute | solution.py:655
  12.9 2.1 %collective-permute-done = f32[2,768]{1,0:T(2,128)S(1)} collective-permute-done((f32[2,768]{1,0:T(2,128)S(1)}, f32[2,768]{1,0:T(2,128)S(1)}, u32[]{:S(2)}, u32[]{:S(2)}) %collective-permute-start) | collective-permute-done | bytes 6176 | tf_op jit(solution)/shard_map/ppermute | solution.py:655
  15.0 2.6 %collective-permute-start.1 = (f32[2,768]{1,0:T(2,128)S(1)}, f32[2,768]{1,0:T(2,128)S(1)}, u32[]{:S(2)}, u32[]{:S(2)}) collective-permute-start(f32[2,768]{1,0:T(2,128)S(1)} %add.6), channel_id=1, source_target_pairs={{0,2},{1,3},{2,0},{3,1},{4,6},{5,7},{6,4},{7,5},{8,10},{9,11},{10,... | collective-permute-start | bytes 18440 | tf_op jit(solution)/shard_map/ppermute | solution.py:655
  17.6 1.9 %collective-permute-done.1 = f32[2,768]{1,0:T(2,128)S(1)} collective-permute-done((f32[2,768]{1,0:T(2,128)S(1)}, f32[2,768]{1,0:T(2,128)S(1)}, u32[]{:S(2)}, u32[]{:S(2)}) %collective-permute-start.1) | collective-permute-done | bytes 6176 | tf_op jit(solution)/shard_map/ppermute | solution.py:655
  19.5 0.0 collective-permute-start.3
  19.6 1.3 %own.1 = (bf16[8,768,128]{2,1,0:T(8,128)(2,1)S(1)}, bf16[3,768,128]{2,1,0:T(8,128)(2,1)S(1)}) custom-call(s32[10]{0:T(128)S(1)} %copy-done.5, bf16[768,1280]{1,0:T(8,128)(2,1)S(1)} %copy-done.1, bf16[768,1280]{1,0:T(8,128)(2,1)S(1)} %copy-done.2, bf16[768,1280]{1,0:T(8,128)(2,1)S(1)} %copy-done, f32[1280]{0:T(1024)S(1)} %copy-done.4, f32[1280]{0:T(1024)S(1)} %copy-done.3, ...), custom_call_target="tpu_custom_call" | custom-call | flops 1000 | bytes 1000 | tf_op jit(solution)/shard_map/own/pallas_call | solution.py:35
  20.9 0.0 collective-permute-done.3.sums_ref
  20.9 1.0 %deal.1 = (bf16[3,3,128,128]{3,2,1,0:T(8,128)(2,1)S(1)}, bf16[3,3,128,128]{3,2,1,0:T(8,128)(2,1)S(1)}, bf16[3,3,128,128]{3,2,1,0:T(8,128)(2,1)S(1)}, bf16[3,3,128,128]{3,2,1,0:T(8,128)(2,1)S(1)}) custom-call(s32[10]{0:T(128)S(1)} %copy-done.5, bf16[3,768,128]{2,1,0:T(8,128)(2,1)S(1)} %get-tuple-element.27.own_ref, ...), custom_call_target="tpu_custom_call" | custom-call | flops 1000 | bytes 1000 | tf_op jit(solution)/shard_map/deal/pallas_call | solution.py:35
  21.9 0.5 collective-permute-start.4
  22.4 0.4 collective-permute-start.5
  22.9 0.0 collective-permute-done.7.k_ref
  22.9 2.6 %collective-permute-start.6 = (bf16[3,3,128,128]{3,2,1,0:T(8,128)(2,1)S(1)}, bf16[3,3,128,128]{3,2,1,0:T(8,128)(2,1)S(1)}, u32[]{:S(2)}, u32[]{:S(2)}) collective-permute-start(bf16[3,3,128,128]{3,2,1,0:T(8,128)(2,1)S(1)} %get-tuple-element.31), channel_id=1, source_target_pairs={{0,24},{4,28},{8,16},{12,20},{16,8},{20,12},{24,0},{28,4},{1,25},{... | collective-permute-start | bytes 884744 | tf_op jit(solution)/shard_map/ppermute | solution.py:643
  25.5 2.6 %collective-permute-start.9 = (f32[2,768]{1,0:T(2,128)S(1)}, f32[2,768]{1,0:T(2,128)S(1)}, u32[]{:S(2)}, u32[]{:S(2)}) collective-permute-start(f32[2,768]{1,0:T(2,128)S(1)} %add.7.total_ref.refs_7_), channel_id=1, source_target_pairs={{12,17},{13,16},{14,19},{15,18},{16,13},{17,12},{18,15},{19,14},{2... | collective-permute-start | bytes 18440 | tf_op jit(solution)/shard_map/ppermute | solution.py:659
  28.0 1.1 %pair.1.kp_ref.refs_3_ = bf16[8,768,128]{2,1,0:T(8,128)(2,1)S(1)} custom-call(s32[10]{0:T(128)S(1)} %copy-done.5, bf16[768,1280]{1,0:T(8,128)(2,1)S(1)} %collective-permute-done.7.k_ref, f32[1280]{0:T(1024)S(1)} %copy-done.3, f32[2,768]{1,0:T(2,128)S(1)} %collective-permute-done.3.sums_ref, bf16[3,3,128,128]{3,2,1,0:T(8,128)(2,1)S(1)} %get-tuple-element.28.after_ref.refs_0_), custom_call_target="tpu_custom_call" | custom-call | flops 1000 | bytes 1000 | tf_op jit(solution)/shard_map/pair/pallas_call | solution.py:35
  29.2 4.1 %near.1.refs_10_.refs_11_ = bf16[8,256,128]{2,1,0:T(8,128)(2,1)S(1)} custom-call(s32[10]{0:T(128)S(1)} %copy-done.5, bf16[768,1280]{1,0:T(8,128)(2,1)S(1)} %copy-done.1, bf16[8,768,128]{2,1,0:T(8,128)(2,1)S(1)} %get-tuple-element.32.k_ref.refs_1_, bf16[768,1280]{1,0:T(8,128)(2,1)S(1)} %copy-done, bf16[8,768,128]{2,1,0:T(8,128)(2,1)S(1)} %pair.1.kp_ref.refs_3_, ...), custom_call_target="tpu_custom_call" | custom-call | flops 1000 | bytes 1000 | tf_op jit(solution)/shard_map/near/pallas_call | solution.py:35
  33.3 0.0 collective-permute-done.9.refs_8_
  33.3 3.8 %far.2.refs_4_.refs_12_ = bf16[4,512,128]{2,1,0:T(8,128)(2,1)S(1)} custom-call(s32[10]{0:T(128)S(1)} %copy-done.5, bf16[768,1280]{1,0:T(8,128)(2,1)S(1)} %copy-done.1, bf16[8,768,128]{2,1,0:T(8,128)(2,1)S(1)} %get-tuple-element.32.k_ref.refs_1_, bf16[768,1280]{1,0:T(8,128)(2,1)S(1)} %copy-done, bf16[8,768,128]{2,1,0:T(8,128)(2,1)S(1)} %pair.1.kp_ref.refs_3_, ...), custom_call_target="tpu_custom_call" | custom-call | flops 1000 | bytes 1000 | tf_op jit(solution)/shard_map/far/pallas_call | solution.py:35
  37.1 5.1 %collective-permute-start.15 = (bf16[2,2,512,128]{3,2,1,0:T(8,128)(2,1)S(1)}, bf16[2,2,512,128]{3,2,1,0:T(8,128)(2,1)S(1)}, u32[]{:S(2)}, u32[]{:S(2)}) collective-permute-start(bf16[2,2,512,128]{3,2,1,0:T(8,128)(2,1)S(1)} %copy-done.6), channel_id=1, source_target_pairs={{12,16},{16,12},{28,0},{0,28},{13,17},{17,13},{29,1},{1,29},{14,18... | collective-permute-start | bytes 1572872 | tf_op jit(solution)/shard_map/ppermute | solution.py:643
  42.2 0.0 collective-permute-done.5.refs_2_
  42.2 0.0 collective-permute-done.6.refs_3_
  42.2 1.8 %frames.1 = (bf16[3,128,128]{2,1,0:T(8,128)(2,1)S(1)}, bf16[3,128,128]{2,1,0:T(8,128)(2,1)S(1)}, bf16[3,128,128]{2,1,0:T(8,128)(2,1)S(1)}, bf16[3,128,128]{2,1,0:T(8,128)(2,1)S(1)}) custom-call(bf16[3,3,128,128]{3,2,1,0:T(8,128)(2,1)S(1)} %get-tuple-element.28.after_ref.refs_0_, bf16[3,3,128,128]{3,2,1,0:T(8,128)(2,1)S(1)} %collective-permute-done.4.refs_1_, ...), custom_call_target="tpu_custom_call" | custom-call | flops 10000000000 | bytes 1000 | tf_op jit(solution)/shard_map/frames/pallas_call | solution.py:35
  44.1 1.8 %collective-permute-start.13 = (bf16[3,128,128]{2,1,0:T(8,128)(2,1)S(1)}, bf16[3,128,128]{2,1,0:T(8,128)(2,1)S(1)}, u32[]{:S(2)}, u32[]{:S(2)}) collective-permute-start(bf16[3,128,128]{2,1,0:T(8,128)(2,1)S(1)} %get-tuple-element.39), channel_id=1, source_target_pairs={{0,24},{4,28},{8,16},{12,20},{16,8},{20,12},{24,0},{28,4},{1,25},{... | collective-permute-start | bytes 294920 | tf_op jit(solution)/shard_map/ppermute | solution.py:643
  45.8 1.1 %collective-permute-start.12 = (bf16[3,128,128]{2,1,0:T(8,128)(2,1)S(1)}, bf16[3,128,128]{2,1,0:T(8,128)(2,1)S(1)}, u32[]{:S(2)}, u32[]{:S(2)}) collective-permute-start(bf16[3,128,128]{2,1,0:T(8,128)(2,1)S(1)} %get-tuple-element.38), channel_id=1, source_target_pairs={{0,16},{4,20},{8,24},{12,28},{16,0},{20,4},{24,8},{28,12},{1,17},{... | collective-permute-start | bytes 294920 | tf_op jit(solution)/shard_map/ppermute | solution.py:643
  46.9 0.7 %collective-permute-start.11 = (bf16[3,128,128]{2,1,0:T(8,128)(2,1)S(1)}, bf16[3,128,128]{2,1,0:T(8,128)(2,1)S(1)}, u32[]{:S(2)}, u32[]{:S(2)}) collective-permute-start(bf16[3,128,128]{2,1,0:T(8,128)(2,1)S(1)} %get-tuple-element.37), channel_id=1, source_target_pairs={{0,8},{4,12},{8,0},{12,4},{16,24},{20,28},{24,16},{28,20},{1,9},{5... | collective-permute-start | bytes 294920 | tf_op jit(solution)/shard_map/ppermute | solution.py:643
  47.6 2.5 %far.3.refs_13_ = bf16[2,512,128]{2,1,0:T(8,128)(2,1)S(1)} custom-call(s32[10]{0:T(128)S(1)} %copy-done.5, bf16[768,1280]{1,0:T(8,128)(2,1)S(1)} %copy-done.1, bf16[8,768,128]{2,1,0:T(8,128)(2,1)S(1)} %get-tuple-element.32.k_ref.refs_1_, bf16[768,1280]{1,0:T(8,128)(2,1)S(1)} %copy-done, bf16[8,768,128]{2,1,0:T(8,128)(2,1)S(1)} %pair.1.kp_ref.refs_3_, ...), custom_call_target="tpu_custom_call" | custom-call | flops 1000 | bytes 1000 | tf_op jit(solution)/shard_map/far/pallas_call | solution.py:35
  50.1 0.7 %collective-permute-done.15.refs_10_ = bf16[2,2,512,128]{3,2,1,0:T(8,128)(2,1)S(1)} collective-permute-done((bf16[2,2,512,128]{3,2,1,0:T(8,128)(2,1)S(1)}, bf16[2,2,512,128]{3,2,1,0:T(8,128)(2,1)S(1)}, u32[]{:S(2)}, u32[]{:S(2)}) %collective-permute-start.15) | collective-permute-done | bytes 524320 | tf_op jit(solution)/shard_map/ppermute | solution.py:643
  50.8 3.5 %rest.1.refs_8_ = bf16[768,1280]{1,0:T(8,128)(2,1)} custom-call(s32[10]{0:T(128)S(1)} %copy-done.5, bf16[768,1280]{1,0:T(8,128)(2,1)S(1)} %copy-done.1, bf16[8,768,128]{2,1,0:T(8,128)(2,1)S(1)} %get-tuple-element.32.k_ref.refs_1_, bf16[768,1280]{1,0:T(8,128)(2,1)S(1)} %copy-done, bf16[8,768,128]{2,1,0:T(8,128)(2,1)S(1)} %pair.1.kp_ref.refs_3_, ...), custom_call_target="tpu_custom_call" | custom-call | flops 1000 | bytes 1000 | tf_op jit(solution)/shard_map/rest/pallas_call | solution.py:35
  54.4 0.0 collective-permute-done.13.refs_3_
  54.4 0.1 collective-permute-start.18
  54.5 0.5 collective-permute-start.17
  54.9 0.0 collective-permute-done.11.refs_1_
  55.0 0.1 collective-permute-start.16
  55.0 0.7 %collective-permute-done.18.refs_7_ = bf16[3,128,128]{2,1,0:T(8,128)(2,1)S(1)} collective-permute-done((bf16[3,128,128]{2,1,0:T(8,128)(2,1)S(1)}, bf16[3,128,128]{2,1,0:T(8,128)(2,1)S(1)}, u32[]{:S(2)}, u32[]{:S(2)}) %collective-permute-start.18) | collective-permute-done | bytes 98336 | tf_op jit(solution)/shard_map/ppermute | solution.py:643
  55.7 0.2 collective-permute-done.17.refs_6_
  55.9 0.4 collective-permute-done.16.refs_5_
  56.3 1.5 %place.1 = bf16[768,1280]{1,0:T(8,128)(2,1)} custom-call(s32[10]{0:T(128)S(1)} %copy-done.5, bf16[3,128,128]{2,1,0:T(8,128)(2,1)S(1)} %get-tuple-element.36.refs_10_.refs_0_, bf16[3,128,128]{2,1,0:T(8,128)(2,1)S(1)} %collective-permute-done.11.refs_1_, bf16[3,128,128]{2,1,0:T(8,128)(2,1)S(1)} %collective-permute-done.12.refs_2_, ...), custom_call_target="tpu_custom_call", output_to_operand_aliasing={{}: (9, {})} | custom-call | flops 1000 | bytes 1000 | tf_op jit(solution)/shard_map/place/pallas_call | solution.py:35
  (18 shorter events, 0.0 us)
Async XLA Ops:
  0.0 3.0 %copy-start.2 = (bf16[768,1280]{1,0:T(8,128)(2,1)S(1)}, bf16[768,1280]{1,0:T(8,128)(2,1)}, u32[]{:S(2)}) copy-start(bf16[768,1280]{1,0:T(8,128)(2,1)} %k_any.1) | copy-start | bytes 5898244
  0.0 3.7 %copy-start = (bf16[768,1280]{1,0:T(8,128)(2,1)S(1)}, bf16[768,1280]{1,0:T(8,128)(2,1)}, u32[]{:S(2)}) copy-start(bf16[768,1280]{1,0:T(8,128)(2,1)} %refs_2_.5) | copy-start | bytes 5898244
  3.0 7.0 %copy-start.1 = (bf16[768,1280]{1,0:T(8,128)(2,1)S(1)}, bf16[768,1280]{1,0:T(8,128)(2,1)}, u32[]{:S(2)}) copy-start(bf16[768,1280]{1,0:T(8,128)(2,1)} %refs_0_.5) | copy-start | bytes 5898244
  3.0 7.0 %copy-start.5 = (s32[10]{0:T(128)S(1)}, s32[10]{0:T(128)}, u32[]{:S(2)}) copy-start(s32[10]{0:T(128)} %kind_ref.17) | copy-start | bytes 124
  3.0 19.8 %collective-permute-start.7 = (bf16[768,1280]{1,0:T(8,128)(2,1)S(1)}, bf16[768,1280]{1,0:T(8,128)(2,1)S(1)}, u32[]{:S(2)}, u32[]{:S(2)}) collective-permute-start(bf16[768,1280]{1,0:T(8,128)(2,1)S(1)} %copy-done.2), channel_id=1, source_target_pairs={{0,4},{4,0},{8,12},{12,8},{16,20},{20,16},{24,28},{28,24},{1,5},{5... | collective-permute-start | bytes 5898248 | tf_op jit(solution)/shard_map/ppermute | solution.py:643
  3.7 21.8 %collective-permute-start.8 = (bf16[768,1280]{1,0:T(8,128)(2,1)S(1)}, bf16[768,1280]{1,0:T(8,128)(2,1)S(1)}, u32[]{:S(2)}, u32[]{:S(2)}) collective-permute-start(bf16[768,1280]{1,0:T(8,128)(2,1)S(1)} %copy-done), channel_id=1, source_target_pairs={{0,4},{4,0},{8,12},{12,8},{16,20},{20,16},{24,28},{28,24},{1,5},{5... | collective-permute-start | bytes 5898248 | tf_op jit(solution)/shard_map/ppermute | solution.py:643
  4.1 29.1 %collective-permute-start.10 = (bf16[2,6,512,128]{3,2,1,0:T(8,128)(2,1)}, bf16[2,6,512,128]{3,2,1,0:T(8,128)(2,1)S(1)}, u32[]{:S(2)}, u32[]{:S(2)}) collective-permute-start(bf16[2,6,512,128]{3,2,1,0:T(8,128)(2,1)} %get-tuple-element.33), channel_id=1, source_target_pairs={{12,16},{16,12},{28,0},{0,28},{13,17},{17,13},{29,1},{1,29},{14,18... | collective-permute-start | bytes 4718600 | tf_op jit(solution)/shard_map/ppermute | solution.py:643
  10.1 9.5 %copy-start.3 = (f32[1280]{0:T(1024)S(1)}, f32[1280]{0:T(1024)}, u32[]{:S(2)}) copy-start(f32[1280]{0:T(1024)} %refs_6_.5) | copy-start | bytes 15364
  10.1 9.5 %copy-start.4 = (f32[1280]{0:T(1024)S(1)}, f32[1280]{0:T(1024)}, u32[]{:S(2)}) copy-start(f32[1280]{0:T(1024)} %refs_5_.5) | copy-start | bytes 15364
  11.2 8.3 %collective-permute-start.2 = (bf16[3,768,128]{2,1,0:T(8,128)(2,1)S(1)}, bf16[3,768,128]{2,1,0:T(8,128)(2,1)S(1)}, u32[]{:S(2)}, u32[]{:S(2)}) collective-permute-start(bf16[3,768,128]{2,1,0:T(8,128)(2,1)S(1)} %get-tuple-element.26), channel_id=1, source_target_pairs={{0,4},{4,0},{8,12},{12,8},{16,20},{20,16},{24,28},{28,24},{1,5},{5... | collective-permute-start | bytes 1769480 | tf_op jit(solution)/shard_map/ppermute | solution.py:643
  11.3 3.7 %collective-permute-start = (f32[2,768]{1,0:T(2,128)S(1)}, f32[2,768]{1,0:T(2,128)S(1)}, u32[]{:S(2)}, u32[]{:S(2)}) collective-permute-start(f32[2,768]{1,0:T(2,128)S(1)} %get-tuple-element.25), channel_id=1, source_target_pairs={{0,1},{1,0},{2,3},{3,2},{4,5},{5,4},{6,7},{7,6},{8,9},{9,8},{10,11... | collective-permute-start | bytes 18440 | tf_op jit(solution)/shard_map/ppermute | solution.py:655
  15.0 4.5 %collective-permute-start.1 = (f32[2,768]{1,0:T(2,128)S(1)}, f32[2,768]{1,0:T(2,128)S(1)}, u32[]{:S(2)}, u32[]{:S(2)}) collective-permute-start(f32[2,768]{1,0:T(2,128)S(1)} %add.6), channel_id=1, source_target_pairs={{0,2},{1,3},{2,0},{3,1},{4,6},{5,7},{6,4},{7,5},{8,10},{9,11},{10,... | collective-permute-start | bytes 18440 | tf_op jit(solution)/shard_map/ppermute | solution.py:655
  19.5 1.3 %collective-permute-start.3 = (f32[2,768]{1,0:T(2,128)S(1)}, f32[2,768]{1,0:T(2,128)S(1)}, u32[]{:S(2)}, u32[]{:S(2)}) collective-permute-start(f32[2,768]{1,0:T(2,128)S(1)} %add.7.total_ref.refs_7_), channel_id=1, source_target_pairs={{0,4},{4,0},{8,12},{12,8},{16,20},{20,16},{24,28},{28,24},{1,5},{5... | collective-permute-start | bytes 18440 | tf_op jit(solution)/shard_map/ppermute | solution.py:643
  21.9 20.3 %collective-permute-start.4 = (bf16[3,3,128,128]{3,2,1,0:T(8,128)(2,1)S(1)}, bf16[3,3,128,128]{3,2,1,0:T(8,128)(2,1)S(1)}, u32[]{:S(2)}, u32[]{:S(2)}) collective-permute-start(bf16[3,3,128,128]{3,2,1,0:T(8,128)(2,1)S(1)} %get-tuple-element.29), channel_id=1, source_target_pairs={{0,8},{4,12},{8,0},{12,4},{16,24},{20,28},{24,16},{28,20},{1,9},{5... | collective-permute-start | bytes 884744 | tf_op jit(solution)/shard_map/ppermute | solution.py:643
  22.4 19.8 %collective-permute-start.5 = (bf16[3,3,128,128]{3,2,1,0:T(8,128)(2,1)S(1)}, bf16[3,3,128,128]{3,2,1,0:T(8,128)(2,1)S(1)}, u32[]{:S(2)}, u32[]{:S(2)}) collective-permute-start(bf16[3,3,128,128]{3,2,1,0:T(8,128)(2,1)S(1)} %get-tuple-element.30), channel_id=1, source_target_pairs={{0,16},{4,20},{8,24},{12,28},{16,0},{20,4},{24,8},{28,12},{1,17},{... | collective-permute-start | bytes 884744 | tf_op jit(solution)/shard_map/ppermute | solution.py:643
  22.9 19.3 %collective-permute-start.6 = (bf16[3,3,128,128]{3,2,1,0:T(8,128)(2,1)S(1)}, bf16[3,3,128,128]{3,2,1,0:T(8,128)(2,1)S(1)}, u32[]{:S(2)}, u32[]{:S(2)}) collective-permute-start(bf16[3,3,128,128]{3,2,1,0:T(8,128)(2,1)S(1)} %get-tuple-element.31), channel_id=1, source_target_pairs={{0,24},{4,28},{8,16},{12,20},{16,8},{20,12},{24,0},{28,4},{1,25},{... | collective-permute-start | bytes 884744 | tf_op jit(solution)/shard_map/ppermute | solution.py:643
  25.5 7.8 %collective-permute-start.9 = (f32[2,768]{1,0:T(2,128)S(1)}, f32[2,768]{1,0:T(2,128)S(1)}, u32[]{:S(2)}, u32[]{:S(2)}) collective-permute-start(f32[2,768]{1,0:T(2,128)S(1)} %add.7.total_ref.refs_7_), channel_id=1, source_target_pairs={{12,17},{13,16},{14,19},{15,18},{16,13},{17,12},{18,15},{19,14},{2... | collective-permute-start | bytes 18440 | tf_op jit(solution)/shard_map/ppermute | solution.py:659
  33.2 3.8 %copy-start.6 = (bf16[2,2,512,128]{3,2,1,0:T(8,128)(2,1)S(1)}, bf16[2,2,512,128]{3,2,1,0:T(8,128)(2,1)}, u32[]{:S(2)}) copy-start(bf16[2,2,512,128]{3,2,1,0:T(8,128)(2,1)} %get-tuple-element.41) | copy-start | bytes 1572868
  37.1 13.7 %collective-permute-start.15 = (bf16[2,2,512,128]{3,2,1,0:T(8,128)(2,1)S(1)}, bf16[2,2,512,128]{3,2,1,0:T(8,128)(2,1)S(1)}, u32[]{:S(2)}, u32[]{:S(2)}) collective-permute-start(bf16[2,2,512,128]{3,2,1,0:T(8,128)(2,1)S(1)} %copy-done.6), channel_id=1, source_target_pairs={{12,16},{16,12},{28,0},{0,28},{13,17},{17,13},{29,1},{1,29},{14,18... | collective-permute-start | bytes 1572872 | tf_op jit(solution)/shard_map/ppermute | solution.py:643
  44.1 10.3 %collective-permute-start.13 = (bf16[3,128,128]{2,1,0:T(8,128)(2,1)S(1)}, bf16[3,128,128]{2,1,0:T(8,128)(2,1)S(1)}, u32[]{:S(2)}, u32[]{:S(2)}) collective-permute-start(bf16[3,128,128]{2,1,0:T(8,128)(2,1)S(1)} %get-tuple-element.39), channel_id=1, source_target_pairs={{0,24},{4,28},{8,16},{12,20},{16,8},{20,12},{24,0},{28,4},{1,25},{... | collective-permute-start | bytes 294920 | tf_op jit(solution)/shard_map/ppermute | solution.py:643
  45.8 8.6 %collective-permute-start.12 = (bf16[3,128,128]{2,1,0:T(8,128)(2,1)S(1)}, bf16[3,128,128]{2,1,0:T(8,128)(2,1)S(1)}, u32[]{:S(2)}, u32[]{:S(2)}) collective-permute-start(bf16[3,128,128]{2,1,0:T(8,128)(2,1)S(1)} %get-tuple-element.38), channel_id=1, source_target_pairs={{0,16},{4,20},{8,24},{12,28},{16,0},{20,4},{24,8},{28,12},{1,17},{... | collective-permute-start | bytes 294920 | tf_op jit(solution)/shard_map/ppermute | solution.py:643
  46.9 8.1 %collective-permute-start.11 = (bf16[3,128,128]{2,1,0:T(8,128)(2,1)S(1)}, bf16[3,128,128]{2,1,0:T(8,128)(2,1)S(1)}, u32[]{:S(2)}, u32[]{:S(2)}) collective-permute-start(bf16[3,128,128]{2,1,0:T(8,128)(2,1)S(1)} %get-tuple-element.37), channel_id=1, source_target_pairs={{0,8},{4,12},{8,0},{12,4},{16,24},{20,28},{24,16},{28,20},{1,9},{5... | collective-permute-start | bytes 294920 | tf_op jit(solution)/shard_map/ppermute | solution.py:643
  47.6 7.4 %collective-permute-start.14 = (bf16[3,128,128]{2,1,0:T(8,128)(2,1)S(1)}, bf16[3,128,128]{2,1,0:T(8,128)(2,1)S(1)}, u32[]{:S(2)}, u32[]{:S(2)}) collective-permute-start(bf16[3,128,128]{2,1,0:T(8,128)(2,1)S(1)} %get-tuple-element.36.refs_10_.refs_0_), channel_id=1, source_target_pairs={{0,4},{4,0},{8,12},{12,8},{16,20},{20,16},{24,28},{28,24},{1,5},{5... | collective-permute-start | bytes 294920 | tf_op jit(solution)/shard_map/ppermute | solution.py:643
  54.4 1.4 %collective-permute-start.18 = (bf16[3,128,128]{2,1,0:T(8,128)(2,1)S(1)}, bf16[3,128,128]{2,1,0:T(8,128)(2,1)S(1)}, u32[]{:S(2)}, u32[]{:S(2)}) collective-permute-start(bf16[3,128,128]{2,1,0:T(8,128)(2,1)S(1)} %collective-permute-done.13.refs_3_), channel_id=1, source_target_pairs={{0,4},{4,0},{8,12},{12,8},{16,20},{20,16},{24,28},{28,24},{1,5},{5... | collective-permute-start | bytes 294920 | tf_op jit(solution)/shard_map/ppermute | solution.py:643
  54.5 1.4 %collective-permute-start.17 = (bf16[3,128,128]{2,1,0:T(8,128)(2,1)S(1)}, bf16[3,128,128]{2,1,0:T(8,128)(2,1)S(1)}, u32[]{:S(2)}, u32[]{:S(2)}) collective-permute-start(bf16[3,128,128]{2,1,0:T(8,128)(2,1)S(1)} %collective-permute-done.12.refs_2_), channel_id=1, source_target_pairs={{0,4},{4,0},{8,12},{12,8},{16,20},{20,16},{24,28},{28,24},{1,5},{5... | collective-permute-start | bytes 294920 | tf_op jit(solution)/shard_map/ppermute | solution.py:643
  55.0 1.3 %collective-permute-start.16 = (bf16[3,128,128]{2,1,0:T(8,128)(2,1)S(1)}, bf16[3,128,128]{2,1,0:T(8,128)(2,1)S(1)}, u32[]{:S(2)}, u32[]{:S(2)}) collective-permute-start(bf16[3,128,128]{2,1,0:T(8,128)(2,1)S(1)} %collective-permute-done.11.refs_1_), channel_id=1, source_target_pairs={{0,4},{4,0},{8,12},{12,8},{16,20},{20,16},{24,28},{28,24},{1,5},{5... | collective-permute-start | bytes 294920 | tf_op jit(solution)/shard_map/ppermute | solution.py:643

commit v8 on v7

--- a/solution.py
+++ b/solution.py
@@ -676,8 +676,8 @@
         head_kind, queries, k, values, kp, v_pair, query_gain, total, spatial, block
     )
     operands = (queries, k, values, kp, v_pair, query_gain, key_gain, total, cross_total, kv_cross)
-    half = spatial // 2
-    far = far_call(head_kind, operands, near, 0, half, spatial, block)
+    ahead = (3 * spatial) // 8
+    far = far_call(head_kind, operands, near, 0, ahead, spatial, block)
     late_cross = send(lax.optimization_barrier((kv_late, far))[0], cross)
     last = far
     if dealt:
@@ -685,7 +685,9 @@
         parts = [send(p, r) for p, r in zip(results[:0:-1], turned[::-1])]
         parts = [results[0]] + parts[::-1]
         last = results[0]
-    mid = far_call(head_kind, operands, last, half, half - late, spatial, block)
+    mid = far_call(
+        head_kind, operands, last, ahead, spatial - ahead - late, spatial, block
+    )
     out = rest_call(
         head_kind, operands + (late_cross,), near, far, mid, spatial - late, late, spatial, block
     )

time: 58 us -> 57.5 us (level)
  waiting for transfers between devices: 5.96 us -> 4.97 us
    ppermute x16, waiting for transfers between devices: 1.96 us -> 0.98 us  [per_device(): send = lambda x, route: lax.ppermute(x, 'seq', route)]
  transfers between devices with their start and end apart: 19 -> 19, of which waited for: 6 -> 5; matrix products, arithmetic and copies ran while one was open for 0% -> 0% of each run, Pallas kernels for 36% -> 36%
where the time goes in v8:
time: 57.5 us; the launch traced here: 57.3 us
  starting transfers between devices  26.6 us (46%)
  Pallas kernels  25.1 us (44%)
  waiting for transfers between devices  4.97 us (9%)
    pallas_call x12, Pallas kernels, call(): pl.pallas_call(kernel, out_shape=out_shape, in_specs=in_specs, out_specs=...  25.1 us
    ppermute x16, starting transfers between devices, per_device(): send = lambda x, route: lax.ppermute(x, 'seq', route)  19.8 us
    ppermute x2, starting transfers between devices, per_device(): lax.ppermute(total, 'head', [(i, i ^ d) for i in range(planes)])  4.23 us
    ppermute x2, waiting for transfers between devices, per_device(): lax.ppermute(total, 'head', [(i, i ^ d) for i in range(planes)])  3.99 us
    ppermute x1, starting transfers between devices, per_device(): lax.ppermute(total, ('seq', 'head'), [(i * planes + p, j * planes + (p ^...  2.56 us
  transfers between devices with their start and end apart: 19, of which 5 were waited for; matrix products, arithmetic and copies ran while one was open for 0% of the time, Pallas kernels for 36%

profile of v8, /device:TPU:0, one launch (start us, length us, event | category | flops | bytes accessed | tf_op | source)
XLA Modules:
  0.0 57.3 jit_solution(2988010779272533986)
XLA Ops:
  0.0 3.0 %pack.1 = (bf16[2,6,512,128]{3,2,1,0:T(8,128)(2,1)}, bf16[2,2,512,128]{3,2,1,0:T(8,128)(2,1)}) custom-call(s32[10]{0:T(128)} %kind_ref.17, bf16[768,1280]{1,0:T(8,128)(2,1)} %k_any.1, bf16[768,1280]{1,0:T(8,128)(2,1)} %refs_2_.5), custom_call_target="tpu_custom_call" | custom-call | flops 1000 | bytes 1000 | tf_op jit(solution)/shard_map/pack/pallas_call | solution.py:35
  3.0 0.0 copy-start.1
  3.0 0.0 copy-start.5
  3.0 0.5 collective-permute-start.7
  3.5 0.1 copy-done
  3.7 0.5 collective-permute-start.8
  4.1 5.5 %collective-permute-start.10 = (bf16[2,6,512,128]{3,2,1,0:T(8,128)(2,1)}, bf16[2,6,512,128]{3,2,1,0:T(8,128)(2,1)S(1)}, u32[]{:S(2)}, u32[]{:S(2)}) collective-permute-start(bf16[2,6,512,128]{3,2,1,0:T(8,128)(2,1)} %get-tuple-element.33), channel_id=1, source_target_pairs={{12,16},{16,12},{28,0},{0,28},{13,17},{17,13},{29,1},{1,29},{14,18... | collective-permute-start | bytes 4718600 | tf_op jit(solution)/shard_map/ppermute | solution.py:643
  9.6 0.5 key_sums.1.key_sums_ref
  10.1 0.0 copy-start.3
  10.1 0.0 copy-start.4
  10.1 1.1 %sums.1 = (f32[2,768]{1,0:T(2,128)S(1)}, bf16[3,768,128]{2,1,0:T(8,128)(2,1)S(1)}) custom-call(s32[10]{0:T(128)S(1)} %copy-done.5, bf16[768,1280]{1,0:T(8,128)(2,1)S(1)} %copy-done.1, bf16[768,1280]{1,0:T(8,128)(2,1)S(1)} %copy-done.2, bf16[768,1280]{1,0:T(8,128)(2,1)S(1)} %copy-done, f32[1,768]{1,0:T(1,128)S(1)} %key_sums.1.key_sums_ref), custom_call_target="tpu_custom_call" | custom-call | flops 1000 | bytes 1000 | tf_op jit(solution)/shard_map/sums/pallas_call | solution.py:35
  11.2 0.1 collective-permute-start.2
  11.3 1.6 %collective-permute-start = (f32[2,768]{1,0:T(2,128)S(1)}, f32[2,768]{1,0:T(2,128)S(1)}, u32[]{:S(2)}, u32[]{:S(2)}) collective-permute-start(f32[2,768]{1,0:T(2,128)S(1)} %get-tuple-element.25), channel_id=1, source_target_pairs={{0,1},{1,0},{2,3},{3,2},{4,5},{5,4},{6,7},{7,6},{8,9},{9,8},{10,11... | collective-permute-start | bytes 18440 | tf_op jit(solution)/shard_map/ppermute | solution.py:655
  12.9 2.1 %collective-permute-done = f32[2,768]{1,0:T(2,128)S(1)} collective-permute-done((f32[2,768]{1,0:T(2,128)S(1)}, f32[2,768]{1,0:T(2,128)S(1)}, u32[]{:S(2)}, u32[]{:S(2)}) %collective-permute-start) | collective-permute-done | bytes 6176 | tf_op jit(solution)/shard_map/ppermute | solution.py:655
  15.0 2.6 %collective-permute-start.1 = (f32[2,768]{1,0:T(2,128)S(1)}, f32[2,768]{1,0:T(2,128)S(1)}, u32[]{:S(2)}, u32[]{:S(2)}) collective-permute-start(f32[2,768]{1,0:T(2,128)S(1)} %add.6), channel_id=1, source_target_pairs={{0,2},{1,3},{2,0},{3,1},{4,6},{5,7},{6,4},{7,5},{8,10},{9,11},{10,... | collective-permute-start | bytes 18440 | tf_op jit(solution)/shard_map/ppermute | solution.py:655
  17.6 1.9 %collective-permute-done.1 = f32[2,768]{1,0:T(2,128)S(1)} collective-permute-done((f32[2,768]{1,0:T(2,128)S(1)}, f32[2,768]{1,0:T(2,128)S(1)}, u32[]{:S(2)}, u32[]{:S(2)}) %collective-permute-start.1) | collective-permute-done | bytes 6176 | tf_op jit(solution)/shard_map/ppermute | solution.py:655
  19.5 0.0 collective-permute-start.3
  19.5 0.0 collective-permute-done.2.refs_0_.got_ref
  19.6 1.3 %own.1 = (bf16[8,768,128]{2,1,0:T(8,128)(2,1)S(1)}, bf16[3,768,128]{2,1,0:T(8,128)(2,1)S(1)}) custom-call(s32[10]{0:T(128)S(1)} %copy-done.5, bf16[768,1280]{1,0:T(8,128)(2,1)S(1)} %copy-done.1, bf16[768,1280]{1,0:T(8,128)(2,1)S(1)} %copy-done.2, bf16[768,1280]{1,0:T(8,128)(2,1)S(1)} %copy-done, f32[1280]{0:T(1024)S(1)} %copy-done.4, f32[1280]{0:T(1024)S(1)} %copy-done.3, ...), custom_call_target="tpu_custom_call" | custom-call | flops 1000 | bytes 1000 | tf_op jit(solution)/shard_map/own/pallas_call | solution.py:35
  20.9 0.0 collective-permute-done.3.sums_ref
  20.9 1.0 %deal.1 = (bf16[3,3,128,128]{3,2,1,0:T(8,128)(2,1)S(1)}, bf16[3,3,128,128]{3,2,1,0:T(8,128)(2,1)S(1)}, bf16[3,3,128,128]{3,2,1,0:T(8,128)(2,1)S(1)}, bf16[3,3,128,128]{3,2,1,0:T(8,128)(2,1)S(1)}) custom-call(s32[10]{0:T(128)S(1)} %copy-done.5, bf16[3,768,128]{2,1,0:T(8,128)(2,1)S(1)} %get-tuple-element.27.own_ref, ...), custom_call_target="tpu_custom_call" | custom-call | flops 1000 | bytes 1000 | tf_op jit(solution)/shard_map/deal/pallas_call | solution.py:35
  21.9 0.5 collective-permute-start.4
  22.4 0.4 collective-permute-start.5
  22.9 0.0 collective-permute-done.7.k_ref
  22.9 2.6 %collective-permute-start.6 = (bf16[3,3,128,128]{3,2,1,0:T(8,128)(2,1)S(1)}, bf16[3,3,128,128]{3,2,1,0:T(8,128)(2,1)S(1)}, u32[]{:S(2)}, u32[]{:S(2)}) collective-permute-start(bf16[3,3,128,128]{3,2,1,0:T(8,128)(2,1)S(1)} %get-tuple-element.31), channel_id=1, source_target_pairs={{0,24},{4,28},{8,16},{12,20},{16,8},{20,12},{24,0},{28,4},{1,25},{... | collective-permute-start | bytes 884744 | tf_op jit(solution)/shard_map/ppermute | solution.py:643
  25.5 0.0 collective-permute-done.8.v_pair_ref.refs_4_
  25.5 2.6 %collective-permute-start.9 = (f32[2,768]{1,0:T(2,128)S(1)}, f32[2,768]{1,0:T(2,128)S(1)}, u32[]{:S(2)}, u32[]{:S(2)}) collective-permute-start(f32[2,768]{1,0:T(2,128)S(1)} %add.7.total_ref.refs_7_), channel_id=1, source_target_pairs={{12,17},{13,16},{14,19},{15,18},{16,13},{17,12},{18,15},{19,14},{2... | collective-permute-start | bytes 18440 | tf_op jit(solution)/shard_map/ppermute | solution.py:659
  28.0 1.1 %pair.1.kp_ref.refs_3_ = bf16[8,768,128]{2,1,0:T(8,128)(2,1)S(1)} custom-call(s32[10]{0:T(128)S(1)} %copy-done.5, bf16[768,1280]{1,0:T(8,128)(2,1)S(1)} %collective-permute-done.7.k_ref, f32[1280]{0:T(1024)S(1)} %copy-done.3, f32[2,768]{1,0:T(2,128)S(1)} %collective-permute-done.3.sums_ref, bf16[3,3,128,128]{3,2,1,0:T(8,128)(2,1)S(1)} %get-tuple-element.28.after_ref.refs_0_), custom_call_target="tpu_custom_call" | custom-call | flops 1000 | bytes 1000 | tf_op jit(solution)/shard_map/pair/pallas_call | solution.py:35
  29.2 4.0 %near.1.refs_10_.refs_11_ = bf16[8,256,128]{2,1,0:T(8,128)(2,1)S(1)} custom-call(s32[10]{0:T(128)S(1)} %copy-done.5, bf16[768,1280]{1,0:T(8,128)(2,1)S(1)} %copy-done.1, bf16[8,768,128]{2,1,0:T(8,128)(2,1)S(1)} %get-tuple-element.32.k_ref.refs_1_, bf16[768,1280]{1,0:T(8,128)(2,1)S(1)} %copy-done, bf16[8,768,128]{2,1,0:T(8,128)(2,1)S(1)} %pair.1.kp_ref.refs_3_, ...), custom_call_target="tpu_custom_call" | custom-call | flops 1000 | bytes 1000 | tf_op jit(solution)/shard_map/near/pallas_call | solution.py:35
  33.2 0.0 collective-permute-done.9.refs_8_
  33.2 3.1 %far.2.refs_4_.refs_12_ = bf16[3,512,128]{2,1,0:T(8,128)(2,1)S(1)} custom-call(s32[10]{0:T(128)S(1)} %copy-done.5, bf16[768,1280]{1,0:T(8,128)(2,1)S(1)} %copy-done.1, bf16[8,768,128]{2,1,0:T(8,128)(2,1)S(1)} %get-tuple-element.32.k_ref.refs_1_, bf16[768,1280]{1,0:T(8,128)(2,1)S(1)} %copy-done, bf16[8,768,128]{2,1,0:T(8,128)(2,1)S(1)} %pair.1.kp_ref.refs_3_, ...), custom_call_target="tpu_custom_call" | custom-call | flops 1000 | bytes 1000 | tf_op jit(solution)/shard_map/far/pallas_call | solution.py:35
  36.4 5.1 %collective-permute-start.15 = (bf16[2,2,512,128]{3,2,1,0:T(8,128)(2,1)S(1)}, bf16[2,2,512,128]{3,2,1,0:T(8,128)(2,1)S(1)}, u32[]{:S(2)}, u32[]{:S(2)}) collective-permute-start(bf16[2,2,512,128]{3,2,1,0:T(8,128)(2,1)S(1)} %copy-done.6), channel_id=1, source_target_pairs={{12,16},{16,12},{28,0},{0,28},{13,17},{17,13},{29,1},{1,29},{14,18... | collective-permute-start | bytes 1572872 | tf_op jit(solution)/shard_map/ppermute | solution.py:643
  41.5 0.0 collective-permute-done.4.refs_1_
  41.5 0.0 collective-permute-done.6.refs_3_
  41.5 1.8 %frames.1 = (bf16[3,128,128]{2,1,0:T(8,128)(2,1)S(1)}, bf16[3,128,128]{2,1,0:T(8,128)(2,1)S(1)}, bf16[3,128,128]{2,1,0:T(8,128)(2,1)S(1)}, bf16[3,128,128]{2,1,0:T(8,128)(2,1)S(1)}) custom-call(bf16[3,3,128,128]{3,2,1,0:T(8,128)(2,1)S(1)} %get-tuple-element.28.after_ref.refs_0_, bf16[3,3,128,128]{3,2,1,0:T(8,128)(2,1)S(1)} %collective-permute-done.4.refs_1_, ...), custom_call_target="tpu_custom_call" | custom-call | flops 10000000000 | bytes 1000 | tf_op jit(solution)/shard_map/frames/pallas_call | solution.py:35
  43.3 2.5 %collective-permute-start.13 = (bf16[3,128,128]{2,1,0:T(8,128)(2,1)S(1)}, bf16[3,128,128]{2,1,0:T(8,128)(2,1)S(1)}, u32[]{:S(2)}, u32[]{:S(2)}) collective-permute-start(bf16[3,128,128]{2,1,0:T(8,128)(2,1)S(1)} %get-tuple-element.39), channel_id=1, source_target_pairs={{0,24},{4,28},{8,16},{12,20},{16,8},{20,12},{24,0},{28,4},{1,25},{... | collective-permute-start | bytes 294920 | tf_op jit(solution)/shard_map/ppermute | solution.py:643
  45.8 1.1 %collective-permute-start.12 = (bf16[3,128,128]{2,1,0:T(8,128)(2,1)S(1)}, bf16[3,128,128]{2,1,0:T(8,128)(2,1)S(1)}, u32[]{:S(2)}, u32[]{:S(2)}) collective-permute-start(bf16[3,128,128]{2,1,0:T(8,128)(2,1)S(1)} %get-tuple-element.38), channel_id=1, source_target_pairs={{0,16},{4,20},{8,24},{12,28},{16,0},{20,4},{24,8},{28,12},{1,17},{... | collective-permute-start | bytes 294920 | tf_op jit(solution)/shard_map/ppermute | solution.py:643
  46.9 0.0 collective-permute-start.11
  46.9 3.2 %far.3.refs_13_ = bf16[3,512,128]{2,1,0:T(8,128)(2,1)S(1)} custom-call(s32[10]{0:T(128)S(1)} %copy-done.5, bf16[768,1280]{1,0:T(8,128)(2,1)S(1)} %copy-done.1, bf16[8,768,128]{2,1,0:T(8,128)(2,1)S(1)} %get-tuple-element.32.k_ref.refs_1_, bf16[768,1280]{1,0:T(8,128)(2,1)S(1)} %copy-done, bf16[8,768,128]{2,1,0:T(8,128)(2,1)S(1)} %pair.1.kp_ref.refs_3_, ...), custom_call_target="tpu_custom_call" | custom-call | flops 1000 | bytes 1000 | tf_op jit(solution)/shard_map/far/pallas_call | solution.py:35
  50.1 0.0 collective-permute-done.15.refs_10_
  50.1 3.5 %rest.1.refs_8_ = bf16[768,1280]{1,0:T(8,128)(2,1)} custom-call(s32[10]{0:T(128)S(1)} %copy-done.5, bf16[768,1280]{1,0:T(8,128)(2,1)S(1)} %copy-done.1, bf16[8,768,128]{2,1,0:T(8,128)(2,1)S(1)} %get-tuple-element.32.k_ref.refs_1_, bf16[768,1280]{1,0:T(8,128)(2,1)S(1)} %copy-done, bf16[8,768,128]{2,1,0:T(8,128)(2,1)S(1)} %pair.1.kp_ref.refs_3_, ...), custom_call_target="tpu_custom_call" | custom-call | flops 1000 | bytes 1000 | tf_op jit(solution)/shard_map/rest/pallas_call | solution.py:35
  53.7 0.6 collective-permute-start.18
  54.2 0.1 collective-permute-start.17
  54.3 0.4 collective-permute-start.16
  54.7 0.4 collective-permute-done.18.refs_7_
  55.2 0.4 collective-permute-done.17.refs_6_
  55.5 0.2 collective-permute-done.16.refs_5_
  55.7 1.5 %place.1 = bf16[768,1280]{1,0:T(8,128)(2,1)} custom-call(s32[10]{0:T(128)S(1)} %copy-done.5, bf16[3,128,128]{2,1,0:T(8,128)(2,1)S(1)} %get-tuple-element.36.refs_10_.refs_0_, bf16[3,128,128]{2,1,0:T(8,128)(2,1)S(1)} %collective-permute-done.11.refs_1_, bf16[3,128,128]{2,1,0:T(8,128)(2,1)S(1)} %collective-permute-done.12.refs_2_, ...), custom_call_target="tpu_custom_call", output_to_operand_aliasing={{}: (9, {})} | custom-call | flops 1000 | bytes 1000 | tf_op jit(solution)/shard_map/place/pallas_call | solution.py:35
  (18 shorter events, 0.0 us)
Async XLA Ops:
  0.0 3.0 %copy-start.2 = (bf16[768,1280]{1,0:T(8,128)(2,1)S(1)}, bf16[768,1280]{1,0:T(8,128)(2,1)}, u32[]{:S(2)}) copy-start(bf16[768,1280]{1,0:T(8,128)(2,1)} %k_any.1) | copy-start | bytes 5898244
  0.0 3.7 %copy-start = (bf16[768,1280]{1,0:T(8,128)(2,1)S(1)}, bf16[768,1280]{1,0:T(8,128)(2,1)}, u32[]{:S(2)}) copy-start(bf16[768,1280]{1,0:T(8,128)(2,1)} %refs_2_.5) | copy-start | bytes 5898244
  3.0 7.0 %copy-start.1 = (bf16[768,1280]{1,0:T(8,128)(2,1)S(1)}, bf16[768,1280]{1,0:T(8,128)(2,1)}, u32[]{:S(2)}) copy-start(bf16[768,1280]{1,0:T(8,128)(2,1)} %refs_0_.5) | copy-start | bytes 5898244
  3.0 7.0 %copy-start.5 = (s32[10]{0:T(128)S(1)}, s32[10]{0:T(128)}, u32[]{:S(2)}) copy-start(s32[10]{0:T(128)} %kind_ref.17) | copy-start | bytes 124
  3.0 19.8 %collective-permute-start.7 = (bf16[768,1280]{1,0:T(8,128)(2,1)S(1)}, bf16[768,1280]{1,0:T(8,128)(2,1)S(1)}, u32[]{:S(2)}, u32[]{:S(2)}) collective-permute-start(bf16[768,1280]{1,0:T(8,128)(2,1)S(1)} %copy-done.2), channel_id=1, source_target_pairs={{0,4},{4,0},{8,12},{12,8},{16,20},{20,16},{24,28},{28,24},{1,5},{5... | collective-permute-start | bytes 5898248 | tf_op jit(solution)/shard_map/ppermute | solution.py:643
  3.7 21.8 %collective-permute-start.8 = (bf16[768,1280]{1,0:T(8,128)(2,1)S(1)}, bf16[768,1280]{1,0:T(8,128)(2,1)S(1)}, u32[]{:S(2)}, u32[]{:S(2)}) collective-permute-start(bf16[768,1280]{1,0:T(8,128)(2,1)S(1)} %copy-done), channel_id=1, source_target_pairs={{0,4},{4,0},{8,12},{12,8},{16,20},{20,16},{24,28},{28,24},{1,5},{5... | collective-permute-start | bytes 5898248 | tf_op jit(solution)/shard_map/ppermute | solution.py:643
  4.1 29.1 %collective-permute-start.10 = (bf16[2,6,512,128]{3,2,1,0:T(8,128)(2,1)}, bf16[2,6,512,128]{3,2,1,0:T(8,128)(2,1)S(1)}, u32[]{:S(2)}, u32[]{:S(2)}) collective-permute-start(bf16[2,6,512,128]{3,2,1,0:T(8,128)(2,1)} %get-tuple-element.33), channel_id=1, source_target_pairs={{12,16},{16,12},{28,0},{0,28},{13,17},{17,13},{29,1},{1,29},{14,18... | collective-permute-start | bytes 4718600 | tf_op jit(solution)/shard_map/ppermute | solution.py:643
  10.1 9.5 %copy-start.3 = (f32[1280]{0:T(1024)S(1)}, f32[1280]{0:T(1024)}, u32[]{:S(2)}) copy-start(f32[1280]{0:T(1024)} %refs_6_.5) | copy-start | bytes 15364
  10.1 9.5 %copy-start.4 = (f32[1280]{0:T(1024)S(1)}, f32[1280]{0:T(1024)}, u32[]{:S(2)}) copy-start(f32[1280]{0:T(1024)} %refs_5_.5) | copy-start | bytes 15364
  11.2 8.3 %collective-permute-start.2 = (bf16[3,768,128]{2,1,0:T(8,128)(2,1)S(1)}, bf16[3,768,128]{2,1,0:T(8,128)(2,1)S(1)}, u32[]{:S(2)}, u32[]{:S(2)}) collective-permute-start(bf16[3,768,128]{2,1,0:T(8,128)(2,1)S(1)} %get-tuple-element.26), channel_id=1, source_target_pairs={{0,4},{4,0},{8,12},{12,8},{16,20},{20,16},{24,28},{28,24},{1,5},{5... | collective-permute-start | bytes 1769480 | tf_op jit(solution)/shard_map/ppermute | solution.py:643
  11.3 3.7 %collective-permute-start = (f32[2,768]{1,0:T(2,128)S(1)}, f32[2,768]{1,0:T(2,128)S(1)}, u32[]{:S(2)}, u32[]{:S(2)}) collective-permute-start(f32[2,768]{1,0:T(2,128)S(1)} %get-tuple-element.25), channel_id=1, source_target_pairs={{0,1},{1,0},{2,3},{3,2},{4,5},{5,4},{6,7},{7,6},{8,9},{9,8},{10,11... | collective-permute-start | bytes 18440 | tf_op jit(solution)/shard_map/ppermute | solution.py:655
  15.0 4.5 %collective-permute-start.1 = (f32[2,768]{1,0:T(2,128)S(1)}, f32[2,768]{1,0:T(2,128)S(1)}, u32[]{:S(2)}, u32[]{:S(2)}) collective-permute-start(f32[2,768]{1,0:T(2,128)S(1)} %add.6), channel_id=1, source_target_pairs={{0,2},{1,3},{2,0},{3,1},{4,6},{5,7},{6,4},{7,5},{8,10},{9,11},{10,... | collective-permute-start | bytes 18440 | tf_op jit(solution)/shard_map/ppermute | solution.py:655
  19.5 1.3 %collective-permute-start.3 = (f32[2,768]{1,0:T(2,128)S(1)}, f32[2,768]{1,0:T(2,128)S(1)}, u32[]{:S(2)}, u32[]{:S(2)}) collective-permute-start(f32[2,768]{1,0:T(2,128)S(1)} %add.7.total_ref.refs_7_), channel_id=1, source_target_pairs={{0,4},{4,0},{8,12},{12,8},{16,20},{20,16},{24,28},{28,24},{1,5},{5... | collective-permute-start | bytes 18440 | tf_op jit(solution)/shard_map/ppermute | solution.py:643
  21.9 19.6 %collective-permute-start.4 = (bf16[3,3,128,128]{3,2,1,0:T(8,128)(2,1)S(1)}, bf16[3,3,128,128]{3,2,1,0:T(8,128)(2,1)S(1)}, u32[]{:S(2)}, u32[]{:S(2)}) collective-permute-start(bf16[3,3,128,128]{3,2,1,0:T(8,128)(2,1)S(1)} %get-tuple-element.29), channel_id=1, source_target_pairs={{0,8},{4,12},{8,0},{12,4},{16,24},{20,28},{24,16},{28,20},{1,9},{5... | collective-permute-start | bytes 884744 | tf_op jit(solution)/shard_map/ppermute | solution.py:643
  22.4 19.0 %collective-permute-start.5 = (bf16[3,3,128,128]{3,2,1,0:T(8,128)(2,1)S(1)}, bf16[3,3,128,128]{3,2,1,0:T(8,128)(2,1)S(1)}, u32[]{:S(2)}, u32[]{:S(2)}) collective-permute-start(bf16[3,3,128,128]{3,2,1,0:T(8,128)(2,1)S(1)} %get-tuple-element.30), channel_id=1, source_target_pairs={{0,16},{4,20},{8,24},{12,28},{16,0},{20,4},{24,8},{28,12},{1,17},{... | collective-permute-start | bytes 884744 | tf_op jit(solution)/shard_map/ppermute | solution.py:643
  22.9 18.6 %collective-permute-start.6 = (bf16[3,3,128,128]{3,2,1,0:T(8,128)(2,1)S(1)}, bf16[3,3,128,128]{3,2,1,0:T(8,128)(2,1)S(1)}, u32[]{:S(2)}, u32[]{:S(2)}) collective-permute-start(bf16[3,3,128,128]{3,2,1,0:T(8,128)(2,1)S(1)} %get-tuple-element.31), channel_id=1, source_target_pairs={{0,24},{4,28},{8,16},{12,20},{16,8},{20,12},{24,0},{28,4},{1,25},{... | collective-permute-start | bytes 884744 | tf_op jit(solution)/shard_map/ppermute | solution.py:643
  25.5 7.7 %collective-permute-start.9 = (f32[2,768]{1,0:T(2,128)S(1)}, f32[2,768]{1,0:T(2,128)S(1)}, u32[]{:S(2)}, u32[]{:S(2)}) collective-permute-start(f32[2,768]{1,0:T(2,128)S(1)} %add.7.total_ref.refs_7_), channel_id=1, source_target_pairs={{12,17},{13,16},{14,19},{15,18},{16,13},{17,12},{18,15},{19,14},{2... | collective-permute-start | bytes 18440 | tf_op jit(solution)/shard_map/ppermute | solution.py:659
  33.2 3.2 %copy-start.6 = (bf16[2,2,512,128]{3,2,1,0:T(8,128)(2,1)S(1)}, bf16[2,2,512,128]{3,2,1,0:T(8,128)(2,1)}, u32[]{:S(2)}) copy-start(bf16[2,2,512,128]{3,2,1,0:T(8,128)(2,1)} %get-tuple-element.41) | copy-start | bytes 1572868
  36.4 13.7 %collective-permute-start.15 = (bf16[2,2,512,128]{3,2,1,0:T(8,128)(2,1)S(1)}, bf16[2,2,512,128]{3,2,1,0:T(8,128)(2,1)S(1)}, u32[]{:S(2)}, u32[]{:S(2)}) collective-permute-start(bf16[2,2,512,128]{3,2,1,0:T(8,128)(2,1)S(1)} %copy-done.6), channel_id=1, source_target_pairs={{12,16},{16,12},{28,0},{0,28},{13,17},{17,13},{29,1},{1,29},{14,18... | collective-permute-start | bytes 1572872 | tf_op jit(solution)/shard_map/ppermute | solution.py:643
  43.3 10.3 %collective-permute-start.13 = (bf16[3,128,128]{2,1,0:T(8,128)(2,1)S(1)}, bf16[3,128,128]{2,1,0:T(8,128)(2,1)S(1)}, u32[]{:S(2)}, u32[]{:S(2)}) collective-permute-start(bf16[3,128,128]{2,1,0:T(8,128)(2,1)S(1)} %get-tuple-element.39), channel_id=1, source_target_pairs={{0,24},{4,28},{8,16},{12,20},{16,8},{20,12},{24,0},{28,4},{1,25},{... | collective-permute-start | bytes 294920 | tf_op jit(solution)/shard_map/ppermute | solution.py:643
  45.8 8.4 %collective-permute-start.12 = (bf16[3,128,128]{2,1,0:T(8,128)(2,1)S(1)}, bf16[3,128,128]{2,1,0:T(8,128)(2,1)S(1)}, u32[]{:S(2)}, u32[]{:S(2)}) collective-permute-start(bf16[3,128,128]{2,1,0:T(8,128)(2,1)S(1)} %get-tuple-element.38), channel_id=1, source_target_pairs={{0,16},{4,20},{8,24},{12,28},{16,0},{20,4},{24,8},{28,12},{1,17},{... | collective-permute-start | bytes 294920 | tf_op jit(solution)/shard_map/ppermute | solution.py:643
  46.9 7.4 %collective-permute-start.11 = (bf16[3,128,128]{2,1,0:T(8,128)(2,1)S(1)}, bf16[3,128,128]{2,1,0:T(8,128)(2,1)S(1)}, u32[]{:S(2)}, u32[]{:S(2)}) collective-permute-start(bf16[3,128,128]{2,1,0:T(8,128)(2,1)S(1)} %get-tuple-element.37), channel_id=1, source_target_pairs={{0,8},{4,12},{8,0},{12,4},{16,24},{20,28},{24,16},{28,20},{1,9},{5... | collective-permute-start | bytes 294920 | tf_op jit(solution)/shard_map/ppermute | solution.py:643
  46.9 7.9 %collective-permute-start.14 = (bf16[3,128,128]{2,1,0:T(8,128)(2,1)S(1)}, bf16[3,128,128]{2,1,0:T(8,128)(2,1)S(1)}, u32[]{:S(2)}, u32[]{:S(2)}) collective-permute-start(bf16[3,128,128]{2,1,0:T(8,128)(2,1)S(1)} %get-tuple-element.36.refs_10_.refs_0_), channel_id=1, source_target_pairs={{0,4},{4,0},{8,12},{12,8},{16,20},{20,16},{24,28},{28,24},{1,5},{5... | collective-permute-start | bytes 294920 | tf_op jit(solution)/shard_map/ppermute | solution.py:643
  53.7 1.5 %collective-permute-start.18 = (bf16[3,128,128]{2,1,0:T(8,128)(2,1)S(1)}, bf16[3,128,128]{2,1,0:T(8,128)(2,1)S(1)}, u32[]{:S(2)}, u32[]{:S(2)}) collective-permute-start(bf16[3,128,128]{2,1,0:T(8,128)(2,1)S(1)} %collective-permute-done.13.refs_3_), channel_id=1, source_target_pairs={{0,4},{4,0},{8,12},{12,8},{16,20},{20,16},{24,28},{28,24},{1,5},{5... | collective-permute-start | bytes 294920 | tf_op jit(solution)/shard_map/ppermute | solution.py:643
  54.2 1.3 %collective-permute-start.17 = (bf16[3,128,128]{2,1,0:T(8,128)(2,1)S(1)}, bf16[3,128,128]{2,1,0:T(8,128)(2,1)S(1)}, u32[]{:S(2)}, u32[]{:S(2)}) collective-permute-start(bf16[3,128,128]{2,1,0:T(8,128)(2,1)S(1)} %collective-permute-done.12.refs_2_), channel_id=1, source_target_pairs={{0,4},{4,0},{8,12},{12,8},{16,20},{20,16},{24,28},{28,24},{1,5},{5... | collective-permute-start | bytes 294920 | tf_op jit(solution)/shard_map/ppermute | solution.py:643
  54.3 1.4 %collective-permute-start.16 = (bf16[3,128,128]{2,1,0:T(8,128)(2,1)S(1)}, bf16[3,128,128]{2,1,0:T(8,128)(2,1)S(1)}, u32[]{:S(2)}, u32[]{:S(2)}) collective-permute-start(bf16[3,128,128]{2,1,0:T(8,128)(2,1)S(1)} %collective-permute-done.11.refs_1_), channel_id=1, source_target_pairs={{0,4},{4,0},{8,12},{12,8},{16,20},{20,16},{24,28},{28,24},{1,5},{5... | collective-permute-start | bytes 294920 | tf_op jit(solution)/shard_map/ppermute | solution.py:643

commit v9 on v8

--- a/solution.py
+++ b/solution.py
@@ -101,8 +101,8 @@
         for i, ref in enumerate((k_any, v_any))
     ]
     kinds = pltpu.make_async_copy(kind_any, kind_ref, in_sems.at[2])
+    start_all(ins)
     kinds.start()
-    start_all(ins)
     kinds.wait()
     put_order(kind_ref, order, spatial)
     early = early_any.shape[1]
@@ -682,8 +682,7 @@
     last = far
     if dealt:
         results = frames_call(arrived, far)
-        parts = [send(p, r) for p, r in zip(results[:0:-1], turned[::-1])]
-        parts = [results[0]] + parts[::-1]
+        parts = [results[0]] + [send(p, r) for p, r in zip(results[1:], turned)]
         last = results[0]
     mid = far_call(
         head_kind, operands, last, ahead, spatial - ahead - late, spatial, block

time: 57.5 us -> 57.5 us (level)
  no operation moved by 1% of the time
where the time goes in v9:
time: 57.5 us; the launch traced here: 57.3 us
  starting transfers between devices  26.6 us (46%)
  Pallas kernels  25.1 us (44%)
  waiting for transfers between devices  4.99 us (9%)
    pallas_call x12, Pallas kernels, call(): pl.pallas_call(kernel, out_shape=out_shape, in_specs=in_specs, out_specs=...  25.1 us
    ppermute x16, starting transfers between devices, per_device(): send = lambda x, route: lax.ppermute(x, 'seq', route)  19.8 us
    ppermute x2, starting transfers between devices, per_device(): lax.ppermute(total, 'head', [(i, i ^ d) for i in range(planes)])  4.23 us
    ppermute x2, waiting for transfers between devices, per_device(): lax.ppermute(total, 'head', [(i, i ^ d) for i in range(planes)])  3.99 us
    ppermute x1, starting transfers between devices, per_device(): lax.ppermute(total, ('seq', 'head'), [(i * planes + p, j * planes + (p ^...  2.57 us
  transfers between devices with their start and end apart: 19, of which 5 were waited for; matrix products, arithmetic and copies ran while one was open for 0% of the time, Pallas kernels for 36%

profile of v9, /device:TPU:0, one launch (start us, length us, event | category | flops | bytes accessed | tf_op | source)
XLA Modules:
  0.0 57.3 jit_solution(9240158814656889394)
XLA Ops:
  0.0 3.0 %pack.1 = (bf16[2,6,512,128]{3,2,1,0:T(8,128)(2,1)}, bf16[2,2,512,128]{3,2,1,0:T(8,128)(2,1)}) custom-call(s32[10]{0:T(128)} %kind_ref.17, bf16[768,1280]{1,0:T(8,128)(2,1)} %k_any.1, bf16[768,1280]{1,0:T(8,128)(2,1)} %refs_2_.5), custom_call_target="tpu_custom_call" | custom-call | flops 1000 | bytes 1000 | tf_op jit(solution)/shard_map/pack/pallas_call | solution.py:35
  3.0 0.0 copy-start.1
  3.0 0.0 copy-start.5
  3.0 0.5 collective-permute-start.7
  3.5 0.1 copy-done
  3.7 0.5 collective-permute-start.8
  4.1 5.5 %collective-permute-start.10 = (bf16[2,6,512,128]{3,2,1,0:T(8,128)(2,1)}, bf16[2,6,512,128]{3,2,1,0:T(8,128)(2,1)S(1)}, u32[]{:S(2)}, u32[]{:S(2)}) collective-permute-start(bf16[2,6,512,128]{3,2,1,0:T(8,128)(2,1)} %get-tuple-element.33), channel_id=1, source_target_pairs={{12,16},{16,12},{28,0},{0,28},{13,17},{17,13},{29,1},{1,29},{14,18... | collective-permute-start | bytes 4718600 | tf_op jit(solution)/shard_map/ppermute | solution.py:643
  9.6 0.5 key_sums.1.key_sums_ref
  10.1 0.0 copy-start.3
  10.1 0.0 copy-start.4
  10.1 1.1 %sums.1 = (f32[2,768]{1,0:T(2,128)S(1)}, bf16[3,768,128]{2,1,0:T(8,128)(2,1)S(1)}) custom-call(s32[10]{0:T(128)S(1)} %copy-done.5, bf16[768,1280]{1,0:T(8,128)(2,1)S(1)} %copy-done.1, bf16[768,1280]{1,0:T(8,128)(2,1)S(1)} %copy-done.2, bf16[768,1280]{1,0:T(8,128)(2,1)S(1)} %copy-done, f32[1,768]{1,0:T(1,128)S(1)} %key_sums.1.key_sums_ref), custom_call_target="tpu_custom_call" | custom-call | flops 1000 | bytes 1000 | tf_op jit(solution)/shard_map/sums/pallas_call | solution.py:35
  11.2 0.1 collective-permute-start.2
  11.3 1.6 %collective-permute-start = (f32[2,768]{1,0:T(2,128)S(1)}, f32[2,768]{1,0:T(2,128)S(1)}, u32[]{:S(2)}, u32[]{:S(2)}) collective-permute-start(f32[2,768]{1,0:T(2,128)S(1)} %get-tuple-element.25), channel_id=1, source_target_pairs={{0,1},{1,0},{2,3},{3,2},{4,5},{5,4},{6,7},{7,6},{8,9},{9,8},{10,11... | collective-permute-start | bytes 18440 | tf_op jit(solution)/shard_map/ppermute | solution.py:655
  12.9 2.1 %collective-permute-done = f32[2,768]{1,0:T(2,128)S(1)} collective-permute-done((f32[2,768]{1,0:T(2,128)S(1)}, f32[2,768]{1,0:T(2,128)S(1)}, u32[]{:S(2)}, u32[]{:S(2)}) %collective-permute-start) | collective-permute-done | bytes 6176 | tf_op jit(solution)/shard_map/ppermute | solution.py:655
  15.0 2.6 %collective-permute-start.1 = (f32[2,768]{1,0:T(2,128)S(1)}, f32[2,768]{1,0:T(2,128)S(1)}, u32[]{:S(2)}, u32[]{:S(2)}) collective-permute-start(f32[2,768]{1,0:T(2,128)S(1)} %add.6), channel_id=1, source_target_pairs={{0,2},{1,3},{2,0},{3,1},{4,6},{5,7},{6,4},{7,5},{8,10},{9,11},{10,... | collective-permute-start | bytes 18440 | tf_op jit(solution)/shard_map/ppermute | solution.py:655
  17.6 1.9 %collective-permute-done.1 = f32[2,768]{1,0:T(2,128)S(1)} collective-permute-done((f32[2,768]{1,0:T(2,128)S(1)}, f32[2,768]{1,0:T(2,128)S(1)}, u32[]{:S(2)}, u32[]{:S(2)}) %collective-permute-start.1) | collective-permute-done | bytes 6176 | tf_op jit(solution)/shard_map/ppermute | solution.py:655
  19.5 0.0 collective-permute-done.2.refs_0_.got_ref
  19.6 1.3 %own.1 = (bf16[8,768,128]{2,1,0:T(8,128)(2,1)S(1)}, bf16[3,768,128]{2,1,0:T(8,128)(2,1)S(1)}) custom-call(s32[10]{0:T(128)S(1)} %copy-done.5, bf16[768,1280]{1,0:T(8,128)(2,1)S(1)} %copy-done.1, bf16[768,1280]{1,0:T(8,128)(2,1)S(1)} %copy-done.2, bf16[768,1280]{1,0:T(8,128)(2,1)S(1)} %copy-done, f32[1280]{0:T(1024)S(1)} %copy-done.4, f32[1280]{0:T(1024)S(1)} %copy-done.3, ...), custom_call_target="tpu_custom_call" | custom-call | flops 1000 | bytes 1000 | tf_op jit(solution)/shard_map/own/pallas_call | solution.py:35
  20.9 1.0 %deal.1 = (bf16[3,3,128,128]{3,2,1,0:T(8,128)(2,1)S(1)}, bf16[3,3,128,128]{3,2,1,0:T(8,128)(2,1)S(1)}, bf16[3,3,128,128]{3,2,1,0:T(8,128)(2,1)S(1)}, bf16[3,3,128,128]{3,2,1,0:T(8,128)(2,1)S(1)}) custom-call(s32[10]{0:T(128)S(1)} %copy-done.5, bf16[3,768,128]{2,1,0:T(8,128)(2,1)S(1)} %get-tuple-element.27.own_ref, ...), custom_call_target="tpu_custom_call" | custom-call | flops 1000 | bytes 1000 | tf_op jit(solution)/shard_map/deal/pallas_call | solution.py:35
  21.9 0.5 collective-permute-start.4
  22.4 0.4 collective-permute-start.5
  22.9 0.0 collective-permute-done.7.k_ref
  22.9 2.6 %collective-permute-start.6 = (bf16[3,3,128,128]{3,2,1,0:T(8,128)(2,1)S(1)}, bf16[3,3,128,128]{3,2,1,0:T(8,128)(2,1)S(1)}, u32[]{:S(2)}, u32[]{:S(2)}) collective-permute-start(bf16[3,3,128,128]{3,2,1,0:T(8,128)(2,1)S(1)} %get-tuple-element.31), channel_id=1, source_target_pairs={{0,24},{4,28},{8,16},{12,20},{16,8},{20,12},{24,0},{28,4},{1,25},{... | collective-permute-start | bytes 884744 | tf_op jit(solution)/shard_map/ppermute | solution.py:643
  25.5 0.0 collective-permute-done.8.v_pair_ref.refs_4_
  25.5 2.6 %collective-permute-start.9 = (f32[2,768]{1,0:T(2,128)S(1)}, f32[2,768]{1,0:T(2,128)S(1)}, u32[]{:S(2)}, u32[]{:S(2)}) collective-permute-start(f32[2,768]{1,0:T(2,128)S(1)} %add.7.total_ref.refs_7_), channel_id=1, source_target_pairs={{12,17},{13,16},{14,19},{15,18},{16,13},{17,12},{18,15},{19,14},{2... | collective-permute-start | bytes 18440 | tf_op jit(solution)/shard_map/ppermute | solution.py:659
  28.0 1.1 %pair.1.kp_ref.refs_3_ = bf16[8,768,128]{2,1,0:T(8,128)(2,1)S(1)} custom-call(s32[10]{0:T(128)S(1)} %copy-done.5, bf16[768,1280]{1,0:T(8,128)(2,1)S(1)} %collective-permute-done.7.k_ref, f32[1280]{0:T(1024)S(1)} %copy-done.3, f32[2,768]{1,0:T(2,128)S(1)} %collective-permute-done.3.sums_ref, bf16[3,3,128,128]{3,2,1,0:T(8,128)(2,1)S(1)} %get-tuple-element.28.after_ref.refs_0_), custom_call_target="tpu_custom_call" | custom-call | flops 1000 | bytes 1000 | tf_op jit(solution)/shard_map/pair/pallas_call | solution.py:35
  29.2 4.0 %near.1.refs_10_.refs_11_ = bf16[8,256,128]{2,1,0:T(8,128)(2,1)S(1)} custom-call(s32[10]{0:T(128)S(1)} %copy-done.5, bf16[768,1280]{1,0:T(8,128)(2,1)S(1)} %copy-done.1, bf16[8,768,128]{2,1,0:T(8,128)(2,1)S(1)} %get-tuple-element.32.k_ref.refs_1_, bf16[768,1280]{1,0:T(8,128)(2,1)S(1)} %copy-done, bf16[8,768,128]{2,1,0:T(8,128)(2,1)S(1)} %pair.1.kp_ref.refs_3_, ...), custom_call_target="tpu_custom_call" | custom-call | flops 1000 | bytes 1000 | tf_op jit(solution)/shard_map/near/pallas_call | solution.py:35
  33.2 0.0 collective-permute-done.10.refs_9_
  33.2 3.1 %far.2.refs_4_.refs_12_ = bf16[3,512,128]{2,1,0:T(8,128)(2,1)S(1)} custom-call(s32[10]{0:T(128)S(1)} %copy-done.5, bf16[768,1280]{1,0:T(8,128)(2,1)S(1)} %copy-done.1, bf16[8,768,128]{2,1,0:T(8,128)(2,1)S(1)} %get-tuple-element.32.k_ref.refs_1_, bf16[768,1280]{1,0:T(8,128)(2,1)S(1)} %copy-done, bf16[8,768,128]{2,1,0:T(8,128)(2,1)S(1)} %pair.1.kp_ref.refs_3_, ...), custom_call_target="tpu_custom_call" | custom-call | flops 1000 | bytes 1000 | tf_op jit(solution)/shard_map/far/pallas_call | solution.py:35
  36.4 5.1 %collective-permute-start.15 = (bf16[2,2,512,128]{3,2,1,0:T(8,128)(2,1)S(1)}, bf16[2,2,512,128]{3,2,1,0:T(8,128)(2,1)S(1)}, u32[]{:S(2)}, u32[]{:S(2)}) collective-permute-start(bf16[2,2,512,128]{3,2,1,0:T(8,128)(2,1)S(1)} %copy-done.6), channel_id=1, source_target_pairs={{12,16},{16,12},{28,0},{0,28},{13,17},{17,13},{29,1},{1,29},{14,18... | collective-permute-start | bytes 1572872 | tf_op jit(solution)/shard_map/ppermute | solution.py:643
  41.5 0.0 collective-permute-done.5.refs_2_
  41.5 0.0 collective-permute-done.6.refs_3_
  41.5 1.8 %frames.1 = (bf16[3,128,128]{2,1,0:T(8,128)(2,1)S(1)}, bf16[3,128,128]{2,1,0:T(8,128)(2,1)S(1)}, bf16[3,128,128]{2,1,0:T(8,128)(2,1)S(1)}, bf16[3,128,128]{2,1,0:T(8,128)(2,1)S(1)}) custom-call(bf16[3,3,128,128]{3,2,1,0:T(8,128)(2,1)S(1)} %get-tuple-element.28.after_ref.refs_0_, bf16[3,3,128,128]{3,2,1,0:T(8,128)(2,1)S(1)} %collective-permute-done.4.refs_1_, ...), custom_call_target="tpu_custom_call" | custom-call | flops 10000000000 | bytes 1000 | tf_op jit(solution)/shard_map/frames/pallas_call | solution.py:35
  43.4 2.5 %collective-permute-start.13 = (bf16[3,128,128]{2,1,0:T(8,128)(2,1)S(1)}, bf16[3,128,128]{2,1,0:T(8,128)(2,1)S(1)}, u32[]{:S(2)}, u32[]{:S(2)}) collective-permute-start(bf16[3,128,128]{2,1,0:T(8,128)(2,1)S(1)} %get-tuple-element.39), channel_id=1, source_target_pairs={{0,24},{4,28},{8,16},{12,20},{16,8},{20,12},{24,0},{28,4},{1,25},{... | collective-permute-start | bytes 294920 | tf_op jit(solution)/shard_map/ppermute | solution.py:643
  45.8 1.1 %collective-permute-start.12 = (bf16[3,128,128]{2,1,0:T(8,128)(2,1)S(1)}, bf16[3,128,128]{2,1,0:T(8,128)(2,1)S(1)}, u32[]{:S(2)}, u32[]{:S(2)}) collective-permute-start(bf16[3,128,128]{2,1,0:T(8,128)(2,1)S(1)} %get-tuple-element.38), channel_id=1, source_target_pairs={{0,16},{4,20},{8,24},{12,28},{16,0},{20,4},{24,8},{28,12},{1,17},{... | collective-permute-start | bytes 294920 | tf_op jit(solution)/shard_map/ppermute | solution.py:643
  46.9 0.0 collective-permute-start.11
  46.9 3.2 %far.3.refs_13_ = bf16[3,512,128]{2,1,0:T(8,128)(2,1)S(1)} custom-call(s32[10]{0:T(128)S(1)} %copy-done.5, bf16[768,1280]{1,0:T(8,128)(2,1)S(1)} %copy-done.1, bf16[8,768,128]{2,1,0:T(8,128)(2,1)S(1)} %get-tuple-element.32.k_ref.refs_1_, bf16[768,1280]{1,0:T(8,128)(2,1)S(1)} %copy-done, bf16[8,768,128]{2,1,0:T(8,128)(2,1)S(1)} %pair.1.kp_ref.refs_3_, ...), custom_call_target="tpu_custom_call" | custom-call | flops 1000 | bytes 1000 | tf_op jit(solution)/shard_map/far/pallas_call | solution.py:35
  50.1 0.0 collective-permute-done.15.refs_10_
  50.1 3.5 %rest.1.refs_8_ = bf16[768,1280]{1,0:T(8,128)(2,1)} custom-call(s32[10]{0:T(128)S(1)} %copy-done.5, bf16[768,1280]{1,0:T(8,128)(2,1)S(1)} %copy-done.1, bf16[8,768,128]{2,1,0:T(8,128)(2,1)S(1)} %get-tuple-element.32.k_ref.refs_1_, bf16[768,1280]{1,0:T(8,128)(2,1)S(1)} %copy-done, bf16[8,768,128]{2,1,0:T(8,128)(2,1)S(1)} %pair.1.kp_ref.refs_3_, ...), custom_call_target="tpu_custom_call" | custom-call | flops 1000 | bytes 1000 | tf_op jit(solution)/shard_map/rest/pallas_call | solution.py:35
  53.6 0.6 collective-permute-start.18
  54.2 0.0 collective-permute-done.12.refs_2_
  54.2 0.1 collective-permute-start.17
  54.3 0.4 collective-permute-start.16
  54.7 0.0 collective-permute-done.14.refs_4_
  54.7 0.4 collective-permute-done.18.refs_7_
  55.1 0.4 collective-permute-done.17.refs_6_
  55.5 0.2 collective-permute-done.16.refs_5_
  55.6 1.5 %place.1 = bf16[768,1280]{1,0:T(8,128)(2,1)} custom-call(s32[10]{0:T(128)S(1)} %copy-done.5, bf16[3,128,128]{2,1,0:T(8,128)(2,1)S(1)} %get-tuple-element.36.refs_10_.refs_0_, bf16[3,128,128]{2,1,0:T(8,128)(2,1)S(1)} %collective-permute-done.11.refs_1_, bf16[3,128,128]{2,1,0:T(8,128)(2,1)S(1)} %collective-permute-done.12.refs_2_, ...), custom_call_target="tpu_custom_call", output_to_operand_aliasing={{}: (9, {})} | custom-call | flops 1000 | bytes 1000 | tf_op jit(solution)/shard_map/place/pallas_call | solution.py:35
  (18 shorter events, 0.0 us)
Async XLA Ops:
  0.0 3.0 %copy-start.2 = (bf16[768,1280]{1,0:T(8,128)(2,1)S(1)}, bf16[768,1280]{1,0:T(8,128)(2,1)}, u32[]{:S(2)}) copy-start(bf16[768,1280]{1,0:T(8,128)(2,1)} %k_any.1) | copy-start | bytes 5898244
  0.0 3.7 %copy-start = (bf16[768,1280]{1,0:T(8,128)(2,1)S(1)}, bf16[768,1280]{1,0:T(8,128)(2,1)}, u32[]{:S(2)}) copy-start(bf16[768,1280]{1,0:T(8,128)(2,1)} %refs_2_.5) | copy-start | bytes 5898244
  3.0 7.0 %copy-start.1 = (bf16[768,1280]{1,0:T(8,128)(2,1)S(1)}, bf16[768,1280]{1,0:T(8,128)(2,1)}, u32[]{:S(2)}) copy-start(bf16[768,1280]{1,0:T(8,128)(2,1)} %refs_0_.5) | copy-start | bytes 5898244
  3.0 7.0 %copy-start.5 = (s32[10]{0:T(128)S(1)}, s32[10]{0:T(128)}, u32[]{:S(2)}) copy-start(s32[10]{0:T(128)} %kind_ref.17) | copy-start | bytes 124
  3.0 19.8 %collective-permute-start.7 = (bf16[768,1280]{1,0:T(8,128)(2,1)S(1)}, bf16[768,1280]{1,0:T(8,128)(2,1)S(1)}, u32[]{:S(2)}, u32[]{:S(2)}) collective-permute-start(bf16[768,1280]{1,0:T(8,128)(2,1)S(1)} %copy-done.2), channel_id=1, source_target_pairs={{0,4},{4,0},{8,12},{12,8},{16,20},{20,16},{24,28},{28,24},{1,5},{5... | collective-permute-start | bytes 5898248 | tf_op jit(solution)/shard_map/ppermute | solution.py:643
  3.7 21.8 %collective-permute-start.8 = (bf16[768,1280]{1,0:T(8,128)(2,1)S(1)}, bf16[768,1280]{1,0:T(8,128)(2,1)S(1)}, u32[]{:S(2)}, u32[]{:S(2)}) collective-permute-start(bf16[768,1280]{1,0:T(8,128)(2,1)S(1)} %copy-done), channel_id=1, source_target_pairs={{0,4},{4,0},{8,12},{12,8},{16,20},{20,16},{24,28},{28,24},{1,5},{5... | collective-permute-start | bytes 5898248 | tf_op jit(solution)/shard_map/ppermute | solution.py:643
  4.1 29.1 %collective-permute-start.10 = (bf16[2,6,512,128]{3,2,1,0:T(8,128)(2,1)}, bf16[2,6,512,128]{3,2,1,0:T(8,128)(2,1)S(1)}, u32[]{:S(2)}, u32[]{:S(2)}) collective-permute-start(bf16[2,6,512,128]{3,2,1,0:T(8,128)(2,1)} %get-tuple-element.33), channel_id=1, source_target_pairs={{12,16},{16,12},{28,0},{0,28},{13,17},{17,13},{29,1},{1,29},{14,18... | collective-permute-start | bytes 4718600 | tf_op jit(solution)/shard_map/ppermute | solution.py:643
  10.1 9.5 %copy-start.3 = (f32[1280]{0:T(1024)S(1)}, f32[1280]{0:T(1024)}, u32[]{:S(2)}) copy-start(f32[1280]{0:T(1024)} %refs_6_.5) | copy-start | bytes 15364
  10.1 9.5 %copy-start.4 = (f32[1280]{0:T(1024)S(1)}, f32[1280]{0:T(1024)}, u32[]{:S(2)}) copy-start(f32[1280]{0:T(1024)} %refs_5_.5) | copy-start | bytes 15364
  11.2 8.3 %collective-permute-start.2 = (bf16[3,768,128]{2,1,0:T(8,128)(2,1)S(1)}, bf16[3,768,128]{2,1,0:T(8,128)(2,1)S(1)}, u32[]{:S(2)}, u32[]{:S(2)}) collective-permute-start(bf16[3,768,128]{2,1,0:T(8,128)(2,1)S(1)} %get-tuple-element.26), channel_id=1, source_target_pairs={{0,4},{4,0},{8,12},{12,8},{16,20},{20,16},{24,28},{28,24},{1,5},{5... | collective-permute-start | bytes 1769480 | tf_op jit(solution)/shard_map/ppermute | solution.py:643
  11.3 3.7 %collective-permute-start = (f32[2,768]{1,0:T(2,128)S(1)}, f32[2,768]{1,0:T(2,128)S(1)}, u32[]{:S(2)}, u32[]{:S(2)}) collective-permute-start(f32[2,768]{1,0:T(2,128)S(1)} %get-tuple-element.25), channel_id=1, source_target_pairs={{0,1},{1,0},{2,3},{3,2},{4,5},{5,4},{6,7},{7,6},{8,9},{9,8},{10,11... | collective-permute-start | bytes 18440 | tf_op jit(solution)/shard_map/ppermute | solution.py:655
  15.0 4.5 %collective-permute-start.1 = (f32[2,768]{1,0:T(2,128)S(1)}, f32[2,768]{1,0:T(2,128)S(1)}, u32[]{:S(2)}, u32[]{:S(2)}) collective-permute-start(f32[2,768]{1,0:T(2,128)S(1)} %add.6), channel_id=1, source_target_pairs={{0,2},{1,3},{2,0},{3,1},{4,6},{5,7},{6,4},{7,5},{8,10},{9,11},{10,... | collective-permute-start | bytes 18440 | tf_op jit(solution)/shard_map/ppermute | solution.py:655
  19.5 1.3 %collective-permute-start.3 = (f32[2,768]{1,0:T(2,128)S(1)}, f32[2,768]{1,0:T(2,128)S(1)}, u32[]{:S(2)}, u32[]{:S(2)}) collective-permute-start(f32[2,768]{1,0:T(2,128)S(1)} %add.7.total_ref.refs_7_), channel_id=1, source_target_pairs={{0,4},{4,0},{8,12},{12,8},{16,20},{20,16},{24,28},{28,24},{1,5},{5... | collective-permute-start | bytes 18440 | tf_op jit(solution)/shard_map/ppermute | solution.py:643
  21.9 19.6 %collective-permute-start.4 = (bf16[3,3,128,128]{3,2,1,0:T(8,128)(2,1)S(1)}, bf16[3,3,128,128]{3,2,1,0:T(8,128)(2,1)S(1)}, u32[]{:S(2)}, u32[]{:S(2)}) collective-permute-start(bf16[3,3,128,128]{3,2,1,0:T(8,128)(2,1)S(1)} %get-tuple-element.29), channel_id=1, source_target_pairs={{0,8},{4,12},{8,0},{12,4},{16,24},{20,28},{24,16},{28,20},{1,9},{5... | collective-permute-start | bytes 884744 | tf_op jit(solution)/shard_map/ppermute | solution.py:643
  22.4 19.1 %collective-permute-start.5 = (bf16[3,3,128,128]{3,2,1,0:T(8,128)(2,1)S(1)}, bf16[3,3,128,128]{3,2,1,0:T(8,128)(2,1)S(1)}, u32[]{:S(2)}, u32[]{:S(2)}) collective-permute-start(bf16[3,3,128,128]{3,2,1,0:T(8,128)(2,1)S(1)} %get-tuple-element.30), channel_id=1, source_target_pairs={{0,16},{4,20},{8,24},{12,28},{16,0},{20,4},{24,8},{28,12},{1,17},{... | collective-permute-start | bytes 884744 | tf_op jit(solution)/shard_map/ppermute | solution.py:643
  22.9 18.6 %collective-permute-start.6 = (bf16[3,3,128,128]{3,2,1,0:T(8,128)(2,1)S(1)}, bf16[3,3,128,128]{3,2,1,0:T(8,128)(2,1)S(1)}, u32[]{:S(2)}, u32[]{:S(2)}) collective-permute-start(bf16[3,3,128,128]{3,2,1,0:T(8,128)(2,1)S(1)} %get-tuple-element.31), channel_id=1, source_target_pairs={{0,24},{4,28},{8,16},{12,20},{16,8},{20,12},{24,0},{28,4},{1,25},{... | collective-permute-start | bytes 884744 | tf_op jit(solution)/shard_map/ppermute | solution.py:643
  25.5 7.7 %collective-permute-start.9 = (f32[2,768]{1,0:T(2,128)S(1)}, f32[2,768]{1,0:T(2,128)S(1)}, u32[]{:S(2)}, u32[]{:S(2)}) collective-permute-start(f32[2,768]{1,0:T(2,128)S(1)} %add.7.total_ref.refs_7_), channel_id=1, source_target_pairs={{12,17},{13,16},{14,19},{15,18},{16,13},{17,12},{18,15},{19,14},{2... | collective-permute-start | bytes 18440 | tf_op jit(solution)/shard_map/ppermute | solution.py:659
  33.2 3.2 %copy-start.6 = (bf16[2,2,512,128]{3,2,1,0:T(8,128)(2,1)S(1)}, bf16[2,2,512,128]{3,2,1,0:T(8,128)(2,1)}, u32[]{:S(2)}) copy-start(bf16[2,2,512,128]{3,2,1,0:T(8,128)(2,1)} %get-tuple-element.41) | copy-start | bytes 1572868
  36.4 13.7 %collective-permute-start.15 = (bf16[2,2,512,128]{3,2,1,0:T(8,128)(2,1)S(1)}, bf16[2,2,512,128]{3,2,1,0:T(8,128)(2,1)S(1)}, u32[]{:S(2)}, u32[]{:S(2)}) collective-permute-start(bf16[2,2,512,128]{3,2,1,0:T(8,128)(2,1)S(1)} %copy-done.6), channel_id=1, source_target_pairs={{12,16},{16,12},{28,0},{0,28},{13,17},{17,13},{29,1},{1,29},{14,18... | collective-permute-start | bytes 1572872 | tf_op jit(solution)/shard_map/ppermute | solution.py:643
  43.4 10.3 %collective-permute-start.13 = (bf16[3,128,128]{2,1,0:T(8,128)(2,1)S(1)}, bf16[3,128,128]{2,1,0:T(8,128)(2,1)S(1)}, u32[]{:S(2)}, u32[]{:S(2)}) collective-permute-start(bf16[3,128,128]{2,1,0:T(8,128)(2,1)S(1)} %get-tuple-element.39), channel_id=1, source_target_pairs={{0,24},{4,28},{8,16},{12,20},{16,8},{20,12},{24,0},{28,4},{1,25},{... | collective-permute-start | bytes 294920 | tf_op jit(solution)/shard_map/ppermute | solution.py:643
  45.8 8.4 %collective-permute-start.12 = (bf16[3,128,128]{2,1,0:T(8,128)(2,1)S(1)}, bf16[3,128,128]{2,1,0:T(8,128)(2,1)S(1)}, u32[]{:S(2)}, u32[]{:S(2)}) collective-permute-start(bf16[3,128,128]{2,1,0:T(8,128)(2,1)S(1)} %get-tuple-element.38), channel_id=1, source_target_pairs={{0,16},{4,20},{8,24},{12,28},{16,0},{20,4},{24,8},{28,12},{1,17},{... | collective-permute-start | bytes 294920 | tf_op jit(solution)/shard_map/ppermute | solution.py:643
  46.9 7.4 %collective-permute-start.11 = (bf16[3,128,128]{2,1,0:T(8,128)(2,1)S(1)}, bf16[3,128,128]{2,1,0:T(8,128)(2,1)S(1)}, u32[]{:S(2)}, u32[]{:S(2)}) collective-permute-start(bf16[3,128,128]{2,1,0:T(8,128)(2,1)S(1)} %get-tuple-element.37), channel_id=1, source_target_pairs={{0,8},{4,12},{8,0},{12,4},{16,24},{20,28},{24,16},{28,20},{1,9},{5... | collective-permute-start | bytes 294920 | tf_op jit(solution)/shard_map/ppermute | solution.py:643
  46.9 7.8 %collective-permute-start.14 = (bf16[3,128,128]{2,1,0:T(8,128)(2,1)S(1)}, bf16[3,128,128]{2,1,0:T(8,128)(2,1)S(1)}, u32[]{:S(2)}, u32[]{:S(2)}) collective-permute-start(bf16[3,128,128]{2,1,0:T(8,128)(2,1)S(1)} %get-tuple-element.36.refs_10_.refs_0_), channel_id=1, source_target_pairs={{0,4},{4,0},{8,12},{12,8},{16,20},{20,16},{24,28},{28,24},{1,5},{5... | collective-permute-start | bytes 294920 | tf_op jit(solution)/shard_map/ppermute | solution.py:643
  53.6 1.5 %collective-permute-start.18 = (bf16[3,128,128]{2,1,0:T(8,128)(2,1)S(1)}, bf16[3,128,128]{2,1,0:T(8,128)(2,1)S(1)}, u32[]{:S(2)}, u32[]{:S(2)}) collective-permute-start(bf16[3,128,128]{2,1,0:T(8,128)(2,1)S(1)} %collective-permute-done.13.refs_3_), channel_id=1, source_target_pairs={{0,4},{4,0},{8,12},{12,8},{16,20},{20,16},{24,28},{28,24},{1,5},{5... | collective-permute-start | bytes 294920 | tf_op jit(solution)/shard_map/ppermute | solution.py:643
  54.2 1.3 %collective-permute-start.17 = (bf16[3,128,128]{2,1,0:T(8,128)(2,1)S(1)}, bf16[3,128,128]{2,1,0:T(8,128)(2,1)S(1)}, u32[]{:S(2)}, u32[]{:S(2)}) collective-permute-start(bf16[3,128,128]{2,1,0:T(8,128)(2,1)S(1)} %collective-permute-done.12.refs_2_), channel_id=1, source_target_pairs={{0,4},{4,0},{8,12},{12,8},{16,20},{20,16},{24,28},{28,24},{1,5},{5... | collective-permute-start | bytes 294920 | tf_op jit(solution)/shard_map/ppermute | solution.py:643
  54.3 1.4 %collective-permute-start.16 = (bf16[3,128,128]{2,1,0:T(8,128)(2,1)S(1)}, bf16[3,128,128]{2,1,0:T(8,128)(2,1)S(1)}, u32[]{:S(2)}, u32[]{:S(2)}) collective-permute-start(bf16[3,128,128]{2,1,0:T(8,128)(2,1)S(1)} %collective-permute-done.11.refs_1_), channel_id=1, source_target_pairs={{0,4},{4,0},{8,12},{12,8},{16,20},{20,16},{24,28},{28,24},{1,5},{5... | collective-permute-start | bytes 294920 | tf_op jit(solution)/shard_map/ppermute | solution.py:643
